TPU v7x, 32 devices: a whole 2x2x4 slice. The times are simulated.
32 devices in a mesh: seq: 8 (over z, x), chan: 4 (over y, core).
Axes of the slice: x: 2, y: 2, z: 4, core: 2. Of those that a mesh axis runs over, the one named last changes fastest.
Arguments:
- residual_in: bfloat16 [8, 1024, 2048], P(None, 'seq', 'chan'), may hold values from -6 to 6
- norm_gain: bfloat16 [2048], replicated, may hold values from 0.5 to 1.5
- in_weight: bfloat16 [2048, 2, 4096], P(None, None, 'chan'), may hold values from -0.125 to 0.125
- conv_weight: bfloat16 [4, 4096], P(None, 'chan'), may hold values from -3 to 3
- conv_bias: bfloat16 [4096], P('chan'), may hold values from -3 to 3
- proj_weight: bfloat16 [160, 4096], P(None, 'chan')
- step_weight: bfloat16 [128, 4096], P(None, 'chan'), may hold values from -0.25 to 0.25
- step_bias: bfloat16 [4096], P('chan')
- decay_log: float32 [16, 4096], P(None, 'chan'), may hold values from 0 to 2.77
- skip_gain: float32 [4096], P('chan'), may hold values from 0.5 to 1.5
- out_weight: bfloat16 [2048, 4096], P(None, 'chan'), may hold values from -0.09375 to 0.09375
- out_grad: bfloat16 [8, 1024, 2048], P(None, 'seq', 'chan'), may hold values from -6 to 6
Outputs:
- block_out: bfloat16 [8, 1024, 2048], P(None, 'seq', 'chan')
- in_grad: bfloat16 [8, 1024, 2048], P(None, 'seq', 'chan')
- gain_grad: float32 [2048], P('chan')
- in_weight_grad: float32 [2048, 2, 4096], P('seq', None, 'chan')
- conv_weight_grad: float32 [4, 4096], P(None, 'chan')
- conv_bias_grad: float32 [4096], P('chan')
- proj_weight_grad: float32 [160, 4096], P('seq', 'chan')
- step_weight_grad: float32 [128, 4096], P('seq', 'chan')
- step_bias_grad: float32 [4096], P('chan')
- decay_log_grad: float32 [16, 4096], P(None, 'chan')
- skip_gain_grad: float32 [4096], P('chan')
- out_weight_grad: float32 [2048, 4096], P('seq', 'chan')
All inputs are finite; a program needn't handle non-finite values.
Results may differ from a plain program's by a relative error of at most 0.011.
Values may be sent and summed in bfloat16 or wider, within the bound.
No kernel may reach another device: no remote copies, remote signals or barrier semaphores. Data moves between devices by JAX's collectives and lax.ppermute only.
A program may use at most 320 MiB of HBM per device.

v0:
```python
import math

import jax
import jax.numpy as jnp
from jax import lax
from jax.sharding import PartitionSpec as P

EPSILON = 1e-05


def passed_along(block, axis, distance):
    devices = range(lax.axis_size(axis))
    route = [(i - distance, i) for i in devices if i - distance in devices]
    return lax.ppermute(block, axis, route)


def entering_2(x, axis, combine, identity, reverse):
    count, index = (lax.axis_size(axis), lax.axis_index(axis))
    everything = jax.tree.map(lambda part: lax.all_gather(part, axis), x)
    start = jax.tree.map(
        lambda part, zero: jnp.broadcast_to(jnp.asarray(zero, part.dtype), part.shape), x, identity
    )

    def turn(k, before):
        at = count - 1 - k if reverse else k
        reached = at > index if reverse else at < index
        new = combine(before, jax.tree.map(lambda part: part[at], everything))
        return jax.tree.map(lambda a, b: jnp.where(reached, a, b), new, before)

    return lax.fori_loop(0, count, turn, start)


def link(earlier, later):
    return (earlier[0] * later[0], later[0] * earlier[1] + later[1])


def silu_slope(pre_value):
    sigmoid_value = jax.nn.sigmoid(pre_value)
    return sigmoid_value * (1.0 + pre_value * (1.0 - sigmoid_value))


def chain_scan(decay, drive, reverse):
    length = decay.shape[0]
    group_len = math.gcd(length, 8)
    groups = length // group_len
    shaped = (groups, group_len) + decay.shape[1:]
    decay_g = decay.reshape(shaped)
    drive_g = drive.reshape(shaped)
    coef_list = [None] * group_len
    acc_list = [None] * group_len
    carry = jnp.zeros(decay.shape[1:], jnp.float32)
    entries = [None] * groups
    if not reverse:
        coef_list[0] = decay_g[:, 0]
        acc_list[0] = drive_g[:, 0]
        for inner_pos in range(1, group_len):
            coef_list[inner_pos] = decay_g[:, inner_pos] * coef_list[inner_pos - 1]
            acc_list[inner_pos] = (
                decay_g[:, inner_pos] * acc_list[inner_pos - 1] + drive_g[:, inner_pos]
            )
        for group_pos in range(groups):
            entries[group_pos] = carry
            carry = acc_list[-1][group_pos] + coef_list[-1][group_pos] * carry
    else:
        coef_list[-1] = jnp.ones_like(decay_g[:, 0])
        acc_list[-1] = drive_g[:, -1]
        for inner_pos in range(group_len - 2, -1, -1):
            coef_list[inner_pos] = decay_g[:, inner_pos + 1] * coef_list[inner_pos + 1]
            acc_list[inner_pos] = (
                drive_g[:, inner_pos] + decay_g[:, inner_pos + 1] * acc_list[inner_pos + 1]
            )
        for group_pos in range(groups - 1, -1, -1):
            entries[group_pos] = carry
            carry = decay_g[group_pos, 0] * (
                acc_list[0][group_pos] + coef_list[0][group_pos] * carry
            )
    entering = jnp.stack(entries, axis=0)[:, None]
    coefs = jnp.stack(coef_list, axis=1)
    accums = jnp.stack(acc_list, axis=1)
    return (accums + coefs * entering).reshape(decay.shape)


def shards(
    residual_in,
    norm_gain,
    in_weight,
    conv_weight,
    conv_bias,
    proj_weight,
    step_weight,
    step_bias,
    decay_log,
    skip_gain,
    out_weight,
    out_grad,
):
    seq_count, tok_count, share_width = residual_in.shape
    model_width = norm_gain.shape[0]
    kernel, inner_width = conv_weight.shape
    state_width = decay_log.shape[0]
    rank_width = step_weight.shape[0]
    row_count = seq_count * tok_count
    contract_last = (((1,), (1,)), ((), ()))
    contract_first = (((0,), (0,)), ((), ()))
    gathered = lax.all_gather(residual_in, "chan", axis=2, tiled=True)
    full_in = gathered.astype(jnp.float32)
    inv_rms = lax.rsqrt(jnp.mean(full_in * full_in, axis=-1, keepdims=True) + EPSILON)
    gain_full = norm_gain.astype(jnp.float32)
    normed = (full_in * inv_rms * gain_full).astype(jnp.bfloat16).reshape(row_count, model_width)
    in_flat = in_weight.reshape(model_width, 2 * inner_width)
    projected_in = jnp.dot(normed, in_flat, preferred_element_type=jnp.float32).reshape(
        seq_count, tok_count, 2, inner_width
    )
    conv_in = projected_in[:, :, 0].astype(jnp.bfloat16)
    gate_pre = projected_in[:, :, 1]
    previous = passed_along(conv_in[:, tok_count - (kernel - 1) :], "seq", 1)
    padded = jnp.concatenate([previous, conv_in], axis=1).astype(jnp.float32)
    conv_taps = conv_weight.astype(jnp.float32)
    conv_out = conv_bias.astype(jnp.float32) + sum(
        (conv_taps[offset] * padded[:, offset : offset + tok_count] for offset in range(kernel))
    )
    mixed_in = jax.nn.silu(conv_out).astype(jnp.bfloat16)
    mixed_flat = mixed_in.reshape(row_count, inner_width)
    mixed_f = mixed_in.astype(jnp.float32)
    partial_proj = lax.dot_general(
        mixed_flat, proj_weight, contract_last, preferred_element_type=jnp.float32
    )
    projected = lax.psum(partial_proj, "chan")
    step_low = projected[:, :rank_width].astype(jnp.bfloat16)
    b_seq_all = projected[:, rank_width : rank_width + state_width].reshape(
        seq_count, tok_count, state_width
    )
    c_seq_all = projected[:, rank_width + state_width :].reshape(seq_count, tok_count, state_width)
    step_pre = jnp.dot(
        step_low, step_weight, preferred_element_type=jnp.float32
    ) + step_bias.astype(jnp.float32)
    step_size = jax.nn.softplus(step_pre).reshape(seq_count, tok_count, inner_width)
    decay_rate = -jnp.exp(decay_log)
    cumul = jnp.cumsum(step_size, axis=1)

    def local_forward(inputs_seq):
        step_seq, mixed_seq, b_seq, c_seq = inputs_seq
        decay_seq = jnp.exp(step_seq[:, None, :] * decay_rate)
        drive_seq = b_seq[:, :, None] * (step_seq * mixed_seq)[:, None, :]
        local_h = chain_scan(decay_seq, drive_seq, False)
        return (jnp.sum(c_seq[:, :, None] * local_h, axis=1), local_h[-1])

    local_out, last_state = lax.map(local_forward, (step_size, mixed_f, b_seq_all, c_seq_all))
    total_decay = jnp.exp(cumul[:, -1][:, None, :] * decay_rate)
    ones_like = jnp.ones_like(total_decay)
    zeros_like = jnp.zeros_like(total_decay)
    enter_h = entering_2((total_decay, last_state), "seq", link, (ones_like, zeros_like), False)[1]

    def read_entry(inputs_seq):
        cum_seq, enter_seq, c_seq = inputs_seq
        growth = jnp.exp(cum_seq[:, None, :] * decay_rate)
        return jnp.sum(c_seq[:, :, None] * growth * enter_seq[None], axis=1)

    entry_out = lax.map(read_entry, (cumul, enter_h, c_seq_all))
    gate_act = jax.nn.silu(gate_pre)
    scan_out = local_out + entry_out + skip_gain * mixed_f
    gated_out = (scan_out * gate_act).astype(jnp.bfloat16).reshape(row_count, inner_width)
    branch = lax.dot_general(
        gated_out, out_weight, contract_last, preferred_element_type=jnp.float32
    ).reshape(seq_count, tok_count, model_width)
    branch_share = lax.psum_scatter(branch, "chan", scatter_dimension=2, tiled=True)
    block_out = (residual_in.astype(jnp.float32) + branch_share).astype(jnp.bfloat16)
    grad_whole = lax.all_gather(out_grad, "chan", axis=2, tiled=True).reshape(
        row_count, model_width
    )
    out_weight_grad = lax.dot_general(
        grad_whole, gated_out, contract_first, preferred_element_type=jnp.float32
    )
    gated_grad = jnp.dot(grad_whole, out_weight, preferred_element_type=jnp.float32).reshape(
        seq_count, tok_count, inner_width
    )
    y_grad = gated_grad * gate_act
    gate_grad = (gated_grad * scan_out * silu_slope(gate_pre)).astype(jnp.bfloat16)
    skip_gain_grad = jnp.sum(y_grad * mixed_f, axis=(0, 1))

    def local_backward(inputs_seq):
        step_seq, y_seq, c_seq = inputs_seq
        decay_seq = jnp.exp(step_seq[:, None, :] * decay_rate)
        source = c_seq[:, :, None] * y_seq[:, None, :]
        adjoint = chain_scan(decay_seq, source, True)
        return decay_seq[0] * adjoint[0]

    first_send = lax.map(local_backward, (step_size, y_grad, c_seq_all))
    enter_g = entering_2((total_decay, first_send), "seq", link, (ones_like, zeros_like), True)[1]

    def local_grads(inputs_seq):
        step_seq, mixed_seq, b_seq, c_seq, y_seq, cum_seq, enter_seq, back_seq = inputs_seq
        decay_seq = jnp.exp(step_seq[:, None, :] * decay_rate)
        drive_seq = b_seq[:, :, None] * (step_seq * mixed_seq)[:, None, :]
        local_h = chain_scan(decay_seq, drive_seq, False)
        full_h = local_h + jnp.exp(cum_seq[:, None, :] * decay_rate) * enter_seq[None]
        source = c_seq[:, :, None] * y_seq[:, None, :]
        adjoint = chain_scan(decay_seq, source, True)
        tail_decay = jnp.exp((cum_seq[-1][None] - cum_seq)[:, None, :] * decay_rate)
        full_g = adjoint + tail_decay * back_seq[None]
        before = jnp.concatenate([enter_seq[None], full_h[:-1]], axis=0)
        weighted = full_g * before * decay_seq
        decay_part = jnp.sum(weighted * step_seq[:, None, :], axis=0)
        along_b = jnp.sum(full_g * b_seq[:, :, None], axis=1)
        size_grad = jnp.sum(weighted * decay_rate, axis=1) + mixed_seq * along_b
        input_grad = step_seq * along_b
        b_grad = jnp.sum(full_g * (step_seq * mixed_seq)[:, None, :], axis=2)
        c_grad = jnp.sum(y_seq[:, None, :] * full_h, axis=2)
        return (decay_part, size_grad, input_grad, b_grad, c_grad)

    decay_parts, size_grads, input_grads, b_grads, c_grads = lax.map(
        local_grads, (step_size, mixed_f, b_seq_all, c_seq_all, y_grad, cumul, enter_h, enter_g)
    )
    decay_log_grad = jnp.sum(decay_parts, axis=0) * decay_rate
    pre_grad = (size_grads.reshape(row_count, inner_width) * jax.nn.sigmoid(step_pre)).astype(
        jnp.bfloat16
    )
    step_bias_grad = jnp.sum(pre_grad.astype(jnp.float32), axis=0)
    step_weight_grad = lax.dot_general(
        step_low, pre_grad, contract_first, preferred_element_type=jnp.float32
    )
    low_grad = lax.dot_general(
        pre_grad, step_weight, contract_last, preferred_element_type=jnp.float32
    )
    proj_partial = jnp.concatenate(
        [
            low_grad,
            b_grads.reshape(row_count, state_width),
            c_grads.reshape(row_count, state_width),
        ],
        axis=1,
    )
    proj_grad = lax.psum(proj_partial, "chan").astype(jnp.bfloat16)
    proj_weight_grad = lax.dot_general(
        proj_grad, mixed_flat, contract_first, preferred_element_type=jnp.float32
    )
    back_proj = jnp.dot(proj_grad, proj_weight, preferred_element_type=jnp.float32).reshape(
        seq_count, tok_count, inner_width
    )
    mixed_grad = input_grads + skip_gain * y_grad + back_proj
    conv_grad = mixed_grad * silu_slope(conv_out)
    conv_bias_grad = jnp.sum(conv_grad, axis=(0, 1))
    conv_weight_grad = jnp.stack(
        [
            jnp.sum(conv_grad * padded[:, offset : offset + tok_count], axis=(0, 1))
            for offset in range(kernel)
        ],
        axis=0,
    )
    incoming = passed_along(conv_grad[:, : kernel - 1], "seq", -1)
    extended = jnp.concatenate([conv_grad, incoming], axis=1)
    conv_in_grad = sum(
        (
            conv_taps[offset] * extended[:, kernel - 1 - offset : kernel - 1 - offset + tok_count]
            for offset in range(kernel)
        )
    )
    pair_grad = jnp.stack([conv_in_grad.astype(jnp.bfloat16), gate_grad], axis=2).reshape(
        row_count, 2 * inner_width
    )
    in_weight_grad = lax.dot_general(
        normed, pair_grad, contract_first, preferred_element_type=jnp.float32
    ).reshape(model_width, 2, inner_width)
    normed_part = lax.dot_general(
        pair_grad, in_flat, contract_last, preferred_element_type=jnp.float32
    ).reshape(seq_count, tok_count, model_width)
    slice_start = lax.axis_index("chan") * share_width
    own_in = residual_in.astype(jnp.float32)
    own_gain = lax.dynamic_slice_in_dim(gain_full, slice_start, share_width, 0)
    normed_grad = lax.psum(normed_part, "chan")
    row_dots = jnp.sum(normed_grad * gain_full * full_in, axis=-1, keepdims=True)
    own_grad = lax.dynamic_slice_in_dim(normed_grad, slice_start, share_width, 2)
    in_grad = (
        out_grad.astype(jnp.float32)
        + inv_rms * own_gain * own_grad
        - own_in * inv_rms * inv_rms * inv_rms / model_width * row_dots
    ).astype(jnp.bfloat16)
    gain_part = jnp.sum(own_grad * own_in * inv_rms, axis=(0, 1))
    in_weight_grad, proj_weight_grad, step_weight_grad, out_weight_grad = (
        lax.psum_scatter(in_weight_grad, "seq", scatter_dimension=0, tiled=True),
        lax.psum_scatter(proj_weight_grad, "seq", scatter_dimension=0, tiled=True),
        lax.psum_scatter(step_weight_grad, "seq", scatter_dimension=0, tiled=True),
        lax.psum_scatter(out_weight_grad, "seq", scatter_dimension=0, tiled=True),
    )
    gain_grad, conv_weight_grad, conv_bias_grad, step_bias_grad, decay_log_grad, skip_gain_grad = (
        lax.psum(
            (
                gain_part,
                conv_weight_grad,
                conv_bias_grad,
                step_bias_grad,
                decay_log_grad,
                skip_gain_grad,
            ),
            "seq",
        )
    )
    return (
        block_out,
        in_grad,
        gain_grad,
        in_weight_grad,
        conv_weight_grad,
        conv_bias_grad,
        proj_weight_grad,
        step_weight_grad,
        step_bias_grad,
        decay_log_grad,
        skip_gain_grad,
        out_weight_grad,
    )


def solution(mesh):
    in_specs = (
        P(None, "seq", "chan"),
        P(),
        P(None, None, "chan"),
        P(None, "chan"),
        P("chan"),
        P(None, "chan"),
        P(None, "chan"),
        P("chan"),
        P(None, "chan"),
        P("chan"),
        P(None, "chan"),
        P(None, "seq", "chan"),
    )
    out_specs = (
        P(None, "seq", "chan"),
        P(None, "seq", "chan"),
        P("chan"),
        P("seq", None, "chan"),
        P(None, "chan"),
        P("chan"),
        P("seq", "chan"),
        P("seq", "chan"),
        P("chan"),
        P(None, "chan"),
        P("chan"),
        P("seq", "chan"),
    )
    return jax.shard_map(shards, mesh=mesh, in_specs=in_specs, out_specs=out_specs, check_vma=False)
```

profile of v0, /device:TPU:0, one launch (start us, length us, event | category | flops | bytes accessed | tf_op | source)
XLA Modules:
  0.0 3114.0 jit_solution(6937848238612288560)
XLA Ops:
  31.4 15.4 all-gather.8.cloned.1.call-done
  82.9 17.9 multiply_reduce_fusion.7
  105.1 31.4 %all-reduce.8.cloned.1.call-done = f32[1024,160]{0,1:T(8,128)} async-done(((f32[1024,160]{0,1:T(8,128)}), f32[1024,160]{0,1:T(8,128)}) %all-reduce.8.cloned.1.call-update) | async-done | bytes 655376 | tf_op jit(solution)/shard_map/psum | solution.py:128
  152.1 464.1 %while.82 = (s32[]{:T(128)}, f32[8,16,1024]{2,1,0:T(8,128)S(1)}, f32[8,128,1024]{2,1,0:T(8,128)}, f32[16,1024]{1,0:T(8,128)S(1)}, f32[8,128,16]{2,1,0:T(8,128)}, /*index=5*/f32[8,128,1024]{2,1,0:T(8,128)}, s32[]{:T(128)}) while((s32[]{:T(128)}, f32[8,16,1024]{2,1,0:T(8,128)S(1)}, f32[8,128,1024]{2,1,0:T(8,128)}, f32[16,1024]{1,0:T(8,128)S(1)}, ...), condition=%wide.region_13.14_spmd, body=%wide.region_12.13_spmd.sunk | while | flops 22052864 | bytes 147247216 | solution.py:188
  619.9 299.3 %while.80 = (s32[]{:T(128)}, f32[8,128,1024]{2,1,0:T(8,128)}, f32[8,16,1024]{2,1,0:T(8,128)S(1)}, f32[8,128,16]{2,1,0:T(8,128)}, f32[8,128,16]{2,1,0:T(8,128)}, ...) while((s32[]{:T(128)}, f32[8,128,1024]{2,1,0:T(8,128)}, ...), condition=%wide.region_4.5_spmd, body=%wide.region_2.4_spmd.sunk | while | flops 21692416 | bytes 126075056 | solution.py:148
  926.7 13.6 while.85
  940.3 53.6 %all-gather.14.cloned.1.call-done = f32[64,16,1024]{2,1,0:T(8,128)} async-done(((f32[8,16,1024]{2,1,0:T(8,128)}), f32[64,16,1024]{2,1,0:T(8,128)}) %all-gather.14.cloned.1.call-update) | async-done | bytes 4194320 | tf_op jit(solution)/shard_map/all_gather | solution.py:19
  994.0 13.5 while.84
  1013.2 1177.2 %while.83 = (s32[]{:T(128)}, f32[8,16,1024]{2,1,0:T(8,128)}, f32[8,128,1024]{2,1,0:T(8,128)}, f32[8,128,1024]{2,1,0:T(8,128)}, f32[8,128,16]{2,1,0:T(8,128)}, /*...) while((s32[]{:T(128)}, f32[8,16,1024]{2,1,0:T(8,128)}, ...), condition=%wide.region_22.23_spmd, body=%wide.region_16.22_spmd.sunk | while | flops 97775616 | bytes 520504384 | solution.py:211
  1104.3 12.7 multiply_reduce_fusion.19
  1137.4 13.6 multiply_reduce_fusion.20
  1249.1 12.7 multiply_reduce_fusion.19
  1282.1 13.6 multiply_reduce_fusion.20
  1393.8 12.7 multiply_reduce_fusion.19
  1426.9 13.6 multiply_reduce_fusion.20
  1538.5 12.7 multiply_reduce_fusion.19
  1571.6 13.6 multiply_reduce_fusion.20
  1716.3 13.6 multiply_reduce_fusion.20
  1861.0 13.6 multiply_reduce_fusion.20
  2005.7 13.6 multiply_reduce_fusion.20
  2150.4 13.6 multiply_reduce_fusion.20
  2192.9 43.9 %while.81 = (s32[]{:T(128)}, f32[8,128,1024]{2,1,0:T(8,128)}, f32[8,128,16]{1,0,2:T(8,128)}, f32[8,128,1024]{2,1,0:T(8,128)}, f32[16,1024]{1,0:T(8,128)S(1)}, /*index=5*/f32[8,16,1024]{2,1,0:T(8,128)S(1)}, s32[]{:T(128)}) while((s32[]{:T(128)}, f32[8,128,1024]{2,1,0:T(8,128)}, f32[8,128,16]{1,0,2:T(8,128)}, f32[8,128,1024]{2,1,0:T(8,128)}, ...), condition=%wide.region_10.11_spmd, body=%wide.region_8.10_spmd.sunk | while | flops 8257538 | bytes 3448933 | solution.py:159
  2244.2 17.4 all-reduce.13
  2262.5 18.5 multiply_reduce_fusion.11
  2354.6 25.9 fusion
  2391.1 64.1 %all-reduce.10.cloned.1.call-done = f32[8,128,2048]{2,1,0:T(8,128)} async-done(((f32[8,128,2048]{2,1,0:T(8,128)}), f32[8,128,2048]{2,1,0:T(8,128)}) %all-reduce.10.cloned.1.call-update) | async-done | bytes 8388624 | tf_op jit(solution)/shard_map/psum | solution.py:270
  2461.1 147.4 %reduce-scatter.13.cloned.1.call-done = f32[256,1024]{0,1:T(8,128)} async-done(((f32[2048,1024]{0,1:T(8,128)}), f32[256,1024]{0,1:T(8,128)}) %reduce-scatter.13.cloned.1.call-update) | async-done | bytes 1048592 | tf_op jit(solution)/shard_map/reduce_scatter | solution.py:283
  2611.0 71.0 %reduce-scatter.7.cloned.1.call-done = f32[8,128,512]{2,1,0:T(8,128)} async-done(((f32[8,128,2048]{2,1,0:T(8,128)}), f32[8,128,512]{2,1,0:T(8,128)}) %reduce-scatter.7.cloned.1.call-update) | async-done | bytes 2097168 | tf_op jit(solution)/shard_map/reduce_scatter | solution.py:166
  2685.7 39.3 %all-reduce.2 = (f32[512]{0:T(512)}, f32[4,1024]{1,0:T(4,128)}, f32[1024]{0:T(1024)}, f32[1024]{0:T(1024)}, f32[1024]{0:T(1024)}) all-reduce(f32[512]{0:T(512)S(1)} %get-tuple-element.922, f32[4,1024]{1,0:T(4,128)S(1)} %pad_maximum_fusion.3, f32[1024]{0:T(1024)S(1)} %get-tuple-element.669, ...), channel_id=1, replica_groups=mesh['seq'=8,'chan'=4] {'seq'}, use_global_device_ids=true, to_apply=%region_27.28 | all-reduce | flops 7680 | bytes 61440 | tf_op jit(solution)/shard_map/psum | solution.py:286
  2725.0 242.4 %reduce-scatter.9.cloned.1.call-done = f32[256,2,1024]{2,0,1:T(8,128)} async-done(((f32[2048,2,1024]{2,0,1:T(8,128)}), f32[256,2,1024]{2,0,1:T(8,128)}) %reduce-scatter.9.cloned.1.call-update) | async-done | bytes 2097168 | tf_op jit(solution)/shard_map/reduce_scatter | solution.py:280
  2971.9 67.4 %all-reduce.12.cloned.1.call-done = f32[16,1024]{1,0:T(8,128)} async-done(((f32[16,1024]{1,0:T(8,128)}), f32[16,1024]{1,0:T(8,128)}) %all-reduce.12.cloned.1.call-update) | async-done | bytes 65552 | tf_op jit(solution)/shard_map/psum | solution.py:286
  3039.3 66.1 %reduce-scatter.11.cloned.1.call-done = f32[16,1024]{1,0:T(8,128)} async-done(((f32[128,1024]{1,0:T(8,128)}), f32[16,1024]{1,0:T(8,128)}) %reduce-scatter.11.cloned.1.call-update) | async-done | bytes 65552 | tf_op jit(solution)/shard_map/reduce_scatter | solution.py:282
  (2003 shorter events, 2035.1 us)
Async XLA Ops:
  7.2 93.6 %copy-start = (bf16[160,1024]{1,0:T(8,128)(2,1)S(1)}, bf16[160,1024]{1,0:T(8,128)(2,1)}, u32[]{:S(2)}) copy-start(bf16[160,1024]{1,0:T(8,128)(2,1)} %param.29) | copy-start | bytes 983044
  7.2 39.6 %all-gather.8.cloned.1.call-start = ((), (), s32[]{:S(2)}) async-start(), calls=%async_computation.4 | async-start | bytes 5242880 | tf_op jit(solution)/shard_map/all_gather | solution.py:105
  7.9 75.0 %all-gather.12.cloned.1.call-start = ((), (), s32[]{:S(2)}) async-start(), calls=%async_computation.8 | async-start | bytes 5242880 | tf_op jit(solution)/shard_map/all_gather | solution.py:168
  8.7 127.8 %all-reduce.8.cloned.1.call-start = ((), (), s32[]{:S(2)}) async-start(), calls=%async_computation.5 | async-start | bytes 1310720 | tf_op jit(solution)/shard_map/psum | solution.py:128
  31.4 31.1 %copy-start.50 = (f32[2048]{0:T(1024)}, f32[2048]{0:T(1024)S(1)}, u32[]{:S(2)}) copy-start(f32[2048]{0:T(1024)S(1)} %convert_element_type.67) | copy-start | bytes 24580
  66.3 5.3 collective-permute-start
  69.7 31.0 copy-start.57
  100.8 43.7 %copy-start.18 = (bf16[8,128,1024]{2,1,0:T(8,128)(2,1)}, bf16[8,128,1024]{2,1,0:T(8,128)(2,1)S(1)}, u32[]{:S(2)}) copy-start(bf16[8,128,1024]{2,1,0:T(8,128)(2,1)S(1)} %get-tuple-element.868) | copy-start | bytes 6291460
  100.8 38.2 %copy-start.48 = (bf16[128,1024]{1,0:T(8,128)(2,1)S(1)}, bf16[128,1024]{1,0:T(8,128)(2,1)}, u32[]{:S(2)}) copy-start(bf16[128,1024]{1,0:T(8,128)(2,1)} %param.30) | copy-start | bytes 786436
  102.5 824.2 %all-gather.10.cloned.1.call-start = ((), (), s32[]{:S(2)}) async-start(), calls=%async_computation.6 | async-start | bytes 4718592 | tf_op jit(solution)/shard_map/all_gather | solution.py:19
  102.6 41.9 %copy-start.55 = (f32[1024]{0:T(1024)}, f32[1024]{0:T(1024)S(1)}, u32[]{:S(2)}) copy-start(f32[1024]{0:T(1024)S(1)} %convert_element_type.72) | copy-start | bytes 12292
  152.0 774.8 %all-gather.16.cloned.1.call-start = ((), (), s32[]{:S(2)}) async-start(), calls=%async_computation.15 | async-start | bytes 4718592 | tf_op jit(solution)/shard_map/all_gather | solution.py:19
  152.1 464.1 %copy-start.47 = (f32[1024,16]{0,1:T(8,128)S(1)}, f32[1024,16]{0,1:T(8,128)}, u32[]{:S(2)}) copy-start(f32[1024,16]{0,1:T(8,128)} %get-tuple-element.925) | copy-start | bytes 196612
  617.2 376.7 %all-gather.14.cloned.1.call-start = ((), (), s32[]{:S(2)}) async-start(), calls=%async_computation.14 | async-start | bytes 4718592 | tf_op jit(solution)/shard_map/all_gather | solution.py:19
  920.0 1535.3 %all-reduce.10.cloned.1.call-start = ((), (), s32[]{:S(2)}) async-start(), calls=%async_computation.9 | async-start | bytes 16777216 | tf_op jit(solution)/shard_map/psum | solution.py:270
  2192.9 43.9 %copy-start.43 = (f32[8,128,16]{2,1,0:T(8,128)S(1)}, f32[8,128,16]{2,1,0:T(8,128)}, u32[]{:S(2)}) copy-start(f32[8,128,16]{2,1,0:T(8,128)} %get-tuple-element.435) | copy-start | bytes 196612
  2192.9 44.1 %copy-start.42 = (f32[8,128,16]{2,1,0:T(8,128)S(1)}, f32[8,128,16]{2,1,0:T(8,128)}, u32[]{:S(2)}) copy-start(f32[8,128,16]{2,1,0:T(8,128)} %get-tuple-element.434) | copy-start | bytes 196612
  2192.9 44.3 %copy-start.56 = (f32[1024]{0:T(1024)S(1)}, f32[1024]{0:T(1024)}, u32[]{:S(2)}) copy-start(f32[1024]{0:T(1024)} %copy-done.55) | copy-start | bytes 12292
  2281.0 7.1 collective-permute-start.1
  2303.5 304.9 %reduce-scatter.13.cloned.1.call-start = ((), (), s32[]{:S(2)}) async-start(), calls=%async_computation.13 | async-start | bytes 9437184 | tf_op jit(solution)/shard_map/reduce_scatter | solution.py:283
  2314.3 367.6 %reduce-scatter.7.cloned.1.call-start = ((), (), s32[]{:S(2)}) async-start(), calls=%async_computation.7 | async-start | bytes 10485760 | tf_op jit(solution)/shard_map/reduce_scatter | solution.py:166
  2325.3 642.1 %reduce-scatter.9.cloned.1.call-start = ((), (), s32[]{:S(2)}) async-start(), calls=%async_computation.10 | async-start | bytes 18874368 | tf_op jit(solution)/shard_map/reduce_scatter | solution.py:280
  2352.1 34.1 %copy-start.46 = (f32[16,1024]{1,0:T(8,128)S(1)}, f32[16,1024]{1,0:T(8,128)}, u32[]{:S(2)}) copy-start(f32[16,1024]{1,0:T(8,128)} %param.32) | copy-start | bytes 196612
  2352.1 103.1 %copy-start.51 = (f32[2048]{0:T(1024)S(1)}, f32[2048]{0:T(1024)}, u32[]{:S(2)}) copy-start(f32[2048]{0:T(1024)} %copy-done.50) | copy-start | bytes 24580
  2352.2 687.1 %all-reduce.12.cloned.1.call-start = ((), (), s32[]{:S(2)}) async-start(), calls=%async_computation.12 | async-start | bytes 131072 | tf_op jit(solution)/shard_map/psum | solution.py:286
  2380.6 9.5 collective-permute-start.2
  2383.4 6.7 collective-permute-start.3
  2386.9 718.6 %reduce-scatter.11.cloned.1.call-start = ((), (), s32[]{:S(2)}) async-start(), calls=%async_computation.11 | async-start | bytes 589824 | tf_op jit(solution)/shard_map/reduce_scatter | solution.py:282
  2390.1 291.9 %copy-start.36 = (bf16[8,128,512]{2,1,0:T(8,128)(2,1)S(1)}, bf16[8,128,512]{2,1,0:T(8,128)(2,1)}, u32[]{:S(2)}) copy-start(bf16[8,128,512]{2,1,0:T(8,128)(2,1)} %param.24) | copy-start | bytes 3145732
  2390.1 291.9 %copy-start.37 = (bf16[8,128,512]{2,1,0:T(8,128)(2,1)S(1)}, bf16[8,128,512]{2,1,0:T(8,128)(2,1)}, u32[]{:S(2)}) copy-start(bf16[8,128,512]{2,1,0:T(8,128)(2,1)} %param.35) | copy-start | bytes 3145732
  2390.1 291.9 %copy-start.53 = (f32[8,128]{1,0:T(8,128)S(1)}, f32[8,128]{1,0:T(8,128)}, u32[]{:S(2)}) copy-start(f32[8,128]{1,0:T(8,128)} %copy-done.52) | copy-start | bytes 12292
  2461.1 224.6 %copy-start.68 = (f32[1024]{0:T(1024)S(1)}, f32[1024]{0:T(1024)}, u32[]{:S(2)}) copy-start(f32[1024]{0:T(1024)} %get-tuple-element.866) | copy-start | bytes 12292
  (272 other events, 2294.8 us)
Sparse Core Ops, SparseCore 0:
  9.6 37.1 all-gather.7
  48.4 34.4 all-gather.11
  102.7 33.7 all-reduce.7
  152.1 73.3 all-gather.9
  617.4 73.4 all-gather.15
  920.1 73.8 all-gather.13
  2303.7 151.5 all-reduce.9
  2458.9 149.5 reduce-scatter.12
  2611.2 70.6 reduce-scatter.6
  2685.5 281.7 reduce-scatter.8
  2971.8 67.5 all-reduce.11
  3043.4 61.9 reduce-scatter.10
where the time goes:
time: 3140 us; the launch traced here: 3110 us
  other arithmetic  1570 us (50%)
  waiting for transfers between devices  776 us (25%)
  local copies, waits for them, and re-layouts  552 us (18%)
  matrix products  83.6 us (3%)
  blocking collectives  82.6 us (3%)
    while x472, other arithmetic  676 us
    reduce_scatter x1, waiting for transfers between devices, shards(): lax.psum_scatter(in_weight_grad, 'seq', scatter_dimension=0, tiled=True)  242 us
    while x816, local copies, waits for them, and re-layouts  236 us
    reduce_scatter x1, waiting for transfers between devices, shards(): lax.psum_scatter(out_weight_grad, 'seq', scatter_dimension=0, tiled=True)  147 us
    reduce_sum x8, other arithmetic, local_grads(): b_grad = jnp.sum(full_g * (step_seq * mixed_seq)[:, None, :], axis=2)  109 us
    reduce_sum x8, other arithmetic, local_grads(): c_grad = jnp.sum(y_seq[:, None, :] * full_h, axis=2)  102 us
    add x8, other arithmetic, chain_scan(): return (accums + coefs * entering).reshape(decay.shape)  97.5 us
    add x16, other arithmetic, chain_scan(): drive_g[:, inner_pos] + decay_g[:, inner_pos + 1] * acc_list[inner_pos + 1]  85.9 us
  transfers between devices with their start and end apart: 16, of which 12 were waited for; matrix products, arithmetic and copies ran while one was open for 29% of the time, Pallas kernels for 0%

commit v1 on v0

v1 whole, which is shorter than its diff:
```python
import functools, math
import jax, jax.numpy as jnp
from jax import lax
from jax.sharding import PartitionSpec as P
from jax.experimental import pallas as pl
from jax.experimental.pallas import tpu as pltpu

LANES = 128
LOG2E = 1.4426950408889634
VM = 56 * 1024 * 1024


def spread(bc_ref, spread_ref, chunk, seqs, count):
    for tok in range(chunk):
        tile = bc_ref[pl.ds(tok * seqs, seqs), :]
        for col in range(count):
            spread_ref[tok, col] = jnp.broadcast_to(tile[:, col : col + 1], (seqs, LANES))


def pre_kernel(chunk, step_ref, mixed_ref, yg_ref, bc_ref, rate_ref, h_ref, q_ref, p_ref, spread_ref):
    states, seqs, width = rate_ref.shape

    @pl.when(pl.program_id(0) == 0)
    def _():
        h_ref[...] = jnp.zeros_like(h_ref)
        q_ref[...] = jnp.zeros_like(q_ref)
        p_ref[...] = jnp.ones_like(p_ref)

    spread(bc_ref, spread_ref, chunk, seqs, 2 * states)
    part = 8

    def tile_step(j, _):
        lanes = pl.ds(pl.multiple_of(j * LANES, LANES), LANES)
        for low in range(0, states, part):
            idx = range(low, low + part)
            h = [h_ref[n, :, lanes] for n in idx]
            q = [q_ref[n, :, lanes] for n in idx]
            p = [p_ref[n, :, lanes] for n in idx]
            for tok in range(chunk):
                rows = pl.ds(tok * seqs, seqs)
                if tok % 2 == 0:
                    pair = mixed_ref[pl.ds(tok * seqs, 2 * seqs), lanes].astype(jnp.float32)
                s = step_ref[rows, lanes]
                y = yg_ref[rows, lanes]
                x = s * pair[(tok % 2) * seqs : (tok % 2 + 1) * seqs]
                for i, n in enumerate(idx):
                    d = jnp.exp2(s * rate_ref[n, :, lanes])
                    h[i] = d * h[i] + spread_ref[tok, n] * x
                    p[i] = d * p[i]
                    q[i] = q[i] + p[i] * (spread_ref[tok, states + n] * y)
            for i, n in enumerate(idx):
                h_ref[n, :, lanes] = h[i]
                q_ref[n, :, lanes] = q[i]
                p_ref[n, :, lanes] = p[i]
        return 0

    lax.fori_loop(0, width // LANES, tile_step, 0)


def prepass(step, mixed, yg, bc, rate, chunk):
    rows, width = step.shape
    states, seqs, _ = rate.shape
    grid = rows // (chunk * seqs)
    row_spec = pl.BlockSpec((chunk * seqs, width), lambda i: (i, 0))
    whole = pl.BlockSpec((states, seqs, width), lambda i: (0, 0, 0))
    return pl.pallas_call(
        functools.partial(pre_kernel, chunk),
        grid=(grid,),
        in_specs=[row_spec, row_spec, row_spec, pl.BlockSpec((chunk * seqs, LANES), lambda i: (i, 0)), whole],
        out_specs=[whole, whole],
        out_shape=[jax.ShapeDtypeStruct(rate.shape, jnp.float32)] * 2,
        scratch_shapes=[pltpu.VMEM(rate.shape, jnp.float32), pltpu.VMEM((chunk, 2 * states, seqs, LANES), jnp.float32)],
        compiler_params=pltpu.CompilerParams(vmem_limit_bytes=VM),
        name="local_ends",
    )(step, mixed, yg, bc, rate)


def fwd_kernel(chunk, step_ref, mixed_ref, gate_ref, gg_ref, bc_ref, rate_ref, hin_ref, skip_ref,
               hist_ref, start_ref, gated_ref, ggrad_ref, state_ref, spread_ref):
    states, seqs, width = rate_ref.shape

    @pl.when(pl.program_id(0) == 0)
    def _():
        state_ref[...] = hin_ref[...]

    start_ref[0] = state_ref[...]
    spread(bc_ref, spread_ref, chunk, seqs, 2 * states)

    def tile_step(j, _):
        lanes = pl.ds(pl.multiple_of(j * LANES, LANES), LANES)
        h = [state_ref[n, :, lanes] for n in range(states)]
        skip = skip_ref[:, lanes]
        for tok in range(0, chunk, 2):
            pair_rows = pl.ds(tok * seqs, 2 * seqs)
            pair = mixed_ref[pair_rows, lanes].astype(jnp.float32)
            gated, ggrad = [], []
            for k in range(2):
                rows = pl.ds((tok + k) * seqs, seqs)
                s = step_ref[rows, lanes]
                m = pair[k * seqs : (k + 1) * seqs]
                x = s * m
                y = skip * m
                for n in range(states):
                    d = jnp.exp2(s * rate_ref[n, :, lanes])
                    h[n] = d * h[n] + spread_ref[tok + k, n] * x
                    y = y + spread_ref[tok + k, states + n] * h[n]
                for n in range(0, states, 2):
                    at = pl.ds(((tok + k) * states + n) * seqs, 2 * seqs)
                    hist_ref[at, lanes] = jnp.concatenate([h[n], h[n + 1]], axis=0).astype(jnp.bfloat16)
                v = gate_ref[rows, lanes]
                sig = 1.0 / (1.0 + jnp.exp2(v * (-LOG2E)))
                gated.append(y * (v * sig))
                ggrad.append(gg_ref[rows, lanes] * y * (sig * (1.0 + v * (1.0 - sig))))
            gated_ref[pair_rows, lanes] = jnp.concatenate(gated, axis=0).astype(jnp.bfloat16)
            ggrad_ref[pair_rows, lanes] = jnp.concatenate(ggrad, axis=0).astype(jnp.bfloat16)
        for n in range(states):
            state_ref[n, :, lanes] = h[n]
        return 0

    lax.fori_loop(0, width // LANES, tile_step, 0)


def forward(step, mixed, gate, gg, bc, rate, hin, skip, chunk):
    rows, width = step.shape
    states, seqs, _ = rate.shape
    grid = rows // (chunk * seqs)
    row_spec = pl.BlockSpec((chunk * seqs, width), lambda i: (i, 0))
    whole = pl.BlockSpec((states, seqs, width), lambda i: (0, 0, 0))
    return pl.pallas_call(
        functools.partial(fwd_kernel, chunk),
        grid=(grid,),
        in_specs=[row_spec, row_spec, row_spec, row_spec, pl.BlockSpec((chunk * seqs, LANES), lambda i: (i, 0)), whole, whole,
                  pl.BlockSpec((seqs, width), lambda i: (0, 0))],
        out_specs=[pl.BlockSpec((chunk * states * seqs, width), lambda i: (i, 0)),
                   pl.BlockSpec((1, states, seqs, width), lambda i: (i, 0, 0, 0)), row_spec, row_spec],
        out_shape=[jax.ShapeDtypeStruct((rows * states, width), jnp.bfloat16),
                   jax.ShapeDtypeStruct((grid, states, seqs, width), jnp.float32),
                   jax.ShapeDtypeStruct((rows, width), jnp.bfloat16),
                   jax.ShapeDtypeStruct((rows, width), jnp.bfloat16)],
        scratch_shapes=[pltpu.VMEM(rate.shape, jnp.float32), pltpu.VMEM((chunk, 2 * states, seqs, LANES), jnp.float32)],
        compiler_params=pltpu.CompilerParams(vmem_limit_bytes=VM),
        name="scan_forward",
    )(step, mixed, gate, gg, bc, rate, hin, skip)


def bwd_kernel(chunk, step_ref, sig_ref, mixed_ref, yg_ref, bc_ref, rate_ref, rate_e_ref, gin_ref, skip_ref, hist_ref, start_ref,
               pre_ref, part_ref, bcg_ref, decay_ref, bias_ref, skipg_ref, state_ref, spread_ref, g_ref, x_ref):
    states, seqs, width = rate_ref.shape

    @pl.when(pl.program_id(0) == 0)
    def _():
        state_ref[...] = gin_ref[...]
        decay_ref[...] = jnp.zeros_like(decay_ref)
        bias_ref[...] = jnp.zeros_like(bias_ref)
        skipg_ref[...] = jnp.zeros_like(skipg_ref)

    spread(bc_ref, spread_ref, chunk, seqs, 2 * states)

    def tile_step(j, _):
        lanes = pl.ds(pl.multiple_of(j * LANES, LANES), LANES)
        q = [state_ref[n, :, lanes] for n in range(states)]
        acc = [decay_ref[n, :, lanes] for n in range(states)]
        skip = skip_ref[:, lanes]
        bias = bias_ref[:, lanes]
        skipg = skipg_ref[:, lanes]
        for tok in range(chunk - 2, -1, -2):
            pair_rows = pl.ds(tok * seqs, 2 * seqs)
            pair = mixed_ref[pair_rows, lanes].astype(jnp.float32)
            pre, xs = [None, None], [None, None]
            for k in (1, 0):
                now = tok + k
                rows = pl.ds(now * seqs, seqs)
                s = step_ref[rows, lanes]
                y = yg_ref[rows, lanes]
                m = pair[k * seqs : (k + 1) * seqs]
                along = jnp.zeros_like(s)
                size = jnp.zeros_like(s)
                for n in range(0, states, 2):
                    if now > 0:
                        at = pl.ds(((now - 1) * states + n) * seqs, 2 * seqs)
                        both = hist_ref[at, lanes].astype(jnp.float32)
                        before = [both[:seqs], both[seqs:]]
                    else:
                        before = [start_ref[0, n, :, lanes], start_ref[0, n + 1, :, lanes]]
                    gs = []
                    for i in range(2):
                        r = rate_ref[n + i, :, lanes]
                        g = spread_ref[now, states + n + i] * y + q[n + i]
                        along = along + g * spread_ref[now, n + i]
                        q[n + i] = jnp.exp2(s * r) * g
                        w = q[n + i] * before[i]
                        acc[n + i] = acc[n + i] + w * s
                        size = size + w * r
                        gs.append(g)
                    at = pl.ds((now * states + n) * seqs, 2 * seqs)
                    g_ref[at, lanes] = jnp.concatenate(gs, axis=0).astype(jnp.bfloat16)
                part_ref[rows, lanes] = s * along + skip * y
                skipg = skipg + y * m
                xs[k] = s * m
                pre[k] = (size * (1.0 / LOG2E) + m * along) * sig_ref[rows, lanes]
            rounded = jnp.concatenate(pre, axis=0).astype(jnp.bfloat16)
            pre_ref[pair_rows, lanes] = rounded
            wide = rounded.astype(jnp.float32)
            bias = bias + wide[:seqs] + wide[seqs:]
            x_ref[pair_rows, lanes] = jnp.concatenate(xs, axis=0).astype(jnp.bfloat16)
        for n in range(states):
            state_ref[n, :, lanes] = q[n]
            decay_ref[n, :, lanes] = acc[n]
        bias_ref[:, lanes] = bias
        skipg_ref[:, lanes] = skipg
        return 0

    lax.fori_loop(0, width // LANES, tile_step, 0)
    span = 2 * states * seqs
    row = lax.broadcasted_iota(jnp.int32, (2 * seqs, span), 0)
    col = lax.broadcasted_iota(jnp.int32, (2 * seqs, span), 1)
    match = (row // seqs == col // (states * seqs)) & (row % seqs == col % seqs)
    contract = (((1,), (1,)), ((), ()))
    b_rows, c_rows = [], []
    for tok in range(0, chunk, 2):
        pair_rows = pl.ds(tok * seqs, 2 * seqs)
        at = pl.ds(tok * states * seqs, span)
        bg = lax.dot_general(x_ref[pair_rows, :], g_ref[at, :], contract, preferred_element_type=jnp.float32)
        cg = lax.dot_general(yg_ref[pair_rows, :].astype(jnp.bfloat16), hist_ref[at, :], contract, preferred_element_type=jnp.float32)
        b_rows.append(jnp.where(match, bg, 0.0))
        c_rows.append(jnp.where(match, cg, 0.0))
    src = lax.broadcasted_iota(jnp.int32, (2 * states, span), 1) // seqs % states
    dst = lax.broadcasted_iota(jnp.int32, (2 * states, span), 0)
    fold_b = (src == dst).astype(jnp.bfloat16)
    fold_c = (src + states == dst).astype(jnp.bfloat16)
    bcg_ref[...] = lax.dot_general(
        fold_b, jnp.concatenate(b_rows, axis=0).astype(jnp.bfloat16), contract, preferred_element_type=jnp.float32
    ) + lax.dot_general(
        fold_c, jnp.concatenate(c_rows, axis=0).astype(jnp.bfloat16), contract, preferred_element_type=jnp.float32
    )


def backward(step, sig, mixed, yg, bc, rate, gin, skip, hist, start, chunk):
    rows, width = step.shape
    states, seqs, _ = rate.shape
    grid = rows // (chunk * seqs)
    back = lambda i: (grid - 1 - i, 0)
    row_spec = pl.BlockSpec((chunk * seqs, width), back)
    bc_spec = pl.BlockSpec((chunk * seqs, LANES), back)
    whole = pl.BlockSpec((states, seqs, width), lambda i: (0, 0, 0))
    one = pl.BlockSpec((seqs, width), lambda i: (0, 0))
    f32 = jnp.float32
    return pl.pallas_call(
        functools.partial(bwd_kernel, chunk),
        grid=(grid,),
        in_specs=[row_spec, row_spec, row_spec, row_spec, bc_spec, whole, whole, whole, one,
                  pl.BlockSpec((chunk * states * seqs, width), back),
                  pl.BlockSpec((1, states, seqs, width), lambda i: (grid - 1 - i, 0, 0, 0))],
        out_specs=[row_spec, row_spec, pl.BlockSpec((2 * states, chunk * seqs), lambda i: (0, grid - 1 - i)), whole, one, one],
        out_shape=[jax.ShapeDtypeStruct((rows, width), jnp.bfloat16), jax.ShapeDtypeStruct((rows, width), f32),
                   jax.ShapeDtypeStruct((2 * states, rows), f32), jax.ShapeDtypeStruct(rate.shape, f32),
                   jax.ShapeDtypeStruct((seqs, width), f32), jax.ShapeDtypeStruct((seqs, width), f32)],
        scratch_shapes=[pltpu.VMEM(rate.shape, f32), pltpu.VMEM((chunk, 2 * states, seqs, LANES), f32),
                        pltpu.VMEM((chunk * states * seqs, width), jnp.bfloat16), pltpu.VMEM((chunk * seqs, width), jnp.bfloat16)],
        compiler_params=pltpu.CompilerParams(vmem_limit_bytes=VM),
        name="scan_backward",
    )(step, sig, mixed, yg, bc, rate, rate, gin, skip, hist, start)


EPSILON = 1e-05
CONTRACT_LAST = (((1,), (1,)), ((), ()))
CONTRACT_FIRST = (((0,), (0,)), ((), ()))


def dot(a, b, dims=(((1,), (0,)), ((), ())), out=jnp.float32):
    return lax.dot_general(a, b, dims, preferred_element_type=out)


def swapped(value, axis, bit):
    count = lax.axis_size(axis)
    return lax.ppermute(value, axis, [(i, i ^ (1 << bit)) for i in range(count)])


def moved(value, axis, distance):
    count = lax.axis_size(axis)
    return lax.ppermute(value, axis, [(i, i + distance) for i in range(count) if 0 <= i + distance < count])


def bits_of(axis):
    return lax.axis_size(axis).bit_length() - 1


def own_bit(axis, bit):
    return (lax.axis_index(axis) >> bit) & 1


def gathered(value, axis):
    count = lax.axis_size(axis)
    parts = {0: value}
    for bit in reversed(range(bits_of(axis))):
        parts |= {mask | (1 << bit): swapped(part, axis, bit) for mask, part in parts.items()}
    for bit in range(bits_of(axis)):
        high = own_bit(axis, bit) == 1
        low_of = lambda m: m & ~(1 << bit)
        parts = {m: jnp.where(high, parts[m ^ (1 << bit)], parts[m]) for m in range(count)}
    return jnp.concatenate([parts[m] for m in range(count)], axis=-1)


def summed(value, axis, narrow_from):
    for bit in range(bits_of(axis)):
        sent = value.astype(jnp.bfloat16) if bit >= narrow_from else value
        value = value + swapped(sent, axis, bit).astype(jnp.float32)
    return value


def pick(value, dim, index):
    return lax.dynamic_index_in_dim(value, index, dim, keepdims=False)


def scattered(blocks, axis):
    bits = bits_of(axis)
    value = blocks.reshape((2,) * bits + blocks.shape[1:])
    for bit in range(bits):
        dim = bits - 1 - bit
        mine = own_bit(axis, bit)
        received = swapped(pick(value, dim, 1 - mine), axis, bit)
        value = pick(value, dim, mine).astype(jnp.float32) + received.astype(jnp.float32)
        if bit < bits - 1:
            value = value.astype(jnp.bfloat16)
    return value


def entering(local, total, rate, axis, direction):
    states = rate.shape[0]
    enter, enter_sum = jnp.zeros_like(local), jnp.zeros_like(total)
    through, through_sum = local, total
    distance = 1
    while distance < lax.axis_size(axis):
        upper = through_sum.astype(jnp.bfloat16)
        lower = (through_sum - upper.astype(jnp.float32)).astype(jnp.bfloat16)
        packet = jnp.concatenate([through.astype(jnp.bfloat16), upper[None], lower[None]], axis=0)
        got = moved(packet, axis, distance * direction).astype(jnp.float32)
        state, step_sum = got[:states], got[states] + got[states + 1]
        enter, enter_sum = enter + jnp.exp2(rate * enter_sum) * state, enter_sum + step_sum
        through, through_sum = through + jnp.exp2(rate * through_sum) * state, through_sum + step_sum
        distance *= 2
    return enter


def silu_slope(pre_value):
    sigmoid_value = jax.nn.sigmoid(pre_value)
    return sigmoid_value * (1.0 + pre_value * (1.0 - sigmoid_value))


def shards(
    residual_in,
    norm_gain,
    in_weight,
    conv_weight,
    conv_bias,
    proj_weight,
    step_weight,
    step_bias,
    decay_log,
    skip_gain,
    out_weight,
    out_grad,
):
    f32, bf16 = jnp.float32, jnp.bfloat16
    seqs, toks, share = residual_in.shape
    model = norm_gain.shape[0]
    taps, inner = conv_weight.shape
    states = decay_log.shape[0]
    rank = step_weight.shape[0]
    rows = seqs * toks
    chunk = math.gcd(toks, 16)
    seq_count = lax.axis_size("seq")
    own_in = residual_in.swapaxes(0, 1).reshape(rows, share)
    own_out_grad = out_grad.swapaxes(0, 1).reshape(rows, share)
    full_in = gathered(own_in, "chan")
    grad_whole = gathered(own_out_grad, "chan")
    wide_in = full_in.astype(f32)
    inv_rms = lax.rsqrt(jnp.mean(wide_in * wide_in, axis=-1, keepdims=True) + EPSILON)
    gain_full = norm_gain.astype(f32)
    normed = (wide_in * inv_rms * gain_full).astype(bf16)
    conv_weights, gate_weights = in_weight[:, 0], in_weight[:, 1]
    conv_in = dot(normed, conv_weights, out=bf16)
    gate_pre = dot(normed, gate_weights)
    halo = (taps - 1) * seqs
    previous = moved(conv_in[rows - halo :], "seq", 1)
    padded = jnp.concatenate([previous, conv_in], axis=0).astype(f32)
    conv_taps = conv_weight.astype(f32)
    conv_out = conv_bias.astype(f32) + sum(
        conv_taps[k] * padded[k * seqs : k * seqs + rows] for k in range(taps)
    )
    mixed = jax.nn.silu(conv_out).astype(bf16)
    projected = summed(dot(proj_weight, mixed, CONTRACT_LAST), "chan", 1)
    step_low = projected[:rank].astype(bf16)
    bc = jnp.pad(projected[rank:].T, ((0, 0), (0, LANES - 2 * states)))
    step_pre = dot(step_low, step_weight, CONTRACT_FIRST) + step_bias.astype(f32)
    step = jax.nn.softplus(step_pre)
    step_slope = jax.nn.sigmoid(step_pre)
    decay_rate = -jnp.exp(decay_log)
    rate = jnp.broadcast_to((decay_rate * LOG2E)[:, None], (states, seqs, inner))
    skip = jnp.broadcast_to(skip_gain, (seqs, inner))
    gated_grad = dot(grad_whole, out_weight)
    y_grad = gated_grad * jax.nn.silu(gate_pre)
    local_end, local_start = prepass(step, mixed, y_grad, bc, rate, chunk)
    step_total = jnp.sum(step.reshape(toks, seqs, inner), axis=0)
    enter_h = entering(local_end, step_total, rate, "seq", 1)
    enter_g = entering(local_start, step_total, rate, "seq", -1)
    history, starts, gated_out, gate_grad = forward(
        step, mixed, gate_pre, gated_grad, bc, rate, enter_h, skip, chunk
    )
    branch = dot(gated_out, out_weight, CONTRACT_LAST, out=bf16)
    chan_bits = bits_of("chan")
    by_owner = lambda value: value.reshape(rows, -1, share).swapaxes(0, 1)
    branch_share = scattered(by_owner(branch), "chan")
    block_rows = (own_in.astype(f32) + branch_share).astype(bf16)
    block_out = block_rows.reshape(toks, seqs, share).swapaxes(0, 1)
    out_weight_part = dot(grad_whole, gated_out, CONTRACT_FIRST, out=bf16)
    out_weight_grad = scattered(out_weight_part.reshape(seq_count, -1, inner), "seq")
    gate_weight_part = dot(normed, gate_grad, CONTRACT_FIRST, out=bf16)
    gate_weight_grad = scattered(gate_weight_part.reshape(seq_count, -1, inner), "seq")
    pre_grad, mixed_part, bc_grads, decay_parts, bias_parts, skip_parts = backward(
        step, step_slope, mixed, y_grad, bc, rate, enter_g, skip, history, starts, chunk
    )
    low_grad = dot(step_weight, pre_grad, CONTRACT_LAST)
    proj_grad = summed(jnp.concatenate([low_grad, bc_grads], axis=0), "chan", 1).astype(bf16)
    proj_weight_part = dot(proj_grad, mixed, out=bf16)
    step_weight_part = dot(step_low, pre_grad, out=bf16)
    mixed_grad = mixed_part + dot(proj_grad, proj_weight, CONTRACT_FIRST)
    conv_grad = mixed_grad * silu_slope(conv_out)
    conv_bias_grad = jnp.sum(conv_grad, axis=0)
    conv_weight_grad = jnp.stack(
        [jnp.sum(conv_grad * padded[k * seqs : k * seqs + rows], axis=0) for k in range(taps)]
    )
    incoming = moved(conv_grad[:halo], "seq", -1)
    extended = jnp.concatenate([conv_grad, incoming], axis=0)
    conv_in_grad = sum(
        conv_taps[k] * extended[(taps - 1 - k) * seqs : (taps - 1 - k) * seqs + rows] for k in range(taps)
    ).astype(bf16)
    conv_weights_part = dot(normed, conv_in_grad, CONTRACT_FIRST, out=bf16)
    conv_weights_grad = scattered(conv_weights_part.reshape(seq_count, -1, inner), "seq")
    small_weights = scattered(
        jnp.concatenate(
            [proj_weight_part.reshape(seq_count, -1, inner), step_weight_part.reshape(seq_count, -1, inner)], axis=1
        ),
        "seq",
    )
    proj_share = proj_weight.shape[0] // seq_count
    normed_part = (dot(conv_in_grad, conv_weights, CONTRACT_LAST) + dot(gate_grad, gate_weights, CONTRACT_LAST)).astype(bf16)
    normed_grad = scattered(by_owner(normed_part), "chan")
    row_dots = jnp.sum(
        conv_in_grad.astype(f32) * conv_in.astype(f32) + gate_grad.astype(f32) * gate_pre, axis=1
    )
    row_dots = summed(row_dots, "chan", chan_bits)[:, None]
    wide_own = own_in.astype(f32)
    own_gain = lax.dynamic_slice_in_dim(gain_full, lax.axis_index("chan") * share, share, 0)
    in_rows = (
        own_out_grad.astype(f32)
        + inv_rms * own_gain * normed_grad
        - wide_own * (inv_rms * inv_rms / model) * row_dots
    ).astype(bf16)
    in_grad = in_rows.reshape(toks, seqs, share).swapaxes(0, 1)
    gain_grad = summed(jnp.sum(normed_grad * wide_own * inv_rms, axis=0), "seq", bits_of("seq"))
    sums = summed(
        jnp.concatenate(
            [
                jnp.sum(decay_parts, axis=1) * decay_rate,
                conv_weight_grad,
                conv_bias_grad[None],
                jnp.sum(bias_parts, axis=0)[None],
                jnp.sum(skip_parts, axis=0)[None],
            ],
            axis=0,
        ),
        "seq",
        bits_of("seq"),
    )
    return (
        block_out,
        in_grad,
        gain_grad,
        jnp.stack([conv_weights_grad, gate_weight_grad], axis=1),
        sums[states : states + taps],
        sums[states + taps],
        small_weights[:proj_share],
        small_weights[proj_share:],
        sums[states + taps + 1],
        sums[:states],
        sums[states + taps + 2],
        out_weight_grad,
    )


def solution(mesh):
    in_specs = (
        P(None, "seq", "chan"),
        P(),
        P(None, None, "chan"),
        P(None, "chan"),
        P("chan"),
        P(None, "chan"),
        P(None, "chan"),
        P("chan"),
        P(None, "chan"),
        P("chan"),
        P(None, "chan"),
        P(None, "seq", "chan"),
    )
    out_specs = (
        P(None, "seq", "chan"),
        P(None, "seq", "chan"),
        P("chan"),
        P("seq", None, "chan"),
        P(None, "chan"),
        P("chan"),
        P("seq", "chan"),
        P("seq", "chan"),
        P("chan"),
        P(None, "chan"),
        P("chan"),
        P("seq", "chan"),
    )
    return jax.shard_map(shards, mesh=mesh, in_specs=in_specs, out_specs=out_specs, check_vma=False)
```

time: 3140 us -> 607 us (0.19)
  other arithmetic: 1570 us -> 53.2 us
  waiting for transfers between devices: 776 us -> 192 us
  local copies, waits for them, and re-layouts: 552 us -> 56.7 us
  Pallas kernels: 0 us -> 142 us
  blocking collectives: 82.6 us -> 0 us
  starting transfers between devices: 9.79 us -> 63.7 us
    while x472 -> x0, other arithmetic: 676 us -> none
    reduce_scatter x4 -> x0, waiting for transfers between devices: 527 us -> none  [the longest x1 242 us: shards(): lax.psum_scatter(in_weight_grad, 'seq', scatter_dimension=0, tiled=True)]
    reduce_sum x46 -> x6, other arithmetic: 387 us -> 11.5 us  [the longest x1 5.15 us: shards(): jnp.sum(conv_grad * padded[k * seqs:k * seqs + rows], axis=0)]
    while x819 -> x0, local copies, waits for them, and re-layouts: 245 us -> none
    add x40 -> x12, other arithmetic: 235 us -> 3.41 us  [the longest x1 1.5 us: entering(): enter + jnp.exp2(rate * enter_sum) * state]
    ppermute x2 -> x42, waiting for transfers between devices: 7.61 us -> 192 us  [the longest x34 149 us: swapped(): return lax.ppermute(value, axis, [(i, i ^ 1 << bit) for i in range(count)])]
    psum x3 -> x0, waiting for transfers between devices: 163 us -> none  [the longest x1 67.4 us: shards(): lax.psum((gain_part, conv_weight_grad, conv_bias_grad, step_bias_grad, de...]
    pallas_call x0 -> x3, Pallas kernels: none -> 142 us  [the longest x1 70.7 us: backward(): pl.pallas_call(functools.partial(bwd_kernel, chunk), grid=(grid,), in_spe...]
  transfers between devices with their start and end apart: 16 -> 42, of which waited for: 12 -> 21; matrix products, arithmetic and copies ran while one was open for 29% -> 22% of each run, Pallas kernels for 0% -> 12%
where the time goes in v1:
time: 607 us; the launch traced here: 600 us
  waiting for transfers between devices  192 us (32%)
  Pallas kernels  142 us (23%)
  matrix products  89.7 us (15%)
  starting transfers between devices  63.7 us (10%)
  local copies, waits for them, and re-layouts  56.7 us (9%)
  other arithmetic  53.2 us (9%)
    ppermute x34, waiting for transfers between devices, swapped(): return lax.ppermute(value, axis, [(i, i ^ 1 << bit) for i in range(count)])  149 us
    dot_general x15, matrix products, dot(): return lax.dot_general(a, b, dims, preferred_element_type=out)  89.7 us
    pallas_call x1, Pallas kernels, backward(): pl.pallas_call(functools.partial(bwd_kernel, chunk), grid=(grid,), in_spe...  70.7 us
    ppermute x8, waiting for transfers between devices, moved(): lax.ppermute(value, axis, [(i, i + distance) for i in range(count) if 0 <...  42.8 us
    ppermute x34, starting transfers between devices, swapped(): return lax.ppermute(value, axis, [(i, i ^ 1 << bit) for i in range(count)])  40.2 us
    pallas_call x1, Pallas kernels, prepass(): pl.pallas_call(functools.partial(pre_kernel, chunk), grid=(grid,), in_spe...  36 us
    pallas_call x1, Pallas kernels, forward(): pl.pallas_call(functools.partial(fwd_kernel, chunk), grid=(grid,), in_spe...  35.1 us
    ppermute x8, starting transfers between devices, moved(): lax.ppermute(value, axis, [(i, i + distance) for i in range(count) if 0 <...  23.4 us
  transfers between devices with their start and end apart: 42, of which 21 were waited for; matrix products, arithmetic and copies ran while one was open for 22% of the time, Pallas kernels for 12%

profile of v1, /device:TPU:0, one launch (start us, length us, event | category | flops | bytes accessed | tf_op | source)
XLA Modules:
  0.0 599.7 jit_solution(3999743730647664987)
XLA Ops:
  9.8 20.8 %collective-permute-done = bf16[1024,512]{1,0:T(8,128)(2,1)S(1)} collective-permute-done((bf16[1024,512]{1,0:T(8,128)(2,1)}, bf16[1024,512]{1,0:T(8,128)(2,1)S(1)}, u32[]{:S(2)}, u32[]{:S(2)}) %collective-permute-start) | collective-permute-done | bytes 1048608 | tf_op jit(solution)/shard_map/ppermute | solution.py:276
  30.6 21.7 %collective-permute-done.6 = bf16[1024,512]{1,0:T(8,128)(2,1)} collective-permute-done((bf16[1024,512]{1,0:T(8,128)(2,1)}, bf16[1024,512]{1,0:T(8,128)(2,1)}, u32[]{:S(2)}, u32[]{:S(2)}) %collective-permute-start.6) | collective-permute-done | bytes 1048608 | tf_op jit(solution)/shard_map/ppermute | solution.py:276
  52.4 17.2 %fusion.59 = (bf16[2048,1,1024]{2,1,0:T(2,128)(2,1)}, bf16[2048,1,1024]{2,1,0:T(2,128)(2,1)}) fusion(bf16[2048,2,1024]{2,1,0:T(2,128)(2,1)} %param.14), kind=kLoop, calls=%fused_computation.190 | loop fusion | bytes 16777216 | tf_op jit(solution)/shard_map/slice | solution.py:381
  71.1 6.3 %broadcast_select_fusion.11 = (bf16[1024,512]{1,0:T(8,128)(2,1)}, bf16[1024,512]{1,0:T(8,128)(2,1)}, bf16[1024,512]{1,0:T(8,128)(2,1)}, bf16[1024,512]{1,0:T(8,1...) fusion(pred[]{:T(512)S(6)} %eq.8, ...), kind=kLoop, calls=%fused_computation.105 | loop fusion | flops 8388608 | bytes 16777218 | tf_op jit(solution)/shard_map/jit(_where)/select_n | solution.py:300
  84.0 4.8 fusion.26
  100.4 11.3 %fusion.28.gate_ref = f32[1024,1024]{1,0:T(8,128)} fusion(bf16[1024,2048]{1,0:T(8,128)(2,1)} %copy-done.18, bf16[2048,1,1024]{2,1,0:T(2,128)(2,1)} %get-tuple-element.93), kind=kOutput, calls=%fused_computation.76 | convolution fusion | flops 4294967296 | bytes 12582912 | tf_op jit(solution)/shard_map/dot_general | solution.py:271
  114.9 10.2 %multiply_multiply_fusion.1 = (f32[1024,1024]{1,0:T(8,128)}, f32[1024,1024]{1,0:T(8,128)}) fusion(f32[1024,1024]{1,0:T(8,128)} %fusion.28.gate_ref, bf16[2048,1024]{1,0:T(8,128)(2,1)} %param.22, bf16[1024,512]{1,0:T(8,128)(2,1)} %get-tuple-element.108, bf16[1024,512]{1,0:T(8,128)(2,1)} %get-tuple-element.107, bf16[1024,512]{1,0:T(8,128)(2,1)} %get-tuple-element.106, ...), kind=kOutput, calls=%fused_computation.43 | convolution fusion | flops 4316987392 | bytes 20971520 | tf_op jit(solution)/shard_map/dot_general | solution.py:271
  127.9 5.8 bitcast_reduce_fusion
  135.4 36.0 %local_ends.1 = (f32[16,8,1024]{2,1,0:T(8,128)}, f32[16,8,1024]{2,1,0:T(8,128)}) custom-call(f32[1024,1024]{1,0:T(8,128)} %get-tuple-element.88.step_ref, bf16[1024,1024]{1,0:T(8,128)(2,1)} %copy-done.2, f32[1024,1024]{1,0:T(8,128)} %get-tuple-element.144.yg_ref, f32[1024,128]{1,0:T(8,128)} %pad.4.bc_ref, f32[16,8,1024]{2,1,0:T(8,128)} %broadcast_in_dim.12.rate_ref.rate_e_ref), custom_call_target="tpu_custom_call" | custom-call | tf_op jit(solution)/shard_map/local_ends/pallas_call | solution.py:66
  175.1 5.0 collective-permute-start.9
  180.1 4.9 collective-permute-done.14
  186.2 5.2 collective-permute-done.9
  195.0 9.3 %collective-permute-done.15 = bf16[18,8,1024]{2,1,0:T(8,128)(2,1)S(1)} collective-permute-done((bf16[18,8,1024]{2,1,0:T(8,128)(2,1)}, bf16[18,8,1024]{2,1,0:T(8,128)(2,1)S(1)}, u32[]{:S(2)}, u32[]{:S(2)}) %collective-permute-start.15) | collective-permute-done | bytes 294944 | tf_op jit(solution)/shard_map/ppermute | solution.py:281
  204.7 3.9 collective-permute-start.10
  213.3 5.4 collective-permute-start.11
  226.5 35.1 %scan_forward.1 = (bf16[16384,1024]{1,0:T(8,128)(2,1)}, f32[8,16,8,1024]{3,2,1,0:T(8,128)}, bf16[1024,1024]{1,0:T(8,128)(2,1)}, bf16[1024,1024]{1,0:T(8,128)(2,1)}) custom-call(f32[1024,1024]{1,0:T(8,128)} %get-tuple-element.88.step_ref, bf16[1024,1024]{1,0:T(8,128)(2,1)} %copy-done.2, f32[1024,1024]{1,0:T(8,128)} %fusion.28.gate_ref, ...), custom_call_target="tpu_custom_call" | custom-call | tf_op jit(solution)/shard_map/scan_forward/pallas_call | solution.py:129
  261.7 7.2 %fusion.33 = bf16[2048,1024]{1,0:T(8,128)(2,1)S(1)} fusion(bf16[1024,1024]{1,0:T(8,128)(2,1)} %get-tuple-element.25, bf16[1024,512]{1,0:T(8,128)(2,1)S(1)} %copy-done.30, bf16[1024,512]{1,0:T(8,128)(2,1)S(1)} %copy-done.29, bf16[1024,512]{1,0:T(8,128)(2,1)S(1)} %copy-done.28, bf16[1024,512]{1,0:T(8,128)(2,1)S(1)} %copy-done.27), kind=kOutput, calls=%fused_computation.112 | convolution fusion | flops 4311744512 | bytes 10485760 | tf_op jit(solution)/shard_map/dot_general | solution.py:271
  268.9 6.2 %fusion.62 = bf16[1024,2048]{1,0:T(8,128)(2,1)} fusion(bf16[1024,1024]{1,0:T(8,128)(2,1)S(1)} %copy-done.52, bf16[2048,1024]{1,0:T(8,128)(2,1)S(1)} %copy-done.51), kind=kOutput, calls=%fused_computation.193 | convolution fusion | flops 4294967296 | bytes 10485760 | tf_op jit(solution)/shard_map/dot_general | solution.py:271
  281.2 70.7 %scan_backward.1 = (bf16[1024,1024]{1,0:T(8,128)(2,1)}, f32[1024,1024]{1,0:T(8,128)}, f32[32,1024]{1,0:T(8,128)}, f32[16,8,1024]{2,1,0:T(8,128)}, f32[8,1024]{1,0:T(8,128)}, /*index=5*/f32[8,1024]{1,0:T(8,128)}) custom-call(f32[1024,1024]{1,0:T(8,128)} %get-tuple-element.88.step_ref, f32[1024,1024]{1,0:T(8,128)} %add_divide_fusion.sig_ref, ...), custom_call_target="tpu_custom_call" | custom-call | tf_op jit(solution)/shard_map/scan_backward/pallas_call | solution.py:248
  358.6 7.2 %fusion.64 = bf16[2048,1024]{1,0:T(8,128)(2,1)S(1)} fusion(bf16[1024,2048]{1,0:T(8,128)(2,1)} %copy-done.18, bf16[1024,1024]{1,0:T(8,128)(2,1)S(1)} %copy-done.22), kind=kOutput, calls=%fused_computation.195 | convolution fusion | flops 4294967296 | bytes 10485760 | tf_op jit(solution)/shard_map/dot_general | solution.py:271
  372.2 7.2 %fusion.27 = f32[1024,2048]{1,0:T(8,128)} fusion(bf16[1024,1024]{1,0:T(8,128)(2,1)S(1)} %copy-done.22, bf16[2048,1,1024]{2,1,0:T(2,128)(2,1)S(1)} %bitcast.237), kind=kOutput, calls=%fused_computation.75 | convolution fusion | flops 4294967296 | bytes 14680064 | tf_op jit(solution)/shard_map/dot_general | solution.py:271
  392.8 5.6 multiply_multiply_fusion
  402.7 17.1 %collective-permute-done.19 = f32[24,1024]{1,0:T(8,128)S(1)} collective-permute-done((f32[24,1024]{1,0:T(8,128)S(1)}, f32[24,1024]{1,0:T(8,128)S(1)}, u32[]{:S(2)}, u32[]{:S(2)}) %collective-permute-start.19) | collective-permute-done | bytes 98336 | tf_op jit(solution)/shard_map/ppermute | solution.py:281
  419.9 5.1 multiply_reduce_fusion
  426.0 7.0 %fusion.63 = bf16[2048,1024]{1,0:T(8,128)(2,1)S(1)} fusion(bf16[1024,2048]{1,0:T(8,128)(2,1)} %copy-done.18, bf16[1024,1024]{1,0:T(8,128)(2,1)S(1)} %get-tuple-element.100), kind=kOutput, calls=%fused_computation.194 | convolution fusion | flops 4294967296 | bytes 10485760 | tf_op jit(solution)/shard_map/dot_general | solution.py:271
  433.1 9.9 %add_convert_fusion = bf16[1024,2048]{1,0:T(8,128)(2,1)S(1)} fusion(f32[1024,2048]{1,0:T(8,128)} %fusion.27, bf16[1024,1024]{1,0:T(8,128)(2,1)S(1)} %get-tuple-element.100, bf16[2048,1,1024]{2,1,0:T(2,128)(2,1)} %get-tuple-element.94), kind=kOutput, calls=%fused_computation.6 | convolution fusion | flops 4299161600 | bytes 18874368 | tf_op jit(solution)/shard_map/dot_general | solution.py:271
  443.1 6.0 collective-permute-start.34
  485.9 30.8 %collective-permute-done.27 = bf16[2,2,256,1024]{3,2,0,1:T(8,128)(2,1)S(1)} collective-permute-done((bf16[2,2,256,1024]{3,2,0,1:T(8,128)(2,1)S(1)}, bf16[2,2,256,1024]{3,2,0,1:T(8,128)(2,1)S(1)}, u32[]{:S(2)}, u32[]{:S(2)}) %collective-permute-start.27) | collective-permute-done | bytes 2097184 | tf_op jit(solution)/shard_map/ppermute | solution.py:276
  520.8 22.1 %collective-permute-done.31 = bf16[2,256,1024]{2,1,0:T(8,128)(2,1)S(1)} collective-permute-done((bf16[2,256,1024]{2,1,0:T(8,128)(2,1)S(1)}, bf16[2,256,1024]{2,1,0:T(8,128)(2,1)S(1)}, u32[]{:S(2)}, u32[]{:S(2)}) %collective-permute-start.31) | collective-permute-done | bytes 1048608 | tf_op jit(solution)/shard_map/ppermute | solution.py:276
  547.0 14.9 %collective-permute-done.28 = bf16[2,256,1024]{2,1,0:T(8,128)(2,1)S(1)} collective-permute-done((bf16[2,256,1024]{2,1,0:T(8,128)(2,1)S(1)}, bf16[2,256,1024]{2,1,0:T(8,128)(2,1)S(1)}, u32[]{:S(2)}, u32[]{:S(2)}) %collective-permute-start.28) | collective-permute-done | bytes 1048608 | tf_op jit(solution)/shard_map/ppermute | solution.py:276
  566.2 10.3 %collective-permute-done.25 = f32[512]{0:T(512)S(1)} collective-permute-done((f32[512]{0:T(512)S(1)}, f32[512]{0:T(512)S(1)}, u32[]{:S(2)}, u32[]{:S(2)}) %collective-permute-start.25) | collective-permute-done | bytes 2080 | tf_op jit(solution)/shard_map/ppermute | solution.py:276
  579.2 10.2 %collective-permute-done.32 = bf16[256,1024]{1,0:T(8,128)(2,1)S(1)} collective-permute-done((bf16[256,1024]{1,0:T(8,128)(2,1)S(1)}, bf16[256,1024]{1,0:T(8,128)(2,1)S(1)}, u32[]{:S(2)}, u32[]{:S(2)}) %collective-permute-start.32) | collective-permute-done | bytes 524320 | tf_op jit(solution)/shard_map/ppermute | solution.py:276
  (293 shorter events, 156.7 us)
Async XLA Ops:
  3.5 27.2 %collective-permute-start = (bf16[1024,512]{1,0:T(8,128)(2,1)}, bf16[1024,512]{1,0:T(8,128)(2,1)S(1)}, u32[]{:S(2)}, u32[]{:S(2)}) collective-permute-start(bf16[1024,512]{1,0:T(8,128)(2,1)} %bitcast.229), channel_id=1, source_target_pairs={{0,2},{1,3},{2,0},{3,1},{4,6},{5,7},{6,4},{7,5},{8,10},{9,11},{10,... | collective-permute-start | bytes 3145736 | tf_op jit(solution)/shard_map/ppermute | solution.py:276
  9.2 43.2 %collective-permute-start.6 = (bf16[1024,512]{1,0:T(8,128)(2,1)}, bf16[1024,512]{1,0:T(8,128)(2,1)}, u32[]{:S(2)}, u32[]{:S(2)}) collective-permute-start(bf16[1024,512]{1,0:T(8,128)(2,1)} %bitcast.228), channel_id=1, source_target_pairs={{0,2},{1,3},{2,0},{3,1},{4,6},{5,7},{6,4},{7,5},{8,10},{9,11},{10,... | collective-permute-start | bytes 3145736 | tf_op jit(solution)/shard_map/ppermute | solution.py:276
  9.2 61.9 %collective-permute-start.2 = (bf16[1024,512]{1,0:T(8,128)(2,1)}, bf16[1024,512]{1,0:T(8,128)(2,1)}, u32[]{:S(2)}, u32[]{:S(2)}) collective-permute-start(bf16[1024,512]{1,0:T(8,128)(2,1)} %bitcast.229), channel_id=1, source_target_pairs={{0,1},{1,0},{2,3},{3,2},{4,5},{5,4},{6,7},{7,6},{8,9},{9,8},{10,11... | collective-permute-start | bytes 3145736 | tf_op jit(solution)/shard_map/ppermute | solution.py:276
  9.3 61.8 %collective-permute-start.8 = (bf16[1024,512]{1,0:T(8,128)(2,1)}, bf16[1024,512]{1,0:T(8,128)(2,1)}, u32[]{:S(2)}, u32[]{:S(2)}) collective-permute-start(bf16[1024,512]{1,0:T(8,128)(2,1)} %bitcast.228), channel_id=1, source_target_pairs={{0,1},{1,0},{2,3},{3,2},{4,5},{5,4},{6,7},{7,6},{8,9},{9,8},{10,11... | collective-permute-start | bytes 3145736 | tf_op jit(solution)/shard_map/ppermute | solution.py:276
  30.6 40.5 %collective-permute-start.1 = (bf16[1024,512]{1,0:T(8,128)(2,1)S(1)}, bf16[1024,512]{1,0:T(8,128)(2,1)}, u32[]{:S(2)}, u32[]{:S(2)}) collective-permute-start(bf16[1024,512]{1,0:T(8,128)(2,1)S(1)} %collective-permute-done), channel_id=1, source_target_pairs={{0,1},{1,0},{2,3},{3,2},{4,5},{5,4},{6,7},{7,6},{8,9},{9,8},{10,11... | collective-permute-start | bytes 3145736 | tf_op jit(solution)/shard_map/ppermute | solution.py:276
  52.4 18.7 %collective-permute-start.7 = (bf16[1024,512]{1,0:T(8,128)(2,1)}, bf16[1024,512]{1,0:T(8,128)(2,1)}, u32[]{:S(2)}, u32[]{:S(2)}) collective-permute-start(bf16[1024,512]{1,0:T(8,128)(2,1)} %collective-permute-done.6), channel_id=1, source_target_pairs={{0,1},{1,0},{2,3},{3,2},{4,5},{5,4},{6,7},{7,6},{8,9},{9,8},{10,11... | collective-permute-start | bytes 3145736 | tf_op jit(solution)/shard_map/ppermute | solution.py:276
  100.4 11.3 %collective-permute-start.4 = (f32[160,1024]{1,0:T(8,128)}, f32[160,1024]{1,0:T(8,128)}, u32[]{:S(2)}, u32[]{:S(2)}) collective-permute-start(f32[160,1024]{1,0:T(8,128)} %copy.82), channel_id=1, source_target_pairs={{0,1},{1,0},{2,3},{3,2},{4,5},{5,4},{6,7},{7,6},{8,9},{9,8},{10,11... | collective-permute-start | bytes 1966088 | tf_op jit(solution)/shard_map/ppermute | solution.py:276
  113.3 14.4 %collective-permute-start.5 = (bf16[160,1024]{0,1:T(8,128)(2,1)S(1)}, bf16[160,1024]{0,1:T(8,128)(2,1)S(1)}, u32[]{:S(2)}, u32[]{:S(2)}) collective-permute-start(bf16[160,1024]{0,1:T(8,128)(2,1)S(1)} %get-tuple-element.89), channel_id=1, source_target_pairs={{0,2},{1,3},{2,0},{3,1},{4,6},{5,7},{6,4},{7,5},{8,10},{9,11},{10,... | collective-permute-start | bytes 983048 | tf_op jit(solution)/shard_map/ppermute | solution.py:276
  175.1 16.4 %collective-permute-start.9 = (bf16[18,8,1024]{2,1,0:T(8,128)(2,1)S(1)}, bf16[18,8,1024]{2,1,0:T(8,128)(2,1)S(1)}, u32[]{:S(2)}, u32[]{:S(2)}) collective-permute-start(bf16[18,8,1024]{2,1,0:T(8,128)(2,1)S(1)} %get-tuple-element.136), channel_id=1, source_target_pairs={{0,4},{4,8},{8,12},{12,16},{16,20},{20,24},{24,28},{1,5},{5,9},{9,... | collective-permute-start | bytes 884744 | tf_op jit(solution)/shard_map/ppermute | solution.py:281
  192.3 11.9 %collective-permute-start.15 = (bf16[18,8,1024]{2,1,0:T(8,128)(2,1)}, bf16[18,8,1024]{2,1,0:T(8,128)(2,1)S(1)}, u32[]{:S(2)}, u32[]{:S(2)}) collective-permute-start(bf16[18,8,1024]{2,1,0:T(8,128)(2,1)} %pad_maximum_fusion.13), channel_id=1, source_target_pairs={{8,0},{12,4},{16,8},{20,12},{24,16},{28,20},{9,1},{13,5},{17,9},{2... | collective-permute-start | bytes 884744 | tf_op jit(solution)/shard_map/ppermute | solution.py:281
  208.7 15.7 %collective-permute-start.16 = (bf16[18,8,1024]{2,1,0:T(8,128)(2,1)S(1)}, bf16[18,8,1024]{2,1,0:T(8,128)(2,1)S(1)}, u32[]{:S(2)}, u32[]{:S(2)}) collective-permute-start(bf16[18,8,1024]{2,1,0:T(8,128)(2,1)S(1)} %pad_maximum_fusion.14), channel_id=1, source_target_pairs={{16,0},{20,4},{24,8},{28,12},{17,1},{21,5},{25,9},{29,13},{18,2},{... | collective-permute-start | bytes 884744 | tf_op jit(solution)/shard_map/ppermute | solution.py:281
  278.5 196.0 %collective-permute-start.39 = (bf16[2,2,256,1024]{3,2,0,1:T(8,128)(2,1)}, bf16[2,2,256,1024]{3,2,0,1:T(8,128)(2,1)}, u32[]{:S(2)}, u32[]{:S(2)}) collective-permute-start(bf16[2,2,256,1024]{3,2,0,1:T(8,128)(2,1)} %bitcast.225), channel_id=1, source_target_pairs={{0,4},{4,0},{8,12},{12,8},{16,20},{20,16},{24,28},{28,24},{1,5},{5... | collective-permute-start | bytes 6291464 | tf_op jit(solution)/shard_map/ppermute | solution.py:276
  356.3 23.1 %collective-permute-start.17 = (f32[160,1024]{1,0:T(8,128)}, f32[160,1024]{1,0:T(8,128)}, u32[]{:S(2)}, u32[]{:S(2)}) collective-permute-start(f32[160,1024]{1,0:T(8,128)} %pad_maximum_fusion.6), channel_id=1, source_target_pairs={{0,1},{1,0},{2,3},{3,2},{4,5},{5,4},{6,7},{7,6},{8,9},{9,8},{10,11... | collective-permute-start | bytes 1966088 | tf_op jit(solution)/shard_map/ppermute | solution.py:276
  369.1 108.4 %collective-permute-start.30 = (bf16[2,2,256,1024]{3,2,0,1:T(8,128)(2,1)}, bf16[2,2,256,1024]{3,2,0,1:T(8,128)(2,1)}, u32[]{:S(2)}, u32[]{:S(2)}) collective-permute-start(bf16[2,2,256,1024]{3,2,0,1:T(8,128)(2,1)} %bitcast.226), channel_id=1, source_target_pairs={{0,4},{4,0},{8,12},{12,8},{16,20},{20,16},{24,28},{28,24},{1,5},{5... | collective-permute-start | bytes 6291464 | tf_op jit(solution)/shard_map/ppermute | solution.py:276
  398.5 21.3 %collective-permute-start.19 = (f32[24,1024]{1,0:T(8,128)S(1)}, f32[24,1024]{1,0:T(8,128)S(1)}, u32[]{:S(2)}, u32[]{:S(2)}) collective-permute-start(f32[24,1024]{1,0:T(8,128)S(1)} %slice.194), channel_id=1, source_target_pairs={{4,0},{8,4},{12,8},{16,12},{20,16},{24,20},{28,24},{5,1},{9,5},{13... | collective-permute-start | bytes 294920 | tf_op jit(solution)/shard_map/ppermute | solution.py:281
  400.0 54.0 %collective-permute-start.36 = (bf16[2,2,36,1024]{3,2,1,0:T(8,128)(2,1)S(1)}, bf16[2,2,36,1024]{3,2,1,0:T(8,128)(2,1)}, u32[]{:S(2)}, u32[]{:S(2)}) collective-permute-start(bf16[2,2,36,1024]{3,2,1,0:T(8,128)(2,1)S(1)} %fusion.37), channel_id=1, source_target_pairs={{0,4},{4,0},{8,12},{12,8},{16,20},{20,16},{24,28},{28,24},{1,5},{5... | collective-permute-start | bytes 884744 | tf_op jit(solution)/shard_map/ppermute | solution.py:276
  425.9 17.1 %collective-permute-start.33 = (f32[23,1024]{1,0:T(8,128)S(1)}, f32[23,1024]{1,0:T(8,128)S(1)}, u32[]{:S(2)}, u32[]{:S(2)}) collective-permute-start(f32[23,1024]{1,0:T(8,128)S(1)} %concatenate.55), channel_id=1, source_target_pairs={{0,4},{4,0},{8,12},{12,8},{16,20},{20,16},{24,28},{28,24},{1,5},{5... | collective-permute-start | bytes 282632 | tf_op jit(solution)/shard_map/ppermute | solution.py:276
  433.0 17.0 %collective-permute-start.22 = (f32[1024]{0:T(1024)S(1)}, f32[1024]{0:T(1024)S(1)}, u32[]{:S(2)}, u32[]{:S(2)}) collective-permute-start(f32[1024]{0:T(1024)S(1)} %get-tuple-element.99), channel_id=1, source_target_pairs={{0,1},{1,0},{2,3},{3,2},{4,5},{5,4},{6,7},{7,6},{8,9},{9,8},{10,11... | collective-permute-start | bytes 12296 | tf_op jit(solution)/shard_map/ppermute | solution.py:276
  451.2 31.1 %collective-permute-start.12 = (bf16[2,1024,512]{2,1,0:T(8,128)(2,1)S(1)}, bf16[2,1024,512]{2,1,0:T(8,128)(2,1)S(1)}, u32[]{:S(2)}, u32[]{:S(2)}) collective-permute-start(bf16[2,1024,512]{2,1,0:T(8,128)(2,1)S(1)} %copy-done.24), channel_id=1, source_target_pairs={{0,1},{1,0},{2,3},{3,2},{4,5},{5,4},{6,7},{7,6},{8,9},{9,8},{10,11... | collective-permute-start | bytes 6291464 | tf_op jit(solution)/shard_map/ppermute | solution.py:276
  462.3 21.6 %collective-permute-start.20 = (bf16[2,1024,512]{2,1,0:T(8,128)(2,1)S(1)}, bf16[2,1024,512]{2,1,0:T(8,128)(2,1)S(1)}, u32[]{:S(2)}, u32[]{:S(2)}) collective-permute-start(bf16[2,1024,512]{2,1,0:T(8,128)(2,1)S(1)} %dynamic-slice_bitcast_fusion), channel_id=1, source_target_pairs={{0,1},{1,0},{2,3},{3,2},{4,5},{5,4},{6,7},{7,6},{8,9},{9,8},{10,11... | collective-permute-start | bytes 6291464 | tf_op jit(solution)/shard_map/ppermute | solution.py:276
  471.3 45.4 %collective-permute-start.27 = (bf16[2,2,256,1024]{3,2,0,1:T(8,128)(2,1)S(1)}, bf16[2,2,256,1024]{3,2,0,1:T(8,128)(2,1)S(1)}, u32[]{:S(2)}, u32[]{:S(2)}) collective-permute-start(bf16[2,2,256,1024]{3,2,0,1:T(8,128)(2,1)S(1)} %bitcast.245), channel_id=1, source_target_pairs={{0,4},{4,0},{8,12},{12,8},{16,20},{20,16},{24,28},{28,24},{1,5},{5... | collective-permute-start | bytes 6291464 | tf_op jit(solution)/shard_map/ppermute | solution.py:276
  477.4 40.6 %collective-permute-start.40 = (bf16[2,256,1024]{2,1,0:T(8,128)(2,1)S(1)}, bf16[2,256,1024]{2,1,0:T(8,128)(2,1)S(1)}, u32[]{:S(2)}, u32[]{:S(2)}) collective-permute-start(bf16[2,256,1024]{2,1,0:T(8,128)(2,1)S(1)} %dynamic-slice_bitcast_fusion.2), channel_id=1, source_target_pairs={{0,8},{4,12},{8,0},{12,4},{16,24},{20,28},{24,16},{28,20},{1,9},{5... | collective-permute-start | bytes 3145736 | tf_op jit(solution)/shard_map/ppermute | solution.py:276
  480.3 62.6 %collective-permute-start.31 = (bf16[2,256,1024]{2,1,0:T(8,128)(2,1)S(1)}, bf16[2,256,1024]{2,1,0:T(8,128)(2,1)S(1)}, u32[]{:S(2)}, u32[]{:S(2)}) collective-permute-start(bf16[2,256,1024]{2,1,0:T(8,128)(2,1)S(1)} %dynamic-slice_bitcast_fusion.3), channel_id=1, source_target_pairs={{0,8},{4,12},{8,0},{12,4},{16,24},{20,28},{24,16},{28,20},{1,9},{5... | collective-permute-start | bytes 3145736 | tf_op jit(solution)/shard_map/ppermute | solution.py:276
  483.0 60.4 %collective-permute-start.13 = (bf16[1024,512]{1,0:T(8,128)(2,1)S(1)}, bf16[1024,512]{1,0:T(8,128)(2,1)S(1)}, u32[]{:S(2)}, u32[]{:S(2)}) collective-permute-start(bf16[1024,512]{1,0:T(8,128)(2,1)S(1)} %dynamic-slice_bitcast_fusion.6), channel_id=1, source_target_pairs={{0,2},{1,3},{2,0},{3,1},{4,6},{5,7},{6,4},{7,5},{8,10},{9,11},{10,... | collective-permute-start | bytes 3145736 | tf_op jit(solution)/shard_map/ppermute | solution.py:276
  484.5 58.9 %collective-permute-start.21 = (bf16[1024,512]{1,0:T(8,128)(2,1)S(1)}, bf16[1024,512]{1,0:T(8,128)(2,1)S(1)}, u32[]{:S(2)}, u32[]{:S(2)}) collective-permute-start(bf16[1024,512]{1,0:T(8,128)(2,1)S(1)} %dynamic-slice_bitcast_fusion.5), channel_id=1, source_target_pairs={{0,2},{1,3},{2,0},{3,1},{4,6},{5,7},{6,4},{7,5},{8,10},{9,11},{10,... | collective-permute-start | bytes 3145736 | tf_op jit(solution)/shard_map/ppermute | solution.py:276
  517.9 44.1 %collective-permute-start.28 = (bf16[2,256,1024]{2,1,0:T(8,128)(2,1)S(1)}, bf16[2,256,1024]{2,1,0:T(8,128)(2,1)S(1)}, u32[]{:S(2)}, u32[]{:S(2)}) collective-permute-start(bf16[2,256,1024]{2,1,0:T(8,128)(2,1)S(1)} %dynamic-slice_bitcast_fusion.4), channel_id=1, source_target_pairs={{0,8},{4,12},{8,0},{12,4},{16,24},{20,28},{24,16},{28,20},{1,9},{5... | collective-permute-start | bytes 3145736 | tf_op jit(solution)/shard_map/ppermute | solution.py:276
  518.4 46.6 %collective-permute-start.41 = (bf16[256,1024]{1,0:T(8,128)(2,1)S(1)}, bf16[256,1024]{1,0:T(8,128)(2,1)S(1)}, u32[]{:S(2)}, u32[]{:S(2)}) collective-permute-start(bf16[256,1024]{1,0:T(8,128)(2,1)S(1)} %dynamic-slice_bitcast_fusion.7), channel_id=1, source_target_pairs={{0,16},{4,20},{8,24},{12,28},{16,0},{20,4},{24,8},{28,12},{1,17},{... | collective-permute-start | bytes 1572872 | tf_op jit(solution)/shard_map/ppermute | solution.py:276
  543.3 46.1 %collective-permute-start.32 = (bf16[256,1024]{1,0:T(8,128)(2,1)S(1)}, bf16[256,1024]{1,0:T(8,128)(2,1)S(1)}, u32[]{:S(2)}, u32[]{:S(2)}) collective-permute-start(bf16[256,1024]{1,0:T(8,128)(2,1)S(1)} %dynamic-slice_bitcast_fusion.8), channel_id=1, source_target_pairs={{0,16},{4,20},{8,24},{12,28},{16,0},{20,4},{24,8},{28,12},{1,17},{... | collective-permute-start | bytes 1572872 | tf_op jit(solution)/shard_map/ppermute | solution.py:276
  546.9 15.7 %collective-permute-start.24 = (f32[512]{0:T(512)S(1)}, f32[512]{0:T(512)S(1)}, u32[]{:S(2)}, u32[]{:S(2)}) collective-permute-start(f32[512]{0:T(512)S(1)} %get-tuple-element.95), channel_id=1, source_target_pairs={{0,4},{4,0},{8,12},{12,8},{16,20},{20,16},{24,28},{28,24},{1,5},{5... | collective-permute-start | bytes 6152 | tf_op jit(solution)/shard_map/ppermute | solution.py:276
  562.4 33.5 %collective-permute-start.29 = (bf16[256,1024]{1,0:T(8,128)(2,1)S(1)}, bf16[256,1024]{1,0:T(8,128)(2,1)S(1)}, u32[]{:S(2)}, u32[]{:S(2)}) collective-permute-start(bf16[256,1024]{1,0:T(8,128)(2,1)S(1)} %dynamic-slice_bitcast_fusion.9), channel_id=1, source_target_pairs={{0,16},{4,20},{8,24},{12,28},{16,0},{20,4},{24,8},{28,12},{1,17},{... | collective-permute-start | bytes 1572872 | tf_op jit(solution)/shard_map/ppermute | solution.py:276
  562.5 13.9 %collective-permute-start.25 = (f32[512]{0:T(512)S(1)}, f32[512]{0:T(512)S(1)}, u32[]{:S(2)}, u32[]{:S(2)}) collective-permute-start(f32[512]{0:T(512)S(1)} %add.380), channel_id=1, source_target_pairs={{0,8},{4,12},{8,0},{12,4},{16,24},{20,28},{24,16},{28,20},{1,9},{5... | collective-permute-start | bytes 6152 | tf_op jit(solution)/shard_map/ppermute | solution.py:276
  576.4 18.9 %collective-permute-start.26 = (f32[512]{0:T(512)S(1)}, f32[512]{0:T(512)S(1)}, u32[]{:S(2)}, u32[]{:S(2)}) collective-permute-start(f32[512]{0:T(512)S(1)} %add.381), channel_id=1, source_target_pairs={{0,16},{4,20},{8,24},{12,28},{16,0},{20,4},{24,8},{28,12},{1,17},{... | collective-permute-start | bytes 6152 | tf_op jit(solution)/shard_map/ppermute | solution.py:276
  (67 other events, 1215.0 us)

commit v2 on v1

v2 whole, which is shorter than its diff:
```python
import functools, math
import jax, jax.numpy as jnp
from jax import lax
from jax.sharding import PartitionSpec as P
from jax.experimental import pallas as pl
from jax.experimental.pallas import tpu as pltpu

LANES = 128
LOG2E = 1.4426950408889634
VM = 56 * 1024 * 1024
F32, BF16 = jnp.float32, jnp.bfloat16


def spread(rows_ref, select_ref, spread_ref, chunk, count, seqs):
    left, parts = rows_ref[...], []
    for _ in range(3):
        parts.append(left.astype(BF16))
        left = left - parts[-1].astype(F32)
    stacked = jnp.concatenate(parts, axis=0)
    for col in range(0, count, 2):
        wide = lax.dot_general(
            stacked, select_ref[:, col * LANES : (col + 2) * LANES], (((0,), (0,)), ((), ())), preferred_element_type=F32
        )
        for tok in range(chunk):
            for i in range(2):
                spread_ref[tok, col + i] = wide[tok * seqs : (tok + 1) * seqs, i * LANES : (i + 1) * LANES]


def ends_kernel(chunk, step_ref, mixed_ref, rows_ref, rate_ref, h_ref, spread_ref, select_ref):
    states, seqs, width = rate_ref.shape

    @pl.when(pl.program_id(0) == 0)
    def _():
        h_ref[...] = jnp.zeros_like(h_ref)
        row = lax.broadcasted_iota(jnp.int32, select_ref.shape, 0)
        col = lax.broadcasted_iota(jnp.int32, select_ref.shape, 1)
        select_ref[...] = (row % (2 * states) == col // LANES).astype(BF16)

    spread(rows_ref, select_ref, spread_ref, chunk, 2 * states, seqs)

    def tile_step(j, _):
        lanes = pl.ds(pl.multiple_of(j * LANES, LANES), LANES)
        h = [h_ref[n, :, lanes] for n in range(states)]
        for tok in range(0, chunk, 2):
            m = mixed_ref[pl.ds(tok * seqs, 2 * seqs), lanes].astype(F32)
            for k in range(2):
                s = step_ref[pl.ds((tok + k) * seqs, seqs), lanes]
                x = s * m[k * seqs : (k + 1) * seqs]
                for n in range(states):
                    h[n] = jnp.exp2(s * rate_ref[n, :, lanes]) * h[n] + spread_ref[tok + k, n] * x
        for n in range(states):
            h_ref[n, :, lanes] = h[n]
        return 0

    lax.fori_loop(0, width // LANES, tile_step, 0, unroll=2)


def starts_kernel(chunk, step_ref, yg_ref, spread_ref, rate_ref, q_ref):
    states, seqs, width = rate_ref.shape

    @pl.when(pl.program_id(0) == 0)
    def _():
        q_ref[...] = jnp.zeros_like(q_ref)

    def tile_step(j, _):
        lanes = pl.ds(pl.multiple_of(j * LANES, LANES), LANES)
        q = [q_ref[n, :, lanes] for n in range(states)]
        for tok in reversed(range(chunk)):
            rows = pl.ds(tok * seqs, seqs)
            s, y = step_ref[rows, lanes], yg_ref[rows, lanes]
            for n in range(states):
                q[n] = jnp.exp2(s * rate_ref[n, :, lanes]) * (q[n] + spread_ref[tok, states + n] * y)
        for n in range(states):
            q_ref[n, :, lanes] = q[n]
        return 0

    lax.fori_loop(0, width // LANES, tile_step, 0, unroll=2)


def spread_spec(chunk, states, seqs, at):
    return pl.BlockSpec((chunk, 2 * states, seqs, LANES), lambda i: (at(i), 0, 0, 0))


def local_ends(step, mixed, rows_t, rate, chunk):
    rows, width = step.shape
    states, seqs, _ = rate.shape
    elements = rows * width * states
    grid = rows // (chunk * seqs)
    row_spec = pl.BlockSpec((chunk * seqs, width), lambda i: (i, 0))
    whole = pl.BlockSpec((states, seqs, width), lambda i: (0, 0, 0))
    return pl.pallas_call(
        functools.partial(ends_kernel, chunk),
        grid=(grid,),
        in_specs=[row_spec, row_spec, pl.BlockSpec((2 * states, chunk * seqs), lambda i: (0, i)), whole],
        out_specs=[whole, spread_spec(chunk, states, seqs, lambda i: i)],
        out_shape=[jax.ShapeDtypeStruct(rate.shape, F32), jax.ShapeDtypeStruct((rows // seqs, 2 * states, seqs, LANES), F32)],
        scratch_shapes=[pltpu.VMEM((6 * states, 2 * states * LANES), BF16)],
        compiler_params=pltpu.CompilerParams(vmem_limit_bytes=VM),
        cost_estimate=pl.CostEstimate(flops=elements, bytes_accessed=elements, transcendentals=0),
        name="local_ends",
    )(step, mixed, rows_t, rate)


def local_starts(step, yg, wide_rows, rate, chunk):
    rows, width = step.shape
    states, seqs, _ = rate.shape
    elements = rows * width * states
    grid = rows // (chunk * seqs)
    at = lambda i: grid - 1 - i
    row_spec = pl.BlockSpec((chunk * seqs, width), lambda i: (at(i), 0))
    whole = pl.BlockSpec((states, seqs, width), lambda i: (0, 0, 0))
    return pl.pallas_call(
        functools.partial(starts_kernel, chunk),
        grid=(grid,),
        in_specs=[row_spec, row_spec, spread_spec(chunk, states, seqs, at), whole],
        out_specs=whole,
        out_shape=jax.ShapeDtypeStruct(rate.shape, F32),
        compiler_params=pltpu.CompilerParams(vmem_limit_bytes=VM),
        cost_estimate=pl.CostEstimate(flops=elements, bytes_accessed=elements, transcendentals=0),
        name="local_starts",
    )(step, yg, wide_rows, rate)


def fwd_kernel(chunk, step_ref, mixed_ref, gate_ref, gg_ref, spread_ref, rate_ref, skip_ref,
               hin_ref, *refs):
    state_ref, hist_ref, start_ref, gated_ref, ggrad_ref = refs[-5:]
    states, seqs, width = rate_ref.shape

    @pl.when(pl.program_id(0) == 0)
    def _():
        state_ref[...] = hin_ref[...]

    start_ref[0] = state_ref[...].astype(BF16)

    def tile_step(j, _):
        lanes = pl.ds(pl.multiple_of(j * LANES, LANES), LANES)
        h = [state_ref[n, :, lanes] for n in range(states)]
        skip = skip_ref[:, lanes]
        for tok in range(0, chunk, 2):
            pair_rows = pl.ds(tok * seqs, 2 * seqs)
            pair = mixed_ref[pair_rows, lanes].astype(F32)
            gated, ggrad = [], []
            for k in range(2):
                rows = pl.ds((tok + k) * seqs, seqs)
                s = step_ref[rows, lanes]
                m = pair[k * seqs : (k + 1) * seqs]
                x = s * m
                y = skip * m
                for n in range(states):
                    h[n] = jnp.exp2(s * rate_ref[n, :, lanes]) * h[n] + spread_ref[tok + k, n] * x
                    y = y + spread_ref[tok + k, states + n] * h[n]
                for n in range(0, states, 2):
                    hist_ref[tok + k, j, pl.ds(n * seqs, 2 * seqs), :] = jnp.concatenate([h[n], h[n + 1]], axis=0).astype(BF16)
                v = gate_ref[rows, lanes]
                sig = 1.0 / (1.0 + jnp.exp2(v * (-LOG2E)))
                gated.append(y * (v * sig))
                ggrad.append(gg_ref[rows, lanes] * y * (sig * (1.0 + v * (1.0 - sig))))
            gated_ref[pair_rows, lanes] = jnp.concatenate(gated, axis=0).astype(BF16)
            ggrad_ref[pair_rows, lanes] = jnp.concatenate(ggrad, axis=0).astype(BF16)
        for n in range(states):
            state_ref[n, :, lanes] = h[n]
        return 0

    lax.fori_loop(0, width // LANES, tile_step, 0, unroll=2)


def forward(arrays, skip, carried, filled, shapes, chunk, first, last):
    step, mixed, gate, gg, wide_rows, rate = arrays
    rows, width = step.shape
    states, seqs, _ = rate.shape
    at = lambda i: first + i
    row_spec = pl.BlockSpec((chunk * seqs, width), lambda i: (at(i), 0))
    whole = pl.BlockSpec((states, seqs, width), lambda i: (0, 0, 0))
    anywhere = pl.BlockSpec(memory_space=pl.ANY)
    elements = (last - first) * chunk * seqs * width * states
    return pl.pallas_call(
        functools.partial(fwd_kernel, chunk),
        grid=(last - first,),
        in_specs=[row_spec, row_spec, row_spec, row_spec, spread_spec(chunk, states, seqs, at), whole,
                  pl.BlockSpec((seqs, width), lambda i: (0, 0)), whole] + [anywhere] * len(filled),
        out_specs=[whole, pl.BlockSpec((chunk, width // LANES, states * seqs, LANES), lambda i: (at(i), 0, 0, 0)),
                   pl.BlockSpec((1, states, seqs, width), lambda i: (at(i), 0, 0, 0)), row_spec, row_spec],
        out_shape=[jax.ShapeDtypeStruct(*shape) for shape in shapes],
        input_output_aliases={7 + i: i for i in range(len(filled) + 1)},
        compiler_params=pltpu.CompilerParams(vmem_limit_bytes=VM),
        cost_estimate=pl.CostEstimate(flops=elements, bytes_accessed=elements, transcendentals=0),
        name="scan_forward",
    )(step, mixed, gate, gg, wide_rows, rate, skip, carried, *filled)


def bwd_kernel(chunk, step_ref, mixed_ref, yg_ref, spread_ref, rate_ref, skip_ref, hist_ref, start_ref, gin_ref,
               decay_ref, bias_ref, skipg_ref, pre_ref, part_ref, bcg_ref, state_ref, b_ref, c_ref):
    states, seqs, width = rate_ref.shape
    span = states * seqs

    @pl.when(pl.program_id(0) == 0)
    def _():
        state_ref[...] = gin_ref[...]
        decay_ref[...] = jnp.zeros_like(decay_ref)
        bias_ref[...] = jnp.zeros_like(bias_ref)
        skipg_ref[...] = jnp.zeros_like(skipg_ref)

    b_ref[...] = jnp.zeros_like(b_ref)
    c_ref[...] = jnp.zeros_like(c_ref)
    contract = (((1,), (1,)), ((), ()))

    def tile_step(j, _):
        lanes = pl.ds(pl.multiple_of(j * LANES, LANES), LANES)
        q = [state_ref[n, :, lanes] for n in range(states)]
        acc = [decay_ref[n, :, lanes] for n in range(states)]
        skip = skip_ref[:, lanes]
        bias = bias_ref[:, lanes]
        skipg = skipg_ref[:, lanes]
        for tok in range(chunk - 2, -1, -2):
            pair_rows = pl.ds(tok * seqs, 2 * seqs)
            pair = mixed_ref[pair_rows, lanes].astype(F32)
            pre, xs, packed = [None, None], [None, None], [None, None]
            for k in (1, 0):
                now = tok + k
                rows = pl.ds(now * seqs, seqs)
                s = step_ref[rows, lanes]
                y = yg_ref[rows, lanes]
                m = pair[k * seqs : (k + 1) * seqs]
                along = jnp.zeros_like(s)
                size = jnp.zeros_like(s)
                gs = []
                for n in range(0, states, 2):
                    if now > 0:
                        both = hist_ref[now - 1, j, pl.ds(n * seqs, 2 * seqs), :].astype(F32)
                        before = [both[:seqs], both[seqs:]]
                    else:
                        before = [start_ref[0, n + i, :, lanes].astype(F32) for i in range(2)]
                    for i in range(2):
                        z = s * rate_ref[n + i, :, lanes]
                        g = spread_ref[now, states + n + i] * y + q[n + i]
                        along = along + g * spread_ref[now, n + i]
                        q[n + i] = jnp.exp2(z) * g
                        r = q[n + i] * before[i] * z
                        acc[n + i] = acc[n + i] + r
                        size = size + r
                        gs.append(g)
                packed[k] = jnp.concatenate(gs, axis=0).astype(BF16)
                part_ref[rows, lanes] = s * along + skip * y
                skipg = skipg + y * m
                xs[k] = s * m
                series = 1.0 - s * (1.0 / 2) * (1.0 - s * (1.0 / 3) * (1.0 - s * (1.0 / 4) * (1.0 - s * (1.0 / 5))))
                ratio = jnp.where(s < 0.1, series, (1.0 - jnp.exp2(s * (-LOG2E))) / jnp.maximum(s, 0.1))
                pre[k] = ratio * (size * (1.0 / LOG2E) + xs[k] * along)
            rounded = jnp.concatenate(pre, axis=0).astype(BF16)
            pre_ref[pair_rows, lanes] = rounded
            wide = rounded.astype(F32)
            bias = bias + wide[:seqs] + wide[seqs:]
            x = jnp.concatenate(xs, axis=0).astype(BF16)
            pair_hist = jnp.concatenate([hist_ref[tok, j], hist_ref[tok + 1, j]], axis=0)
            b_ref[tok // 2] += lax.dot_general(x, jnp.concatenate(packed, axis=0), contract, preferred_element_type=F32)
            c_ref[tok // 2] += lax.dot_general(
                yg_ref[pair_rows, lanes].astype(BF16), pair_hist, contract, preferred_element_type=F32
            )
        for n in range(states):
            state_ref[n, :, lanes] = q[n]
            decay_ref[n, :, lanes] = acc[n]
        bias_ref[:, lanes] = bias
        skipg_ref[:, lanes] = skipg
        return 0

    lax.fori_loop(0, width // LANES, tile_step, 0, unroll=2)
    wide = 2 * span
    row = lax.broadcasted_iota(jnp.int32, (2 * seqs, wide), 0)
    col = lax.broadcasted_iota(jnp.int32, (2 * seqs, wide), 1)
    match = (row // seqs == col // span) & (row % seqs == col % seqs)
    b_rows = [jnp.where(match, b_ref[i], 0.0) for i in range(chunk // 2)]
    c_rows = [jnp.where(match, c_ref[i], 0.0) for i in range(chunk // 2)]
    src = lax.broadcasted_iota(jnp.int32, (2 * states, wide), 1) // seqs % states
    dst = lax.broadcasted_iota(jnp.int32, (2 * states, wide), 0)
    fold_b = (src == dst).astype(BF16)
    fold_c = (src + states == dst).astype(BF16)
    bcg_ref[...] = lax.dot_general(
        fold_b, jnp.concatenate(b_rows, axis=0).astype(BF16), contract, preferred_element_type=F32
    ) + lax.dot_general(fold_c, jnp.concatenate(c_rows, axis=0).astype(BF16), contract, preferred_element_type=F32)


def backward(step, mixed, yg, wide_rows, rate, skip, hist, start, gin, chunk):
    rows, width = step.shape
    states, seqs, _ = rate.shape
    grid = rows // (chunk * seqs)
    elements = rows * width * states
    at = lambda i: grid - 1 - i
    row_spec = pl.BlockSpec((chunk * seqs, width), lambda i: (at(i), 0))
    col_spec = pl.BlockSpec((2 * states, chunk * seqs), lambda i: (0, at(i)))
    whole = pl.BlockSpec((states, seqs, width), lambda i: (0, 0, 0))
    one = pl.BlockSpec((seqs, width), lambda i: (0, 0))
    return pl.pallas_call(
        functools.partial(bwd_kernel, chunk),
        grid=(grid,),
        in_specs=[row_spec, row_spec, row_spec, spread_spec(chunk, states, seqs, at), whole, one,
                  pl.BlockSpec((chunk, width // LANES, states * seqs, LANES), lambda i: (at(i), 0, 0, 0)),
                  pl.BlockSpec((1, states, seqs, width), lambda i: (at(i), 0, 0, 0)), whole],
        out_specs=[whole, one, one, row_spec, row_spec, col_spec],
        out_shape=[jax.ShapeDtypeStruct(rate.shape, F32), jax.ShapeDtypeStruct((seqs, width), F32),
                   jax.ShapeDtypeStruct((seqs, width), F32), jax.ShapeDtypeStruct((rows, width), BF16),
                   jax.ShapeDtypeStruct((rows, width), F32), jax.ShapeDtypeStruct((2 * states, rows), F32)],
        scratch_shapes=[pltpu.VMEM(rate.shape, F32)] + [pltpu.VMEM((chunk // 2, 2 * seqs, 2 * states * seqs), F32)] * 2,
        compiler_params=pltpu.CompilerParams(vmem_limit_bytes=VM),
        cost_estimate=pl.CostEstimate(flops=elements, bytes_accessed=elements, transcendentals=0),
        name="scan_backward",
    )(step, mixed, yg, wide_rows, rate, skip, hist, start, gin)


EPSILON = 1e-05
CONTRACT_LAST = (((1,), (1,)), ((), ()))
CONTRACT_FIRST = (((0,), (0,)), ((), ()))


def dot(a, b, dims=(((1,), (0,)), ((), ())), out=F32):
    return lax.dot_general(a, b, dims, preferred_element_type=out)


def after(value, *done):
    return lax.optimization_barrier((value, done))[0]


def swapped(value, axis, bit):
    count = lax.axis_size(axis)
    return lax.ppermute(value, axis, [(i, i ^ (1 << bit)) for i in range(count)])


def moved(value, axis, distance):
    count = lax.axis_size(axis)
    return lax.ppermute(value, axis, [(i, i + distance) for i in range(count) if 0 <= i + distance < count])


def bits_of(axis):
    return lax.axis_size(axis).bit_length() - 1


def own_bit(axis, bit):
    return (lax.axis_index(axis) >> bit) & 1


def gathered(value, axis, meanwhile=()):
    count = lax.axis_size(axis)
    parts = {0: value}
    for bit in reversed(range(bits_of(axis))):
        fresh = {mask | (1 << bit): swapped(part, axis, bit) for mask, part in parts.items()}
        if len(parts) == 1:
            fresh, meanwhile = lax.optimization_barrier((fresh, meanwhile))
        parts |= fresh
    for bit in range(bits_of(axis)):
        high = own_bit(axis, bit) == 1
        parts = {m: jnp.where(high, parts[m ^ (1 << bit)], parts[m]) for m in range(count)}
    return jnp.concatenate([parts[m] for m in range(count)], axis=-1), meanwhile


def summed(value, axis, narrow_from):
    for bit in range(bits_of(axis)):
        sent = value.astype(BF16) if bit >= narrow_from else value
        value = value + swapped(sent, axis, bit).astype(F32)
    return value


def pick(value, dim, index):
    return lax.dynamic_index_in_dim(value, index, dim, keepdims=False)


class Scattered:
    def __init__(self, blocks, axis, order=None, halves=None):
        bits = bits_of(axis)
        self.axis, self.left, self.order = axis, list(range(bits)), list(order or range(bits))
        self.got, self.kept, self.sent = None, None, None
        if halves:
            self.kept, self.sent = halves
        else:
            self.value = blocks.reshape((2,) * bits + blocks.shape[1:])

    def split(self):
        if self.sent is not None:
            return
        bit = self.order[0]
        dim = len(self.left) - 1 - self.left.index(bit)
        mine = own_bit(self.axis, bit)
        self.kept, self.sent = pick(self.value, dim, mine), pick(self.value, dim, 1 - mine)

    def send(self):
        self.got = swapped(self.sent, self.axis, self.order[0])

    def add(self):
        bit = self.order.pop(0)
        self.left.remove(bit)
        value = self.kept.astype(F32) + self.got.astype(F32)
        self.value = value.astype(BF16) if self.left else value
        self.got, self.kept, self.sent = None, None, None


def start_all(sums, *values):
    sums = [s for s in sums if s.order]
    for s in sums:
        s.split()
    sent, values = lax.optimization_barrier(([s.sent for s in sums], values))
    for s, message in zip(sums, sent):
        s.sent = message
        s.send()
    return values


def end_all(sums, *values):
    sums = [s for s in sums if s.got is not None]
    got, values = lax.optimization_barrier(([s.got for s in sums], values))
    for s, message in zip(sums, got):
        s.got = message
        s.add()
    return values


def padded_rows(value, dim, multiple):
    width = -value.shape[dim] % multiple
    return jnp.pad(value, [(0, width if i == dim else 0) for i in range(value.ndim)])


class ScatteredWith(Scattered):
    def __init__(self, blocks, axis, order, extra):
        super().__init__(blocks, axis, order)
        self.extra = extra

    def split(self):
        super().split()
        upper = self.extra.astype(BF16)
        lower = (self.extra - upper.astype(F32)).astype(BF16)
        self.extra = upper.astype(F32) + lower.astype(F32)
        self.shape = self.sent.shape
        self.sent = jnp.concatenate([self.sent.reshape(-1, self.shape[-1]), upper, lower], axis=0)

    def add(self):
        count = self.extra.shape[0]
        upper, lower = self.got[-2 * count : -count], self.got[-count:]
        self.extra = self.extra + (upper.astype(F32) + lower.astype(F32))
        self.got = self.got[: -2 * count].reshape(self.shape)
        super().add()


def columns_by(value, axis, bit):
    count = lax.axis_size(axis)
    width = value.shape[1] // (count >> bit)
    parts = [value[:, i * width : (i + 1) * width] for i in range(count >> bit)]
    high = own_bit(axis, bit) == 1
    low, up = parts[0::2], parts[1::2]
    return [
        jnp.concatenate([jnp.where(high, b, a) for a, b in zip(one, two)], axis=1) for one, two in ((low, up), (up, low))
    ]


def rest_scattered(value, axis, bit):
    count = lax.axis_size(axis)
    groups = [[i for i in range(count) if (i >> bit) & 1 == side] for side in range(2)]
    value = value.reshape(-1, value.shape[-1])
    return lax.psum_scatter(value, axis, scatter_dimension=0, tiled=True, axis_index_groups=groups).astype(F32)


def finished_on_the_way(s):
    if s.got is not None:
        s.add()
    while s.order:
        s.split()
        s.send()
        s.add()
    return s.value


def entering(local, total, rate, axis, direction, fillers):
    states = rate.shape[0]
    enter, enter_sum = jnp.zeros_like(local), jnp.zeros_like(total)
    through, through_sum = local, total
    distance = 1
    filled, fillers = [], list(fillers)
    while distance < lax.axis_size(axis):
        upper = through_sum.astype(BF16)
        lower = (through_sum - upper.astype(F32)).astype(BF16)
        packet = jnp.concatenate([through.astype(BF16), upper[None], lower[None]], axis=0)
        got = moved(packet, axis, distance * direction)
        if fillers:
            out = fillers.pop(0)(packet, filled)
            got, out = lax.optimization_barrier((got, out))
            filled.append(out)
        got = got.astype(F32)
        state, step_sum = got[:states], got[states] + got[states + 1]
        enter, enter_sum = enter + jnp.exp2(rate * enter_sum) * state, enter_sum + step_sum
        through, through_sum = through + jnp.exp2(rate * through_sum) * state, through_sum + step_sum
        distance *= 2
    for filler in fillers:
        filled.append(filler(enter, filled))
    return enter, filled


def silu_slope(pre_value):
    sigmoid_value = jax.nn.sigmoid(pre_value)
    return sigmoid_value * (1.0 + pre_value * (1.0 - sigmoid_value))


def shards(
    residual_in,
    norm_gain,
    in_weight,
    conv_weight,
    conv_bias,
    proj_weight,
    step_weight,
    step_bias,
    decay_log,
    skip_gain,
    out_weight,
    out_grad,
):
    seqs, toks, share = residual_in.shape
    model = norm_gain.shape[0]
    taps, inner = conv_weight.shape
    states = decay_log.shape[0]
    rank = step_weight.shape[0]
    rows = seqs * toks
    chunk = math.gcd(toks, 16)
    chunks = toks // chunk
    seq_count = lax.axis_size("seq")
    chan_bits = bits_of("chan")
    own_in = residual_in.swapaxes(0, 1).reshape(rows, share)
    own_out_grad = out_grad.swapaxes(0, 1).reshape(rows, share)
    full_in, (conv_weights, gate_weights) = gathered(own_in, "chan", (in_weight[:, 0], in_weight[:, 1]))
    wide_in = full_in.astype(F32)
    inv_rms = lax.rsqrt(jnp.mean(wide_in * wide_in, axis=-1, keepdims=True) + EPSILON)
    gain_full = norm_gain.astype(F32)
    normed = (wide_in * inv_rms * gain_full).astype(BF16)
    conv_in = dot(normed, conv_weights, out=BF16)
    halo = (taps - 1) * seqs
    normed_halo = moved(normed[rows - halo :], "seq", 1)
    previous = dot(normed_halo, conv_weights, out=BF16)
    padded = jnp.concatenate([previous, conv_in], axis=0).astype(F32)
    conv_taps = conv_weight.astype(F32)
    conv_out = conv_bias.astype(F32) + sum(
        conv_taps[k] * padded[k * seqs : k * seqs + rows] for k in range(taps)
    )
    mixed = jax.nn.silu(conv_out).astype(BF16)
    proj_part = dot(proj_weight, mixed, CONTRACT_LAST)
    for bit in range(chan_bits):
        received = swapped(proj_part.astype(BF16) if bit else proj_part, "chan", bit)
        if bit == chan_bits - 1:
            gate_pre = dot(after(normed, proj_part), gate_weights)
            extended_normed = jnp.concatenate([normed_halo, after(normed, gate_pre)], axis=0)
            received, gate_pre, extended_normed = lax.optimization_barrier((received, gate_pre, extended_normed))
        proj_part = proj_part + received.astype(F32)
    projected = proj_part
    step_low = projected[:rank].astype(BF16)
    step_pre = dot(step_low, step_weight, CONTRACT_FIRST) + step_bias.astype(F32)
    step = jax.nn.softplus(step_pre)
    decay_rate = -jnp.exp(decay_log)
    rate = jnp.broadcast_to((decay_rate * LOG2E)[:, None], (states, seqs, inner))
    skip = jnp.broadcast_to(skip_gain, (seqs, inner))
    local_end, wide_rows = local_ends(step, mixed, projected[rank:], rate, chunk)
    step_total = jnp.sum(step.reshape(toks, seqs, inner), axis=0)
    grad_whole, _ = gathered(after(own_out_grad, gate_pre), "chan", local_end)

    def output_side(sent, _):
        gated_grad = dot(after(grad_whole, sent), out_weight)
        return gated_grad, gated_grad * jax.nn.silu(gate_pre)

    def starts_side(sent, filled):
        return local_starts(step, after(filled[0][1], sent), wide_rows, rate, chunk)

    seq_bits = list(range(bits_of("seq")))
    other_bits = [1, 0] + seq_bits[2:] if len(seq_bits) > 1 else seq_bits
    def columns_side(sent, _):
        return columns_by(after(grad_whole, sent), "seq", 0), columns_by(after(normed, sent), "seq", other_bits[0])

    enter_h, filled = entering(local_end, step_total, rate, "seq", 1, [output_side, starts_side, columns_side])
    (gated_grad, y_grad), local_start, sides = filled[:3]
    shapes = [
        (rate.shape, F32),
        ((toks, inner // LANES, states * seqs, LANES), BF16),
        ((chunks, states, seqs, inner), BF16),
        ((rows, inner), BF16),
        ((rows, inner), BF16),
    ]
    arrays = (step, mixed, gate_pre, gated_grad, wide_rows, rate)
    middle = chunks // 2

    def first_side(sent, _):
        return forward(arrays, skip, after(enter_h, sent), (), shapes, chunk, 0, middle)

    def second_side(sent, filled):
        state, *done = after(filled[1], sent)
        return forward(arrays, skip, state, done, shapes, chunk, middle, chunks)

    enter_g, filled = entering(
        local_start, step_total, rate, "seq", -1, [lambda sent, _: enter_h, first_side, second_side]
    )
    _, history, starts, gated_out, gate_grad = filled[2]
    by_owner = lambda value: value.reshape(rows, -1, share).swapaxes(0, 1)
    by_part = lambda value: value.reshape(seq_count, -1, value.shape[-1])
    first_product = lambda columns, value: dot(columns, value, CONTRACT_FIRST, out=BF16).reshape(
        (2,) * (len(seq_bits) - 1) + (-1, inner)
    )
    out_weight_sum = Scattered(None, "seq", seq_bits, (None, first_product(sides[0][1], gated_out)))
    gate_weight_sum = Scattered(None, "seq", other_bits, (None, first_product(sides[1][1], gate_grad)))
    weight_sums = [out_weight_sum, gate_weight_sum]
    start_all(weight_sums)
    for s, columns, value in zip(weight_sums, (sides[0][0], sides[1][0]), (gated_out, gate_grad)):
        s.kept = first_product(columns, after(value, *[s.sent for s in weight_sums]))
    enter_g = after(enter_g, [s.kept for s in weight_sums])
    decay_parts, bias_parts, skip_parts, pre_grad, mixed_part, bc_grads = backward(
        step, mixed, y_grad, wide_rows, rate, skip, history, starts, enter_g, chunk
    )
    pre_grad, bc_grads = end_all(weight_sums, pre_grad, bc_grads)
    out_weight_grad = rest_scattered(out_weight_sum.value, "seq", seq_bits[0])
    gate_weight_grad = rest_scattered(after(gate_weight_sum.value, out_weight_grad), "seq", other_bits[0])
    low_grad = dot(step_weight, pre_grad, CONTRACT_LAST)
    proj_sum = jnp.concatenate([low_grad, bc_grads], axis=0)
    for bit in range(chan_bits):
        received = swapped(proj_sum.astype(BF16) if bit else proj_sum, "chan", bit)
        if bit == chan_bits - 1:
            branch = dot(after(gated_out, proj_sum), out_weight, CONTRACT_LAST, out=BF16)
            received, branch = lax.optimization_barrier((received, branch))
        proj_sum = proj_sum + received.astype(F32)
    proj_grad = proj_sum.astype(BF16)
    branch_sum = Scattered(by_owner(branch), "chan")
    (proj_grad,) = start_all([branch_sum], proj_grad)
    proj_weight_part = dot(proj_grad, mixed, out=BF16)
    step_weight_part = dot(step_low, pre_grad, out=BF16)
    mixed_grad = mixed_part + dot(proj_grad, proj_weight, CONTRACT_FIRST)
    conv_grad = mixed_grad * silu_slope(conv_out)
    conv_bias_grad = jnp.sum(conv_grad, axis=0)
    conv_weight_grad = jnp.stack(
        [jnp.sum(conv_grad * padded[k * seqs : k * seqs + rows], axis=0) for k in range(taps)]
    )
    incoming = moved(conv_grad[:halo], "seq", -1)

    def spread_back(grads, count):
        return sum(conv_taps[k] * grads[(taps - 1 - k) * seqs : (taps - 1 - k) * seqs + count] for k in range(taps))

    none = jnp.zeros((halo, inner), F32)
    own_spread = spread_back(jnp.concatenate([none, conv_grad, none], axis=0), rows + halo).astype(BF16)
    own_spread, out_weight_grad = end_all([branch_sum], own_spread, out_weight_grad)
    half = inner // 2
    sums = jnp.concatenate(
        [
            jnp.sum(decay_parts, axis=1),
            conv_weight_grad,
            conv_bias_grad[None],
            jnp.sum(bias_parts, axis=0)[None],
            jnp.sum(skip_parts, axis=0)[None],
        ],
        axis=0,
    )

    sum_rows = sums.shape[0]
    sums = padded_rows(jnp.concatenate([sums[:, :half], sums[:, half:]], axis=0), 0, 16)

    def last_blocks(columns):
        conv_weights_part = dot(extended_normed, own_spread[:, columns], CONTRACT_FIRST, out=BF16)
        blocks = [by_part(conv_weights_part), by_part(proj_weight_part[:, columns]), by_part(step_weight_part[:, columns])]
        return padded_rows(jnp.concatenate(blocks, axis=1), 1, 16)

    last_sums = [
        ScatteredWith(last_blocks(slice(0, half)), "seq", seq_bits, sums),
        Scattered(last_blocks(slice(half, inner)), "seq", other_bits),
    ]
    last_sent = start_all([*last_sums, branch_sum], conv_grad, incoming)
    conv_grad, incoming = last_sent
    conv_in_grad = spread_back(jnp.concatenate([conv_grad, incoming], axis=0), rows).astype(BF16)
    gate_side = dot(gate_grad, after(gate_weights, [s.sent for s in last_sums]), CONTRACT_LAST)
    normed_part = (dot(conv_in_grad, conv_weights, CONTRACT_LAST) + gate_side).astype(BF16)
    (normed_part,) = end_all([*last_sums, branch_sum], normed_part)
    normed_sum = Scattered(by_owner(normed_part), "chan")
    conv_in_grad, row_gate = start_all([normed_sum, *last_sums], conv_in_grad, gate_grad)
    row_dots = jnp.sum(
        conv_in_grad.astype(F32) * conv_in.astype(F32) + row_gate.astype(F32) * gate_pre, axis=1
    )
    row_dots = summed(row_dots, "chan", chan_bits)[:, None]
    row_dots, gate_weight_grad = end_all([normed_sum, *last_sums], row_dots, gate_weight_grad)
    (row_dots,) = start_all([normed_sum, *last_sums], row_dots)
    (row_dots,) = end_all([normed_sum, *last_sums], row_dots)
    normed_grad = finished_on_the_way(normed_sum)
    wide_own = own_in.astype(F32)
    own_gain = lax.dynamic_slice_in_dim(gain_full, lax.axis_index("chan") * share, share, 0)
    in_rows = (
        own_out_grad.astype(F32)
        + inv_rms * own_gain * normed_grad
        - wide_own * (inv_rms * inv_rms / model) * row_dots
    ).astype(BF16)
    in_grad = in_rows.reshape(toks, seqs, share).swapaxes(0, 1)
    gain_grad = summed(jnp.sum(normed_grad * wide_own * inv_rms, axis=0), "seq", bits_of("seq"))
    last = jnp.concatenate([finished_on_the_way(s) for s in last_sums], axis=-1)
    sums = last_sums[0].extra
    sums = jnp.concatenate([sums[:sum_rows], sums[sum_rows : 2 * sum_rows]], axis=1)
    weight_share, proj_share, step_share = (count // seq_count for count in (model, proj_weight.shape[0], rank))
    block_rows = (own_in.astype(F32) + finished_on_the_way(branch_sum)).astype(BF16)
    block_out = block_rows.reshape(toks, seqs, share).swapaxes(0, 1)
    return (
        block_out,
        in_grad,
        gain_grad,
        jnp.stack([last[:weight_share], gate_weight_grad], axis=1),
        sums[states : states + taps],
        sums[states + taps],
        last[weight_share : weight_share + proj_share],
        last[weight_share + proj_share : weight_share + proj_share + step_share],
        sums[states + taps + 1],
        sums[:states] * (1.0 / LOG2E),
        sums[states + taps + 2],
        out_weight_grad.astype(F32),
    )


def solution(mesh):
    in_specs = (
        P(None, "seq", "chan"),
        P(),
        P(None, None, "chan"),
        P(None, "chan"),
        P("chan"),
        P(None, "chan"),
        P(None, "chan"),
        P("chan"),
        P(None, "chan"),
        P("chan"),
        P(None, "chan"),
        P(None, "seq", "chan"),
    )
    out_specs = (
        P(None, "seq", "chan"),
        P(None, "seq", "chan"),
        P("chan"),
        P("seq", None, "chan"),
        P(None, "chan"),
        P("chan"),
        P("seq", "chan"),
        P("seq", "chan"),
        P("chan"),
        P(None, "chan"),
        P("chan"),
        P("seq", "chan"),
    )
    return jax.shard_map(shards, mesh=mesh, in_specs=in_specs, out_specs=out_specs, check_vma=False)
```

time: 607 us -> 494 us (0.81)
  waiting for transfers between devices: 192 us -> 98 us
  other arithmetic: 53.2 us -> 84.4 us
  Pallas kernels: 142 us -> 116 us
  starting transfers between devices: 63.7 us -> 39.6 us
  matrix products: 89.7 us -> 71.5 us
  between operations: 2.41 us -> 16.2 us
    ppermute x34 -> x27, waiting for transfers between devices: 149 us -> 89 us  [swapped(): return lax.ppermute(value, axis, [(i, i ^ 1 << bit) for i in range(count)])]
    ppermute x8, waiting for transfers between devices: 42.8 us -> 1.55 us  [moved(): lax.ppermute(value, axis, [(i, i + distance) for i in range(count) if 0 <...]
    pallas_call x1, Pallas kernels: 70.7 us -> 44.8 us  [backward(): pl.pallas_call(functools.partial(bwd_kernel, chunk), grid=(grid,), in_spe...]
    ppermute x34 -> x27, starting transfers between devices: 40.2 us -> 20.1 us  [swapped(): return lax.ppermute(value, axis, [(i, i ^ 1 << bit) for i in range(count)])]
    dot_general x15 -> x19, matrix products: 89.7 us -> 71.5 us  [dot(): return lax.dot_general(a, b, dims, preferred_element_type=out)]
    convert_element_type x31 -> x37, other arithmetic: 21.9 us -> 39.7 us  [the longest x8 17.7 us: add(): self.value = value.astype(BF16) if self.left else value]
    concatenate x6 -> x22, other arithmetic: 2.73 us -> 18.3 us  [the longest x4 5.28 us: columns_by(): jnp.concatenate([jnp.where(high, b, a) for a, b in zip(one, two)], axis=1)]
    reduce_scatter x0 -> x2, waiting for transfers between devices: none -> 7.35 us  [rest_scattered(): lax.psum_scatter(value, axis, scatter_dimension=0, tiled=True, axis_index...]
  transfers between devices with their start and end apart: 42 -> 37, of which waited for: 21 -> 17; matrix products, arithmetic and copies ran while one was open for 22% -> 31% of each run, Pallas kernels for 12% -> 24%
where the time goes in v2:
time: 494 us; the launch traced here: 488 us
  Pallas kernels  116 us (23%)
  waiting for transfers between devices  98 us (20%)
  other arithmetic  84.4 us (17%)
  matrix products  71.5 us (14%)
  local copies, waits for them, and re-layouts  61.7 us (12%)
  starting transfers between devices  39.6 us (8%)
  between operations  16.2 us (3%)
    ppermute x27, waiting for transfers between devices, swapped(): return lax.ppermute(value, axis, [(i, i ^ 1 << bit) for i in range(count)])  89 us
    dot_general x19, matrix products, dot(): return lax.dot_general(a, b, dims, preferred_element_type=out)  71.5 us
    pallas_call x1, Pallas kernels, backward(): pl.pallas_call(functools.partial(bwd_kernel, chunk), grid=(grid,), in_spe...  44.8 us
    pallas_call x2, Pallas kernels, forward(): pl.pallas_call(functools.partial(fwd_kernel, chunk), grid=(last - first,)...  35.7 us
    unnamed x184, local copies, waits for them, and re-layouts  23.4 us
    ppermute x27, starting transfers between devices, swapped(): return lax.ppermute(value, axis, [(i, i ^ 1 << bit) for i in range(count)])  20.1 us
    ppermute x8, starting transfers between devices, moved(): lax.ppermute(value, axis, [(i, i + distance) for i in range(count) if 0 <...  19.5 us
    pallas_call x1, Pallas kernels, local_ends(): pl.pallas_call(functools.partial(ends_kernel, chunk), grid=(grid,), in_sp...  19.1 us
  transfers between devices with their start and end apart: 37, of which 17 were waited for; matrix products, arithmetic and copies ran while one was open for 31% of the time, Pallas kernels for 24%

profile of v2, /device:TPU:0, one launch (start us, length us, event | category | flops | bytes accessed | tf_op | source)
XLA Modules:
  0.0 487.6 jit_solution(6158507715179474463)
XLA Ops:
  13.0 16.3 %fusion.67 = (bf16[2048,1,1024]{2,1,0:T(2,128)(2,1)S(1)}, bf16[2048,1,1024]{2,1,0:T(2,128)(2,1)S(1)}) fusion(bf16[2048,2,1024]{2,1,0:T(2,128)(2,1)} %param.14), kind=kLoop, calls=%fused_computation.221 | loop fusion | bytes 16777216 | tf_op jit(solution)/shard_map/slice | solution.py:524
  29.4 5.9 %copy_bitcast_fusion.2 = (bf16[2048,1024]{1,0:T(8,128)(2,1)}, bf16[2048,1024]{1,0:T(8,128)(2,1)}) fusion(bf16[2048,1,1024]{2,1,0:T(2,128)(2,1)S(1)} %get-tuple-element.284, bf16[2048,1,1024]{2,1,0:T(2,128)(2,1)S(1)} %get-tuple-element.285), kind=kLoop, calls=%fused_computation.33 | loop fusion | bytes 16777216 | tf_op jit(solution)/shard_map/squeeze | solution.py:524
  44.2 3.8 collective-permute-start.3
  48.0 4.7 fusion.74
  54.1 3.9 multiply_convert_fusion
  61.1 4.5 fusion.75.gate_ref
  69.8 5.7 %collective-permute-done.5 = bf16[160,1024]{1,0:T(8,128)(2,1)S(1)} collective-permute-done((bf16[160,1024]{1,0:T(8,128)(2,1)S(1)}, bf16[160,1024]{1,0:T(8,128)(2,1)S(1)}, u32[]{:S(2)}, u32[]{:S(2)}) %collective-permute-start.5) | collective-permute-done | bytes 327712 | tf_op jit(solution)/shard_map/ppermute | solution.py:324
  78.0 4.8 bitcast_reduce_fusion
  83.6 19.1 %local_ends.1 = (f32[16,8,1024]{2,1,0:T(8,128)}, f32[128,32,8,128]{3,2,1,0:T(8,128)}) custom-call(f32[1024,1024]{1,0:T(8,128)} %get-tuple-element.343.step_ref, bf16[1024,1024]{1,0:T(8,128)(2,1)} %copy-done.4, f32[32,1024]{1,0:T(8,128)} %slice.323.rows_ref, f32[16,8,1024]{2,1,0:T(8,128)} %broadcast_in_dim.16.rate_ref), custom_call_target="tpu_custom_call" | custom-call | flops 16777216 | bytes 16777216 | tf_op jit(solution)/shard_map/local_ends/pallas_call | solution.py:91
  110.4 7.1 %multiply_multiply_fusion.1 = (f32[1024,1024]{1,0:T(8,128)}, f32[1024,1024]{1,0:T(8,128)}) fusion(f32[1024,1024]{1,0:T(8,128)S(1)} %fusion.75.gate_ref, bf16[1024,2048]{1,0:T(8,128)(2,1)S(1)} %pad_maximum_fusion.3, bf16[2048,1024]{1,0:T(8,128)(2,1)S(1)} %copy-done.83), kind=kOutput, calls=%fused_computation.48 | convolution fusion | flops 4300210176 | bytes 20971520 | tf_op jit(solution)/shard_map/dot_general | solution.py:315
  121.3 16.6 %local_starts.1 = f32[16,8,1024]{2,1,0:T(8,128)} custom-call(f32[1024,1024]{1,0:T(8,128)} %get-tuple-element.343.step_ref, f32[1024,1024]{1,0:T(8,128)} %get-tuple-element.130.yg_ref, f32[128,32,8,128]{3,2,1,0:T(8,128)} %get-tuple-element.131.spread_ref, f32[16,8,1024]{2,1,0:T(8,128)} %broadcast_in_dim.16.rate_ref), custom_call_target="tpu_custom_call" | custom-call | flops 16777216 | bytes 16777216 | tf_op jit(solution)/shard_map/local_starts/pallas_call | solution.py:112
  155.4 17.7 %scan_forward.2 = (f32[16,8,1024]{2,1,0:T(8,128)}, bf16[128,8,128,128]{3,2,1,0:T(8,128)(2,1)}, bf16[8,16,8,1024]{3,2,1,0:T(8,128)(2,1)}, bf16[1024,1024]{1,0:T(8,128)(2,1)}, bf16[1024,1024]{1,0:T(8,128)(2,1)}) custom-call(f32[1024,1024]{1,0:T(8,128)} %get-tuple-element.343.step_ref, bf16[1024,1024]{1,0:T(8,128)(2,1)} %copy-done.4, ...), custom_call_target="tpu_custom_call", output_to_operand_aliasing={{0}: (7, {})} | custom-call | flops 8388608 | bytes 8388608 | tf_op jit(solution)/shard_map/scan_forward/pallas_call | solution.py:176
  174.7 18.1 %scan_forward.3 = (f32[16,8,1024]{2,1,0:T(8,128)}, bf16[128,8,128,128]{3,2,1,0:T(8,128)(2,1)}, bf16[8,16,8,1024]{3,2,1,0:T(8,128)(2,1)}, bf16[1024,1024]{1,0:T(8,128)(2,1)}, bf16[1024,1024]{1,0:T(8,128)(2,1)}) custom-call(f32[1024,1024]{1,0:T(8,128)} %get-tuple-element.343.step_ref, ...), custom_call_target="tpu_custom_call", output_to_operand_aliasing={{0}: (7, {}), {1}: (8, {}), {2}: (9, {}), {3}: (10, {}), {4... | custom-call | flops 8388608 | bytes 8388608 | tf_op jit(solution)/shard_map/scan_forward/pallas_call | solution.py:176
  192.8 5.4 %fusion.77 = bf16[1024,1024]{1,0:T(8,128)(2,1)} fusion(bf16[1024,1024]{1,0:T(8,128)(2,1)S(1)} %pad_maximum_fusion.7, bf16[1024,1024]{1,0:T(8,128)(2,1)} %get-tuple-element.205), kind=kOutput, calls=%fused_computation.231 | convolution fusion | flops 2147483648 | bytes 6291456 | tf_op jit(solution)/shard_map/dot_general | solution.py:315
  198.2 3.8 fusion.76
  209.1 5.4 %fusion.79 = bf16[1024,1024]{1,0:T(8,128)(2,1)} fusion(bf16[1024,1024]{1,0:T(8,128)(2,1)} %pad_maximum_fusion.6, bf16[1024,1024]{1,0:T(8,128)(2,1)S(1)} %copy-done.27), kind=kOutput, calls=%fused_computation.233 | convolution fusion | flops 2147483648 | bytes 6291456 | tf_op jit(solution)/shard_map/dot_general | solution.py:315
  214.6 3.8 fusion.78
  218.4 44.8 %scan_backward.1 = (f32[16,8,1024]{2,1,0:T(8,128)}, f32[8,1024]{1,0:T(8,128)}, f32[8,1024]{1,0:T(8,128)}, bf16[1024,1024]{1,0:T(8,128)(2,1)}, f32[1024,1024]{1,0:T(8,128)}, /*index=5*/f32[32,1024]{1,0:T(8,128)}) custom-call(f32[1024,1024]{1,0:T(8,128)} %get-tuple-element.343.step_ref, bf16[1024,1024]{1,0:T(8,128)(2,1)} %copy-done.4, ...), custom_call_target="tpu_custom_call" | custom-call | flops 16777216 | bytes 16777216 | tf_op jit(solution)/shard_map/scan_backward/pallas_call | solution.py:292
  266.1 4.6 add_convert_fusion.2
  273.1 4.7 add_convert_fusion.1
  279.5 4.8 fusion.80
  284.3 5.0 %collective-permute-done.18 = bf16[160,1024]{1,0:T(8,128)(2,1)S(1)} collective-permute-done((bf16[160,1024]{1,0:T(8,128)(2,1)S(1)}, bf16[160,1024]{1,0:T(8,128)(2,1)S(1)}, u32[]{:S(2)}, u32[]{:S(2)}) %collective-permute-start.18) | collective-permute-done | bytes 327712 | tf_op jit(solution)/shard_map/ppermute | solution.py:324
  296.3 5.2 %multiply_reduce_fusion = (f32[1024]{0:T(1024)S(1)}, f32[1024]{0:T(1024)S(1)}, f32[1024]{0:T(1024)S(1)}, f32[1024]{0:T(1024)S(1)}, f32[1024]{0:T(1024)S(1)}, /*index=5*/f32[1024,1024]{1,0:T(8,128)}) fusion(f32[1048,1024]{1,0:T(8,128)S(1)} %bitcast.204, f32[1024,1024]{1,0:T(8,128)S(1)} %copy-done.18, f32[1024,1024]{1,0:T(8,128)S(1)} %copy-done.43, ...), kind=kLoop, calls=%fused_computation.42 | loop fusion | flops 18869248 | bytes 33574912 | tf_op jit(solution)/shard_map/reduce_sum | solution.py:628
  311.2 7.4 %reduce-scatter.3.cloned.1.call-done = bf16[256,1024]{1,0:T(8,128)(2,1)} async-done(((bf16[1024,1024]{1,0:T(8,128)(2,1)}), bf16[256,1024]{1,0:T(8,128)(2,1)}) %reduce-scatter.3.cloned.1.call-update) | async-done | bytes 524304 | tf_op jit(solution)/shard_map/reduce_scatter | solution.py:455
  320.9 5.8 %fusion.33 = bf16[2048,512]{1,0:T(8,128)(2,1)S(1)} fusion(bf16[1048,2048]{1,0:T(8,128)(2,1)} %pad_maximum_fusion.1, bf16[1048,1024]{1,0:T(8,128)(2,1)S(1)} %fusion.11), kind=kOutput, calls=%fused_computation.92 | convolution fusion | flops 2197815296 | bytes 7462912 | tf_op jit(solution)/shard_map/dot_general | solution.py:315
  342.7 6.8 %fusion.83 = f32[1024,2048]{1,0:T(8,128)} fusion(bf16[1024,1024]{1,0:T(8,128)(2,1)S(1)} %copy-done.28, bf16[2048,1024]{1,0:T(8,128)(2,1)S(1)} %copy-done.42), kind=kOutput, calls=%fused_computation.237 | convolution fusion | flops 4294967296 | bytes 14680064 | tf_op jit(solution)/shard_map/dot_general | solution.py:315
  353.5 7.3 %add_convert_fusion = bf16[1024,2048]{1,0:T(8,128)(2,1)S(1)} fusion(f32[1024,2048]{1,0:T(8,128)} %fusion.83, bf16[1024,1024]{1,0:T(8,128)(2,1)S(1)} %fusion.15, bf16[2048,1024]{1,0:T(8,128)(2,1)S(1)} %copy-done.17), kind=kOutput, calls=%fused_computation.6 | convolution fusion | flops 4299161600 | bytes 18874368 | tf_op jit(solution)/shard_map/dot_general | solution.py:315
  360.8 16.0 %collective-permute-done.23 = bf16[1024,512]{1,0:T(8,128)(2,1)S(1)} collective-permute-done((bf16[1024,512]{1,0:T(8,128)(2,1)S(1)}, bf16[1024,512]{1,0:T(8,128)(2,1)S(1)}, u32[]{:S(2)}, u32[]{:S(2)}) %collective-permute-start.23) | collective-permute-done | bytes 1048608 | tf_op jit(solution)/shard_map/ppermute | solution.py:324
  379.1 4.5 collective-permute-done.21
  403.9 6.5 %collective-permute-done.26 = bf16[2,304,512]{2,1,0:T(8,128)(2,1)} collective-permute-done((bf16[2,304,512]{2,1,0:T(8,128)(2,1)S(1)}, bf16[2,304,512]{2,1,0:T(8,128)(2,1)}, u32[]{:S(2)}, u32[]{:S(2)}) %collective-permute-start.26) | collective-permute-done | bytes 622624 | tf_op jit(solution)/shard_map/ppermute | solution.py:324
  426.4 31.1 %collective-permute-done.31 = bf16[304,512]{1,0:T(8,128)(2,1)} collective-permute-done((bf16[304,512]{1,0:T(8,128)(2,1)}, bf16[304,512]{1,0:T(8,128)(2,1)}, u32[]{:S(2)}, u32[]{:S(2)}) %collective-permute-start.31) | collective-permute-done | bytes 311328 | tf_op jit(solution)/shard_map/ppermute | solution.py:324
  462.1 4.3 fusion.30
  (376 shorter events, 166.2 us)
Async XLA Ops:
  7.2 311.4 %reduce-scatter.3.cloned.1.call-start = ((), (), s32[]{:S(2)}) async-start(), calls=%async_computation.2 | async-start | bytes 2621440 | tf_op jit(solution)/shard_map/reduce_scatter | solution.py:455
  10.0 26.3 %collective-permute-start = (bf16[1024,512]{1,0:T(8,128)(2,1)}, bf16[1024,512]{1,0:T(8,128)(2,1)S(1)}, u32[]{:S(2)}, u32[]{:S(2)}) collective-permute-start(bf16[1024,512]{1,0:T(8,128)(2,1)} %bitcast.202), channel_id=1, source_target_pairs={{0,2},{1,3},{2,0},{3,1},{4,6},{5,7},{6,4},{7,5},{8,10},{9,11},{10,... | collective-permute-start | bytes 3145736 | tf_op jit(solution)/shard_map/ppermute | solution.py:324
  13.0 23.5 %collective-permute-start.2 = (bf16[1024,512]{1,0:T(8,128)(2,1)}, bf16[1024,512]{1,0:T(8,128)(2,1)S(1)}, u32[]{:S(2)}, u32[]{:S(2)}) collective-permute-start(bf16[1024,512]{1,0:T(8,128)(2,1)} %bitcast.202), channel_id=1, source_target_pairs={{0,1},{1,0},{2,3},{3,2},{4,5},{5,4},{6,7},{7,6},{8,9},{9,8},{10,11... | collective-permute-start | bytes 3145736 | tf_op jit(solution)/shard_map/ppermute | solution.py:324
  44.2 8.5 %collective-permute-start.3 = (bf16[24,2048]{1,0:T(8,128)(2,1)S(1)}, bf16[24,2048]{1,0:T(8,128)(2,1)S(1)}, u32[]{:S(2)}, u32[]{:S(2)}) collective-permute-start(bf16[24,2048]{1,0:T(8,128)(2,1)S(1)} %slice.314), channel_id=1, source_target_pairs={{0,4},{4,8},{8,12},{12,16},{16,20},{20,24},{24,28},{1,5},{5,9},{9,... | collective-permute-start | bytes 294920 | tf_op jit(solution)/shard_map/ppermute | solution.py:329
  65.7 9.8 %collective-permute-start.5 = (bf16[160,1024]{1,0:T(8,128)(2,1)S(1)}, bf16[160,1024]{1,0:T(8,128)(2,1)S(1)}, u32[]{:S(2)}, u32[]{:S(2)}) collective-permute-start(bf16[160,1024]{1,0:T(8,128)(2,1)S(1)} %get-tuple-element.280), channel_id=1, source_target_pairs={{0,2},{1,3},{2,0},{3,1},{4,6},{5,7},{6,4},{7,5},{8,10},{9,11},{10,... | collective-permute-start | bytes 983048 | tf_op jit(solution)/shard_map/ppermute | solution.py:324
  75.5 27.2 %collective-permute-start.7 = (bf16[1024,512]{1,0:T(8,128)(2,1)S(1)}, bf16[1024,512]{1,0:T(8,128)(2,1)S(1)}, u32[]{:S(2)}, u32[]{:S(2)}) collective-permute-start(bf16[1024,512]{1,0:T(8,128)(2,1)S(1)} %bitcast.218), channel_id=1, source_target_pairs={{0,2},{1,3},{2,0},{3,1},{4,6},{5,7},{6,4},{7,5},{8,10},{9,11},{10,... | collective-permute-start | bytes 3145736 | tf_op jit(solution)/shard_map/ppermute | solution.py:324
  77.0 30.8 %collective-permute-start.9 = (bf16[1024,512]{1,0:T(8,128)(2,1)S(1)}, bf16[1024,512]{1,0:T(8,128)(2,1)S(1)}, u32[]{:S(2)}, u32[]{:S(2)}) collective-permute-start(bf16[1024,512]{1,0:T(8,128)(2,1)S(1)} %bitcast.219), channel_id=1, source_target_pairs={{0,1},{1,0},{2,3},{3,2},{4,5},{5,4},{6,7},{7,6},{8,9},{9,8},{10,11... | collective-permute-start | bytes 3145736 | tf_op jit(solution)/shard_map/ppermute | solution.py:324
  102.7 5.1 %collective-permute-start.8 = (bf16[1024,512]{1,0:T(8,128)(2,1)S(1)}, bf16[1024,512]{1,0:T(8,128)(2,1)S(1)}, u32[]{:S(2)}, u32[]{:S(2)}) collective-permute-start(bf16[1024,512]{1,0:T(8,128)(2,1)S(1)} %collective-permute-done.7), channel_id=1, source_target_pairs={{0,1},{1,0},{2,3},{3,2},{4,5},{5,4},{6,7},{7,6},{8,9},{9,8},{10,11... | collective-permute-start | bytes 3145736 | tf_op jit(solution)/shard_map/ppermute | solution.py:324
  104.4 13.2 %collective-permute-start.6 = (bf16[18,8,1024]{2,1,0:T(8,128)(2,1)S(1)}, bf16[18,8,1024]{2,1,0:T(8,128)(2,1)S(1)}, u32[]{:S(2)}, u32[]{:S(2)}) collective-permute-start(bf16[18,8,1024]{2,1,0:T(8,128)(2,1)S(1)} %pad_maximum_fusion.14), channel_id=1, source_target_pairs={{0,4},{4,8},{8,12},{12,16},{16,20},{20,24},{24,28},{1,5},{5,9},{9,... | collective-permute-start | bytes 884744 | tf_op jit(solution)/shard_map/ppermute | solution.py:329
  117.8 20.1 %collective-permute-start.10 = (bf16[18,8,1024]{2,1,0:T(8,128)(2,1)S(1)}, bf16[18,8,1024]{2,1,0:T(8,128)(2,1)S(1)}, u32[]{:S(2)}, u32[]{:S(2)}) collective-permute-start(bf16[18,8,1024]{2,1,0:T(8,128)(2,1)S(1)} %pad_maximum_fusion.17), channel_id=1, source_target_pairs={{0,8},{4,12},{8,16},{12,20},{16,24},{20,28},{1,9},{5,13},{9,17},{1... | collective-permute-start | bytes 884744 | tf_op jit(solution)/shard_map/ppermute | solution.py:329
  138.3 12.3 %collective-permute-start.11 = (bf16[18,8,1024]{2,1,0:T(8,128)(2,1)S(1)}, bf16[18,8,1024]{2,1,0:T(8,128)(2,1)S(1)}, u32[]{:S(2)}, u32[]{:S(2)}) collective-permute-start(bf16[18,8,1024]{2,1,0:T(8,128)(2,1)S(1)} %pad_maximum_fusion.18), channel_id=1, source_target_pairs={{0,16},{4,20},{8,24},{12,28},{1,17},{5,21},{9,25},{13,29},{2,18},{... | collective-permute-start | bytes 884744 | tf_op jit(solution)/shard_map/ppermute | solution.py:329
  142.7 10.4 %collective-permute-start.12 = (bf16[18,8,1024]{2,1,0:T(8,128)(2,1)S(1)}, bf16[18,8,1024]{2,1,0:T(8,128)(2,1)S(1)}, u32[]{:S(2)}, u32[]{:S(2)}) collective-permute-start(bf16[18,8,1024]{2,1,0:T(8,128)(2,1)S(1)} %pad_maximum_fusion.13), channel_id=1, source_target_pairs={{4,0},{8,4},{12,8},{16,12},{20,16},{24,20},{28,24},{5,1},{9,5},{13... | collective-permute-start | bytes 884744 | tf_op jit(solution)/shard_map/ppermute | solution.py:329
  153.4 19.6 %collective-permute-start.13 = (bf16[18,8,1024]{2,1,0:T(8,128)(2,1)S(1)}, bf16[18,8,1024]{2,1,0:T(8,128)(2,1)S(1)}, u32[]{:S(2)}, u32[]{:S(2)}) collective-permute-start(bf16[18,8,1024]{2,1,0:T(8,128)(2,1)S(1)} %pad_maximum_fusion.19), channel_id=1, source_target_pairs={{8,0},{12,4},{16,8},{20,12},{24,16},{28,20},{9,1},{13,5},{17,9},{2... | collective-permute-start | bytes 884744 | tf_op jit(solution)/shard_map/ppermute | solution.py:329
  173.4 19.4 %collective-permute-start.14 = (bf16[18,8,1024]{2,1,0:T(8,128)(2,1)S(1)}, bf16[18,8,1024]{2,1,0:T(8,128)(2,1)S(1)}, u32[]{:S(2)}, u32[]{:S(2)}) collective-permute-start(bf16[18,8,1024]{2,1,0:T(8,128)(2,1)S(1)} %pad_maximum_fusion.20), channel_id=1, source_target_pairs={{16,0},{20,4},{24,8},{28,12},{17,1},{21,5},{25,9},{29,13},{18,2},{... | collective-permute-start | bytes 884744 | tf_op jit(solution)/shard_map/ppermute | solution.py:329
  202.0 64.1 %collective-permute-start.15 = (bf16[2,2,256,1024]{3,2,1,0:T(8,128)(2,1)}, bf16[2,2,256,1024]{3,2,1,0:T(8,128)(2,1)}, u32[]{:S(2)}, u32[]{:S(2)}) collective-permute-start(bf16[2,2,256,1024]{3,2,1,0:T(8,128)(2,1)} %bitcast.18), channel_id=1, source_target_pairs={{0,4},{4,0},{8,12},{12,8},{16,20},{20,16},{24,28},{28,24},{1,5},{5... | collective-permute-start | bytes 6291464 | tf_op jit(solution)/shard_map/ppermute | solution.py:324
  204.4 61.7 %collective-permute-start.16 = (bf16[2,2,256,1024]{3,2,1,0:T(8,128)(2,1)}, bf16[2,2,256,1024]{3,2,1,0:T(8,128)(2,1)}, u32[]{:S(2)}, u32[]{:S(2)}) collective-permute-start(bf16[2,2,256,1024]{3,2,1,0:T(8,128)(2,1)} %bitcast.19), channel_id=1, source_target_pairs={{0,8},{4,12},{8,0},{12,4},{16,24},{20,28},{24,16},{28,20},{1,9},{5... | collective-permute-start | bytes 6291464 | tf_op jit(solution)/shard_map/ppermute | solution.py:324
  272.5 5.3 %collective-permute-start.17 = (f32[160,1024]{1,0:T(8,128)}, f32[160,1024]{1,0:T(8,128)}, u32[]{:S(2)}, u32[]{:S(2)}) collective-permute-start(f32[160,1024]{1,0:T(8,128)} %pad_maximum_fusion.11), channel_id=1, source_target_pairs={{0,1},{1,0},{2,3},{3,2},{4,5},{5,4},{6,7},{7,6},{8,9},{9,8},{10,11... | collective-permute-start | bytes 1966088 | tf_op jit(solution)/shard_map/ppermute | solution.py:324
  273.0 128.6 %reduce-scatter.5.cloned.1.call-start = ((), (), s32[]{:S(2)}) async-start(), calls=%async_computation.3 | async-start | bytes 2621440 | tf_op jit(solution)/shard_map/reduce_scatter | solution.py:455
  279.1 10.2 %collective-permute-start.18 = (bf16[160,1024]{1,0:T(8,128)(2,1)S(1)}, bf16[160,1024]{1,0:T(8,128)(2,1)S(1)}, u32[]{:S(2)}, u32[]{:S(2)}) collective-permute-start(bf16[160,1024]{1,0:T(8,128)(2,1)S(1)} %get-tuple-element.270), channel_id=1, source_target_pairs={{0,2},{1,3},{2,0},{3,1},{4,6},{5,7},{6,4},{7,5},{8,10},{9,11},{10,... | collective-permute-start | bytes 983048 | tf_op jit(solution)/shard_map/ppermute | solution.py:324
  291.3 29.6 %collective-permute-start.19 = (bf16[2,1024,512]{2,1,0:T(8,128)(2,1)}, bf16[2,1024,512]{2,1,0:T(8,128)(2,1)}, u32[]{:S(2)}, u32[]{:S(2)}) collective-permute-start(bf16[2,1024,512]{2,1,0:T(8,128)(2,1)} %dynamic-slice_bitcast_fusion.1), channel_id=1, source_target_pairs={{0,1},{1,0},{2,3},{3,2},{4,5},{5,4},{6,7},{7,6},{8,9},{9,8},{10,11... | collective-permute-start | bytes 6291464 | tf_op jit(solution)/shard_map/ppermute | solution.py:324
  303.7 34.9 %collective-permute-start.20 = (f32[24,1024]{1,0:T(8,128)}, f32[24,1024]{1,0:T(8,128)S(1)}, u32[]{:S(2)}, u32[]{:S(2)}) collective-permute-start(f32[24,1024]{1,0:T(8,128)} %slice.344), channel_id=1, source_target_pairs={{4,0},{8,4},{12,8},{16,12},{20,16},{24,20},{28,24},{5,1},{9,5},{13... | collective-permute-start | bytes 294920 | tf_op jit(solution)/shard_map/ppermute | solution.py:329
  338.6 45.0 %collective-permute-start.21 = (bf16[1312,512]{1,0:T(8,128)(2,1)}, bf16[1312,512]{1,0:T(8,128)(2,1)}, u32[]{:S(2)}, u32[]{:S(2)}) collective-permute-start(bf16[1312,512]{1,0:T(8,128)(2,1)} %pad_maximum_fusion.9), channel_id=1, source_target_pairs={{0,4},{4,0},{8,12},{12,8},{16,20},{20,16},{24,28},{28,24},{1,5},{5... | collective-permute-start | bytes 4030472 | tf_op jit(solution)/shard_map/ppermute | solution.py:324
  338.6 40.5 %collective-permute-start.22 = (bf16[2,2,304,512]{3,2,0,1:T(8,128)(2,1)}, bf16[2,2,304,512]{3,2,0,1:T(8,128)(2,1)}, u32[]{:S(2)}, u32[]{:S(2)}) collective-permute-start(bf16[2,2,304,512]{3,2,0,1:T(8,128)(2,1)} %bitcast.200), channel_id=1, source_target_pairs={{0,8},{4,12},{8,0},{12,4},{16,24},{20,28},{24,16},{28,20},{1,9},{5... | collective-permute-start | bytes 3735560 | tf_op jit(solution)/shard_map/ppermute | solution.py:324
  352.0 24.8 %collective-permute-start.23 = (bf16[1024,512]{1,0:T(8,128)(2,1)S(1)}, bf16[1024,512]{1,0:T(8,128)(2,1)S(1)}, u32[]{:S(2)}, u32[]{:S(2)}) collective-permute-start(bf16[1024,512]{1,0:T(8,128)(2,1)S(1)} %copy-done.55), channel_id=1, source_target_pairs={{0,2},{1,3},{2,0},{3,1},{4,6},{5,7},{6,4},{7,5},{8,10},{9,11},{10,... | collective-permute-start | bytes 3145736 | tf_op jit(solution)/shard_map/ppermute | solution.py:324
  393.8 18.9 %collective-permute-start.24 = (bf16[2,1024,512]{2,1,0:T(8,128)(2,1)}, bf16[2,1024,512]{2,1,0:T(8,128)(2,1)}, u32[]{:S(2)}, u32[]{:S(2)}) collective-permute-start(bf16[2,1024,512]{2,1,0:T(8,128)(2,1)} %dynamic-slice_bitcast_fusion), channel_id=1, source_target_pairs={{0,1},{1,0},{2,3},{3,2},{4,5},{5,4},{6,7},{7,6},{8,9},{9,8},{10,11... | collective-permute-start | bytes 6291464 | tf_op jit(solution)/shard_map/ppermute | solution.py:324
  393.8 18.9 %collective-permute-start.25 = (bf16[704,512]{1,0:T(8,128)(2,1)}, bf16[704,512]{1,0:T(8,128)(2,1)}, u32[]{:S(2)}, u32[]{:S(2)}) collective-permute-start(bf16[704,512]{1,0:T(8,128)(2,1)} %pad_maximum_fusion.10), channel_id=1, source_target_pairs={{0,8},{4,12},{8,0},{12,4},{16,24},{20,28},{24,16},{28,20},{1,9},{5... | collective-permute-start | bytes 2162696 | tf_op jit(solution)/shard_map/ppermute | solution.py:324
  393.8 16.5 %collective-permute-start.26 = (bf16[2,304,512]{2,1,0:T(8,128)(2,1)S(1)}, bf16[2,304,512]{2,1,0:T(8,128)(2,1)}, u32[]{:S(2)}, u32[]{:S(2)}) collective-permute-start(bf16[2,304,512]{2,1,0:T(8,128)(2,1)S(1)} %dynamic-slice_bitcast_fusion.4), channel_id=1, source_target_pairs={{0,4},{4,0},{8,12},{12,8},{16,20},{20,16},{24,28},{28,24},{1,5},{5... | collective-permute-start | bytes 1867784 | tf_op jit(solution)/shard_map/ppermute | solution.py:324
  421.9 35.5 %collective-permute-start.29 = (bf16[1024,512]{1,0:T(8,128)(2,1)}, bf16[1024,512]{1,0:T(8,128)(2,1)}, u32[]{:S(2)}, u32[]{:S(2)}) collective-permute-start(bf16[1024,512]{1,0:T(8,128)(2,1)} %dynamic-slice_bitcast_fusion.2), channel_id=1, source_target_pairs={{0,2},{1,3},{2,0},{3,1},{4,6},{5,7},{6,4},{7,5},{8,10},{9,11},{10,... | collective-permute-start | bytes 3145736 | tf_op jit(solution)/shard_map/ppermute | solution.py:324
  423.4 34.1 %collective-permute-start.30 = (bf16[400,512]{1,0:T(8,128)(2,1)}, bf16[400,512]{1,0:T(8,128)(2,1)}, u32[]{:S(2)}, u32[]{:S(2)}) collective-permute-start(bf16[400,512]{1,0:T(8,128)(2,1)} %pad_maximum_fusion.12), channel_id=1, source_target_pairs={{0,16},{4,20},{8,24},{12,28},{16,0},{20,4},{24,8},{28,12},{1,17},{... | collective-permute-start | bytes 1228808 | tf_op jit(solution)/shard_map/ppermute | solution.py:324
  424.5 32.9 %collective-permute-start.31 = (bf16[304,512]{1,0:T(8,128)(2,1)}, bf16[304,512]{1,0:T(8,128)(2,1)}, u32[]{:S(2)}, u32[]{:S(2)}) collective-permute-start(bf16[304,512]{1,0:T(8,128)(2,1)} %dynamic-slice_bitcast_fusion.5), channel_id=1, source_target_pairs={{0,16},{4,20},{8,24},{12,28},{16,0},{20,4},{24,8},{28,12},{1,17},{... | collective-permute-start | bytes 933896 | tf_op jit(solution)/shard_map/ppermute | solution.py:324
  466.4 3.7 collective-permute-start.32
  473.7 6.1 %collective-permute-start.34 = (f32[512]{0:T(512)S(1)}, f32[512]{0:T(512)S(1)}, u32[]{:S(2)}, u32[]{:S(2)}) collective-permute-start(f32[512]{0:T(512)S(1)} %add.410), channel_id=1, source_target_pairs={{0,16},{4,20},{8,24},{12,28},{16,0},{20,4},{24,8},{28,12},{1,17},{... | collective-permute-start | bytes 6152 | tf_op jit(solution)/shard_map/ppermute | solution.py:324
  (94 other events, 973.0 us)
Sparse Core Ops, SparseCore 0:
  273.1 45.4 reduce-scatter.2
  338.7 54.3 reduce-scatter.4

commit v3 on v2

--- a/solution.py
+++ b/solution.py
@@ -188,8 +188,8 @@
     )(step, mixed, gate, gg, wide_rows, rate, skip, carried, *filled)
 
 
-def bwd_kernel(chunk, step_ref, mixed_ref, yg_ref, spread_ref, rate_ref, skip_ref, hist_ref, start_ref, gin_ref,
-               decay_ref, bias_ref, skipg_ref, pre_ref, part_ref, bcg_ref, state_ref, b_ref, c_ref):
+def bwd_kernel(chunk, step_ref, mixed_ref, yg_ref, spread_ref, rate_ref, skip_ref, low_ref, hist_ref, start_ref, gin_ref,
+               sums_ref, pre_ref, part_ref, proj_ref, decay_ref, bias_ref, skipg_ref, state_ref, b_ref, c_ref):
     states, seqs, width = rate_ref.shape
     span = states * seqs
 
@@ -274,36 +274,207 @@
     dst = lax.broadcasted_iota(jnp.int32, (2 * states, wide), 0)
     fold_b = (src == dst).astype(BF16)
     fold_c = (src + states == dst).astype(BF16)
-    bcg_ref[...] = lax.dot_general(
+    rank = low_ref.shape[0]
+    proj_ref[:rank] = lax.dot_general(low_ref[...], pre_ref[...], contract, preferred_element_type=F32)
+    proj_ref[rank:] = lax.dot_general(
         fold_b, jnp.concatenate(b_rows, axis=0).astype(BF16), contract, preferred_element_type=F32
     ) + lax.dot_general(fold_c, jnp.concatenate(c_rows, axis=0).astype(BF16), contract, preferred_element_type=F32)
 
-
-def backward(step, mixed, yg, wide_rows, rate, skip, hist, start, gin, chunk):
+    @pl.when(pl.program_id(0) == pl.num_programs(0) - 1)
+    def _():
+        sums_ref[:states] = jnp.sum(decay_ref[...], axis=1) * (1.0 / LOG2E)
+        sums_ref[states : states + 1] = jnp.sum(bias_ref[...], axis=0, keepdims=True)
+        sums_ref[states + 1 : states + 2] = jnp.sum(skipg_ref[...], axis=0, keepdims=True)
+
+
+def backward(step, mixed, yg, wide_rows, rate, skip, low_weight, hist, start, gin, chunk):
     rows, width = step.shape
     states, seqs, _ = rate.shape
     grid = rows // (chunk * seqs)
     elements = rows * width * states
     at = lambda i: grid - 1 - i
     row_spec = pl.BlockSpec((chunk * seqs, width), lambda i: (at(i), 0))
-    col_spec = pl.BlockSpec((2 * states, chunk * seqs), lambda i: (0, at(i)))
+    rank = low_weight.shape[0]
     whole = pl.BlockSpec((states, seqs, width), lambda i: (0, 0, 0))
     one = pl.BlockSpec((seqs, width), lambda i: (0, 0))
     return pl.pallas_call(
         functools.partial(bwd_kernel, chunk),
         grid=(grid,),
         in_specs=[row_spec, row_spec, row_spec, spread_spec(chunk, states, seqs, at), whole, one,
+                  pl.BlockSpec((rank, width), lambda i: (0, 0)),
                   pl.BlockSpec((chunk, width // LANES, states * seqs, LANES), lambda i: (at(i), 0, 0, 0)),
                   pl.BlockSpec((1, states, seqs, width), lambda i: (at(i), 0, 0, 0)), whole],
-        out_specs=[whole, one, one, row_spec, row_spec, col_spec],
-        out_shape=[jax.ShapeDtypeStruct(rate.shape, F32), jax.ShapeDtypeStruct((seqs, width), F32),
-                   jax.ShapeDtypeStruct((seqs, width), F32), jax.ShapeDtypeStruct((rows, width), BF16),
-                   jax.ShapeDtypeStruct((rows, width), F32), jax.ShapeDtypeStruct((2 * states, rows), F32)],
-        scratch_shapes=[pltpu.VMEM(rate.shape, F32)] + [pltpu.VMEM((chunk // 2, 2 * seqs, 2 * states * seqs), F32)] * 2,
+        out_specs=[pl.BlockSpec((states + 2, width), lambda i: (0, 0)), row_spec, row_spec,
+                   pl.BlockSpec((rank + 2 * states, chunk * seqs), lambda i: (0, at(i)))],
+        out_shape=[jax.ShapeDtypeStruct((states + 2, width), F32), jax.ShapeDtypeStruct((rows, width), BF16),
+                   jax.ShapeDtypeStruct((rows, width), F32), jax.ShapeDtypeStruct((rank + 2 * states, rows), F32)],
+        scratch_shapes=[pltpu.VMEM(rate.shape, F32), pltpu.VMEM((seqs, width), F32), pltpu.VMEM((seqs, width), F32),
+                        pltpu.VMEM(rate.shape, F32)] + [pltpu.VMEM((chunk // 2, 2 * seqs, 2 * states * seqs), F32)] * 2,
         compiler_params=pltpu.CompilerParams(vmem_limit_bytes=VM),
         cost_estimate=pl.CostEstimate(flops=elements, bytes_accessed=elements, transcendentals=0),
         name="scan_backward",
-    )(step, mixed, yg, wide_rows, rate, skip, hist, start, gin)
+    )(step, mixed, yg, wide_rows, rate, skip, low_weight, hist, start, gin)
+
+
+def conv_kernel(chunk, taps, proj_ref, weight_ref, part_ref, conv_ref, in_ref, before_ref, taps_ref,
+                spread_ref, first_ref, sums_ref, grad_ref, back_ref):
+    rows, width = part_ref.shape
+    seqs = rows // chunk
+    halo = (taps - 1) * seqs
+    lead = before_ref.shape[0]
+    step = pl.program_id(0)
+    block = pl.num_programs(0) - 1 - step
+
+    @pl.when(step == 0)
+    def _():
+        grad_ref[rows:] = jnp.zeros_like(grad_ref[rows:])
+        sums_ref[...] = jnp.zeros_like(sums_ref)
+
+    @pl.when(step > 0)
+    def _():
+        grad_ref[rows : rows + halo] = grad_ref[:halo]
+
+    back_ref[...] = lax.dot_general(
+        proj_ref[...], weight_ref[...], (((0,), (0,)), ((), ())), preferred_element_type=F32
+    )
+
+    def tile_step(j, _):
+        lanes = pl.ds(pl.multiple_of(j * LANES, LANES), LANES)
+        tap = [taps_ref[k : k + 1, lanes] for k in range(taps)]
+        sums = [sums_ref[k, :, lanes] for k in range(taps + 1)]
+        for tok in reversed(range(0, chunk, 2)):
+            at = pl.ds(tok * seqs, 2 * seqs)
+            v = conv_ref[at, lanes]
+            sig = 1.0 / (1.0 + jnp.exp2(v * (-LOG2E)))
+            grad = (part_ref[at, lanes] + back_ref[at, lanes]) * (sig * (1.0 + v * (1.0 - sig)))
+            grad_ref[at, lanes] = grad
+            given = in_ref[at, lanes].astype(F32)
+            spread = jnp.zeros_like(grad)
+            for k in range(taps):
+                later = grad_ref[pl.ds((tok + taps - 1 - k) * seqs, 2 * seqs), lanes]
+                spread = spread + tap[k] * later
+                use = given * later
+                sums[k] = sums[k] + use[:seqs] + use[seqs:]
+            sums[taps] = sums[taps] + grad[:seqs] + grad[seqs:]
+            out_at = pl.multiple_of(lead + block * rows + tok * seqs, 2 * seqs)
+            spread_ref[pl.ds(out_at, 2 * seqs), lanes] = spread.astype(BF16)
+        for k in range(taps + 1):
+            sums_ref[k, :, lanes] = sums[k]
+        return 0
+
+    lax.fori_loop(0, width // LANES, tile_step, 0, unroll=2)
+
+    @pl.when(block == 0)
+    def _():
+        first_ref[...] = grad_ref[:halo]
+        given = before_ref[...].astype(F32)
+        parts = [jnp.zeros((lead - halo, width), F32)]
+        for tok in range(taps - 1):
+            spread = jnp.zeros((seqs, width), F32)
+            own = given[lead - halo + tok * seqs : lead - halo + (tok + 1) * seqs]
+            for k in range(tok + 1):
+                later = grad_ref[(tok - k) * seqs : (tok - k + 1) * seqs]
+                spread = spread + taps_ref[k : k + 1] * later
+                sums_ref[k] = sums_ref[k] + own * later
+            parts.append(spread)
+        spread_ref[:lead] = jnp.concatenate(parts, axis=0).astype(BF16)
+
+
+def conv_back(proj_grad, weight, part, conv_out, conv_in, before, conv_taps, chunk):
+    rows, width = part.shape
+    taps = conv_taps.shape[0]
+    columns = proj_grad.shape[0]
+    seqs, lead = 8, before.shape[0]
+    halo = (taps - 1) * seqs
+    grid = rows // (chunk * seqs)
+    at = lambda i: grid - 1 - i
+    row_spec = pl.BlockSpec((chunk * seqs, width), lambda i: (at(i), 0))
+    fixed = lambda *shape: pl.BlockSpec(shape, lambda i: (0,) * len(shape))
+    return pl.pallas_call(
+        functools.partial(conv_kernel, chunk, taps),
+        grid=(grid,),
+        in_specs=[pl.BlockSpec((columns, chunk * seqs), lambda i: (0, at(i))), fixed(columns, width), row_spec, row_spec, row_spec,
+                  fixed(lead, width), fixed(taps, width)],
+        out_specs=[fixed(rows + lead, width), fixed(halo, width), fixed(taps + 1, seqs, width)],
+        out_shape=[jax.ShapeDtypeStruct((rows + lead, width), BF16), jax.ShapeDtypeStruct((halo, width), F32),
+                   jax.ShapeDtypeStruct((taps + 1, seqs, width), F32)],
+        scratch_shapes=[pltpu.VMEM((chunk * seqs + lead, width), F32), pltpu.VMEM((chunk * seqs, width), F32)],
+        compiler_params=pltpu.CompilerParams(vmem_limit_bytes=VM),
+        cost_estimate=pl.CostEstimate(flops=rows * width, bytes_accessed=rows * width, transcendentals=0),
+        name="conv_backward",
+    )(proj_grad, weight, part, conv_out, conv_in, before, conv_taps)
+
+
+def merge_kernel(plan, messages, bits_ref, *refs):
+    refs = list(refs)
+    inputs = [[refs.pop(0) for _ in range(len(sizes) + 1 + (extra > 0))] for _, _, sizes, extra, *_ in plan]
+    outputs = [[refs.pop(0) for _ in range(len(sizes) + (extra > 0))] for _, _, sizes, extra, *_ in plan]
+    sent = [refs.pop(0) for _ in range(messages)]
+    for index, (levels, dim, sizes, extra, got_at, message, sent_at) in enumerate(plan):
+        bit = bits_ref[index]
+        kept, got, whole = inputs[index][: len(sizes)], inputs[index][len(sizes)], inputs[index][-1]
+        kept_out, whole_out, sent_out = outputs[index][: len(sizes)], outputs[index][-1], sent[message]
+        after_dim = 1 << (levels - 1 - dim)
+        for size, source, target in zip(sizes, kept, kept_out):
+            for rest in range(1 << (levels - 1)):
+                high, low = divmod(rest, after_dim)
+                for side in range(2):
+                    own = bit if side == 0 else 1 - bit
+                    at = pl.multiple_of(((high * 2 + own) * after_dim + low) * size, 16)
+                    total = source[pl.ds(at, size), :].astype(F32) + got[pl.ds(got_at + at, size), :].astype(F32)
+                    if side == 0:
+                        target[rest * size : (rest + 1) * size, :] = total.astype(BF16)
+                    else:
+                        sent_out[sent_at + rest * size : sent_at + (rest + 1) * size, :] = total.astype(BF16)
+            got_at += size << levels
+            sent_at += size << (levels - 1)
+        if extra:
+            other = got[got_at : got_at + extra, :].astype(F32) + got[got_at + extra : got_at + 2 * extra, :].astype(F32)
+            total = whole[...] + other
+            upper = total.astype(BF16)
+            lower = (total - upper.astype(F32)).astype(BF16)
+            sent_out[sent_at : sent_at + extra, :] = upper
+            sent_out[sent_at + extra : sent_at + 2 * extra, :] = lower
+            whole_out[...] = upper.astype(F32) + lower.astype(F32)
+
+
+def product_kernel(count, core_ref, *refs):
+    del core_ref
+    kept_ref, sent_ref = refs[-2:]
+    total = None
+    for a_ref, b_ref in zip(refs[:count], refs[count : 2 * count]):
+        part = lax.dot_general(a_ref[...], b_ref[...], (((1,), (1,)), ((), ())), preferred_element_type=F32)
+        total = part if total is None else total + part
+    side = pl.program_id(1)
+
+    @pl.when(side == 0)
+    def _():
+        kept_ref[0] = total.astype(BF16)
+
+    @pl.when(side == 1)
+    def _():
+        sent_ref[0] = total.astype(BF16)
+
+
+def product_sides(core, share, *pairs):
+    rows, columns = pairs[0][0].shape[0], pairs[0][1].shape[0]
+    chips = columns // share // 2
+    mine = lambda far, side, core_ref: (far * 2 + jnp.where(side == 0, core_ref[0], 1 - core_ref[0]), 0)
+    out_spec = pl.BlockSpec((1, rows, share), lambda far, side, core_ref: (far, 0, 0))
+    return pl.pallas_call(
+        functools.partial(product_kernel, len(pairs)),
+        grid_spec=pltpu.PrefetchScalarGridSpec(
+            num_scalar_prefetch=1,
+            grid=(chips, 2),
+            in_specs=[pl.BlockSpec(a.shape, lambda far, side, core_ref: (0, 0)) for a, _ in pairs]
+            + [pl.BlockSpec((share, b.shape[1]), mine) for _, b in pairs],
+            out_specs=[out_spec, out_spec],
+        ),
+        out_shape=[jax.ShapeDtypeStruct((chips, rows, share), BF16)] * 2,
+        compiler_params=pltpu.CompilerParams(vmem_limit_bytes=VM),
+        cost_estimate=pl.CostEstimate(flops=1024, bytes_accessed=1024, transcendentals=0),
+        name="product_sides",
+    )(core.reshape(1).astype(jnp.int32), *[a for a, _ in pairs], *[b for _, b in pairs])
 
 
 EPSILON = 1e-05
@@ -416,25 +587,98 @@
     return jnp.pad(value, [(0, width if i == dim else 0) for i in range(value.ndim)])
 
 
-class ScatteredWith(Scattered):
-    def __init__(self, blocks, axis, order, extra):
-        super().__init__(blocks, axis, order)
-        self.extra = extra
-
-    def split(self):
-        super().split()
-        upper = self.extra.astype(BF16)
-        lower = (self.extra - upper.astype(F32)).astype(BF16)
-        self.extra = upper.astype(F32) + lower.astype(F32)
-        self.shape = self.sent.shape
-        self.sent = jnp.concatenate([self.sent.reshape(-1, self.shape[-1]), upper, lower], axis=0)
-
-    def add(self):
-        count = self.extra.shape[0]
-        upper, lower = self.got[-2 * count : -count], self.got[-count:]
-        self.extra = self.extra + (upper.astype(F32) + lower.astype(F32))
-        self.got = self.got[: -2 * count].reshape(self.shape)
-        super().add()
+def two_parts(value):
+    upper = value.astype(BF16)
+    return upper, (value - upper.astype(F32)).astype(BF16)
+
+
+class Chain:
+    def __init__(self, pieces, axis, order, whole=None, halves=None):
+        bits = bits_of(axis)
+        self.axis, self.order, self.left, self.whole, self.at = axis, list(order), list(range(bits)), [], 0
+        if halves:
+            self.sizes = [halves[1].shape[0] >> (bits - 1)]
+            self.kept, self.sent = [halves[0]], halves[1]
+            return
+        self.sizes = [piece.shape[1] for piece in pieces]
+        dim = bits - 1 - self.order[0]
+        mine = own_bit(axis, self.order[0])
+        halves = [piece.reshape((2,) * bits + piece.shape[1:]) for piece in pieces]
+        flat = lambda value: value.reshape(-1, value.shape[-1])
+        self.kept = [flat(pick(value, dim, mine)) for value in halves]
+        message = [flat(pick(value, dim, 1 - mine)) for value in halves]
+        if whole is not None:
+            upper, lower = two_parts(whole)
+            self.whole = [upper.astype(F32) + lower.astype(F32)]
+            message += [upper, lower]
+        self.sent = jnp.concatenate(message, axis=0) if len(message) > 1 else message[0]
+
+    def finish(self):
+        rows, values = self.at, []
+        for size, kept in zip(self.sizes, self.kept):
+            values.append(kept.astype(F32) + self.got[rows : rows + size].astype(F32))
+            rows += size
+        if self.whole:
+            count = self.whole[0].shape[0]
+            upper, lower = (self.got[rows + i * count : rows + (i + 1) * count].astype(F32) for i in range(2))
+            values.append(self.whole[0] + (upper + lower))
+        return values
+
+
+def send_chains(groups, messages, *values):
+    messages, values = lax.optimization_barrier((messages, values))
+    for group, message in zip(groups, messages):
+        got = swapped(message, group[0].axis, group[0].order[0])
+        for c in group:
+            c.got = got
+            c.left.remove(c.order.pop(0))
+    return values
+
+
+def end_chains(groups, *values):
+    got, values = lax.optimization_barrier(([group[0].got for group in groups], values))
+    for group, message in zip(groups, got):
+        for c in group:
+            c.got = message
+    return values
+
+
+def last_of(chain):
+    while chain.order:
+        send_chains([[chain]], merge([[chain]]))
+    return chain.finish()
+
+
+def merge(groups):
+    plan, operands, outputs, messages = [], [], [], []
+    for number, group in enumerate(groups):
+        rows = 0
+        for c in group:
+            levels, extra = len(c.left), c.whole[0].shape[0] if c.whole else 0
+            columns = c.got.shape[1]
+            plan.append((levels, levels - 1 - c.left.index(c.order[0]), tuple(c.sizes), extra, c.at, number, rows))
+            operands += [*c.kept, c.got, *c.whole]
+            outputs += [((size << (levels - 1), columns), BF16) for size in c.sizes] + [((extra, columns), F32)] * (extra > 0)
+            c.at = rows
+            rows += sum(size << (levels - 1) for size in c.sizes) + 2 * extra
+        messages.append(((rows, columns), BF16))
+    chains = [c for group in groups for c in group]
+    bits = jnp.stack([own_bit(c.axis, c.order[0]) for c in chains]).astype(jnp.int32)
+    outs = list(
+        pl.pallas_call(
+            functools.partial(merge_kernel, plan, len(messages)),
+            in_specs=[pl.BlockSpec(memory_space=pltpu.SMEM)] + [pl.BlockSpec(memory_space=pltpu.VMEM)] * len(operands),
+            out_specs=[pl.BlockSpec(memory_space=pltpu.VMEM)] * (len(outputs) + len(messages)),
+            out_shape=[jax.ShapeDtypeStruct(*shape) for shape in outputs + messages],
+            compiler_params=pltpu.CompilerParams(vmem_limit_bytes=VM),
+            cost_estimate=pl.CostEstimate(flops=1024, bytes_accessed=1024, transcendentals=0),
+            name="merge_messages",
+        )(bits, *operands)
+    )
+    for c in chains:
+        c.kept = [outs.pop(0) for _ in c.sizes]
+        c.whole = [outs.pop(0) for _ in c.whole]
+    return outs
 
 
 def columns_by(value, axis, bit):
@@ -446,13 +690,6 @@
     return [
         jnp.concatenate([jnp.where(high, b, a) for a, b in zip(one, two)], axis=1) for one, two in ((low, up), (up, low))
     ]
-
-
-def rest_scattered(value, axis, bit):
-    count = lax.axis_size(axis)
-    groups = [[i for i in range(count) if (i >> bit) & 1 == side] for side in range(2)]
-    value = value.reshape(-1, value.shape[-1])
-    return lax.psum_scatter(value, axis, scatter_dimension=0, tiled=True, axis_index_groups=groups).astype(F32)
 
 
 def finished_on_the_way(s):
@@ -528,9 +765,10 @@
     normed = (wide_in * inv_rms * gain_full).astype(BF16)
     conv_in = dot(normed, conv_weights, out=BF16)
     halo = (taps - 1) * seqs
-    normed_halo = moved(normed[rows - halo :], "seq", 1)
+    lead = halo + -halo % 16
+    normed_halo = moved(normed[rows - lead :], "seq", 1)
     previous = dot(normed_halo, conv_weights, out=BF16)
-    padded = jnp.concatenate([previous, conv_in], axis=0).astype(F32)
+    padded = jnp.concatenate([previous[lead - halo :], conv_in], axis=0).astype(F32)
     conv_taps = conv_weight.astype(F32)
     conv_out = conv_bias.astype(F32) + sum(
         conv_taps[k] * padded[k * seqs : k * seqs + rows] for k in range(taps)
@@ -590,91 +828,98 @@
         local_start, step_total, rate, "seq", -1, [lambda sent, _: enter_h, first_side, second_side]
     )
     _, history, starts, gated_out, gate_grad = filled[2]
-    by_owner = lambda value: value.reshape(rows, -1, share).swapaxes(0, 1)
     by_part = lambda value: value.reshape(seq_count, -1, value.shape[-1])
-    first_product = lambda columns, value: dot(columns, value, CONTRACT_FIRST, out=BF16).reshape(
-        (2,) * (len(seq_bits) - 1) + (-1, inner)
-    )
-    out_weight_sum = Scattered(None, "seq", seq_bits, (None, first_product(sides[0][1], gated_out)))
-    gate_weight_sum = Scattered(None, "seq", other_bits, (None, first_product(sides[1][1], gate_grad)))
-    weight_sums = [out_weight_sum, gate_weight_sum]
-    start_all(weight_sums)
-    for s, columns, value in zip(weight_sums, (sides[0][0], sides[1][0]), (gated_out, gate_grad)):
-        s.kept = first_product(columns, after(value, *[s.sent for s in weight_sums]))
-    enter_g = after(enter_g, [s.kept for s in weight_sums])
-    decay_parts, bias_parts, skip_parts, pre_grad, mixed_part, bc_grads = backward(
-        step, mixed, y_grad, wide_rows, rate, skip, history, starts, enter_g, chunk
-    )
-    pre_grad, bc_grads = end_all(weight_sums, pre_grad, bc_grads)
-    out_weight_grad = rest_scattered(out_weight_sum.value, "seq", seq_bits[0])
-    gate_weight_grad = rest_scattered(after(gate_weight_sum.value, out_weight_grad), "seq", other_bits[0])
-    low_grad = dot(step_weight, pre_grad, CONTRACT_LAST)
-    proj_sum = jnp.concatenate([low_grad, bc_grads], axis=0)
+    first_product = lambda columns, value: dot(columns, value, CONTRACT_FIRST, out=BF16)
+    out_sent, gate_sent = (
+        first_product(columns[1], value) for columns, value in zip(sides, (gated_out, gate_grad))
+    )
+    out_kept, gate_kept = (
+        first_product(columns[0], after(value, out_sent, gate_sent)) for columns, value in zip(sides, (gated_out, gate_grad))
+    )
+    out_chain = Chain(None, "seq", seq_bits, halves=(out_kept, out_sent))
+    gate_chain = Chain(None, "seq", other_bits, halves=(gate_kept, gate_sent))
+    apart, joint = [[out_chain], [gate_chain]], [[out_chain, gate_chain]]
+    (enter_g,) = send_chains(apart, [out_sent, gate_sent], enter_g)
+    enter_g = after(enter_g, out_kept, gate_kept)
+    chips = (2,) * (chan_bits - 1)
+
+    def features(*pairs):
+        sides = product_sides(own_bit("chan", 0), share, *pairs)
+        return tuple(side.reshape(chips + side.shape[1:]) for side in sides)
+
+    scan_sums, pre_grad, mixed_part, proj_sum = backward(
+        step, mixed, y_grad, wide_rows, rate, skip, step_weight, history, starts, enter_g, chunk
+    )
+    pre_grad, proj_sum = end_chains(apart, pre_grad, proj_sum)
     for bit in range(chan_bits):
         received = swapped(proj_sum.astype(BF16) if bit else proj_sum, "chan", bit)
+        if bit == 0:
+            (received,) = send_chains(apart, merge(apart), received)
         if bit == chan_bits - 1:
-            branch = dot(after(gated_out, proj_sum), out_weight, CONTRACT_LAST, out=BF16)
-            received, branch = lax.optimization_barrier((received, branch))
+            branch_sum = Scattered(None, "chan", halves=features((after(gated_out, proj_sum), out_weight)))
+            received, branch_sum.kept, branch_sum.sent = lax.optimization_barrier(
+                (received, branch_sum.kept, branch_sum.sent)
+            )
         proj_sum = proj_sum + received.astype(F32)
     proj_grad = proj_sum.astype(BF16)
-    branch_sum = Scattered(by_owner(branch), "chan")
-    (proj_grad,) = start_all([branch_sum], proj_grad)
-    proj_weight_part = dot(proj_grad, mixed, out=BF16)
-    step_weight_part = dot(step_low, pre_grad, out=BF16)
-    mixed_grad = mixed_part + dot(proj_grad, proj_weight, CONTRACT_FIRST)
-    conv_grad = mixed_grad * silu_slope(conv_out)
-    conv_bias_grad = jnp.sum(conv_grad, axis=0)
-    conv_weight_grad = jnp.stack(
-        [jnp.sum(conv_grad * padded[k * seqs : k * seqs + rows], axis=0) for k in range(taps)]
-    )
-    incoming = moved(conv_grad[:halo], "seq", -1)
-
-    def spread_back(grads, count):
-        return sum(conv_taps[k] * grads[(taps - 1 - k) * seqs : (taps - 1 - k) * seqs + count] for k in range(taps))
-
-    none = jnp.zeros((halo, inner), F32)
-    own_spread = spread_back(jnp.concatenate([none, conv_grad, none], axis=0), rows + halo).astype(BF16)
-    own_spread, out_weight_grad = end_all([branch_sum], own_spread, out_weight_grad)
+    own_spread, first_grad, conv_sums = conv_back(
+        proj_grad, proj_weight, mixed_part, conv_out, conv_in, previous, conv_taps, chunk
+    )
+    incoming = moved(first_grad, "seq", -1)
+    (own_spread,) = end_chains(apart, own_spread)
     half = inner // 2
-    sums = jnp.concatenate(
-        [
-            jnp.sum(decay_parts, axis=1),
-            conv_weight_grad,
-            conv_bias_grad[None],
-            jnp.sum(bias_parts, axis=0)[None],
-            jnp.sum(skip_parts, axis=0)[None],
-        ],
-        axis=0,
-    )
-
+    first_last, second_last = (
+        by_part(dot(extended_normed, own_spread[:, at : at + half], CONTRACT_FIRST, out=BF16)) for at in (0, half)
+    )
+    first, second = Chain([first_last], "seq", seq_bits), Chain([second_last], "seq", other_bits)
+    weight_message = merge(apart)
+    in_window = [[first], [second], [out_chain]]
+    (own_spread,) = start_all([branch_sum], own_spread)
+    own_spread, incoming = send_chains(in_window, [first.sent, second.sent, weight_message[0]], own_spread, incoming)
+    zeros = jnp.zeros((halo, inner), F32)
+    from_after = jnp.concatenate([zeros, incoming, zeros], axis=0)
+    late = sum(
+        conv_taps[k] * from_after[(2 * taps - 2 - k) * seqs - halo : (2 * taps - 2 - k) * seqs] for k in range(taps)
+    )
+    conv_in_grad = jnp.concatenate(
+        [own_spread[lead : lead + rows - halo], (own_spread[lead + rows - halo :].astype(F32) + late).astype(BF16)], axis=0
+    )
+    late_proj, late_pre, late_sums = after((proj_grad, pre_grad, conv_sums), own_spread)
+    proj_weight_part = dot(late_proj, mixed, out=BF16)
+    step_weight_part = dot(step_low, late_pre, out=BF16)
+    sums = jnp.concatenate([scan_sums, jnp.sum(late_sums, axis=1)], axis=0)
     sum_rows = sums.shape[0]
     sums = padded_rows(jnp.concatenate([sums[:, :half], sums[:, half:]], axis=0), 0, 16)
-
-    def last_blocks(columns):
-        conv_weights_part = dot(extended_normed, own_spread[:, columns], CONTRACT_FIRST, out=BF16)
-        blocks = [by_part(conv_weights_part), by_part(proj_weight_part[:, columns]), by_part(step_weight_part[:, columns])]
-        return padded_rows(jnp.concatenate(blocks, axis=1), 1, 16)
-
-    last_sums = [
-        ScatteredWith(last_blocks(slice(0, half)), "seq", seq_bits, sums),
-        Scattered(last_blocks(slice(half, inner)), "seq", other_bits),
-    ]
-    last_sent = start_all([*last_sums, branch_sum], conv_grad, incoming)
-    conv_grad, incoming = last_sent
-    conv_in_grad = spread_back(jnp.concatenate([conv_grad, incoming], axis=0), rows).astype(BF16)
-    gate_side = dot(gate_grad, after(gate_weights, [s.sent for s in last_sums]), CONTRACT_LAST)
-    normed_part = (dot(conv_in_grad, conv_weights, CONTRACT_LAST) + gate_side).astype(BF16)
-    (normed_part,) = end_all([*last_sums, branch_sum], normed_part)
-    normed_sum = Scattered(by_owner(normed_part), "chan")
-    conv_in_grad, row_gate = start_all([normed_sum, *last_sums], conv_in_grad, gate_grad)
+    small_blocks = jnp.concatenate([by_part(proj_weight_part), by_part(step_weight_part)], axis=1)
+    small_blocks = padded_rows(jnp.concatenate([small_blocks[..., :half], small_blocks[..., half:]], axis=1), 1, 16)
+    third = Chain([small_blocks], "seq", seq_bits, sums)
     row_dots = jnp.sum(
-        conv_in_grad.astype(F32) * conv_in.astype(F32) + row_gate.astype(F32) * gate_pre, axis=1
-    )
-    row_dots = summed(row_dots, "chan", chan_bits)[:, None]
-    row_dots, gate_weight_grad = end_all([normed_sum, *last_sums], row_dots, gate_weight_grad)
-    (row_dots,) = start_all([normed_sum, *last_sums], row_dots)
-    (row_dots,) = end_all([normed_sum, *last_sums], row_dots)
+        conv_in_grad.astype(F32) * conv_in.astype(F32) + gate_grad.astype(F32) * gate_pre, axis=1
+    )
+    last_pair = (gate_grad, after(gate_weights, third.sent, row_dots))
+    normed_sum = Scattered(None, "chan", halves=features((conv_in_grad, conv_weights), last_pair))
+    normed_sum.sent, normed_sum.kept, third.sent = end_chains(
+        in_window, normed_sum.sent, normed_sum.kept, third.sent
+    )
+    row_dots, third.sent = end_all([branch_sum], row_dots, third.sent)
+    groups = [[first], [second]]
+    messages = merge(groups)
+    (row_dots,) = start_all([normed_sum, branch_sum], row_dots)
+    in_window = [*groups, [third], [gate_chain]]
+    (row_dots,) = send_chains(in_window, [*messages, third.sent, weight_message[1]], row_dots)
+    row_dots = row_dots + swapped(row_dots, "chan", 0)
+    (row_dots,) = end_all([normed_sum, branch_sum], row_dots)
+    (row_dots,) = end_chains(in_window, row_dots)
+    groups = [[first], [second], [third]]
+    messages = merge(groups)
+    (row_dots,) = start_all([normed_sum], row_dots)
+    (row_dots,) = send_chains(groups, messages, row_dots)
+    for bit in range(1, chan_bits):
+        row_dots = row_dots + swapped(row_dots, "chan", bit)
+    (row_dots,) = end_all([normed_sum], row_dots)
+    (row_dots,) = end_chains(groups, row_dots)
     normed_grad = finished_on_the_way(normed_sum)
+    row_dots = row_dots[:, None]
     wide_own = own_in.astype(F32)
     own_gain = lax.dynamic_slice_in_dim(gain_full, lax.axis_index("chan") * share, share, 0)
     in_rows = (
@@ -684,25 +929,28 @@
     ).astype(BF16)
     in_grad = in_rows.reshape(toks, seqs, share).swapaxes(0, 1)
     gain_grad = summed(jnp.sum(normed_grad * wide_own * inv_rms, axis=0), "seq", bits_of("seq"))
-    last = jnp.concatenate([finished_on_the_way(s) for s in last_sums], axis=-1)
-    sums = last_sums[0].extra
+    (first_last,), (second_last,), (small, sums) = last_of(first), last_of(second), last_of(third)
+    (out_weight_grad,), (gate_weight_grad,) = last_of(out_chain), last_of(gate_chain)
+    last = jnp.concatenate([first_last, second_last], axis=1)
     sums = jnp.concatenate([sums[:sum_rows], sums[sum_rows : 2 * sum_rows]], axis=1)
-    weight_share, proj_share, step_share = (count // seq_count for count in (model, proj_weight.shape[0], rank))
+    proj_share, step_share = proj_weight.shape[0] // seq_count, rank // seq_count
+    each = proj_share + step_share
+    small_of = lambda start, count: jnp.concatenate([small[start : start + count], small[each + start : each + start + count]], axis=1)
     block_rows = (own_in.astype(F32) + finished_on_the_way(branch_sum)).astype(BF16)
     block_out = block_rows.reshape(toks, seqs, share).swapaxes(0, 1)
     return (
         block_out,
         in_grad,
         gain_grad,
-        jnp.stack([last[:weight_share], gate_weight_grad], axis=1),
-        sums[states : states + taps],
-        sums[states + taps],
-        last[weight_share : weight_share + proj_share],
-        last[weight_share + proj_share : weight_share + proj_share + step_share],
-        sums[states + taps + 1],
-        sums[:states] * (1.0 / LOG2E),
-        sums[states + taps + 2],
-        out_weight_grad.astype(F32),
+        jnp.stack([last, gate_weight_grad], axis=1),
+        sums[states + 2 : states + 2 + taps],
+        sums[states + 2 + taps],
+        small_of(0, proj_share),
+        small_of(proj_share, step_share),
+        sums[states],
+        sums[:states],
+        sums[states + 1],
+        out_weight_grad,
     )
 
 

time: 494 us -> 456 us (0.923)
  Pallas kernels: 116 us -> 172 us
  waiting for transfers between devices: 98 us -> 60.5 us
  other arithmetic: 84.4 us -> 53.1 us
  starting transfers between devices: 39.6 us -> 65.1 us
  matrix products: 71.5 us -> 49.6 us
  local copies, waits for them, and re-layouts: 61.7 us -> 46.6 us
  between operations: 16.2 us -> 2.33 us
    pallas_call x0 -> x8, Pallas kernels: none -> 55 us  [the longest x2 24.2 us: product_sides(): pl.pallas_call(functools.partial(product_kernel, len(pairs)), grid_spec=p...]
    ppermute x27 -> x34, waiting for transfers between devices: 89 us -> 59 us  [swapped(): return lax.ppermute(value, axis, [(i, i ^ 1 << bit) for i in range(count)])]
    ppermute x27 -> x34, starting transfers between devices: 20.1 us -> 45.1 us  [swapped(): return lax.ppermute(value, axis, [(i, i ^ 1 << bit) for i in range(count)])]
    dot_general x19 -> x14, matrix products: 71.5 us -> 49.6 us  [dot(): return lax.dot_general(a, b, dims, preferred_element_type=out)]
    convert_element_type x8 -> x2, other arithmetic: 17.7 us -> 2.78 us  [add(): self.value = value.astype(BF16) if self.left else value]
    unnamed x184 -> x141, local copies, waits for them, and re-layouts: 23.4 us -> 9 us
    convert_element_type x8 -> x4, other arithmetic: 12.2 us -> 2.86 us  [the longest x1 0.97 us: two_parts(): upper = value.astype(BF16)]
    reduce_scatter x2 -> x0, waiting for transfers between devices: 7.35 us -> none  [rest_scattered(): lax.psum_scatter(value, axis, scatter_dimension=0, tiled=True, axis_index...]
  transfers between devices with their start and end apart: 37 -> 42, of which waited for: 17 -> 16; matrix products, arithmetic and copies ran while one was open for 31% -> 24% of each run, Pallas kernels for 24% -> 38%
where the time goes in v3:
time: 456 us; the launch traced here: 450 us
  Pallas kernels  172 us (38%)
  starting transfers between devices  65.1 us (14%)
  waiting for transfers between devices  60.5 us (13%)
  other arithmetic  53.1 us (12%)
  matrix products  49.6 us (11%)
  local copies, waits for them, and re-layouts  46.6 us (10%)
    ppermute x34, waiting for transfers between devices, swapped(): return lax.ppermute(value, axis, [(i, i ^ 1 << bit) for i in range(count)])  59 us
    dot_general x14, matrix products, dot(): return lax.dot_general(a, b, dims, preferred_element_type=out)  49.6 us
    pallas_call x1, Pallas kernels, backward(): pl.pallas_call(functools.partial(bwd_kernel, chunk), grid=(grid,), in_spe...  45.9 us
    ppermute x34, starting transfers between devices, swapped(): return lax.ppermute(value, axis, [(i, i ^ 1 << bit) for i in range(count)])  45.1 us
    pallas_call x2, Pallas kernels, forward(): pl.pallas_call(functools.partial(fwd_kernel, chunk), grid=(last - first,)...  35.6 us
    pallas_call x2, Pallas kernels, product_sides(): pl.pallas_call(functools.partial(product_kernel, len(pairs)), grid_spec=p...  24.2 us
    ppermute x8, starting transfers between devices, moved(): lax.ppermute(value, axis, [(i, i + distance) for i in range(count) if 0 <...  20 us
    pallas_call x1, Pallas kernels, local_ends(): pl.pallas_call(functools.partial(ends_kernel, chunk), grid=(grid,), in_sp...  19.3 us
  transfers between devices with their start and end apart: 42, of which 16 were waited for; matrix products, arithmetic and copies ran while one was open for 24% of the time, Pallas kernels for 38%

profile of v3, /device:TPU:0, one launch (start us, length us, event | category | flops | bytes accessed | tf_op | source)
XLA Modules:
  0.0 449.7 jit_solution(15797260357974044863)
XLA Ops:
  6.4 16.1 %fusion.49 = (bf16[2048,1,1024]{2,1,0:T(2,128)(2,1)S(1)}, bf16[2048,1,1024]{2,1,0:T(2,128)(2,1)S(1)}) fusion(bf16[2048,2,1024]{2,1,0:T(2,128)(2,1)} %param.14), kind=kLoop, calls=%fused_computation.188 | loop fusion | bytes 16777216 | tf_op jit(solution)/shard_map/slice | solution.py:761
  22.6 5.9 %copy_bitcast_fusion = (bf16[2048,1024]{1,0:T(8,128)(2,1)}, bf16[2048,1024]{1,0:T(8,128)(2,1)}) fusion(bf16[2048,1,1024]{2,1,0:T(2,128)(2,1)S(1)} %get-tuple-element.358, bf16[2048,1,1024]{2,1,0:T(2,128)(2,1)S(1)} %get-tuple-element.359), kind=kLoop, calls=%fused_computation.17 | loop fusion | bytes 16777216 | tf_op jit(solution)/shard_map/squeeze | solution.py:761
  37.6 3.8 collective-permute-start.3
  41.4 4.7 %fusion.55.in_ref = bf16[1024,1024]{1,0:T(8,128)(2,1)S(1)} fusion(bf16[1024,2048]{1,0:T(8,128)(2,1)S(1)} %fusion.2, bf16[2048,1024]{1,0:T(8,128)(2,1)S(1)} %copy-done.6), kind=kOutput, calls=%fused_computation.194 | convolution fusion | flops 4294967296 | bytes 10485760 | tf_op jit(solution)/shard_map/dot_general | solution.py:486
  47.5 3.8 multiply_convert_fusion
  54.5 4.5 %fusion.56.gate_ref = f32[1024,1024]{1,0:T(8,128)S(1)} fusion(bf16[1024,2048]{1,0:T(8,128)(2,1)S(1)} %fusion.2, bf16[2048,1024]{1,0:T(8,128)(2,1)S(1)} %copy-done.13), kind=kOutput, calls=%fused_computation.195 | convolution fusion | flops 4294967296 | bytes 12582912 | tf_op jit(solution)/shard_map/dot_general | solution.py:486
  63.2 5.7 %collective-permute-done.5 = bf16[160,1024]{1,0:T(8,128)(2,1)S(1)} collective-permute-done((bf16[160,1024]{1,0:T(8,128)(2,1)S(1)}, bf16[160,1024]{1,0:T(8,128)(2,1)S(1)}, u32[]{:S(2)}, u32[]{:S(2)}) %collective-permute-start.5) | collective-permute-done | bytes 327712 | tf_op jit(solution)/shard_map/ppermute | solution.py:495
  71.3 4.7 %bitcast_reduce_fusion = (f32[8,1024]{1,0:T(8,128)S(1)}, f32[1024,1024]{1,0:T(8,128)}) fusion(f32[1024]{0:T(1024)S(1)} %convert_element_type.288, bf16[128,1024]{1,0:T(8,128)(2,1)S(1)} %copy-done.44, f32[160,1024]{1,0:T(8,128)S(1)} %convert_add_fusion.4), kind=kOutput, calls=%fused_computation.19 | convolution fusion | flops 276815872 | bytes 4755456 | tf_op jit(solution)/shard_map/dot_general | solution.py:486
  76.9 19.3 %local_ends.1 = (f32[16,8,1024]{2,1,0:T(8,128)}, f32[128,32,8,128]{3,2,1,0:T(8,128)}) custom-call(f32[1024,1024]{1,0:T(8,128)} %get-tuple-element.421.step_ref, bf16[1024,1024]{1,0:T(8,128)(2,1)} %copy-done, f32[32,1024]{1,0:T(8,128)} %slice.282.rows_ref, f32[16,8,1024]{2,1,0:T(8,128)} %broadcast_in_dim.8.rate_ref), custom_call_target="tpu_custom_call" | custom-call | flops 16777216 | bytes 16777216 | tf_op jit(solution)/shard_map/local_ends/pallas_call | solution.py:91
  103.9 7.2 %multiply_multiply_fusion = (f32[1024,1024]{1,0:T(8,128)}, f32[1024,1024]{1,0:T(8,128)}) fusion(f32[1024,1024]{1,0:T(8,128)S(1)} %fusion.56.gate_ref, bf16[1024,2048]{1,0:T(8,128)(2,1)S(1)} %pad_maximum_fusion.2, bf16[2048,1024]{1,0:T(8,128)(2,1)S(1)} %copy-done.23), kind=kOutput, calls=%fused_computation.23 | convolution fusion | flops 4300210176 | bytes 20971520 | tf_op jit(solution)/shard_map/dot_general | solution.py:486
  114.8 16.6 %local_starts.1 = f32[16,8,1024]{2,1,0:T(8,128)} custom-call(f32[1024,1024]{1,0:T(8,128)} %get-tuple-element.421.step_ref, f32[1024,1024]{1,0:T(8,128)} %get-tuple-element.179.yg_ref, f32[128,32,8,128]{3,2,1,0:T(8,128)} %get-tuple-element.180.spread_ref, f32[16,8,1024]{2,1,0:T(8,128)} %broadcast_in_dim.8.rate_ref), custom_call_target="tpu_custom_call" | custom-call | flops 16777216 | bytes 16777216 | tf_op jit(solution)/shard_map/local_starts/pallas_call | solution.py:112
  131.8 3.8 collective-permute-start.11
  149.2 17.7 %scan_forward.2 = (f32[16,8,1024]{2,1,0:T(8,128)}, bf16[128,8,128,128]{3,2,1,0:T(8,128)(2,1)}, bf16[8,16,8,1024]{3,2,1,0:T(8,128)(2,1)}, bf16[1024,1024]{1,0:T(8,128)(2,1)}, bf16[1024,1024]{1,0:T(8,128)(2,1)}) custom-call(f32[1024,1024]{1,0:T(8,128)} %get-tuple-element.421.step_ref, bf16[1024,1024]{1,0:T(8,128)(2,1)} %copy-done, ...), custom_call_target="tpu_custom_call", output_to_operand_aliasing={{0}: (7, {})} | custom-call | flops 8388608 | bytes 8388608 | tf_op jit(solution)/shard_map/scan_forward/pallas_call | solution.py:176
  168.5 17.9 %scan_forward.3 = (f32[16,8,1024]{2,1,0:T(8,128)}, bf16[128,8,128,128]{3,2,1,0:T(8,128)(2,1)}, bf16[8,16,8,1024]{3,2,1,0:T(8,128)(2,1)}, bf16[1024,1024]{1,0:T(8,128)(2,1)}, bf16[1024,1024]{1,0:T(8,128)(2,1)}) custom-call(f32[1024,1024]{1,0:T(8,128)} %get-tuple-element.421.step_ref, ...), custom_call_target="tpu_custom_call", output_to_operand_aliasing={{0}: (7, {}), {1}: (8, {}), {2}: (9, {}), {3}: (10, {}), {4... | custom-call | flops 8388608 | bytes 8388608 | tf_op jit(solution)/shard_map/scan_forward/pallas_call | solution.py:176
  186.4 5.5 %fusion.58 = bf16[1024,1024]{1,0:T(8,128)(2,1)} fusion(bf16[1024,1024]{1,0:T(8,128)(2,1)S(1)} %pad_maximum_fusion.6, bf16[1024,1024]{1,0:T(8,128)(2,1)} %get-tuple-element.222.refs_1_), kind=kOutput, calls=%fused_computation.197 | convolution fusion | flops 2147483648 | bytes 6291456 | tf_op jit(solution)/shard_map/dot_general | solution.py:486
  203.9 3.8 fusion.59.refs_0_
  207.7 45.9 %scan_backward.1 = (f32[18,1024]{1,0:T(8,128)}, bf16[1024,1024]{1,0:T(8,128)(2,1)}, f32[1024,1024]{1,0:T(8,128)}, f32[160,1024]{1,0:T(8,128)}) custom-call(f32[1024,1024]{1,0:T(8,128)} %get-tuple-element.421.step_ref, bf16[1024,1024]{1,0:T(8,128)(2,1)} %copy-done, f32[1024,1024]{1,0:T(8,128)} %get-tuple-element.179.yg_ref, ...), custom_call_target="tpu_custom_call" | custom-call | flops 16777216 | bytes 16777216 | tf_op jit(solution)/shard_map/scan_backward/pallas_call | solution.py:300
  254.4 6.4 %merge_messages.5 = (bf16[512,1024]{1,0:T(8,128)(2,1)}, bf16[512,1024]{1,0:T(8,128)(2,1)}, bf16[512,1024]{1,0:T(8,128)(2,1)}, bf16[512,1024]{1,0:T(8,128)(2,1)}) custom-call(s32[2]{0:T(128)} %get-tuple-element.426.bits_ref, bf16[1024,1024]{1,0:T(8,128)(2,1)} %fusion.59.refs_0_, bf16[1024,1024]{1,0:T(8,128)(2,1)} %collective-permute-done.15.refs_1_, ...), custom_call_target="tpu_custom_call" | custom-call | flops 1024 | bytes 1024 | tf_op jit(solution)/shard_map/merge_messages/pallas_call | solution.py:668
  262.9 9.6 %product_sides.2 = (bf16[2,1024,512]{2,1,0:T(8,128)(2,1)}, bf16[2,1024,512]{2,1,0:T(8,128)(2,1)}) custom-call(s32[1]{0:T(128)} %bitcast.21.core_ref, bf16[1024,1024]{1,0:T(8,128)(2,1)} %get-tuple-element.232.refs_0_, bf16[2048,1024]{1,0:T(8,128)(2,1)} %refs_1_.1), custom_call_target="tpu_custom_call" | custom-call | flops 1024 | bytes 1024 | tf_op jit(solution)/shard_map/product_sides/pallas_call | solution.py:464
  273.3 11.7 %conv_backward.1 = (bf16[1056,1024]{1,0:T(8,128)(2,1)}, f32[24,1024]{1,0:T(8,128)}, f32[5,8,1024]{2,1,0:T(8,128)}) custom-call(bf16[160,1024]{1,0:T(8,128)(2,1)} %add_convert_fusion.2.proj_ref, bf16[160,1024]{1,0:T(8,128)(2,1)} %weight_ref.1, f32[1024,1024]{1,0:T(8,128)} %get-tuple-element.240.part_ref, f32[1024,1024]{1,0:T(8,128)} %get-tuple-element.357.conv_ref, ...), custom_call_target="tpu_custom_call" | custom-call | flops 1048576 | bytes 1048576 | tf_op jit(solution)/shard_map/conv_backward/pallas_call | solution.py:393
  286.8 4.5 %fusion.16 = bf16[2048,512]{1,0:T(8,128)(2,1)S(1)} fusion(bf16[1056,2048]{1,0:T(8,128)(2,1)S(1)} %bitcast.134, bf16[1056,1024]{1,0:T(8,128)(2,1)} %get-tuple-element.252), kind=kOutput, calls=%fused_computation.48 | convolution fusion | flops 2214592512 | bytes 7503872 | tf_op jit(solution)/shard_map/dot_general | solution.py:486
  291.3 4.3 fusion.18
  297.1 4.0 merge_messages.6
  324.7 14.6 %product_sides.3 = (bf16[2,1024,512]{2,1,0:T(8,128)(2,1)}, bf16[2,1024,512]{2,1,0:T(8,128)(2,1)}) custom-call(s32[1]{0:T(128)} %bitcast.21.core_ref, bf16[1024,1024]{1,0:T(8,128)(2,1)} %pad_maximum_fusion.7.refs_0_, bf16[1024,1024]{1,0:T(8,128)(2,1)} %get-tuple-element.222.refs_1_, bf16[2048,1024]{1,0:T(8,128)(2,1)} %get-tuple-element.167.refs_2_, ...), custom_call_target="tpu_custom_call" | custom-call | flops 1024 | bytes 1024 | tf_op jit(solution)/shard_map/product_sides/pallas_call | solution.py:464
  339.3 4.0 collective-permute-done.25
  348.8 3.9 merge_messages.7
  359.7 13.3 %collective-permute-done.27 = bf16[1024,512]{1,0:T(8,128)(2,1)S(1)} collective-permute-done((bf16[1024,512]{1,0:T(8,128)(2,1)}, bf16[1024,512]{1,0:T(8,128)(2,1)S(1)}, u32[]{:S(2)}, u32[]{:S(2)}) %collective-permute-start.27) | collective-permute-done | bytes 1048608 | tf_op jit(solution)/shard_map/ppermute | solution.py:495
  374.6 10.2 %collective-permute-done.31.refs_5_ = bf16[416,512]{1,0:T(8,128)(2,1)S(1)} collective-permute-done((bf16[416,512]{1,0:T(8,128)(2,1)}, bf16[416,512]{1,0:T(8,128)(2,1)S(1)}, u32[]{:S(2)}, u32[]{:S(2)}) %collective-permute-start.31) | collective-permute-done | bytes 426016 | tf_op jit(solution)/shard_map/ppermute | solution.py:495
  406.5 7.4 %collective-permute-done.34 = f32[1024]{0:T(1024)S(1)} collective-permute-done((f32[1024]{0:T(1024)S(1)}, f32[1024]{0:T(1024)S(1)}, u32[]{:S(2)}, u32[]{:S(2)}) %collective-permute-start.34) | collective-permute-done | bytes 4128 | tf_op jit(solution)/shard_map/ppermute | solution.py:495
  413.9 5.0 %collective-permute-done.35 = bf16[256,512]{1,0:T(8,128)(2,1)S(1)} collective-permute-done((bf16[256,512]{1,0:T(8,128)(2,1)}, bf16[256,512]{1,0:T(8,128)(2,1)S(1)}, u32[]{:S(2)}, u32[]{:S(2)}) %collective-permute-start.35) | collective-permute-done | bytes 262176 | tf_op jit(solution)/shard_map/ppermute | solution.py:495
  425.0 4.5 fusion.12
  433.2 4.1 collective-permute-start.39
  (325 shorter events, 153.0 us)
Async XLA Ops:
  3.4 26.3 %collective-permute-start = (bf16[1024,512]{1,0:T(8,128)(2,1)}, bf16[1024,512]{1,0:T(8,128)(2,1)S(1)}, u32[]{:S(2)}, u32[]{:S(2)}) collective-permute-start(bf16[1024,512]{1,0:T(8,128)(2,1)} %bitcast.129), channel_id=1, source_target_pairs={{0,2},{1,3},{2,0},{3,1},{4,6},{5,7},{6,4},{7,5},{8,10},{9,11},{10,... | collective-permute-start | bytes 3145736 | tf_op jit(solution)/shard_map/ppermute | solution.py:495
  6.4 23.5 %collective-permute-start.2 = (bf16[1024,512]{1,0:T(8,128)(2,1)}, bf16[1024,512]{1,0:T(8,128)(2,1)S(1)}, u32[]{:S(2)}, u32[]{:S(2)}) collective-permute-start(bf16[1024,512]{1,0:T(8,128)(2,1)} %bitcast.129), channel_id=1, source_target_pairs={{0,1},{1,0},{2,3},{3,2},{4,5},{5,4},{6,7},{7,6},{8,9},{9,8},{10,11... | collective-permute-start | bytes 3145736 | tf_op jit(solution)/shard_map/ppermute | solution.py:495
  68.9 27.3 %collective-permute-start.7 = (bf16[1024,512]{1,0:T(8,128)(2,1)S(1)}, bf16[1024,512]{1,0:T(8,128)(2,1)S(1)}, u32[]{:S(2)}, u32[]{:S(2)}) collective-permute-start(bf16[1024,512]{1,0:T(8,128)(2,1)S(1)} %bitcast.139), channel_id=1, source_target_pairs={{0,2},{1,3},{2,0},{3,1},{4,6},{5,7},{6,4},{7,5},{8,10},{9,11},{10,... | collective-permute-start | bytes 3145736 | tf_op jit(solution)/shard_map/ppermute | solution.py:495
  70.4 30.9 %collective-permute-start.9 = (bf16[1024,512]{1,0:T(8,128)(2,1)S(1)}, bf16[1024,512]{1,0:T(8,128)(2,1)S(1)}, u32[]{:S(2)}, u32[]{:S(2)}) collective-permute-start(bf16[1024,512]{1,0:T(8,128)(2,1)S(1)} %bitcast.140), channel_id=1, source_target_pairs={{0,1},{1,0},{2,3},{3,2},{4,5},{5,4},{6,7},{7,6},{8,9},{9,8},{10,11... | collective-permute-start | bytes 3145736 | tf_op jit(solution)/shard_map/ppermute | solution.py:495
  97.8 13.3 %collective-permute-start.6 = (bf16[18,8,1024]{2,1,0:T(8,128)(2,1)S(1)}, bf16[18,8,1024]{2,1,0:T(8,128)(2,1)S(1)}, u32[]{:S(2)}, u32[]{:S(2)}) collective-permute-start(bf16[18,8,1024]{2,1,0:T(8,128)(2,1)S(1)} %pad_maximum_fusion.11), channel_id=1, source_target_pairs={{0,4},{4,8},{8,12},{12,16},{16,20},{20,24},{24,28},{1,5},{5,9},{9,... | collective-permute-start | bytes 884744 | tf_op jit(solution)/shard_map/ppermute | solution.py:500
  111.3 20.1 %collective-permute-start.10 = (bf16[18,8,1024]{2,1,0:T(8,128)(2,1)S(1)}, bf16[18,8,1024]{2,1,0:T(8,128)(2,1)S(1)}, u32[]{:S(2)}, u32[]{:S(2)}) collective-permute-start(bf16[18,8,1024]{2,1,0:T(8,128)(2,1)S(1)} %pad_maximum_fusion.14), channel_id=1, source_target_pairs={{0,8},{4,12},{8,16},{12,20},{16,24},{20,28},{1,9},{5,13},{9,17},{1... | collective-permute-start | bytes 884744 | tf_op jit(solution)/shard_map/ppermute | solution.py:500
  131.8 12.7 %collective-permute-start.11 = (bf16[18,8,1024]{2,1,0:T(8,128)(2,1)S(1)}, bf16[18,8,1024]{2,1,0:T(8,128)(2,1)S(1)}, u32[]{:S(2)}, u32[]{:S(2)}) collective-permute-start(bf16[18,8,1024]{2,1,0:T(8,128)(2,1)S(1)} %pad_maximum_fusion.15), channel_id=1, source_target_pairs={{0,16},{4,20},{8,24},{12,28},{1,17},{5,21},{9,25},{13,29},{2,18},{... | collective-permute-start | bytes 884744 | tf_op jit(solution)/shard_map/ppermute | solution.py:500
  136.7 10.2 %collective-permute-start.12 = (bf16[18,8,1024]{2,1,0:T(8,128)(2,1)S(1)}, bf16[18,8,1024]{2,1,0:T(8,128)(2,1)S(1)}, u32[]{:S(2)}, u32[]{:S(2)}) collective-permute-start(bf16[18,8,1024]{2,1,0:T(8,128)(2,1)S(1)} %pad_maximum_fusion.10), channel_id=1, source_target_pairs={{4,0},{8,4},{12,8},{16,12},{20,16},{24,20},{28,24},{5,1},{9,5},{13... | collective-permute-start | bytes 884744 | tf_op jit(solution)/shard_map/ppermute | solution.py:500
  147.2 19.6 %collective-permute-start.13 = (bf16[18,8,1024]{2,1,0:T(8,128)(2,1)S(1)}, bf16[18,8,1024]{2,1,0:T(8,128)(2,1)S(1)}, u32[]{:S(2)}, u32[]{:S(2)}) collective-permute-start(bf16[18,8,1024]{2,1,0:T(8,128)(2,1)S(1)} %pad_maximum_fusion.16), channel_id=1, source_target_pairs={{8,0},{12,4},{16,8},{20,12},{24,16},{28,20},{9,1},{13,5},{17,9},{2... | collective-permute-start | bytes 884744 | tf_op jit(solution)/shard_map/ppermute | solution.py:500
  167.2 19.2 %collective-permute-start.14 = (bf16[18,8,1024]{2,1,0:T(8,128)(2,1)S(1)}, bf16[18,8,1024]{2,1,0:T(8,128)(2,1)S(1)}, u32[]{:S(2)}, u32[]{:S(2)}) collective-permute-start(bf16[18,8,1024]{2,1,0:T(8,128)(2,1)S(1)} %pad_maximum_fusion.17), channel_id=1, source_target_pairs={{16,0},{20,4},{24,8},{28,12},{17,1},{21,5},{25,9},{29,13},{18,2},{... | collective-permute-start | bytes 884744 | tf_op jit(solution)/shard_map/ppermute | solution.py:500
  195.4 58.3 %collective-permute-start.15 = (bf16[1024,1024]{1,0:T(8,128)(2,1)S(1)}, bf16[1024,1024]{1,0:T(8,128)(2,1)}, u32[]{:S(2)}, u32[]{:S(2)}) collective-permute-start(bf16[1024,1024]{1,0:T(8,128)(2,1)S(1)} %fusion.57), channel_id=1, source_target_pairs={{0,4},{4,0},{8,12},{12,8},{16,20},{20,16},{24,28},{28,24},{1,5},{5... | collective-permute-start | bytes 6291464 | tf_op jit(solution)/shard_map/ppermute | solution.py:495
  197.5 56.2 %collective-permute-start.16 = (bf16[1024,1024]{1,0:T(8,128)(2,1)}, bf16[1024,1024]{1,0:T(8,128)(2,1)}, u32[]{:S(2)}, u32[]{:S(2)}) collective-permute-start(bf16[1024,1024]{1,0:T(8,128)(2,1)} %fusion.58), channel_id=1, source_target_pairs={{0,8},{4,12},{8,0},{12,4},{16,24},{20,28},{24,16},{28,20},{1,9},{5... | collective-permute-start | bytes 6291464 | tf_op jit(solution)/shard_map/ppermute | solution.py:495
  260.8 25.9 %collective-permute-start.19 = (bf16[512,1024]{1,0:T(8,128)(2,1)}, bf16[512,1024]{1,0:T(8,128)(2,1)}, u32[]{:S(2)}, u32[]{:S(2)}) collective-permute-start(bf16[512,1024]{1,0:T(8,128)(2,1)} %get-tuple-element.237), channel_id=1, source_target_pairs={{0,8},{4,12},{8,0},{12,4},{16,24},{20,28},{24,16},{28,20},{1,9},{5... | collective-permute-start | bytes 3145736 | tf_op jit(solution)/shard_map/ppermute | solution.py:495
  260.8 25.9 %collective-permute-start.20 = (bf16[512,1024]{1,0:T(8,128)(2,1)}, bf16[512,1024]{1,0:T(8,128)(2,1)}, u32[]{:S(2)}, u32[]{:S(2)}) collective-permute-start(bf16[512,1024]{1,0:T(8,128)(2,1)} %get-tuple-element.238), channel_id=1, source_target_pairs={{0,4},{4,0},{8,12},{12,8},{16,20},{20,16},{24,28},{28,24},{1,5},{5... | collective-permute-start | bytes 3145736 | tf_op jit(solution)/shard_map/ppermute | solution.py:495
  261.8 10.7 %collective-permute-start.18 = (bf16[160,1024]{1,0:T(8,128)(2,1)}, bf16[160,1024]{1,0:T(8,128)(2,1)S(1)}, u32[]{:S(2)}, u32[]{:S(2)}) collective-permute-start(bf16[160,1024]{1,0:T(8,128)(2,1)} %get-tuple-element.344), channel_id=1, source_target_pairs={{0,2},{1,3},{2,0},{3,1},{4,6},{5,7},{6,4},{7,5},{8,10},{9,11},{10,... | collective-permute-start | bytes 983048 | tf_op jit(solution)/shard_map/ppermute | solution.py:495
  285.0 17.6 %collective-permute-start.22 = (f32[24,1024]{1,0:T(8,128)}, f32[24,1024]{1,0:T(8,128)S(1)}, u32[]{:S(2)}, u32[]{:S(2)}) collective-permute-start(f32[24,1024]{1,0:T(8,128)} %get-tuple-element.251), channel_id=1, source_target_pairs={{4,0},{8,4},{12,8},{16,12},{20,16},{24,20},{28,24},{5,1},{9,5},{13... | collective-permute-start | bytes 294920 | tf_op jit(solution)/shard_map/ppermute | solution.py:500
  302.6 41.4 %collective-permute-start.21 = (bf16[2,1024,512]{2,1,0:T(8,128)(2,1)}, bf16[2,1024,512]{2,1,0:T(8,128)(2,1)}, u32[]{:S(2)}, u32[]{:S(2)}) collective-permute-start(bf16[2,1024,512]{2,1,0:T(8,128)(2,1)} %get-tuple-element.243), channel_id=1, source_target_pairs={{0,1},{1,0},{2,3},{3,2},{4,5},{5,4},{6,7},{7,6},{8,9},{9,8},{10,11... | collective-permute-start | bytes 6291464 | tf_op jit(solution)/shard_map/ppermute | solution.py:495
  305.0 38.2 %collective-permute-start.23 = (bf16[1024,512]{1,0:T(8,128)(2,1)}, bf16[1024,512]{1,0:T(8,128)(2,1)}, u32[]{:S(2)}, u32[]{:S(2)}) collective-permute-start(bf16[1024,512]{1,0:T(8,128)(2,1)} %bitcast.150), channel_id=1, source_target_pairs={{0,4},{4,0},{8,12},{12,8},{16,20},{20,16},{24,28},{28,24},{1,5},{5... | collective-permute-start | bytes 3145736 | tf_op jit(solution)/shard_map/ppermute | solution.py:495
  307.3 36.7 %collective-permute-start.24 = (bf16[1024,512]{1,0:T(8,128)(2,1)}, bf16[1024,512]{1,0:T(8,128)(2,1)}, u32[]{:S(2)}, u32[]{:S(2)}) collective-permute-start(bf16[1024,512]{1,0:T(8,128)(2,1)} %bitcast.149), channel_id=1, source_target_pairs={{0,8},{4,12},{8,0},{12,4},{16,24},{20,28},{24,16},{28,20},{1,9},{5... | collective-permute-start | bytes 3145736 | tf_op jit(solution)/shard_map/ppermute | solution.py:495
  309.2 34.1 %collective-permute-start.25 = (bf16[256,1024]{1,0:T(8,128)(2,1)}, bf16[256,1024]{1,0:T(8,128)(2,1)}, u32[]{:S(2)}, u32[]{:S(2)}) collective-permute-start(bf16[256,1024]{1,0:T(8,128)(2,1)} %get-tuple-element.256), channel_id=1, source_target_pairs={{0,16},{4,20},{8,24},{12,28},{16,0},{20,4},{24,8},{28,12},{1,17},{... | collective-permute-start | bytes 1572872 | tf_op jit(solution)/shard_map/ppermute | solution.py:495
  347.3 27.3 %collective-permute-start.26 = (bf16[2,1024,512]{2,1,0:T(8,128)(2,1)}, bf16[2,1024,512]{2,1,0:T(8,128)(2,1)S(1)}, u32[]{:S(2)}, u32[]{:S(2)}) collective-permute-start(bf16[2,1024,512]{2,1,0:T(8,128)(2,1)} %get-tuple-element.270), channel_id=1, source_target_pairs={{0,1},{1,0},{2,3},{3,2},{4,5},{5,4},{6,7},{7,6},{8,9},{9,8},{10,11... | collective-permute-start | bytes 6291464 | tf_op jit(solution)/shard_map/ppermute | solution.py:495
  347.3 25.8 %collective-permute-start.27 = (bf16[1024,512]{1,0:T(8,128)(2,1)}, bf16[1024,512]{1,0:T(8,128)(2,1)S(1)}, u32[]{:S(2)}, u32[]{:S(2)}) collective-permute-start(bf16[1024,512]{1,0:T(8,128)(2,1)} %dynamic-slice_bitcast_fusion.1), channel_id=1, source_target_pairs={{0,2},{1,3},{2,0},{3,1},{4,6},{5,7},{6,4},{7,5},{8,10},{9,11},{10,... | collective-permute-start | bytes 3145736 | tf_op jit(solution)/shard_map/ppermute | solution.py:495
  352.9 31.9 %collective-permute-start.29 = (bf16[512,512]{1,0:T(8,128)(2,1)}, bf16[512,512]{1,0:T(8,128)(2,1)S(1)}, u32[]{:S(2)}, u32[]{:S(2)}) collective-permute-start(bf16[512,512]{1,0:T(8,128)(2,1)} %get-tuple-element.283), channel_id=1, source_target_pairs={{0,8},{4,12},{8,0},{12,4},{16,24},{20,28},{24,16},{28,20},{1,9},{5... | collective-permute-start | bytes 1572872 | tf_op jit(solution)/shard_map/ppermute | solution.py:495
  356.5 28.3 %collective-permute-start.30 = (bf16[512,512]{1,0:T(8,128)(2,1)}, bf16[512,512]{1,0:T(8,128)(2,1)S(1)}, u32[]{:S(2)}, u32[]{:S(2)}) collective-permute-start(bf16[512,512]{1,0:T(8,128)(2,1)} %get-tuple-element.284), channel_id=1, source_target_pairs={{0,4},{4,0},{8,12},{12,8},{16,20},{20,16},{24,28},{28,24},{1,5},{5... | collective-permute-start | bytes 1572872 | tf_op jit(solution)/shard_map/ppermute | solution.py:495
  358.0 28.4 %collective-permute-start.32 = (bf16[256,1024]{1,0:T(8,128)(2,1)}, bf16[256,1024]{1,0:T(8,128)(2,1)}, u32[]{:S(2)}, u32[]{:S(2)}) collective-permute-start(bf16[256,1024]{1,0:T(8,128)(2,1)} %get-tuple-element.286), channel_id=1, source_target_pairs={{0,16},{4,20},{8,24},{12,28},{16,0},{20,4},{24,8},{28,12},{1,17},{... | collective-permute-start | bytes 1572872 | tf_op jit(solution)/shard_map/ppermute | solution.py:495
  373.1 11.8 %collective-permute-start.31 = (bf16[416,512]{1,0:T(8,128)(2,1)}, bf16[416,512]{1,0:T(8,128)(2,1)S(1)}, u32[]{:S(2)}, u32[]{:S(2)}) collective-permute-start(bf16[416,512]{1,0:T(8,128)(2,1)} %pad_maximum_fusion.9), channel_id=1, source_target_pairs={{0,4},{4,0},{8,12},{12,8},{16,20},{20,16},{24,28},{28,24},{1,5},{5... | collective-permute-start | bytes 1277960 | tf_op jit(solution)/shard_map/ppermute | solution.py:495
  389.4 24.6 %collective-permute-start.33 = (bf16[1024,512]{1,0:T(8,128)(2,1)}, bf16[1024,512]{1,0:T(8,128)(2,1)}, u32[]{:S(2)}, u32[]{:S(2)}) collective-permute-start(bf16[1024,512]{1,0:T(8,128)(2,1)} %dynamic-slice_bitcast_fusion), channel_id=1, source_target_pairs={{0,2},{1,3},{2,0},{3,1},{4,6},{5,7},{6,4},{7,5},{8,10},{9,11},{10,... | collective-permute-start | bytes 3145736 | tf_op jit(solution)/shard_map/ppermute | solution.py:495
  397.3 21.6 %collective-permute-start.35 = (bf16[256,512]{1,0:T(8,128)(2,1)}, bf16[256,512]{1,0:T(8,128)(2,1)S(1)}, u32[]{:S(2)}, u32[]{:S(2)}) collective-permute-start(bf16[256,512]{1,0:T(8,128)(2,1)} %get-tuple-element.301), channel_id=1, source_target_pairs={{0,16},{4,20},{8,24},{12,28},{16,0},{20,4},{24,8},{28,12},{1,17},{... | collective-permute-start | bytes 786440 | tf_op jit(solution)/shard_map/ppermute | solution.py:495
  400.1 22.2 %collective-permute-start.36 = (bf16[256,512]{1,0:T(8,128)(2,1)}, bf16[256,512]{1,0:T(8,128)(2,1)S(1)}, u32[]{:S(2)}, u32[]{:S(2)}) collective-permute-start(bf16[256,512]{1,0:T(8,128)(2,1)} %get-tuple-element.302), channel_id=1, source_target_pairs={{0,16},{4,20},{8,24},{12,28},{16,0},{20,4},{24,8},{28,12},{1,17},{... | collective-permute-start | bytes 786440 | tf_op jit(solution)/shard_map/ppermute | solution.py:495
  400.2 22.1 %collective-permute-start.37 = (bf16[256,512]{1,0:T(8,128)(2,1)}, bf16[256,512]{1,0:T(8,128)(2,1)S(1)}, u32[]{:S(2)}, u32[]{:S(2)}) collective-permute-start(bf16[256,512]{1,0:T(8,128)(2,1)} %get-tuple-element.303), channel_id=1, source_target_pairs={{0,8},{4,12},{8,0},{12,4},{16,24},{20,28},{24,16},{28,20},{1,9},{5... | collective-permute-start | bytes 786440 | tf_op jit(solution)/shard_map/ppermute | solution.py:495
  403.8 10.1 %collective-permute-start.34 = (f32[1024]{0:T(1024)S(1)}, f32[1024]{0:T(1024)S(1)}, u32[]{:S(2)}, u32[]{:S(2)}) collective-permute-start(f32[1024]{0:T(1024)S(1)} %add.308), channel_id=1, source_target_pairs={{0,2},{1,3},{2,0},{3,1},{4,6},{5,7},{6,4},{7,5},{8,10},{9,11},{10,... | collective-permute-start | bytes 12296 | tf_op jit(solution)/shard_map/ppermute | solution.py:495
  424.9 21.1 %collective-permute-start.41 = (bf16[176,512]{1,0:T(8,128)(2,1)}, bf16[176,512]{1,0:T(8,128)(2,1)S(1)}, u32[]{:S(2)}, u32[]{:S(2)}) collective-permute-start(bf16[176,512]{1,0:T(8,128)(2,1)} %get-tuple-element.316), channel_id=1, source_target_pairs={{0,16},{4,20},{8,24},{12,28},{16,0},{20,4},{24,8},{28,12},{1,17},{... | collective-permute-start | bytes 540680 | tf_op jit(solution)/shard_map/ppermute | solution.py:495
  (80 other events, 791.9 us)

commit v4 on v3

--- a/solution.py
+++ b/solution.py
@@ -11,7 +11,7 @@
 F32, BF16 = jnp.float32, jnp.bfloat16
 
 
-def spread(rows_ref, select_ref, spread_ref, chunk, count, seqs):
+def spread(rows_ref, select_ref, spread_ref, narrow_ref, chunk, count, seqs):
     left, parts = rows_ref[...], []
     for _ in range(3):
         parts.append(left.astype(BF16))
@@ -22,11 +22,13 @@
             stacked, select_ref[:, col * LANES : (col + 2) * LANES], (((0,), (0,)), ((), ())), preferred_element_type=F32
         )
         for tok in range(chunk):
+            both = [wide[tok * seqs : (tok + 1) * seqs, i * LANES : (i + 1) * LANES] for i in range(2)]
             for i in range(2):
-                spread_ref[tok, col + i] = wide[tok * seqs : (tok + 1) * seqs, i * LANES : (i + 1) * LANES]
-
-
-def ends_kernel(chunk, step_ref, mixed_ref, rows_ref, rate_ref, h_ref, spread_ref, select_ref):
+                spread_ref[tok, col + i] = both[i]
+            narrow_ref[tok, pl.ds(col * seqs, 2 * seqs), :] = jnp.concatenate(both, axis=0).astype(BF16)
+
+
+def ends_kernel(chunk, step_ref, mixed_ref, rows_ref, rate_ref, h_ref, spread_ref, narrow_ref, select_ref):
     states, seqs, width = rate_ref.shape
 
     @pl.when(pl.program_id(0) == 0)
@@ -36,7 +38,7 @@
         col = lax.broadcasted_iota(jnp.int32, select_ref.shape, 1)
         select_ref[...] = (row % (2 * states) == col // LANES).astype(BF16)
 
-    spread(rows_ref, select_ref, spread_ref, chunk, 2 * states, seqs)
+    spread(rows_ref, select_ref, spread_ref, narrow_ref, chunk, 2 * states, seqs)
 
     def tile_step(j, _):
         lanes = pl.ds(pl.multiple_of(j * LANES, LANES), LANES)
@@ -69,7 +71,7 @@
             rows = pl.ds(tok * seqs, seqs)
             s, y = step_ref[rows, lanes], yg_ref[rows, lanes]
             for n in range(states):
-                q[n] = jnp.exp2(s * rate_ref[n, :, lanes]) * (q[n] + spread_ref[tok, states + n] * y)
+                q[n] = jnp.exp2(s * rate_ref[n, :, lanes]) * (q[n] + spread_ref[tok, n] * y)
         for n in range(states):
             q_ref[n, :, lanes] = q[n]
         return 0
@@ -77,8 +79,20 @@
     lax.fori_loop(0, width // LANES, tile_step, 0, unroll=2)
 
 
-def spread_spec(chunk, states, seqs, at):
-    return pl.BlockSpec((chunk, 2 * states, seqs, LANES), lambda i: (at(i), 0, 0, 0))
+def spread_spec(chunk, count, seqs, part, at):
+    return pl.BlockSpec((chunk, count, seqs, LANES), lambda i: (at(i), part, 0, 0))
+
+
+def narrow_spec(chunk, count, seqs, part, at):
+    return pl.BlockSpec((chunk, count * seqs, LANES), lambda i: (at(i), part, 0))
+
+
+def halves_sum(parts):
+    while len(parts) > 1:
+        parts = [a + b for a, b in zip(parts[::2], parts[1::2])]
+    total = parts[0].astype(F32)
+    seqs = total.shape[0] // 2
+    return total[:seqs] + total[seqs:]
 
 
 def local_ends(step, mixed, rows_t, rate, chunk):
@@ -92,8 +106,9 @@
         functools.partial(ends_kernel, chunk),
         grid=(grid,),
         in_specs=[row_spec, row_spec, pl.BlockSpec((2 * states, chunk * seqs), lambda i: (0, i)), whole],
-        out_specs=[whole, spread_spec(chunk, states, seqs, lambda i: i)],
-        out_shape=[jax.ShapeDtypeStruct(rate.shape, F32), jax.ShapeDtypeStruct((rows // seqs, 2 * states, seqs, LANES), F32)],
+        out_specs=[whole, spread_spec(chunk, 2 * states, seqs, 0, lambda i: i), narrow_spec(chunk, 2 * states, seqs, 0, lambda i: i)],
+        out_shape=[jax.ShapeDtypeStruct(rate.shape, F32), jax.ShapeDtypeStruct((rows // seqs, 2 * states, seqs, LANES), F32),
+                   jax.ShapeDtypeStruct((rows // seqs, 2 * states * seqs, LANES), BF16)],
         scratch_shapes=[pltpu.VMEM((6 * states, 2 * states * LANES), BF16)],
         compiler_params=pltpu.CompilerParams(vmem_limit_bytes=VM),
         cost_estimate=pl.CostEstimate(flops=elements, bytes_accessed=elements, transcendentals=0),
@@ -112,7 +127,7 @@
     return pl.pallas_call(
         functools.partial(starts_kernel, chunk),
         grid=(grid,),
-        in_specs=[row_spec, row_spec, spread_spec(chunk, states, seqs, at), whole],
+        in_specs=[row_spec, row_spec, spread_spec(chunk, states, seqs, 1, at), whole],
         out_specs=whole,
         out_shape=jax.ShapeDtypeStruct(rate.shape, F32),
         compiler_params=pltpu.CompilerParams(vmem_limit_bytes=VM),
@@ -121,7 +136,7 @@
     )(step, yg, wide_rows, rate)
 
 
-def fwd_kernel(chunk, step_ref, mixed_ref, gate_ref, gg_ref, spread_ref, rate_ref, skip_ref,
+def fwd_kernel(chunk, step_ref, mixed_ref, gate_ref, gg_ref, spread_ref, narrow_ref, rate_ref, skip_ref,
                hin_ref, *refs):
     state_ref, hist_ref, start_ref, gated_ref, ggrad_ref = refs[-5:]
     states, seqs, width = rate_ref.shape
@@ -145,12 +160,14 @@
                 s = step_ref[rows, lanes]
                 m = pair[k * seqs : (k + 1) * seqs]
                 x = s * m
-                y = skip * m
-                for n in range(states):
-                    h[n] = jnp.exp2(s * rate_ref[n, :, lanes]) * h[n] + spread_ref[tok + k, n] * x
-                    y = y + spread_ref[tok + k, states + n] * h[n]
+                terms = []
                 for n in range(0, states, 2):
-                    hist_ref[tok + k, j, pl.ds(n * seqs, 2 * seqs), :] = jnp.concatenate([h[n], h[n + 1]], axis=0).astype(BF16)
+                    for i in (n, n + 1):
+                        h[i] = jnp.exp2(s * rate_ref[i, :, lanes]) * h[i] + spread_ref[tok + k, i] * x
+                    both = jnp.concatenate([h[n], h[n + 1]], axis=0).astype(BF16)
+                    hist_ref[tok + k, j, pl.ds(n * seqs, 2 * seqs), :] = both
+                    terms.append(both * narrow_ref[tok + k, pl.ds(n * seqs, 2 * seqs), :])
+                y = skip * m + halves_sum(terms)
                 v = gate_ref[rows, lanes]
                 sig = 1.0 / (1.0 + jnp.exp2(v * (-LOG2E)))
                 gated.append(y * (v * sig))
@@ -165,7 +182,7 @@
 
 
 def forward(arrays, skip, carried, filled, shapes, chunk, first, last):
-    step, mixed, gate, gg, wide_rows, rate = arrays
+    step, mixed, gate, gg, wide_rows, narrow_rows, rate = arrays
     rows, width = step.shape
     states, seqs, _ = rate.shape
     at = lambda i: first + i
@@ -176,19 +193,19 @@
     return pl.pallas_call(
         functools.partial(fwd_kernel, chunk),
         grid=(last - first,),
-        in_specs=[row_spec, row_spec, row_spec, row_spec, spread_spec(chunk, states, seqs, at), whole,
+        in_specs=[row_spec, row_spec, row_spec, row_spec, spread_spec(chunk, states, seqs, 0, at), narrow_spec(chunk, states, seqs, 1, at), whole,
                   pl.BlockSpec((seqs, width), lambda i: (0, 0)), whole] + [anywhere] * len(filled),
         out_specs=[whole, pl.BlockSpec((chunk, width // LANES, states * seqs, LANES), lambda i: (at(i), 0, 0, 0)),
                    pl.BlockSpec((1, states, seqs, width), lambda i: (at(i), 0, 0, 0)), row_spec, row_spec],
         out_shape=[jax.ShapeDtypeStruct(*shape) for shape in shapes],
-        input_output_aliases={7 + i: i for i in range(len(filled) + 1)},
+        input_output_aliases={8 + i: i for i in range(len(filled) + 1)},
         compiler_params=pltpu.CompilerParams(vmem_limit_bytes=VM),
         cost_estimate=pl.CostEstimate(flops=elements, bytes_accessed=elements, transcendentals=0),
         name="scan_forward",
-    )(step, mixed, gate, gg, wide_rows, rate, skip, carried, *filled)
-
-
-def bwd_kernel(chunk, step_ref, mixed_ref, yg_ref, spread_ref, rate_ref, skip_ref, low_ref, hist_ref, start_ref, gin_ref,
+    )(step, mixed, gate, gg, wide_rows, narrow_rows, rate, skip, carried, *filled)
+
+
+def bwd_kernel(chunk, step_ref, mixed_ref, yg_ref, spread_ref, narrow_ref, rate_ref, skip_ref, low_ref, hist_ref, start_ref, gin_ref,
                sums_ref, pre_ref, part_ref, proj_ref, decay_ref, bias_ref, skipg_ref, state_ref, b_ref, c_ref):
     states, seqs, width = rate_ref.shape
     span = states * seqs
@@ -214,38 +231,42 @@
         for tok in range(chunk - 2, -1, -2):
             pair_rows = pl.ds(tok * seqs, 2 * seqs)
             pair = mixed_ref[pair_rows, lanes].astype(F32)
-            pre, xs, packed = [None, None], [None, None], [None, None]
+            pre, xs, packed, weights = [None, None], [None, None], [None, None], [None, None]
             for k in (1, 0):
                 now = tok + k
                 rows = pl.ds(now * seqs, seqs)
                 s = step_ref[rows, lanes]
                 y = yg_ref[rows, lanes]
                 m = pair[k * seqs : (k + 1) * seqs]
-                along = jnp.zeros_like(s)
-                size = jnp.zeros_like(s)
-                gs = []
+                gs, along_terms, size_terms = [], [], []
                 for n in range(0, states, 2):
                     if now > 0:
-                        both = hist_ref[now - 1, j, pl.ds(n * seqs, 2 * seqs), :].astype(F32)
-                        before = [both[:seqs], both[seqs:]]
+                        before = hist_ref[now - 1, j, pl.ds(n * seqs, 2 * seqs), :]
                     else:
-                        before = [start_ref[0, n + i, :, lanes].astype(F32) for i in range(2)]
-                    for i in range(2):
-                        z = s * rate_ref[n + i, :, lanes]
-                        g = spread_ref[now, states + n + i] * y + q[n + i]
-                        along = along + g * spread_ref[now, n + i]
-                        q[n + i] = jnp.exp2(z) * g
-                        r = q[n + i] * before[i] * z
-                        acc[n + i] = acc[n + i] + r
-                        size = size + r
-                        gs.append(g)
-                packed[k] = jnp.concatenate(gs, axis=0).astype(BF16)
+                        before = jnp.concatenate([start_ref[0, n + i, :, lanes] for i in range(2)], axis=0)
+                    both, moves = [], []
+                    for i in (n, n + 1):
+                        z = s * rate_ref[i, :, lanes]
+                        g = spread_ref[now, i] * y + q[i]
+                        q[i] = jnp.exp2(z) * g
+                        both.append(g)
+                        moves.append(q[i] * z)
+                    gs.append(jnp.concatenate(both, axis=0).astype(BF16))
+                    along_terms.append(gs[-1] * narrow_ref[now, pl.ds(n * seqs, 2 * seqs), :])
+                    size_terms.append(jnp.concatenate(moves, axis=0).astype(BF16) * before)
+                packed[k] = jnp.concatenate(gs, axis=0)
+                weights[k] = size_terms
+                along, size = halves_sum(along_terms), halves_sum(size_terms)
                 part_ref[rows, lanes] = s * along + skip * y
                 skipg = skipg + y * m
                 xs[k] = s * m
                 series = 1.0 - s * (1.0 / 2) * (1.0 - s * (1.0 / 3) * (1.0 - s * (1.0 / 4) * (1.0 - s * (1.0 / 5))))
                 ratio = jnp.where(s < 0.1, series, (1.0 - jnp.exp2(s * (-LOG2E))) / jnp.maximum(s, 0.1))
                 pre[k] = ratio * (size * (1.0 / LOG2E) + xs[k] * along)
+            for n in range(0, states, 2):
+                total = (weights[0][n // 2] + weights[1][n // 2]).astype(F32)
+                acc[n] = acc[n] + total[:seqs]
+                acc[n + 1] = acc[n + 1] + total[seqs:]
             rounded = jnp.concatenate(pre, axis=0).astype(BF16)
             pre_ref[pair_rows, lanes] = rounded
             wide = rounded.astype(F32)
@@ -287,7 +308,7 @@
         sums_ref[states + 1 : states + 2] = jnp.sum(skipg_ref[...], axis=0, keepdims=True)
 
 
-def backward(step, mixed, yg, wide_rows, rate, skip, low_weight, hist, start, gin, chunk):
+def backward(step, mixed, yg, wide_rows, narrow_rows, rate, skip, low_weight, hist, start, gin, chunk):
     rows, width = step.shape
     states, seqs, _ = rate.shape
     grid = rows // (chunk * seqs)
@@ -300,7 +321,8 @@
     return pl.pallas_call(
         functools.partial(bwd_kernel, chunk),
         grid=(grid,),
-        in_specs=[row_spec, row_spec, row_spec, spread_spec(chunk, states, seqs, at), whole, one,
+        in_specs=[row_spec, row_spec, row_spec, spread_spec(chunk, states, seqs, 1, at),
+                  narrow_spec(chunk, states, seqs, 0, at), whole, one,
                   pl.BlockSpec((rank, width), lambda i: (0, 0)),
                   pl.BlockSpec((chunk, width // LANES, states * seqs, LANES), lambda i: (at(i), 0, 0, 0)),
                   pl.BlockSpec((1, states, seqs, width), lambda i: (at(i), 0, 0, 0)), whole],
@@ -313,7 +335,7 @@
         compiler_params=pltpu.CompilerParams(vmem_limit_bytes=VM),
         cost_estimate=pl.CostEstimate(flops=elements, bytes_accessed=elements, transcendentals=0),
         name="scan_backward",
-    )(step, mixed, yg, wide_rows, rate, skip, low_weight, hist, start, gin)
+    )(step, mixed, yg, wide_rows, narrow_rows, rate, skip, low_weight, hist, start, gin)
 
 
 def conv_kernel(chunk, taps, proj_ref, weight_ref, part_ref, conv_ref, in_ref, before_ref, taps_ref,
@@ -527,6 +549,17 @@
         sent = value.astype(BF16) if bit >= narrow_from else value
         value = value + swapped(sent, axis, bit).astype(F32)
     return value
+
+
+def summed_near(value, axis, narrow_from):
+    if bits_of(axis) > 1 and narrow_from > 1:
+        count = lax.axis_size(axis)
+        near = [lax.ppermute(value, axis, [(i, i ^ mask) for i in range(count)]) for mask in (1, 2, 3)]
+        value = (value + near[0]) + (near[1] + near[2])
+        for bit in range(2, bits_of(axis)):
+            value = value + swapped(value, axis, bit)
+        return value
+    return summed(value, axis, narrow_from)
 
 
 def pick(value, dim, index):
@@ -789,7 +822,7 @@
     decay_rate = -jnp.exp(decay_log)
     rate = jnp.broadcast_to((decay_rate * LOG2E)[:, None], (states, seqs, inner))
     skip = jnp.broadcast_to(skip_gain, (seqs, inner))
-    local_end, wide_rows = local_ends(step, mixed, projected[rank:], rate, chunk)
+    local_end, wide_rows, narrow_rows = local_ends(step, mixed, projected[rank:], rate, chunk)
     step_total = jnp.sum(step.reshape(toks, seqs, inner), axis=0)
     grad_whole, _ = gathered(after(own_out_grad, gate_pre), "chan", local_end)
 
@@ -814,7 +847,7 @@
         ((rows, inner), BF16),
         ((rows, inner), BF16),
     ]
-    arrays = (step, mixed, gate_pre, gated_grad, wide_rows, rate)
+    arrays = (step, mixed, gate_pre, gated_grad, wide_rows, narrow_rows, rate)
     middle = chunks // 2
 
     def first_side(sent, _):
@@ -848,7 +881,7 @@
         return tuple(side.reshape(chips + side.shape[1:]) for side in sides)
 
     scan_sums, pre_grad, mixed_part, proj_sum = backward(
-        step, mixed, y_grad, wide_rows, rate, skip, step_weight, history, starts, enter_g, chunk
+        step, mixed, y_grad, wide_rows, narrow_rows, rate, skip, step_weight, history, starts, enter_g, chunk
     )
     pre_grad, proj_sum = end_chains(apart, pre_grad, proj_sum)
     for bit in range(chan_bits):
@@ -908,16 +941,15 @@
     in_window = [*groups, [third], [gate_chain]]
     (row_dots,) = send_chains(in_window, [*messages, third.sent, weight_message[1]], row_dots)
     row_dots = row_dots + swapped(row_dots, "chan", 0)
-    (row_dots,) = end_all([normed_sum, branch_sum], row_dots)
+    (row_dots,) = end_all([normed_sum], row_dots)
+    (row_dots,) = start_all([normed_sum], row_dots)
+    (row_dots,) = end_all([branch_sum], row_dots)
     (row_dots,) = end_chains(in_window, row_dots)
     groups = [[first], [second], [third]]
-    messages = merge(groups)
-    (row_dots,) = start_all([normed_sum], row_dots)
-    (row_dots,) = send_chains(groups, messages, row_dots)
+    (row_dots,) = send_chains(groups, merge(groups), row_dots)
     for bit in range(1, chan_bits):
         row_dots = row_dots + swapped(row_dots, "chan", bit)
     (row_dots,) = end_all([normed_sum], row_dots)
-    (row_dots,) = end_chains(groups, row_dots)
     normed_grad = finished_on_the_way(normed_sum)
     row_dots = row_dots[:, None]
     wide_own = own_in.astype(F32)
@@ -928,7 +960,11 @@
         - wide_own * (inv_rms * inv_rms / model) * row_dots
     ).astype(BF16)
     in_grad = in_rows.reshape(toks, seqs, share).swapaxes(0, 1)
-    gain_grad = summed(jnp.sum(normed_grad * wide_own * inv_rms, axis=0), "seq", bits_of("seq"))
+    gain_grad = jnp.sum(normed_grad * wide_own * inv_rms, axis=0)
+    in_grad, gain_grad = end_chains(groups, in_grad, gain_grad)
+    if third.order:
+        (gain_grad,) = send_chains([[third]], merge([[third]]), gain_grad)
+    gain_grad = summed_near(gain_grad, "seq", bits_of("seq"))
     (first_last,), (second_last,), (small, sums) = last_of(first), last_of(second), last_of(third)
     (out_weight_grad,), (gate_weight_grad,) = last_of(out_chain), last_of(gate_chain)
     last = jnp.concatenate([first_last, second_last], axis=1)

time: 456 us -> 434 us (0.952)
  waiting for transfers between devices: 60.5 us -> 51.1 us
  Pallas kernels: 172 us -> 163 us
    ppermute x34 -> x32, waiting for transfers between devices: 59 us -> 49.6 us  [swapped(): return lax.ppermute(value, axis, [(i, i ^ 1 << bit) for i in range(count)])]
    ppermute x34 -> x32, starting transfers between devices: 45.1 us -> 38.3 us  [swapped(): return lax.ppermute(value, axis, [(i, i ^ 1 << bit) for i in range(count)])]
    pallas_call x1, Pallas kernels: 45.9 us -> 40.9 us  [backward(): pl.pallas_call(functools.partial(bwd_kernel, chunk), grid=(grid,), in_spe...]
  transfers between devices with their start and end apart: 42 -> 43, of which waited for: 16 -> 16; matrix products, arithmetic and copies ran while one was open for 24% -> 26% of each run, Pallas kernels for 38% -> 38%
where the time goes in v4:
time: 434 us; the launch traced here: 428 us
  Pallas kernels  163 us (38%)
  starting transfers between devices  61.8 us (14%)
  other arithmetic  55 us (13%)
  waiting for transfers between devices  51.1 us (12%)
  matrix products  49.5 us (11%)
  local copies, waits for them, and re-layouts  45.4 us (10%)
    ppermute x32, waiting for transfers between devices, swapped(): return lax.ppermute(value, axis, [(i, i ^ 1 << bit) for i in range(count)])  49.6 us
    dot_general x14, matrix products, dot(): return lax.dot_general(a, b, dims, preferred_element_type=out)  49.5 us
    pallas_call x1, Pallas kernels, backward(): pl.pallas_call(functools.partial(bwd_kernel, chunk), grid=(grid,), in_spe...  40.9 us
    ppermute x32, starting transfers between devices, swapped(): return lax.ppermute(value, axis, [(i, i ^ 1 << bit) for i in range(count)])  38.3 us
    pallas_call x2, Pallas kernels, forward(): pl.pallas_call(functools.partial(fwd_kernel, chunk), grid=(last - first,)...  32.7 us
    pallas_call x2, Pallas kernels, product_sides(): pl.pallas_call(functools.partial(product_kernel, len(pairs)), grid_spec=p...  24.1 us
    ppermute x8, starting transfers between devices, moved(): lax.ppermute(value, axis, [(i, i + distance) for i in range(count) if 0 <...  20 us
    pallas_call x1, Pallas kernels, local_ends(): pl.pallas_call(functools.partial(ends_kernel, chunk), grid=(grid,), in_sp...  19.8 us
  transfers between devices with their start and end apart: 43, of which 16 were waited for; matrix products, arithmetic and copies ran while one was open for 26% of the time, Pallas kernels for 38%

profile of v4, /device:TPU:0, one launch (start us, length us, event | category | flops | bytes accessed | tf_op | source)
XLA Modules:
  0.0 428.3 jit_solution(17649329453182518330)
XLA Ops:
  6.4 16.3 %fusion.49 = (bf16[2048,1,1024]{2,1,0:T(2,128)(2,1)S(1)}, bf16[2048,1,1024]{2,1,0:T(2,128)(2,1)S(1)}) fusion(bf16[2048,2,1024]{2,1,0:T(2,128)(2,1)} %param.14), kind=kLoop, calls=%fused_computation.189 | loop fusion | bytes 16777216 | tf_op jit(solution)/shard_map/slice | solution.py:794
  22.8 5.9 %copy_bitcast_fusion = (bf16[2048,1024]{1,0:T(8,128)(2,1)}, bf16[2048,1024]{1,0:T(8,128)(2,1)}) fusion(bf16[2048,1,1024]{2,1,0:T(2,128)(2,1)S(1)} %get-tuple-element.368, bf16[2048,1,1024]{2,1,0:T(2,128)(2,1)S(1)} %get-tuple-element.369), kind=kLoop, calls=%fused_computation.17 | loop fusion | bytes 16777216 | tf_op jit(solution)/shard_map/squeeze | solution.py:794
  37.6 3.8 collective-permute-start.3
  41.4 4.7 %fusion.55.in_ref = bf16[1024,1024]{1,0:T(8,128)(2,1)S(1)} fusion(bf16[1024,2048]{1,0:T(8,128)(2,1)S(1)} %fusion.2, bf16[2048,1024]{1,0:T(8,128)(2,1)S(1)} %copy-done.6), kind=kOutput, calls=%fused_computation.195 | convolution fusion | flops 4294967296 | bytes 10485760 | tf_op jit(solution)/shard_map/dot_general | solution.py:508
  47.5 3.8 multiply_convert_fusion
  54.5 4.5 %fusion.56.gate_ref = f32[1024,1024]{1,0:T(8,128)S(1)} fusion(bf16[1024,2048]{1,0:T(8,128)(2,1)S(1)} %fusion.2, bf16[2048,1024]{1,0:T(8,128)(2,1)S(1)} %copy-done.13), kind=kOutput, calls=%fused_computation.196 | convolution fusion | flops 4294967296 | bytes 12582912 | tf_op jit(solution)/shard_map/dot_general | solution.py:508
  63.3 5.5 %collective-permute-done.5 = bf16[160,1024]{1,0:T(8,128)(2,1)S(1)} collective-permute-done((bf16[160,1024]{1,0:T(8,128)(2,1)S(1)}, bf16[160,1024]{1,0:T(8,128)(2,1)S(1)}, u32[]{:S(2)}, u32[]{:S(2)}) %collective-permute-start.5) | collective-permute-done | bytes 327712 | tf_op jit(solution)/shard_map/ppermute | solution.py:517
  71.3 4.7 %bitcast_reduce_fusion = (f32[8,1024]{1,0:T(8,128)S(1)}, f32[1024,1024]{1,0:T(8,128)}) fusion(f32[1024]{0:T(1024)S(1)} %convert_element_type.288, bf16[128,1024]{1,0:T(8,128)(2,1)S(1)} %copy-done.40, f32[160,1024]{1,0:T(8,128)S(1)} %convert_add_fusion.4), kind=kOutput, calls=%fused_computation.19 | convolution fusion | flops 276815872 | bytes 4755456 | tf_op jit(solution)/shard_map/dot_general | solution.py:508
  76.9 19.8 %local_ends.1 = (f32[16,8,1024]{2,1,0:T(8,128)}, f32[128,32,8,128]{3,2,1,0:T(8,128)}, bf16[128,256,128]{2,1,0:T(8,128)(2,1)}) custom-call(f32[1024,1024]{1,0:T(8,128)} %get-tuple-element.431.step_ref, bf16[1024,1024]{1,0:T(8,128)(2,1)} %copy-done, f32[32,1024]{1,0:T(8,128)} %slice.282.rows_ref, f32[16,8,1024]{2,1,0:T(8,128)} %broadcast_in_dim.8.rate_ref), custom_call_target="tpu_custom_call" | custom-call | flops 16777216 | bytes 16777216 | tf_op jit(solution)/shard_map/local_ends/pallas_call | solution.py:105
  104.4 7.2 %multiply_multiply_fusion = (f32[1024,1024]{1,0:T(8,128)}, f32[1024,1024]{1,0:T(8,128)}) fusion(f32[1024,1024]{1,0:T(8,128)S(1)} %fusion.56.gate_ref, bf16[1024,2048]{1,0:T(8,128)(2,1)S(1)} %pad_maximum_fusion.2, bf16[2048,1024]{1,0:T(8,128)(2,1)S(1)} %copy-done.23), kind=kOutput, calls=%fused_computation.23 | convolution fusion | flops 4300210176 | bytes 20971520 | tf_op jit(solution)/shard_map/dot_general | solution.py:508
  115.3 14.7 %local_starts.1 = f32[16,8,1024]{2,1,0:T(8,128)} custom-call(f32[1024,1024]{1,0:T(8,128)} %get-tuple-element.431.step_ref, f32[1024,1024]{1,0:T(8,128)} %get-tuple-element.184.yg_ref, f32[128,32,8,128]{3,2,1,0:T(8,128)} %get-tuple-element.185.spread_ref, f32[16,8,1024]{2,1,0:T(8,128)} %broadcast_in_dim.8.rate_ref), custom_call_target="tpu_custom_call" | custom-call | flops 16777216 | bytes 16777216 | tf_op jit(solution)/shard_map/local_starts/pallas_call | solution.py:127
  130.3 3.8 collective-permute-start.11
  147.7 16.3 %scan_forward.2 = (f32[16,8,1024]{2,1,0:T(8,128)}, bf16[128,8,128,128]{3,2,1,0:T(8,128)(2,1)}, bf16[8,16,8,1024]{3,2,1,0:T(8,128)(2,1)}, bf16[1024,1024]{1,0:T(8,128)(2,1)}, bf16[1024,1024]{1,0:T(8,128)(2,1)}) custom-call(f32[1024,1024]{1,0:T(8,128)} %get-tuple-element.431.step_ref, bf16[1024,1024]{1,0:T(8,128)(2,1)} %copy-done, ...), custom_call_target="tpu_custom_call", output_to_operand_aliasing={{0}: (8, {})} | custom-call | flops 8388608 | bytes 8388608 | tf_op jit(solution)/shard_map/scan_forward/pallas_call | solution.py:193
  165.6 16.5 %scan_forward.3 = (f32[16,8,1024]{2,1,0:T(8,128)}, bf16[128,8,128,128]{3,2,1,0:T(8,128)(2,1)}, bf16[8,16,8,1024]{3,2,1,0:T(8,128)(2,1)}, bf16[1024,1024]{1,0:T(8,128)(2,1)}, bf16[1024,1024]{1,0:T(8,128)(2,1)}) custom-call(f32[1024,1024]{1,0:T(8,128)} %get-tuple-element.431.step_ref, ...), custom_call_target="tpu_custom_call", output_to_operand_aliasing={{0}: (8, {}), {1}: (9, {}), {2}: (10, {}), {3}: (11, {}), {... | custom-call | flops 8388608 | bytes 8388608 | tf_op jit(solution)/shard_map/scan_forward/pallas_call | solution.py:193
  182.1 5.5 %fusion.58 = bf16[1024,1024]{1,0:T(8,128)(2,1)} fusion(bf16[1024,1024]{1,0:T(8,128)(2,1)S(1)} %pad_maximum_fusion.6, bf16[1024,1024]{1,0:T(8,128)(2,1)} %get-tuple-element.228.refs_1_), kind=kOutput, calls=%fused_computation.198 | convolution fusion | flops 2147483648 | bytes 6291456 | tf_op jit(solution)/shard_map/dot_general | solution.py:508
  195.9 3.8 fusion.60.refs_2_
  199.6 3.7 fusion.59.refs_0_
  203.4 40.9 %scan_backward.1 = (f32[18,1024]{1,0:T(8,128)}, bf16[1024,1024]{1,0:T(8,128)(2,1)}, f32[1024,1024]{1,0:T(8,128)}, f32[160,1024]{1,0:T(8,128)}) custom-call(f32[1024,1024]{1,0:T(8,128)} %get-tuple-element.431.step_ref, bf16[1024,1024]{1,0:T(8,128)(2,1)} %copy-done, f32[1024,1024]{1,0:T(8,128)} %get-tuple-element.184.yg_ref, ...), custom_call_target="tpu_custom_call" | custom-call | flops 16777216 | bytes 16777216 | tf_op jit(solution)/shard_map/scan_backward/pallas_call | solution.py:321
  245.0 6.4 %merge_messages.5 = (bf16[512,1024]{1,0:T(8,128)(2,1)}, bf16[512,1024]{1,0:T(8,128)(2,1)}, bf16[512,1024]{1,0:T(8,128)(2,1)}, bf16[512,1024]{1,0:T(8,128)(2,1)}) custom-call(s32[2]{0:T(128)} %get-tuple-element.436.bits_ref, bf16[1024,1024]{1,0:T(8,128)(2,1)} %fusion.59.refs_0_, bf16[1024,1024]{1,0:T(8,128)(2,1)} %collective-permute-done.15.refs_1_, ...), custom_call_target="tpu_custom_call" | custom-call | flops 1024 | bytes 1024 | tf_op jit(solution)/shard_map/merge_messages/pallas_call | solution.py:701
  253.5 9.6 %product_sides.2 = (bf16[2,1024,512]{2,1,0:T(8,128)(2,1)}, bf16[2,1024,512]{2,1,0:T(8,128)(2,1)}) custom-call(s32[1]{0:T(128)} %bitcast.21.core_ref, bf16[1024,1024]{1,0:T(8,128)(2,1)} %get-tuple-element.238.refs_0_, bf16[2048,1024]{1,0:T(8,128)(2,1)} %refs_1_.1), custom_call_target="tpu_custom_call" | custom-call | flops 1024 | bytes 1024 | tf_op jit(solution)/shard_map/product_sides/pallas_call | solution.py:486
  263.8 11.7 %conv_backward.1 = (bf16[1056,1024]{1,0:T(8,128)(2,1)}, f32[24,1024]{1,0:T(8,128)}, f32[5,8,1024]{2,1,0:T(8,128)}) custom-call(bf16[160,1024]{1,0:T(8,128)(2,1)} %add_convert_fusion.2.proj_ref, bf16[160,1024]{1,0:T(8,128)(2,1)} %weight_ref.1, f32[1024,1024]{1,0:T(8,128)} %get-tuple-element.246.part_ref, f32[1024,1024]{1,0:T(8,128)} %get-tuple-element.367.conv_ref, ...), custom_call_target="tpu_custom_call" | custom-call | flops 1048576 | bytes 1048576 | tf_op jit(solution)/shard_map/conv_backward/pallas_call | solution.py:415
  277.4 4.5 %fusion.16 = bf16[2048,512]{1,0:T(8,128)(2,1)S(1)} fusion(bf16[1056,2048]{1,0:T(8,128)(2,1)S(1)} %bitcast.134, bf16[1056,1024]{1,0:T(8,128)(2,1)} %get-tuple-element.258), kind=kOutput, calls=%fused_computation.48 | convolution fusion | flops 2214592512 | bytes 7503872 | tf_op jit(solution)/shard_map/dot_general | solution.py:508
  281.9 4.3 %fusion.18 = bf16[2048,512]{1,0:T(8,128)(2,1)} fusion(bf16[1056,2048]{1,0:T(8,128)(2,1)S(1)} %bitcast.134, bf16[1056,1024]{1,0:T(8,128)(2,1)S(1)} %copy-done.34), kind=kOutput, calls=%fused_computation.50 | convolution fusion | flops 2214592512 | bytes 7503872 | tf_op jit(solution)/shard_map/dot_general | solution.py:508
  287.8 4.1 merge_messages.6
  315.4 14.6 %product_sides.3 = (bf16[2,1024,512]{2,1,0:T(8,128)(2,1)}, bf16[2,1024,512]{2,1,0:T(8,128)(2,1)}) custom-call(s32[1]{0:T(128)} %bitcast.21.core_ref, bf16[1024,1024]{1,0:T(8,128)(2,1)} %pad_maximum_fusion.7.refs_0_, bf16[1024,1024]{1,0:T(8,128)(2,1)} %get-tuple-element.228.refs_1_, bf16[2048,1024]{1,0:T(8,128)(2,1)} %get-tuple-element.172.refs_2_, ...), custom_call_target="tpu_custom_call" | custom-call | flops 1024 | bytes 1024 | tf_op jit(solution)/shard_map/product_sides/pallas_call | solution.py:486
  330.0 3.9 collective-permute-done.25
  339.4 3.9 merge_messages.7
  354.8 9.3 %collective-permute-done.26 = bf16[1024,512]{1,0:T(8,128)(2,1)} collective-permute-done((bf16[1024,512]{1,0:T(8,128)(2,1)}, bf16[1024,512]{1,0:T(8,128)(2,1)}, u32[]{:S(2)}, u32[]{:S(2)}) %collective-permute-start.26) | collective-permute-done | bytes 1048608 | tf_op jit(solution)/shard_map/ppermute | solution.py:517
  369.0 6.5 %collective-permute-done.31.refs_5_ = bf16[416,512]{1,0:T(8,128)(2,1)} collective-permute-done((bf16[416,512]{1,0:T(8,128)(2,1)}, bf16[416,512]{1,0:T(8,128)(2,1)}, u32[]{:S(2)}, u32[]{:S(2)}) %collective-permute-start.31) | collective-permute-done | bytes 426016 | tf_op jit(solution)/shard_map/ppermute | solution.py:517
  388.9 4.5 %fusion.12 = (f32[512]{0:T(512)S(1)}, bf16[128,8,512]{2,1,0:T(8,128)(2,1)S(1)}, bf16[128,8,512]{2,1,0:T(8,128)(2,1)S(1)}) fusion(bf16[1024,512]{1,0:T(8,128)(2,1)} %collective-permute-done.36, f32[1024]{0:T(1024)S(1)} %copy-done.54, bf16[2,1024,512]{2,1,0:T(8,128)(2,1)S(1)} %copy-done.17, s32[]{:T(128)S(6)} %select_n.192, ...), kind=kLoop, calls=%fused_computation.34 | loop fusion | flops 10485248 | bytes 8404996 | tf_op jit(solution)/shard_map/reduce_sum | solution.py:963
  394.7 7.2 %collective-permute-done.33 = bf16[256,512]{1,0:T(8,128)(2,1)S(1)} collective-permute-done((bf16[256,512]{1,0:T(8,128)(2,1)}, bf16[256,512]{1,0:T(8,128)(2,1)S(1)}, u32[]{:S(2)}, u32[]{:S(2)}) %collective-permute-start.33) | collective-permute-done | bytes 262176 | tf_op jit(solution)/shard_map/ppermute | solution.py:517
  402.0 5.5 %collective-permute-done.34 = bf16[256,512]{1,0:T(8,128)(2,1)S(1)} collective-permute-done((bf16[256,512]{1,0:T(8,128)(2,1)}, bf16[256,512]{1,0:T(8,128)(2,1)S(1)}, u32[]{:S(2)}, u32[]{:S(2)}) %collective-permute-start.34) | collective-permute-done | bytes 262176 | tf_op jit(solution)/shard_map/ppermute | solution.py:517
  (324 shorter events, 148.6 us)
Async XLA Ops:
  3.4 26.3 %collective-permute-start = (bf16[1024,512]{1,0:T(8,128)(2,1)}, bf16[1024,512]{1,0:T(8,128)(2,1)S(1)}, u32[]{:S(2)}, u32[]{:S(2)}) collective-permute-start(bf16[1024,512]{1,0:T(8,128)(2,1)} %bitcast.129), channel_id=1, source_target_pairs={{0,2},{1,3},{2,0},{3,1},{4,6},{5,7},{6,4},{7,5},{8,10},{9,11},{10,... | collective-permute-start | bytes 3145736 | tf_op jit(solution)/shard_map/ppermute | solution.py:517
  6.4 23.5 %collective-permute-start.2 = (bf16[1024,512]{1,0:T(8,128)(2,1)}, bf16[1024,512]{1,0:T(8,128)(2,1)S(1)}, u32[]{:S(2)}, u32[]{:S(2)}) collective-permute-start(bf16[1024,512]{1,0:T(8,128)(2,1)} %bitcast.129), channel_id=1, source_target_pairs={{0,1},{1,0},{2,3},{3,2},{4,5},{5,4},{6,7},{7,6},{8,9},{9,8},{10,11... | collective-permute-start | bytes 3145736 | tf_op jit(solution)/shard_map/ppermute | solution.py:517
  37.6 8.6 %collective-permute-start.3 = (bf16[32,2048]{1,0:T(8,128)(2,1)S(1)}, bf16[32,2048]{1,0:T(8,128)(2,1)S(1)}, u32[]{:S(2)}, u32[]{:S(2)}) collective-permute-start(bf16[32,2048]{1,0:T(8,128)(2,1)S(1)} %slice.272), channel_id=1, source_target_pairs={{0,4},{4,8},{8,12},{12,16},{16,20},{20,24},{24,28},{1,5},{5,9},{9,... | collective-permute-start | bytes 393224 | tf_op jit(solution)/shard_map/ppermute | solution.py:522
  59.1 9.8 %collective-permute-start.5 = (bf16[160,1024]{1,0:T(8,128)(2,1)S(1)}, bf16[160,1024]{1,0:T(8,128)(2,1)S(1)}, u32[]{:S(2)}, u32[]{:S(2)}) collective-permute-start(bf16[160,1024]{1,0:T(8,128)(2,1)S(1)} %get-tuple-element.364), channel_id=1, source_target_pairs={{0,2},{1,3},{2,0},{3,1},{4,6},{5,7},{6,4},{7,5},{8,10},{9,11},{10,... | collective-permute-start | bytes 983048 | tf_op jit(solution)/shard_map/ppermute | solution.py:517
  68.9 27.7 %collective-permute-start.7 = (bf16[1024,512]{1,0:T(8,128)(2,1)S(1)}, bf16[1024,512]{1,0:T(8,128)(2,1)S(1)}, u32[]{:S(2)}, u32[]{:S(2)}) collective-permute-start(bf16[1024,512]{1,0:T(8,128)(2,1)S(1)} %bitcast.139), channel_id=1, source_target_pairs={{0,2},{1,3},{2,0},{3,1},{4,6},{5,7},{6,4},{7,5},{8,10},{9,11},{10,... | collective-permute-start | bytes 3145736 | tf_op jit(solution)/shard_map/ppermute | solution.py:517
  70.4 31.4 %collective-permute-start.9 = (bf16[1024,512]{1,0:T(8,128)(2,1)S(1)}, bf16[1024,512]{1,0:T(8,128)(2,1)S(1)}, u32[]{:S(2)}, u32[]{:S(2)}) collective-permute-start(bf16[1024,512]{1,0:T(8,128)(2,1)S(1)} %bitcast.140), channel_id=1, source_target_pairs={{0,1},{1,0},{2,3},{3,2},{4,5},{5,4},{6,7},{7,6},{8,9},{9,8},{10,11... | collective-permute-start | bytes 3145736 | tf_op jit(solution)/shard_map/ppermute | solution.py:517
  98.3 13.2 %collective-permute-start.6 = (bf16[18,8,1024]{2,1,0:T(8,128)(2,1)S(1)}, bf16[18,8,1024]{2,1,0:T(8,128)(2,1)S(1)}, u32[]{:S(2)}, u32[]{:S(2)}) collective-permute-start(bf16[18,8,1024]{2,1,0:T(8,128)(2,1)S(1)} %pad_maximum_fusion.11), channel_id=1, source_target_pairs={{0,4},{4,8},{8,12},{12,16},{16,20},{20,24},{24,28},{1,5},{5,9},{9,... | collective-permute-start | bytes 884744 | tf_op jit(solution)/shard_map/ppermute | solution.py:522
  111.8 18.2 %collective-permute-start.10 = (bf16[18,8,1024]{2,1,0:T(8,128)(2,1)S(1)}, bf16[18,8,1024]{2,1,0:T(8,128)(2,1)S(1)}, u32[]{:S(2)}, u32[]{:S(2)}) collective-permute-start(bf16[18,8,1024]{2,1,0:T(8,128)(2,1)S(1)} %pad_maximum_fusion.14), channel_id=1, source_target_pairs={{0,8},{4,12},{8,16},{12,20},{16,24},{20,28},{1,9},{5,13},{9,17},{1... | collective-permute-start | bytes 884744 | tf_op jit(solution)/shard_map/ppermute | solution.py:522
  130.3 12.7 %collective-permute-start.11 = (bf16[18,8,1024]{2,1,0:T(8,128)(2,1)S(1)}, bf16[18,8,1024]{2,1,0:T(8,128)(2,1)S(1)}, u32[]{:S(2)}, u32[]{:S(2)}) collective-permute-start(bf16[18,8,1024]{2,1,0:T(8,128)(2,1)S(1)} %pad_maximum_fusion.15), channel_id=1, source_target_pairs={{0,16},{4,20},{8,24},{12,28},{1,17},{5,21},{9,25},{13,29},{2,18},{... | collective-permute-start | bytes 884744 | tf_op jit(solution)/shard_map/ppermute | solution.py:522
  135.2 10.2 %collective-permute-start.12 = (bf16[18,8,1024]{2,1,0:T(8,128)(2,1)S(1)}, bf16[18,8,1024]{2,1,0:T(8,128)(2,1)S(1)}, u32[]{:S(2)}, u32[]{:S(2)}) collective-permute-start(bf16[18,8,1024]{2,1,0:T(8,128)(2,1)S(1)} %pad_maximum_fusion.10), channel_id=1, source_target_pairs={{4,0},{8,4},{12,8},{16,12},{20,16},{24,20},{28,24},{5,1},{9,5},{13... | collective-permute-start | bytes 884744 | tf_op jit(solution)/shard_map/ppermute | solution.py:522
  145.7 18.2 %collective-permute-start.13 = (bf16[18,8,1024]{2,1,0:T(8,128)(2,1)S(1)}, bf16[18,8,1024]{2,1,0:T(8,128)(2,1)S(1)}, u32[]{:S(2)}, u32[]{:S(2)}) collective-permute-start(bf16[18,8,1024]{2,1,0:T(8,128)(2,1)S(1)} %pad_maximum_fusion.16), channel_id=1, source_target_pairs={{8,0},{12,4},{16,8},{20,12},{24,16},{28,20},{9,1},{13,5},{17,9},{2... | collective-permute-start | bytes 884744 | tf_op jit(solution)/shard_map/ppermute | solution.py:522
  164.3 17.8 %collective-permute-start.14 = (bf16[18,8,1024]{2,1,0:T(8,128)(2,1)S(1)}, bf16[18,8,1024]{2,1,0:T(8,128)(2,1)S(1)}, u32[]{:S(2)}, u32[]{:S(2)}) collective-permute-start(bf16[18,8,1024]{2,1,0:T(8,128)(2,1)S(1)} %pad_maximum_fusion.17), channel_id=1, source_target_pairs={{16,0},{20,4},{24,8},{28,12},{17,1},{21,5},{25,9},{29,13},{18,2},{... | collective-permute-start | bytes 884744 | tf_op jit(solution)/shard_map/ppermute | solution.py:522
  191.1 53.2 %collective-permute-start.15 = (bf16[1024,1024]{1,0:T(8,128)(2,1)S(1)}, bf16[1024,1024]{1,0:T(8,128)(2,1)}, u32[]{:S(2)}, u32[]{:S(2)}) collective-permute-start(bf16[1024,1024]{1,0:T(8,128)(2,1)S(1)} %fusion.57), channel_id=1, source_target_pairs={{0,4},{4,0},{8,12},{12,8},{16,20},{20,16},{24,28},{28,24},{1,5},{5... | collective-permute-start | bytes 6291464 | tf_op jit(solution)/shard_map/ppermute | solution.py:517
  193.2 51.1 %collective-permute-start.16 = (bf16[1024,1024]{1,0:T(8,128)(2,1)}, bf16[1024,1024]{1,0:T(8,128)(2,1)}, u32[]{:S(2)}, u32[]{:S(2)}) collective-permute-start(bf16[1024,1024]{1,0:T(8,128)(2,1)} %fusion.58), channel_id=1, source_target_pairs={{0,8},{4,12},{8,0},{12,4},{16,24},{20,28},{24,16},{28,20},{1,9},{5... | collective-permute-start | bytes 6291464 | tf_op jit(solution)/shard_map/ppermute | solution.py:517
  251.4 25.9 %collective-permute-start.19 = (bf16[512,1024]{1,0:T(8,128)(2,1)}, bf16[512,1024]{1,0:T(8,128)(2,1)}, u32[]{:S(2)}, u32[]{:S(2)}) collective-permute-start(bf16[512,1024]{1,0:T(8,128)(2,1)} %get-tuple-element.243), channel_id=1, source_target_pairs={{0,8},{4,12},{8,0},{12,4},{16,24},{20,28},{24,16},{28,20},{1,9},{5... | collective-permute-start | bytes 3145736 | tf_op jit(solution)/shard_map/ppermute | solution.py:517
  251.4 25.9 %collective-permute-start.20 = (bf16[512,1024]{1,0:T(8,128)(2,1)}, bf16[512,1024]{1,0:T(8,128)(2,1)}, u32[]{:S(2)}, u32[]{:S(2)}) collective-permute-start(bf16[512,1024]{1,0:T(8,128)(2,1)} %get-tuple-element.244), channel_id=1, source_target_pairs={{0,4},{4,0},{8,12},{12,8},{16,20},{20,16},{24,28},{28,24},{1,5},{5... | collective-permute-start | bytes 3145736 | tf_op jit(solution)/shard_map/ppermute | solution.py:517
  252.3 10.7 %collective-permute-start.18 = (bf16[160,1024]{1,0:T(8,128)(2,1)}, bf16[160,1024]{1,0:T(8,128)(2,1)S(1)}, u32[]{:S(2)}, u32[]{:S(2)}) collective-permute-start(bf16[160,1024]{1,0:T(8,128)(2,1)} %get-tuple-element.354), channel_id=1, source_target_pairs={{0,2},{1,3},{2,0},{3,1},{4,6},{5,7},{6,4},{7,5},{8,10},{9,11},{10,... | collective-permute-start | bytes 983048 | tf_op jit(solution)/shard_map/ppermute | solution.py:517
  275.5 17.8 %collective-permute-start.22 = (f32[24,1024]{1,0:T(8,128)}, f32[24,1024]{1,0:T(8,128)S(1)}, u32[]{:S(2)}, u32[]{:S(2)}) collective-permute-start(f32[24,1024]{1,0:T(8,128)} %get-tuple-element.257), channel_id=1, source_target_pairs={{4,0},{8,4},{12,8},{16,12},{20,16},{24,20},{28,24},{5,1},{9,5},{13... | collective-permute-start | bytes 294920 | tf_op jit(solution)/shard_map/ppermute | solution.py:522
  293.3 41.4 %collective-permute-start.21 = (bf16[2,1024,512]{2,1,0:T(8,128)(2,1)}, bf16[2,1024,512]{2,1,0:T(8,128)(2,1)}, u32[]{:S(2)}, u32[]{:S(2)}) collective-permute-start(bf16[2,1024,512]{2,1,0:T(8,128)(2,1)} %get-tuple-element.249), channel_id=1, source_target_pairs={{0,1},{1,0},{2,3},{3,2},{4,5},{5,4},{6,7},{7,6},{8,9},{9,8},{10,11... | collective-permute-start | bytes 6291464 | tf_op jit(solution)/shard_map/ppermute | solution.py:517
  295.7 38.2 %collective-permute-start.23 = (bf16[1024,512]{1,0:T(8,128)(2,1)}, bf16[1024,512]{1,0:T(8,128)(2,1)}, u32[]{:S(2)}, u32[]{:S(2)}) collective-permute-start(bf16[1024,512]{1,0:T(8,128)(2,1)} %bitcast.150), channel_id=1, source_target_pairs={{0,4},{4,0},{8,12},{12,8},{16,20},{20,16},{24,28},{28,24},{1,5},{5... | collective-permute-start | bytes 3145736 | tf_op jit(solution)/shard_map/ppermute | solution.py:517
  297.9 36.7 %collective-permute-start.24 = (bf16[1024,512]{1,0:T(8,128)(2,1)}, bf16[1024,512]{1,0:T(8,128)(2,1)}, u32[]{:S(2)}, u32[]{:S(2)}) collective-permute-start(bf16[1024,512]{1,0:T(8,128)(2,1)} %bitcast.149), channel_id=1, source_target_pairs={{0,8},{4,12},{8,0},{12,4},{16,24},{20,28},{24,16},{28,20},{1,9},{5... | collective-permute-start | bytes 3145736 | tf_op jit(solution)/shard_map/ppermute | solution.py:517
  299.8 34.1 %collective-permute-start.25 = (bf16[256,1024]{1,0:T(8,128)(2,1)}, bf16[256,1024]{1,0:T(8,128)(2,1)}, u32[]{:S(2)}, u32[]{:S(2)}) collective-permute-start(bf16[256,1024]{1,0:T(8,128)(2,1)} %get-tuple-element.262), channel_id=1, source_target_pairs={{0,16},{4,20},{8,24},{12,28},{16,0},{20,4},{24,8},{28,12},{1,17},{... | collective-permute-start | bytes 1572872 | tf_op jit(solution)/shard_map/ppermute | solution.py:517
  337.9 26.3 %collective-permute-start.26 = (bf16[1024,512]{1,0:T(8,128)(2,1)}, bf16[1024,512]{1,0:T(8,128)(2,1)}, u32[]{:S(2)}, u32[]{:S(2)}) collective-permute-start(bf16[1024,512]{1,0:T(8,128)(2,1)} %dynamic-slice_bitcast_fusion.1), channel_id=1, source_target_pairs={{0,2},{1,3},{2,0},{3,1},{4,6},{5,7},{6,4},{7,5},{8,10},{9,11},{10,... | collective-permute-start | bytes 3145736 | tf_op jit(solution)/shard_map/ppermute | solution.py:517
  347.5 41.4 %collective-permute-start.36 = (bf16[1024,512]{1,0:T(8,128)(2,1)}, bf16[1024,512]{1,0:T(8,128)(2,1)}, u32[]{:S(2)}, u32[]{:S(2)}) collective-permute-start(bf16[1024,512]{1,0:T(8,128)(2,1)} %dynamic-slice_bitcast_fusion), channel_id=1, source_target_pairs={{0,2},{1,3},{2,0},{3,1},{4,6},{5,7},{6,4},{7,5},{8,10},{9,11},{10,... | collective-permute-start | bytes 3145736 | tf_op jit(solution)/shard_map/ppermute | solution.py:517
  348.0 27.6 %collective-permute-start.29 = (bf16[512,512]{1,0:T(8,128)(2,1)}, bf16[512,512]{1,0:T(8,128)(2,1)}, u32[]{:S(2)}, u32[]{:S(2)}) collective-permute-start(bf16[512,512]{1,0:T(8,128)(2,1)} %get-tuple-element.292), channel_id=1, source_target_pairs={{0,8},{4,12},{8,0},{12,4},{16,24},{20,28},{24,16},{28,20},{1,9},{5... | collective-permute-start | bytes 1572872 | tf_op jit(solution)/shard_map/ppermute | solution.py:517
  351.6 24.0 %collective-permute-start.30 = (bf16[512,512]{1,0:T(8,128)(2,1)}, bf16[512,512]{1,0:T(8,128)(2,1)}, u32[]{:S(2)}, u32[]{:S(2)}) collective-permute-start(bf16[512,512]{1,0:T(8,128)(2,1)} %get-tuple-element.293), channel_id=1, source_target_pairs={{0,4},{4,0},{8,12},{12,8},{16,20},{20,16},{24,28},{28,24},{1,5},{5... | collective-permute-start | bytes 1572872 | tf_op jit(solution)/shard_map/ppermute | solution.py:517
  353.1 25.7 %collective-permute-start.32 = (bf16[256,1024]{1,0:T(8,128)(2,1)}, bf16[256,1024]{1,0:T(8,128)(2,1)}, u32[]{:S(2)}, u32[]{:S(2)}) collective-permute-start(bf16[256,1024]{1,0:T(8,128)(2,1)} %get-tuple-element.295), channel_id=1, source_target_pairs={{0,16},{4,20},{8,24},{12,28},{16,0},{20,4},{24,8},{28,12},{1,17},{... | collective-permute-start | bytes 1572872 | tf_op jit(solution)/shard_map/ppermute | solution.py:517
  364.2 11.4 %collective-permute-start.31 = (bf16[416,512]{1,0:T(8,128)(2,1)}, bf16[416,512]{1,0:T(8,128)(2,1)}, u32[]{:S(2)}, u32[]{:S(2)}) collective-permute-start(bf16[416,512]{1,0:T(8,128)(2,1)} %pad_maximum_fusion.9), channel_id=1, source_target_pairs={{0,4},{4,0},{8,12},{12,8},{16,20},{20,16},{24,28},{28,24},{1,5},{5... | collective-permute-start | bytes 1277960 | tf_op jit(solution)/shard_map/ppermute | solution.py:517
  383.4 18.6 %collective-permute-start.33 = (bf16[256,512]{1,0:T(8,128)(2,1)}, bf16[256,512]{1,0:T(8,128)(2,1)S(1)}, u32[]{:S(2)}, u32[]{:S(2)}) collective-permute-start(bf16[256,512]{1,0:T(8,128)(2,1)} %get-tuple-element.305), channel_id=1, source_target_pairs={{0,16},{4,20},{8,24},{12,28},{16,0},{20,4},{24,8},{28,12},{1,17},{... | collective-permute-start | bytes 786440 | tf_op jit(solution)/shard_map/ppermute | solution.py:517
  383.4 24.1 %collective-permute-start.34 = (bf16[256,512]{1,0:T(8,128)(2,1)}, bf16[256,512]{1,0:T(8,128)(2,1)S(1)}, u32[]{:S(2)}, u32[]{:S(2)}) collective-permute-start(bf16[256,512]{1,0:T(8,128)(2,1)} %get-tuple-element.306), channel_id=1, source_target_pairs={{0,16},{4,20},{8,24},{12,28},{16,0},{20,4},{24,8},{28,12},{1,17},{... | collective-permute-start | bytes 786440 | tf_op jit(solution)/shard_map/ppermute | solution.py:517
  386.3 21.2 %collective-permute-start.35 = (bf16[256,512]{1,0:T(8,128)(2,1)}, bf16[256,512]{1,0:T(8,128)(2,1)S(1)}, u32[]{:S(2)}, u32[]{:S(2)}) collective-permute-start(bf16[256,512]{1,0:T(8,128)(2,1)} %get-tuple-element.307), channel_id=1, source_target_pairs={{0,8},{4,12},{8,0},{12,4},{16,24},{20,28},{24,16},{28,20},{1,9},{5... | collective-permute-start | bytes 786440 | tf_op jit(solution)/shard_map/ppermute | solution.py:517
  413.6 11.0 %collective-permute-start.42 = (bf16[176,512]{1,0:T(8,128)(2,1)}, bf16[176,512]{1,0:T(8,128)(2,1)S(1)}, u32[]{:S(2)}, u32[]{:S(2)}) collective-permute-start(bf16[176,512]{1,0:T(8,128)(2,1)} %get-tuple-element.326), channel_id=1, source_target_pairs={{0,16},{4,20},{8,24},{12,28},{16,0},{20,4},{24,8},{28,12},{1,17},{... | collective-permute-start | bytes 540680 | tf_op jit(solution)/shard_map/ppermute | solution.py:517
  (80 other events, 834.4 us)

commit v5 on v4

--- a/solution.py
+++ b/solution.py
@@ -811,9 +811,9 @@
     for bit in range(chan_bits):
         received = swapped(proj_part.astype(BF16) if bit else proj_part, "chan", bit)
         if bit == chan_bits - 1:
-            gate_pre = dot(after(normed, proj_part), gate_weights)
-            extended_normed = jnp.concatenate([normed_halo, after(normed, gate_pre)], axis=0)
-            received, gate_pre, extended_normed = lax.optimization_barrier((received, gate_pre, extended_normed))
+            extended_normed = jnp.concatenate([normed_halo, after(normed, proj_part)], axis=0)
+            gate_pre = dot(after(normed, extended_normed), gate_weights)
+            received, gate_pre = lax.optimization_barrier((received, gate_pre))
         proj_part = proj_part + received.astype(F32)
     projected = proj_part
     step_low = projected[:rank].astype(BF16)
@@ -896,7 +896,7 @@
         proj_sum = proj_sum + received.astype(F32)
     proj_grad = proj_sum.astype(BF16)
     own_spread, first_grad, conv_sums = conv_back(
-        proj_grad, proj_weight, mixed_part, conv_out, conv_in, previous, conv_taps, chunk
+        proj_grad, proj_weight, mixed_part, conv_out, conv_in, previous, conv_taps, math.gcd(toks, 32)
     )
     incoming = moved(first_grad, "seq", -1)
     (own_spread,) = end_chains(apart, own_spread)
@@ -905,10 +905,12 @@
         by_part(dot(extended_normed, own_spread[:, at : at + half], CONTRACT_FIRST, out=BF16)) for at in (0, half)
     )
     first, second = Chain([first_last], "seq", seq_bits), Chain([second_last], "seq", other_bits)
+    out_chain.got, first.sent, second.sent = lax.optimization_barrier((out_chain.got, first.sent, second.sent))
     weight_message = merge(apart)
     in_window = [[first], [second], [out_chain]]
     (own_spread,) = start_all([branch_sum], own_spread)
-    own_spread, incoming = send_chains(in_window, [first.sent, second.sent, weight_message[0]], own_spread, incoming)
+    own_spread, incoming = send_chains(in_window[:2], [first.sent, second.sent], own_spread, incoming)
+    (own_spread,) = send_chains(in_window[2:], weight_message[:1], own_spread)
     zeros = jnp.zeros((halo, inner), F32)
     from_after = jnp.concatenate([zeros, incoming, zeros], axis=0)
     late = sum(

time: 434 us -> 432 us (level)
    unnamed x139 -> x144, local copies, waits for them, and re-layouts: 7.46 us -> 8.83 us
  transfers between devices with their start and end apart: 43 -> 43, of which waited for: 16 -> 17; matrix products, arithmetic and copies ran while one was open for 26% -> 27% of each run, Pallas kernels for 38% -> 37%
where the time goes in v5:
time: 432 us; the launch traced here: 426 us
  Pallas kernels  161 us (37%)
  starting transfers between devices  57.6 us (13%)
  other arithmetic  55.3 us (13%)
  matrix products  52 us (12%)
  waiting for transfers between devices  49.8 us (12%)
  local copies, waits for them, and re-layouts  47.3 us (11%)
    dot_general x14, matrix products, dot(): return lax.dot_general(a, b, dims, preferred_element_type=out)  52 us
    ppermute x32, waiting for transfers between devices, swapped(): return lax.ppermute(value, axis, [(i, i ^ 1 << bit) for i in range(count)])  48.8 us
    pallas_call x1, Pallas kernels, backward(): pl.pallas_call(functools.partial(bwd_kernel, chunk), grid=(grid,), in_spe...  40.9 us
    ppermute x32, starting transfers between devices, swapped(): return lax.ppermute(value, axis, [(i, i ^ 1 << bit) for i in range(count)])  34 us
    pallas_call x2, Pallas kernels, forward(): pl.pallas_call(functools.partial(fwd_kernel, chunk), grid=(last - first,)...  32.8 us
    pallas_call x2, Pallas kernels, product_sides(): pl.pallas_call(functools.partial(product_kernel, len(pairs)), grid_spec=p...  24.2 us
    ppermute x8, starting transfers between devices, moved(): lax.ppermute(value, axis, [(i, i + distance) for i in range(count) if 0 <...  20.1 us
    pallas_call x1, Pallas kernels, local_ends(): pl.pallas_call(functools.partial(ends_kernel, chunk), grid=(grid,), in_sp...  19.7 us
  transfers between devices with their start and end apart: 43, of which 17 were waited for; matrix products, arithmetic and copies ran while one was open for 27% of the time, Pallas kernels for 37%

profile of v5, /device:TPU:0, one launch (start us, length us, event | category | flops | bytes accessed | tf_op | source)
XLA Modules:
  0.0 425.8 jit_solution(235911418097958680)
XLA Ops:
  6.4 16.3 %fusion.49 = (bf16[2048,1,1024]{2,1,0:T(2,128)(2,1)S(1)}, bf16[2048,1,1024]{2,1,0:T(2,128)(2,1)S(1)}) fusion(bf16[2048,2,1024]{2,1,0:T(2,128)(2,1)} %param.14), kind=kLoop, calls=%fused_computation.190 | loop fusion | bytes 16777216 | tf_op jit(solution)/shard_map/slice | solution.py:794
  22.7 5.9 %copy_bitcast_fusion = (bf16[2048,1024]{1,0:T(8,128)(2,1)}, bf16[2048,1024]{1,0:T(8,128)(2,1)}) fusion(bf16[2048,1,1024]{2,1,0:T(2,128)(2,1)S(1)} %get-tuple-element.374, bf16[2048,1,1024]{2,1,0:T(2,128)(2,1)S(1)} %get-tuple-element.375), kind=kLoop, calls=%fused_computation.16 | loop fusion | bytes 16777216 | tf_op jit(solution)/shard_map/squeeze | solution.py:794
  37.6 3.8 collective-permute-start.3
  41.4 4.7 %fusion.55.in_ref = bf16[1024,1024]{1,0:T(8,128)(2,1)S(1)} fusion(bf16[1024,2048]{1,0:T(8,128)(2,1)S(1)} %fusion.2, bf16[2048,1024]{1,0:T(8,128)(2,1)S(1)} %copy-done.6), kind=kOutput, calls=%fused_computation.196 | convolution fusion | flops 4294967296 | bytes 10485760 | tf_op jit(solution)/shard_map/dot_general | solution.py:508
  47.7 3.8 multiply_convert_fusion
  58.4 4.5 %fusion.56.gate_ref = f32[1024,1024]{1,0:T(8,128)S(1)} fusion(bf16[1024,2048]{1,0:T(8,128)(2,1)S(1)} %fusion.2, bf16[2048,1024]{1,0:T(8,128)(2,1)S(1)} %copy-done.13), kind=kOutput, calls=%fused_computation.197 | convolution fusion | flops 4294967296 | bytes 12582912 | tf_op jit(solution)/shard_map/dot_general | solution.py:508
  67.6 4.7 %bitcast_reduce_fusion = (f32[8,1024]{1,0:T(8,128)S(1)}, f32[1024,1024]{1,0:T(8,128)}) fusion(f32[1024]{0:T(1024)S(1)} %convert_element_type.288, bf16[128,1024]{1,0:T(8,128)(2,1)S(1)} %copy-done.41, f32[160,1024]{1,0:T(8,128)S(1)} %convert_add_fusion.4), kind=kOutput, calls=%fused_computation.18 | convolution fusion | flops 276815872 | bytes 4755456 | tf_op jit(solution)/shard_map/dot_general | solution.py:508
  73.1 19.7 %local_ends.1 = (f32[16,8,1024]{2,1,0:T(8,128)}, f32[128,32,8,128]{3,2,1,0:T(8,128)}, bf16[128,256,128]{2,1,0:T(8,128)(2,1)}) custom-call(f32[1024,1024]{1,0:T(8,128)} %get-tuple-element.437.step_ref, bf16[1024,1024]{1,0:T(8,128)(2,1)} %copy-done, f32[32,1024]{1,0:T(8,128)} %slice.282.rows_ref, f32[16,8,1024]{2,1,0:T(8,128)} %broadcast_in_dim.8.rate_ref), custom_call_target="tpu_custom_call" | custom-call | flops 16777216 | bytes 16777216 | tf_op jit(solution)/shard_map/local_ends/pallas_call | solution.py:105
  102.1 7.1 %multiply_multiply_fusion = (f32[1024,1024]{1,0:T(8,128)}, f32[1024,1024]{1,0:T(8,128)}) fusion(f32[1024,1024]{1,0:T(8,128)S(1)} %fusion.56.gate_ref, bf16[1024,2048]{1,0:T(8,128)(2,1)S(1)} %pad_maximum_fusion.1, bf16[2048,1024]{1,0:T(8,128)(2,1)S(1)} %copy-done.23), kind=kOutput, calls=%fused_computation.22 | convolution fusion | flops 4300210176 | bytes 20971520 | tf_op jit(solution)/shard_map/dot_general | solution.py:508
  113.0 14.7 %local_starts.1 = f32[16,8,1024]{2,1,0:T(8,128)} custom-call(f32[1024,1024]{1,0:T(8,128)} %get-tuple-element.437.step_ref, f32[1024,1024]{1,0:T(8,128)} %get-tuple-element.187.yg_ref, f32[128,32,8,128]{3,2,1,0:T(8,128)} %get-tuple-element.188.spread_ref, f32[16,8,1024]{2,1,0:T(8,128)} %broadcast_in_dim.8.rate_ref), custom_call_target="tpu_custom_call" | custom-call | flops 16777216 | bytes 16777216 | tf_op jit(solution)/shard_map/local_starts/pallas_call | solution.py:127
  128.1 3.7 collective-permute-start.11
  145.7 16.3 %scan_forward.2 = (f32[16,8,1024]{2,1,0:T(8,128)}, bf16[128,8,128,128]{3,2,1,0:T(8,128)(2,1)}, bf16[8,16,8,1024]{3,2,1,0:T(8,128)(2,1)}, bf16[1024,1024]{1,0:T(8,128)(2,1)}, bf16[1024,1024]{1,0:T(8,128)(2,1)}) custom-call(f32[1024,1024]{1,0:T(8,128)} %get-tuple-element.437.step_ref, bf16[1024,1024]{1,0:T(8,128)(2,1)} %copy-done, ...), custom_call_target="tpu_custom_call", output_to_operand_aliasing={{0}: (8, {})} | custom-call | flops 8388608 | bytes 8388608 | tf_op jit(solution)/shard_map/scan_forward/pallas_call | solution.py:193
  163.8 16.5 %scan_forward.3 = (f32[16,8,1024]{2,1,0:T(8,128)}, bf16[128,8,128,128]{3,2,1,0:T(8,128)(2,1)}, bf16[8,16,8,1024]{3,2,1,0:T(8,128)(2,1)}, bf16[1024,1024]{1,0:T(8,128)(2,1)}, bf16[1024,1024]{1,0:T(8,128)(2,1)}) custom-call(f32[1024,1024]{1,0:T(8,128)} %get-tuple-element.437.step_ref, ...), custom_call_target="tpu_custom_call", output_to_operand_aliasing={{0}: (8, {}), {1}: (9, {}), {2}: (10, {}), {3}: (11, {}), {... | custom-call | flops 8388608 | bytes 8388608 | tf_op jit(solution)/shard_map/scan_forward/pallas_call | solution.py:193
  180.8 5.4 %fusion.58 = bf16[1024,1024]{1,0:T(8,128)(2,1)} fusion(bf16[1024,1024]{1,0:T(8,128)(2,1)S(1)} %copy-done.33, bf16[1024,1024]{1,0:T(8,128)(2,1)} %get-tuple-element.231.refs_1_), kind=kOutput, calls=%fused_computation.199 | convolution fusion | flops 2147483648 | bytes 6291456 | tf_op jit(solution)/shard_map/dot_general | solution.py:508
  186.3 3.8 fusion.57
  195.3 3.7 fusion.60.refs_2_
  199.1 3.8 fusion.59.refs_0_
  202.9 40.9 %scan_backward.1 = (f32[18,1024]{1,0:T(8,128)}, bf16[1024,1024]{1,0:T(8,128)(2,1)}, f32[1024,1024]{1,0:T(8,128)}, f32[160,1024]{1,0:T(8,128)}) custom-call(f32[1024,1024]{1,0:T(8,128)} %get-tuple-element.437.step_ref, bf16[1024,1024]{1,0:T(8,128)(2,1)} %copy-done, f32[1024,1024]{1,0:T(8,128)} %get-tuple-element.187.yg_ref, ...), custom_call_target="tpu_custom_call" | custom-call | flops 16777216 | bytes 16777216 | tf_op jit(solution)/shard_map/scan_backward/pallas_call | solution.py:321
  244.6 6.5 %merge_messages.5 = (bf16[512,1024]{1,0:T(8,128)(2,1)}, bf16[512,1024]{1,0:T(8,128)(2,1)}, bf16[512,1024]{1,0:T(8,128)(2,1)}, bf16[512,1024]{1,0:T(8,128)(2,1)}) custom-call(s32[2]{0:T(128)} %get-tuple-element.440.bits_ref, bf16[1024,1024]{1,0:T(8,128)(2,1)} %fusion.59.refs_0_, bf16[1024,1024]{1,0:T(8,128)(2,1)} %collective-permute-done.15.refs_1_, ...), custom_call_target="tpu_custom_call" | custom-call | flops 1024 | bytes 1024 | tf_op jit(solution)/shard_map/merge_messages/pallas_call | solution.py:701
  253.3 9.6 %product_sides.2 = (bf16[2,1024,512]{2,1,0:T(8,128)(2,1)}, bf16[2,1024,512]{2,1,0:T(8,128)(2,1)}) custom-call(s32[1]{0:T(128)} %bitcast.21.core_ref, bf16[1024,1024]{1,0:T(8,128)(2,1)} %get-tuple-element.241.refs_0_, bf16[2048,1024]{1,0:T(8,128)(2,1)} %refs_1_.1), custom_call_target="tpu_custom_call" | custom-call | flops 1024 | bytes 1024 | tf_op jit(solution)/shard_map/product_sides/pallas_call | solution.py:486
  263.7 9.8 %conv_backward.1 = (bf16[1056,1024]{1,0:T(8,128)(2,1)}, f32[24,1024]{1,0:T(8,128)}, f32[5,8,1024]{2,1,0:T(8,128)}) custom-call(bf16[160,1024]{1,0:T(8,128)(2,1)} %add_convert_fusion.2.proj_ref, bf16[160,1024]{1,0:T(8,128)(2,1)} %weight_ref.1, f32[1024,1024]{1,0:T(8,128)} %get-tuple-element.249.part_ref, f32[1024,1024]{1,0:T(8,128)} %get-tuple-element.373.conv_ref, ...), custom_call_target="tpu_custom_call" | custom-call | flops 1048576 | bytes 1048576 | tf_op jit(solution)/shard_map/conv_backward/pallas_call | solution.py:415
  277.0 4.5 %fusion.16 = bf16[2048,512]{1,0:T(8,128)(2,1)S(1)} fusion(bf16[1056,2048]{1,0:T(8,128)(2,1)S(1)} %bitcast.165, bf16[1056,1024]{1,0:T(8,128)(2,1)} %get-tuple-element.264), kind=kOutput, calls=%fused_computation.47 | convolution fusion | flops 2214592512 | bytes 7503872 | tf_op jit(solution)/shard_map/dot_general | solution.py:508
  281.6 5.5 %fusion.18 = bf16[2048,512]{1,0:T(8,128)(2,1)S(1)} fusion(bf16[1056,2048]{1,0:T(8,128)(2,1)} %copy-done.66, bf16[1056,1024]{1,0:T(8,128)(2,1)S(1)} %copy-done.34), kind=kOutput, calls=%fused_computation.49 | convolution fusion | flops 2214592512 | bytes 7503872 | tf_op jit(solution)/shard_map/dot_general | solution.py:508
  290.1 4.1 merge_messages.6
  314.4 14.6 %product_sides.3 = (bf16[2,1024,512]{2,1,0:T(8,128)(2,1)}, bf16[2,1024,512]{2,1,0:T(8,128)(2,1)}) custom-call(s32[1]{0:T(128)} %bitcast.21.core_ref, bf16[1024,1024]{1,0:T(8,128)(2,1)} %pad_maximum_fusion.6.refs_0_, bf16[1024,1024]{1,0:T(8,128)(2,1)} %get-tuple-element.231.refs_1_, bf16[2048,1024]{1,0:T(8,128)(2,1)} %get-tuple-element.175.refs_2_, ...), custom_call_target="tpu_custom_call" | custom-call | flops 1024 | bytes 1024 | tf_op jit(solution)/shard_map/product_sides/pallas_call | solution.py:486
  329.0 6.9 %collective-permute-done.24.refs_3_ = bf16[1024,512]{1,0:T(8,128)(2,1)} collective-permute-done((bf16[1024,512]{1,0:T(8,128)(2,1)}, bf16[1024,512]{1,0:T(8,128)(2,1)}, u32[]{:S(2)}, u32[]{:S(2)}) %collective-permute-start.24) | collective-permute-done | bytes 1048608 | tf_op jit(solution)/shard_map/ppermute | solution.py:517
  340.2 3.9 merge_messages.7
  354.0 11.5 %collective-permute-done.26 = bf16[1024,512]{1,0:T(8,128)(2,1)} collective-permute-done((bf16[1024,512]{1,0:T(8,128)(2,1)}, bf16[1024,512]{1,0:T(8,128)(2,1)}, u32[]{:S(2)}, u32[]{:S(2)}) %collective-permute-start.26) | collective-permute-done | bytes 1048608 | tf_op jit(solution)/shard_map/ppermute | solution.py:517
  369.9 6.9 %collective-permute-done.31.refs_5_ = bf16[416,512]{1,0:T(8,128)(2,1)} collective-permute-done((bf16[416,512]{1,0:T(8,128)(2,1)}, bf16[416,512]{1,0:T(8,128)(2,1)}, u32[]{:S(2)}, u32[]{:S(2)}) %collective-permute-start.31) | collective-permute-done | bytes 426016 | tf_op jit(solution)/shard_map/ppermute | solution.py:517
  387.6 4.5 %fusion.12 = (f32[512]{0:T(512)S(1)}, bf16[128,8,512]{2,1,0:T(8,128)(2,1)S(1)}, bf16[128,8,512]{2,1,0:T(8,128)(2,1)S(1)}) fusion(bf16[1024,512]{1,0:T(8,128)(2,1)} %collective-permute-done.36, f32[1024]{0:T(1024)S(1)} %copy-done.55, bf16[2,1024,512]{2,1,0:T(8,128)(2,1)S(1)} %copy-done.17, s32[]{:T(128)S(6)} %select_n.192, ...), kind=kLoop, calls=%fused_computation.33 | loop fusion | flops 10485248 | bytes 8404996 | tf_op jit(solution)/shard_map/reduce_sum | solution.py:965
  393.4 7.2 %collective-permute-done.33 = bf16[256,512]{1,0:T(8,128)(2,1)S(1)} collective-permute-done((bf16[256,512]{1,0:T(8,128)(2,1)}, bf16[256,512]{1,0:T(8,128)(2,1)S(1)}, u32[]{:S(2)}, u32[]{:S(2)}) %collective-permute-start.33) | collective-permute-done | bytes 262176 | tf_op jit(solution)/shard_map/ppermute | solution.py:517
  400.6 4.7 %collective-permute-done.34 = bf16[256,512]{1,0:T(8,128)(2,1)S(1)} collective-permute-done((bf16[256,512]{1,0:T(8,128)(2,1)}, bf16[256,512]{1,0:T(8,128)(2,1)S(1)}, u32[]{:S(2)}, u32[]{:S(2)}) %collective-permute-start.34) | collective-permute-done | bytes 262176 | tf_op jit(solution)/shard_map/ppermute | solution.py:517
  (329 shorter events, 143.8 us)
Async XLA Ops:
  3.4 26.3 %collective-permute-start = (bf16[1024,512]{1,0:T(8,128)(2,1)}, bf16[1024,512]{1,0:T(8,128)(2,1)S(1)}, u32[]{:S(2)}, u32[]{:S(2)}) collective-permute-start(bf16[1024,512]{1,0:T(8,128)(2,1)} %bitcast.129), channel_id=1, source_target_pairs={{0,2},{1,3},{2,0},{3,1},{4,6},{5,7},{6,4},{7,5},{8,10},{9,11},{10,... | collective-permute-start | bytes 3145736 | tf_op jit(solution)/shard_map/ppermute | solution.py:517
  6.4 23.5 %collective-permute-start.2 = (bf16[1024,512]{1,0:T(8,128)(2,1)}, bf16[1024,512]{1,0:T(8,128)(2,1)S(1)}, u32[]{:S(2)}, u32[]{:S(2)}) collective-permute-start(bf16[1024,512]{1,0:T(8,128)(2,1)} %bitcast.129), channel_id=1, source_target_pairs={{0,1},{1,0},{2,3},{3,2},{4,5},{5,4},{6,7},{7,6},{8,9},{9,8},{10,11... | collective-permute-start | bytes 3145736 | tf_op jit(solution)/shard_map/ppermute | solution.py:517
  37.6 8.6 %collective-permute-start.3 = (bf16[32,2048]{1,0:T(8,128)(2,1)S(1)}, bf16[32,2048]{1,0:T(8,128)(2,1)S(1)}, u32[]{:S(2)}, u32[]{:S(2)}) collective-permute-start(bf16[32,2048]{1,0:T(8,128)(2,1)S(1)} %slice.272), channel_id=1, source_target_pairs={{0,4},{4,8},{8,12},{12,16},{16,20},{20,24},{24,28},{1,5},{5,9},{9,... | collective-permute-start | bytes 393224 | tf_op jit(solution)/shard_map/ppermute | solution.py:522
  55.3 9.8 %collective-permute-start.5 = (bf16[160,1024]{1,0:T(8,128)(2,1)S(1)}, bf16[160,1024]{1,0:T(8,128)(2,1)S(1)}, u32[]{:S(2)}, u32[]{:S(2)}) collective-permute-start(bf16[160,1024]{1,0:T(8,128)(2,1)S(1)} %get-tuple-element.370), channel_id=1, source_target_pairs={{0,2},{1,3},{2,0},{3,1},{4,6},{5,7},{6,4},{7,5},{8,10},{9,11},{10,... | collective-permute-start | bytes 983048 | tf_op jit(solution)/shard_map/ppermute | solution.py:517
  65.1 27.7 %collective-permute-start.7 = (bf16[1024,512]{1,0:T(8,128)(2,1)S(1)}, bf16[1024,512]{1,0:T(8,128)(2,1)S(1)}, u32[]{:S(2)}, u32[]{:S(2)}) collective-permute-start(bf16[1024,512]{1,0:T(8,128)(2,1)S(1)} %bitcast.137), channel_id=1, source_target_pairs={{0,2},{1,3},{2,0},{3,1},{4,6},{5,7},{6,4},{7,5},{8,10},{9,11},{10,... | collective-permute-start | bytes 3145736 | tf_op jit(solution)/shard_map/ppermute | solution.py:517
  66.7 31.3 %collective-permute-start.9 = (bf16[1024,512]{1,0:T(8,128)(2,1)S(1)}, bf16[1024,512]{1,0:T(8,128)(2,1)}, u32[]{:S(2)}, u32[]{:S(2)}) collective-permute-start(bf16[1024,512]{1,0:T(8,128)(2,1)S(1)} %bitcast.138), channel_id=1, source_target_pairs={{0,1},{1,0},{2,3},{3,2},{4,5},{5,4},{6,7},{7,6},{8,9},{9,8},{10,11... | collective-permute-start | bytes 3145736 | tf_op jit(solution)/shard_map/ppermute | solution.py:517
  94.5 14.7 %collective-permute-start.6 = (bf16[18,8,1024]{2,1,0:T(8,128)(2,1)S(1)}, bf16[18,8,1024]{2,1,0:T(8,128)(2,1)S(1)}, u32[]{:S(2)}, u32[]{:S(2)}) collective-permute-start(bf16[18,8,1024]{2,1,0:T(8,128)(2,1)S(1)} %pad_maximum_fusion.10), channel_id=1, source_target_pairs={{0,4},{4,8},{8,12},{12,16},{16,20},{20,24},{24,28},{1,5},{5,9},{9,... | collective-permute-start | bytes 884744 | tf_op jit(solution)/shard_map/ppermute | solution.py:522
  109.5 18.2 %collective-permute-start.10 = (bf16[18,8,1024]{2,1,0:T(8,128)(2,1)S(1)}, bf16[18,8,1024]{2,1,0:T(8,128)(2,1)S(1)}, u32[]{:S(2)}, u32[]{:S(2)}) collective-permute-start(bf16[18,8,1024]{2,1,0:T(8,128)(2,1)S(1)} %pad_maximum_fusion.13), channel_id=1, source_target_pairs={{0,8},{4,12},{8,16},{12,20},{16,24},{20,28},{1,9},{5,13},{9,17},{1... | collective-permute-start | bytes 884744 | tf_op jit(solution)/shard_map/ppermute | solution.py:522
  128.1 14.0 %collective-permute-start.11 = (bf16[18,8,1024]{2,1,0:T(8,128)(2,1)S(1)}, bf16[18,8,1024]{2,1,0:T(8,128)(2,1)S(1)}, u32[]{:S(2)}, u32[]{:S(2)}) collective-permute-start(bf16[18,8,1024]{2,1,0:T(8,128)(2,1)S(1)} %pad_maximum_fusion.14), channel_id=1, source_target_pairs={{0,16},{4,20},{8,24},{12,28},{1,17},{5,21},{9,25},{13,29},{2,18},{... | collective-permute-start | bytes 884744 | tf_op jit(solution)/shard_map/ppermute | solution.py:522
  133.0 10.5 %collective-permute-start.12 = (bf16[18,8,1024]{2,1,0:T(8,128)(2,1)S(1)}, bf16[18,8,1024]{2,1,0:T(8,128)(2,1)S(1)}, u32[]{:S(2)}, u32[]{:S(2)}) collective-permute-start(bf16[18,8,1024]{2,1,0:T(8,128)(2,1)S(1)} %pad_maximum_fusion.9), channel_id=1, source_target_pairs={{4,0},{8,4},{12,8},{16,12},{20,16},{24,20},{28,24},{5,1},{9,5},{13... | collective-permute-start | bytes 884744 | tf_op jit(solution)/shard_map/ppermute | solution.py:522
  143.8 18.2 %collective-permute-start.13 = (bf16[18,8,1024]{2,1,0:T(8,128)(2,1)S(1)}, bf16[18,8,1024]{2,1,0:T(8,128)(2,1)S(1)}, u32[]{:S(2)}, u32[]{:S(2)}) collective-permute-start(bf16[18,8,1024]{2,1,0:T(8,128)(2,1)S(1)} %pad_maximum_fusion.15), channel_id=1, source_target_pairs={{8,0},{12,4},{16,8},{20,12},{24,16},{28,20},{9,1},{13,5},{17,9},{2... | collective-permute-start | bytes 884744 | tf_op jit(solution)/shard_map/ppermute | solution.py:522
  162.4 18.5 %collective-permute-start.14 = (bf16[18,8,1024]{2,1,0:T(8,128)(2,1)S(1)}, bf16[18,8,1024]{2,1,0:T(8,128)(2,1)S(1)}, u32[]{:S(2)}, u32[]{:S(2)}) collective-permute-start(bf16[18,8,1024]{2,1,0:T(8,128)(2,1)S(1)} %pad_maximum_fusion.16), channel_id=1, source_target_pairs={{16,0},{20,4},{24,8},{28,12},{17,1},{21,5},{25,9},{29,13},{18,2},{... | collective-permute-start | bytes 884744 | tf_op jit(solution)/shard_map/ppermute | solution.py:522
  191.1 52.7 %collective-permute-start.15 = (bf16[1024,1024]{1,0:T(8,128)(2,1)}, bf16[1024,1024]{1,0:T(8,128)(2,1)}, u32[]{:S(2)}, u32[]{:S(2)}) collective-permute-start(bf16[1024,1024]{1,0:T(8,128)(2,1)} %fusion.57), channel_id=1, source_target_pairs={{0,4},{4,0},{8,12},{12,8},{16,20},{20,16},{24,28},{28,24},{1,5},{5... | collective-permute-start | bytes 6291464 | tf_op jit(solution)/shard_map/ppermute | solution.py:517
  192.7 51.1 %collective-permute-start.16 = (bf16[1024,1024]{1,0:T(8,128)(2,1)}, bf16[1024,1024]{1,0:T(8,128)(2,1)}, u32[]{:S(2)}, u32[]{:S(2)}) collective-permute-start(bf16[1024,1024]{1,0:T(8,128)(2,1)} %fusion.58), channel_id=1, source_target_pairs={{0,8},{4,12},{8,0},{12,4},{16,24},{20,28},{24,16},{28,20},{1,9},{5... | collective-permute-start | bytes 6291464 | tf_op jit(solution)/shard_map/ppermute | solution.py:517
  251.0 25.9 %collective-permute-start.19 = (bf16[512,1024]{1,0:T(8,128)(2,1)}, bf16[512,1024]{1,0:T(8,128)(2,1)}, u32[]{:S(2)}, u32[]{:S(2)}) collective-permute-start(bf16[512,1024]{1,0:T(8,128)(2,1)} %get-tuple-element.246), channel_id=1, source_target_pairs={{0,8},{4,12},{8,0},{12,4},{16,24},{20,28},{24,16},{28,20},{1,9},{5... | collective-permute-start | bytes 3145736 | tf_op jit(solution)/shard_map/ppermute | solution.py:517
  251.1 25.9 %collective-permute-start.20 = (bf16[512,1024]{1,0:T(8,128)(2,1)}, bf16[512,1024]{1,0:T(8,128)(2,1)}, u32[]{:S(2)}, u32[]{:S(2)}) collective-permute-start(bf16[512,1024]{1,0:T(8,128)(2,1)} %get-tuple-element.247), channel_id=1, source_target_pairs={{0,4},{4,0},{8,12},{12,8},{16,20},{20,16},{24,28},{28,24},{1,5},{5... | collective-permute-start | bytes 3145736 | tf_op jit(solution)/shard_map/ppermute | solution.py:517
  252.2 10.7 %collective-permute-start.18 = (bf16[160,1024]{1,0:T(8,128)(2,1)}, bf16[160,1024]{1,0:T(8,128)(2,1)S(1)}, u32[]{:S(2)}, u32[]{:S(2)}) collective-permute-start(bf16[160,1024]{1,0:T(8,128)(2,1)} %get-tuple-element.360), channel_id=1, source_target_pairs={{0,2},{1,3},{2,0},{3,1},{4,6},{5,7},{6,4},{7,5},{8,10},{9,11},{10,... | collective-permute-start | bytes 983048 | tf_op jit(solution)/shard_map/ppermute | solution.py:517
  273.5 16.6 %collective-permute-start.22 = (f32[24,1024]{1,0:T(8,128)}, f32[24,1024]{1,0:T(8,128)S(1)}, u32[]{:S(2)}, u32[]{:S(2)}) collective-permute-start(f32[24,1024]{1,0:T(8,128)} %get-tuple-element.262), channel_id=1, source_target_pairs={{4,0},{8,4},{12,8},{16,12},{20,16},{24,20},{28,24},{5,1},{9,5},{13... | collective-permute-start | bytes 294920 | tf_op jit(solution)/shard_map/ppermute | solution.py:522
  294.2 41.7 %collective-permute-start.21 = (bf16[2,1024,512]{2,1,0:T(8,128)(2,1)}, bf16[2,1024,512]{2,1,0:T(8,128)(2,1)}, u32[]{:S(2)}, u32[]{:S(2)}) collective-permute-start(bf16[2,1024,512]{2,1,0:T(8,128)(2,1)} %get-tuple-element.252), channel_id=1, source_target_pairs={{0,1},{1,0},{2,3},{3,2},{4,5},{5,4},{6,7},{7,6},{8,9},{9,8},{10,11... | collective-permute-start | bytes 6291464 | tf_op jit(solution)/shard_map/ppermute | solution.py:517
  296.3 32.6 %collective-permute-start.25 = (bf16[256,1024]{1,0:T(8,128)(2,1)}, bf16[256,1024]{1,0:T(8,128)(2,1)}, u32[]{:S(2)}, u32[]{:S(2)}) collective-permute-start(bf16[256,1024]{1,0:T(8,128)(2,1)} %get-tuple-element.268), channel_id=1, source_target_pairs={{0,16},{4,20},{8,24},{12,28},{16,0},{20,4},{24,8},{28,12},{1,17},{... | collective-permute-start | bytes 1572872 | tf_op jit(solution)/shard_map/ppermute | solution.py:517
  299.9 29.0 %collective-permute-start.23 = (bf16[1024,512]{1,0:T(8,128)(2,1)}, bf16[1024,512]{1,0:T(8,128)(2,1)}, u32[]{:S(2)}, u32[]{:S(2)}) collective-permute-start(bf16[1024,512]{1,0:T(8,128)(2,1)} %bitcast.148), channel_id=1, source_target_pairs={{0,4},{4,0},{8,12},{12,8},{16,20},{20,16},{24,28},{28,24},{1,5},{5... | collective-permute-start | bytes 3145736 | tf_op jit(solution)/shard_map/ppermute | solution.py:517
  300.4 35.5 %collective-permute-start.24 = (bf16[1024,512]{1,0:T(8,128)(2,1)}, bf16[1024,512]{1,0:T(8,128)(2,1)}, u32[]{:S(2)}, u32[]{:S(2)}) collective-permute-start(bf16[1024,512]{1,0:T(8,128)(2,1)} %bitcast.147), channel_id=1, source_target_pairs={{0,8},{4,12},{8,0},{12,4},{16,24},{20,28},{24,16},{28,20},{1,9},{5... | collective-permute-start | bytes 3145736 | tf_op jit(solution)/shard_map/ppermute | solution.py:517
  339.1 26.3 %collective-permute-start.26 = (bf16[1024,512]{1,0:T(8,128)(2,1)}, bf16[1024,512]{1,0:T(8,128)(2,1)}, u32[]{:S(2)}, u32[]{:S(2)}) collective-permute-start(bf16[1024,512]{1,0:T(8,128)(2,1)} %dynamic-slice_bitcast_fusion.1), channel_id=1, source_target_pairs={{0,2},{1,3},{2,0},{3,1},{4,6},{5,7},{6,4},{7,5},{8,10},{9,11},{10,... | collective-permute-start | bytes 3145736 | tf_op jit(solution)/shard_map/ppermute | solution.py:517
  348.3 39.2 %collective-permute-start.36 = (bf16[1024,512]{1,0:T(8,128)(2,1)}, bf16[1024,512]{1,0:T(8,128)(2,1)}, u32[]{:S(2)}, u32[]{:S(2)}) collective-permute-start(bf16[1024,512]{1,0:T(8,128)(2,1)} %dynamic-slice_bitcast_fusion), channel_id=1, source_target_pairs={{0,2},{1,3},{2,0},{3,1},{4,6},{5,7},{6,4},{7,5},{8,10},{9,11},{10,... | collective-permute-start | bytes 3145736 | tf_op jit(solution)/shard_map/ppermute | solution.py:517
  349.2 27.6 %collective-permute-start.29 = (bf16[512,512]{1,0:T(8,128)(2,1)}, bf16[512,512]{1,0:T(8,128)(2,1)}, u32[]{:S(2)}, u32[]{:S(2)}) collective-permute-start(bf16[512,512]{1,0:T(8,128)(2,1)} %get-tuple-element.298), channel_id=1, source_target_pairs={{0,8},{4,12},{8,0},{12,4},{16,24},{20,28},{24,16},{28,20},{1,9},{5... | collective-permute-start | bytes 1572872 | tf_op jit(solution)/shard_map/ppermute | solution.py:517
  350.4 26.4 %collective-permute-start.30 = (bf16[512,512]{1,0:T(8,128)(2,1)}, bf16[512,512]{1,0:T(8,128)(2,1)}, u32[]{:S(2)}, u32[]{:S(2)}) collective-permute-start(bf16[512,512]{1,0:T(8,128)(2,1)} %get-tuple-element.299), channel_id=1, source_target_pairs={{0,4},{4,0},{8,12},{12,8},{16,20},{20,16},{24,28},{28,24},{1,5},{5... | collective-permute-start | bytes 1572872 | tf_op jit(solution)/shard_map/ppermute | solution.py:517
  350.9 26.1 %collective-permute-start.32 = (bf16[256,1024]{1,0:T(8,128)(2,1)}, bf16[256,1024]{1,0:T(8,128)(2,1)}, u32[]{:S(2)}, u32[]{:S(2)}) collective-permute-start(bf16[256,1024]{1,0:T(8,128)(2,1)} %get-tuple-element.301), channel_id=1, source_target_pairs={{0,16},{4,20},{8,24},{12,28},{16,0},{20,4},{24,8},{28,12},{1,17},{... | collective-permute-start | bytes 1572872 | tf_op jit(solution)/shard_map/ppermute | solution.py:517
  365.4 11.4 %collective-permute-start.31 = (bf16[416,512]{1,0:T(8,128)(2,1)}, bf16[416,512]{1,0:T(8,128)(2,1)}, u32[]{:S(2)}, u32[]{:S(2)}) collective-permute-start(bf16[416,512]{1,0:T(8,128)(2,1)} %pad_maximum_fusion.8), channel_id=1, source_target_pairs={{0,4},{4,0},{8,12},{12,8},{16,20},{20,16},{24,28},{28,24},{1,5},{5... | collective-permute-start | bytes 1277960 | tf_op jit(solution)/shard_map/ppermute | solution.py:517
  381.6 19.0 %collective-permute-start.33 = (bf16[256,512]{1,0:T(8,128)(2,1)}, bf16[256,512]{1,0:T(8,128)(2,1)S(1)}, u32[]{:S(2)}, u32[]{:S(2)}) collective-permute-start(bf16[256,512]{1,0:T(8,128)(2,1)} %get-tuple-element.311), channel_id=1, source_target_pairs={{0,16},{4,20},{8,24},{12,28},{16,0},{20,4},{24,8},{28,12},{1,17},{... | collective-permute-start | bytes 786440 | tf_op jit(solution)/shard_map/ppermute | solution.py:517
  382.6 22.7 %collective-permute-start.34 = (bf16[256,512]{1,0:T(8,128)(2,1)}, bf16[256,512]{1,0:T(8,128)(2,1)S(1)}, u32[]{:S(2)}, u32[]{:S(2)}) collective-permute-start(bf16[256,512]{1,0:T(8,128)(2,1)} %get-tuple-element.312), channel_id=1, source_target_pairs={{0,16},{4,20},{8,24},{12,28},{16,0},{20,4},{24,8},{28,12},{1,17},{... | collective-permute-start | bytes 786440 | tf_op jit(solution)/shard_map/ppermute | solution.py:517
  384.5 20.8 %collective-permute-start.35 = (bf16[256,512]{1,0:T(8,128)(2,1)}, bf16[256,512]{1,0:T(8,128)(2,1)S(1)}, u32[]{:S(2)}, u32[]{:S(2)}) collective-permute-start(bf16[256,512]{1,0:T(8,128)(2,1)} %get-tuple-element.313), channel_id=1, source_target_pairs={{0,8},{4,12},{8,0},{12,4},{16,24},{20,28},{24,16},{28,20},{1,9},{5... | collective-permute-start | bytes 786440 | tf_op jit(solution)/shard_map/ppermute | solution.py:517
  411.4 10.6 %collective-permute-start.42 = (bf16[176,512]{1,0:T(8,128)(2,1)}, bf16[176,512]{1,0:T(8,128)(2,1)S(1)}, u32[]{:S(2)}, u32[]{:S(2)}) collective-permute-start(bf16[176,512]{1,0:T(8,128)(2,1)} %get-tuple-element.332), channel_id=1, source_target_pairs={{0,16},{4,20},{8,24},{12,28},{16,0},{20,4},{24,8},{28,12},{1,17},{... | collective-permute-start | bytes 540680 | tf_op jit(solution)/shard_map/ppermute | solution.py:517
  (82 other events, 832.7 us)

commit v6 on v5

--- a/solution.py
+++ b/solution.py
@@ -54,7 +54,7 @@
             h_ref[n, :, lanes] = h[n]
         return 0
 
-    lax.fori_loop(0, width // LANES, tile_step, 0, unroll=2)
+    lax.fori_loop(0, width // LANES, tile_step, 0, unroll=4)
 
 
 def starts_kernel(chunk, step_ref, yg_ref, spread_ref, rate_ref, q_ref):
@@ -76,7 +76,7 @@
             q_ref[n, :, lanes] = q[n]
         return 0
 
-    lax.fori_loop(0, width // LANES, tile_step, 0, unroll=2)
+    lax.fori_loop(0, width // LANES, tile_step, 0, unroll=4)
 
 
 def spread_spec(chunk, count, seqs, part, at):
@@ -178,7 +178,7 @@
             state_ref[n, :, lanes] = h[n]
         return 0
 
-    lax.fori_loop(0, width // LANES, tile_step, 0, unroll=2)
+    lax.fori_loop(0, width // LANES, tile_step, 0, unroll=4)
 
 
 def forward(arrays, skip, carried, filled, shapes, chunk, first, last):
@@ -284,7 +284,7 @@
         skipg_ref[:, lanes] = skipg
         return 0
 
-    lax.fori_loop(0, width // LANES, tile_step, 0, unroll=2)
+    lax.fori_loop(0, width // LANES, tile_step, 0, unroll=4)
     wide = 2 * span
     row = lax.broadcasted_iota(jnp.int32, (2 * seqs, wide), 0)
     col = lax.broadcasted_iota(jnp.int32, (2 * seqs, wide), 1)
@@ -384,7 +384,7 @@
             sums_ref[k, :, lanes] = sums[k]
         return 0
 
-    lax.fori_loop(0, width // LANES, tile_step, 0, unroll=2)
+    lax.fori_loop(0, width // LANES, tile_step, 0, unroll=4)
 
     @pl.when(block == 0)
     def _():

time: 432 us -> 430 us (level)
  transfers between devices with their start and end apart: 43 -> 43, of which waited for: 17 -> 17; matrix products, arithmetic and copies ran while one was open for 27% -> 28% of each run, Pallas kernels for 37% -> 36%
where the time goes in v6:
time: 430 us; the launch traced here: 424 us
  Pallas kernels  159 us (37%)
  starting transfers between devices  57.8 us (13%)
  other arithmetic  55.3 us (13%)
  matrix products  52.2 us (12%)
  waiting for transfers between devices  49.7 us (12%)
  local copies, waits for them, and re-layouts  47.3 us (11%)
    dot_general x14, matrix products, dot(): return lax.dot_general(a, b, dims, preferred_element_type=out)  52.2 us
    ppermute x32, waiting for transfers between devices, swapped(): return lax.ppermute(value, axis, [(i, i ^ 1 << bit) for i in range(count)])  48.6 us
    pallas_call x1, Pallas kernels, backward(): pl.pallas_call(functools.partial(bwd_kernel, chunk), grid=(grid,), in_spe...  38.9 us
    ppermute x32, starting transfers between devices, swapped(): return lax.ppermute(value, axis, [(i, i ^ 1 << bit) for i in range(count)])  34.3 us
    pallas_call x2, Pallas kernels, forward(): pl.pallas_call(functools.partial(fwd_kernel, chunk), grid=(last - first,)...  32.6 us
    pallas_call x2, Pallas kernels, product_sides(): pl.pallas_call(functools.partial(product_kernel, len(pairs)), grid_spec=p...  24.2 us
    ppermute x8, starting transfers between devices, moved(): lax.ppermute(value, axis, [(i, i + distance) for i in range(count) if 0 <...  20.1 us
    pallas_call x1, Pallas kernels, local_ends(): pl.pallas_call(functools.partial(ends_kernel, chunk), grid=(grid,), in_sp...  19.6 us
  transfers between devices with their start and end apart: 43, of which 17 were waited for; matrix products, arithmetic and copies ran while one was open for 28% of the time, Pallas kernels for 36%

profile of v6, /device:TPU:0, one launch (start us, length us, event | category | flops | bytes accessed | tf_op | source)
XLA Modules:
  0.0 423.8 jit_solution(17929388174487364391)
XLA Ops:
  6.4 16.3 %fusion.49 = (bf16[2048,1,1024]{2,1,0:T(2,128)(2,1)S(1)}, bf16[2048,1,1024]{2,1,0:T(2,128)(2,1)S(1)}) fusion(bf16[2048,2,1024]{2,1,0:T(2,128)(2,1)} %param.14), kind=kLoop, calls=%fused_computation.190 | loop fusion | bytes 16777216 | tf_op jit(solution)/shard_map/slice | solution.py:794
  22.7 5.9 %copy_bitcast_fusion = (bf16[2048,1024]{1,0:T(8,128)(2,1)}, bf16[2048,1024]{1,0:T(8,128)(2,1)}) fusion(bf16[2048,1,1024]{2,1,0:T(2,128)(2,1)S(1)} %get-tuple-element.374, bf16[2048,1,1024]{2,1,0:T(2,128)(2,1)S(1)} %get-tuple-element.375), kind=kLoop, calls=%fused_computation.16 | loop fusion | bytes 16777216 | tf_op jit(solution)/shard_map/squeeze | solution.py:794
  37.6 3.8 collective-permute-start.3
  41.4 4.7 %fusion.55.in_ref = bf16[1024,1024]{1,0:T(8,128)(2,1)S(1)} fusion(bf16[1024,2048]{1,0:T(8,128)(2,1)S(1)} %fusion.2, bf16[2048,1024]{1,0:T(8,128)(2,1)S(1)} %copy-done.6), kind=kOutput, calls=%fused_computation.196 | convolution fusion | flops 4294967296 | bytes 10485760 | tf_op jit(solution)/shard_map/dot_general | solution.py:508
  47.7 3.8 multiply_convert_fusion
  58.4 4.5 %fusion.56.gate_ref = f32[1024,1024]{1,0:T(8,128)S(1)} fusion(bf16[1024,2048]{1,0:T(8,128)(2,1)S(1)} %fusion.2, bf16[2048,1024]{1,0:T(8,128)(2,1)S(1)} %copy-done.13), kind=kOutput, calls=%fused_computation.197 | convolution fusion | flops 4294967296 | bytes 12582912 | tf_op jit(solution)/shard_map/dot_general | solution.py:508
  67.6 4.7 %bitcast_reduce_fusion = (f32[8,1024]{1,0:T(8,128)S(1)}, f32[1024,1024]{1,0:T(8,128)}) fusion(f32[1024]{0:T(1024)S(1)} %convert_element_type.288, bf16[128,1024]{1,0:T(8,128)(2,1)S(1)} %copy-done.41, f32[160,1024]{1,0:T(8,128)S(1)} %convert_add_fusion.4), kind=kOutput, calls=%fused_computation.18 | convolution fusion | flops 276815872 | bytes 4755456 | tf_op jit(solution)/shard_map/dot_general | solution.py:508
  73.1 19.6 %local_ends.1 = (f32[16,8,1024]{2,1,0:T(8,128)}, f32[128,32,8,128]{3,2,1,0:T(8,128)}, bf16[128,256,128]{2,1,0:T(8,128)(2,1)}) custom-call(f32[1024,1024]{1,0:T(8,128)} %get-tuple-element.437.step_ref, bf16[1024,1024]{1,0:T(8,128)(2,1)} %copy-done, f32[32,1024]{1,0:T(8,128)} %slice.282.rows_ref, f32[16,8,1024]{2,1,0:T(8,128)} %broadcast_in_dim.8.rate_ref), custom_call_target="tpu_custom_call" | custom-call | flops 16777216 | bytes 16777216 | tf_op jit(solution)/shard_map/local_ends/pallas_call | solution.py:105
  102.0 7.1 %multiply_multiply_fusion = (f32[1024,1024]{1,0:T(8,128)}, f32[1024,1024]{1,0:T(8,128)}) fusion(f32[1024,1024]{1,0:T(8,128)S(1)} %fusion.56.gate_ref, bf16[1024,2048]{1,0:T(8,128)(2,1)S(1)} %pad_maximum_fusion.1, bf16[2048,1024]{1,0:T(8,128)(2,1)S(1)} %copy-done.23), kind=kOutput, calls=%fused_computation.22 | convolution fusion | flops 4300210176 | bytes 20971520 | tf_op jit(solution)/shard_map/dot_general | solution.py:508
  112.9 14.6 %local_starts.1 = f32[16,8,1024]{2,1,0:T(8,128)} custom-call(f32[1024,1024]{1,0:T(8,128)} %get-tuple-element.437.step_ref, f32[1024,1024]{1,0:T(8,128)} %get-tuple-element.187.yg_ref, f32[128,32,8,128]{3,2,1,0:T(8,128)} %get-tuple-element.188.spread_ref, f32[16,8,1024]{2,1,0:T(8,128)} %broadcast_in_dim.8.rate_ref), custom_call_target="tpu_custom_call" | custom-call | flops 16777216 | bytes 16777216 | tf_op jit(solution)/shard_map/local_starts/pallas_call | solution.py:127
  127.9 3.8 collective-permute-start.11
  145.5 16.2 %scan_forward.2 = (f32[16,8,1024]{2,1,0:T(8,128)}, bf16[128,8,128,128]{3,2,1,0:T(8,128)(2,1)}, bf16[8,16,8,1024]{3,2,1,0:T(8,128)(2,1)}, bf16[1024,1024]{1,0:T(8,128)(2,1)}, bf16[1024,1024]{1,0:T(8,128)(2,1)}) custom-call(f32[1024,1024]{1,0:T(8,128)} %get-tuple-element.437.step_ref, bf16[1024,1024]{1,0:T(8,128)(2,1)} %copy-done, ...), custom_call_target="tpu_custom_call", output_to_operand_aliasing={{0}: (8, {})} | custom-call | flops 8388608 | bytes 8388608 | tf_op jit(solution)/shard_map/scan_forward/pallas_call | solution.py:193
  163.5 16.4 %scan_forward.3 = (f32[16,8,1024]{2,1,0:T(8,128)}, bf16[128,8,128,128]{3,2,1,0:T(8,128)(2,1)}, bf16[8,16,8,1024]{3,2,1,0:T(8,128)(2,1)}, bf16[1024,1024]{1,0:T(8,128)(2,1)}, bf16[1024,1024]{1,0:T(8,128)(2,1)}) custom-call(f32[1024,1024]{1,0:T(8,128)} %get-tuple-element.437.step_ref, ...), custom_call_target="tpu_custom_call", output_to_operand_aliasing={{0}: (8, {}), {1}: (9, {}), {2}: (10, {}), {3}: (11, {}), {... | custom-call | flops 8388608 | bytes 8388608 | tf_op jit(solution)/shard_map/scan_forward/pallas_call | solution.py:193
  180.6 5.4 %fusion.58 = bf16[1024,1024]{1,0:T(8,128)(2,1)} fusion(bf16[1024,1024]{1,0:T(8,128)(2,1)S(1)} %copy-done.33, bf16[1024,1024]{1,0:T(8,128)(2,1)} %get-tuple-element.231.refs_1_), kind=kOutput, calls=%fused_computation.199 | convolution fusion | flops 2147483648 | bytes 6291456 | tf_op jit(solution)/shard_map/dot_general | solution.py:508
  186.0 3.8 fusion.57
  195.0 3.7 fusion.60.refs_2_
  198.7 3.8 fusion.59.refs_0_
  202.5 38.9 %scan_backward.1 = (f32[18,1024]{1,0:T(8,128)}, bf16[1024,1024]{1,0:T(8,128)(2,1)}, f32[1024,1024]{1,0:T(8,128)}, f32[160,1024]{1,0:T(8,128)}) custom-call(f32[1024,1024]{1,0:T(8,128)} %get-tuple-element.437.step_ref, bf16[1024,1024]{1,0:T(8,128)(2,1)} %copy-done, f32[1024,1024]{1,0:T(8,128)} %get-tuple-element.187.yg_ref, ...), custom_call_target="tpu_custom_call" | custom-call | flops 16777216 | bytes 16777216 | tf_op jit(solution)/shard_map/scan_backward/pallas_call | solution.py:321
  242.2 6.5 %merge_messages.5 = (bf16[512,1024]{1,0:T(8,128)(2,1)}, bf16[512,1024]{1,0:T(8,128)(2,1)}, bf16[512,1024]{1,0:T(8,128)(2,1)}, bf16[512,1024]{1,0:T(8,128)(2,1)}) custom-call(s32[2]{0:T(128)} %get-tuple-element.440.bits_ref, bf16[1024,1024]{1,0:T(8,128)(2,1)} %fusion.59.refs_0_, bf16[1024,1024]{1,0:T(8,128)(2,1)} %collective-permute-done.15.refs_1_, ...), custom_call_target="tpu_custom_call" | custom-call | flops 1024 | bytes 1024 | tf_op jit(solution)/shard_map/merge_messages/pallas_call | solution.py:701
  251.3 9.6 %product_sides.2 = (bf16[2,1024,512]{2,1,0:T(8,128)(2,1)}, bf16[2,1024,512]{2,1,0:T(8,128)(2,1)}) custom-call(s32[1]{0:T(128)} %bitcast.21.core_ref, bf16[1024,1024]{1,0:T(8,128)(2,1)} %get-tuple-element.241.refs_0_, bf16[2048,1024]{1,0:T(8,128)(2,1)} %refs_1_.1), custom_call_target="tpu_custom_call" | custom-call | flops 1024 | bytes 1024 | tf_op jit(solution)/shard_map/product_sides/pallas_call | solution.py:486
  261.7 9.7 %conv_backward.1 = (bf16[1056,1024]{1,0:T(8,128)(2,1)}, f32[24,1024]{1,0:T(8,128)}, f32[5,8,1024]{2,1,0:T(8,128)}) custom-call(bf16[160,1024]{1,0:T(8,128)(2,1)} %add_convert_fusion.2.proj_ref, bf16[160,1024]{1,0:T(8,128)(2,1)} %weight_ref.1, f32[1024,1024]{1,0:T(8,128)} %get-tuple-element.249.part_ref, f32[1024,1024]{1,0:T(8,128)} %get-tuple-element.373.conv_ref, ...), custom_call_target="tpu_custom_call" | custom-call | flops 1048576 | bytes 1048576 | tf_op jit(solution)/shard_map/conv_backward/pallas_call | solution.py:415
  274.7 4.8 %fusion.16 = bf16[2048,512]{1,0:T(8,128)(2,1)S(1)} fusion(bf16[1056,2048]{1,0:T(8,128)(2,1)S(1)} %bitcast.165, bf16[1056,1024]{1,0:T(8,128)(2,1)} %get-tuple-element.264), kind=kOutput, calls=%fused_computation.47 | convolution fusion | flops 2214592512 | bytes 7503872 | tf_op jit(solution)/shard_map/dot_general | solution.py:508
  279.4 5.5 %fusion.18 = bf16[2048,512]{1,0:T(8,128)(2,1)S(1)} fusion(bf16[1056,2048]{1,0:T(8,128)(2,1)} %copy-done.66, bf16[1056,1024]{1,0:T(8,128)(2,1)S(1)} %copy-done.34), kind=kOutput, calls=%fused_computation.49 | convolution fusion | flops 2214592512 | bytes 7503872 | tf_op jit(solution)/shard_map/dot_general | solution.py:508
  288.0 4.1 merge_messages.6
  312.2 14.6 %product_sides.3 = (bf16[2,1024,512]{2,1,0:T(8,128)(2,1)}, bf16[2,1024,512]{2,1,0:T(8,128)(2,1)}) custom-call(s32[1]{0:T(128)} %bitcast.21.core_ref, bf16[1024,1024]{1,0:T(8,128)(2,1)} %pad_maximum_fusion.6.refs_0_, bf16[1024,1024]{1,0:T(8,128)(2,1)} %get-tuple-element.231.refs_1_, bf16[2048,1024]{1,0:T(8,128)(2,1)} %get-tuple-element.175.refs_2_, ...), custom_call_target="tpu_custom_call" | custom-call | flops 1024 | bytes 1024 | tf_op jit(solution)/shard_map/product_sides/pallas_call | solution.py:486
  326.9 6.9 %collective-permute-done.24.refs_3_ = bf16[1024,512]{1,0:T(8,128)(2,1)} collective-permute-done((bf16[1024,512]{1,0:T(8,128)(2,1)}, bf16[1024,512]{1,0:T(8,128)(2,1)}, u32[]{:S(2)}, u32[]{:S(2)}) %collective-permute-start.24) | collective-permute-done | bytes 1048608 | tf_op jit(solution)/shard_map/ppermute | solution.py:517
  338.1 3.9 merge_messages.7
  351.8 11.5 %collective-permute-done.26 = bf16[1024,512]{1,0:T(8,128)(2,1)} collective-permute-done((bf16[1024,512]{1,0:T(8,128)(2,1)}, bf16[1024,512]{1,0:T(8,128)(2,1)}, u32[]{:S(2)}, u32[]{:S(2)}) %collective-permute-start.26) | collective-permute-done | bytes 1048608 | tf_op jit(solution)/shard_map/ppermute | solution.py:517
  367.9 6.8 %collective-permute-done.31.refs_5_ = bf16[416,512]{1,0:T(8,128)(2,1)} collective-permute-done((bf16[416,512]{1,0:T(8,128)(2,1)}, bf16[416,512]{1,0:T(8,128)(2,1)}, u32[]{:S(2)}, u32[]{:S(2)}) %collective-permute-start.31) | collective-permute-done | bytes 426016 | tf_op jit(solution)/shard_map/ppermute | solution.py:517
  385.5 4.5 %fusion.12 = (f32[512]{0:T(512)S(1)}, bf16[128,8,512]{2,1,0:T(8,128)(2,1)S(1)}, bf16[128,8,512]{2,1,0:T(8,128)(2,1)S(1)}) fusion(bf16[1024,512]{1,0:T(8,128)(2,1)} %collective-permute-done.36, f32[1024]{0:T(1024)S(1)} %copy-done.55, bf16[2,1024,512]{2,1,0:T(8,128)(2,1)S(1)} %copy-done.17, s32[]{:T(128)S(6)} %select_n.192, ...), kind=kLoop, calls=%fused_computation.33 | loop fusion | flops 10485248 | bytes 8404996 | tf_op jit(solution)/shard_map/reduce_sum | solution.py:965
  391.3 7.1 %collective-permute-done.33 = bf16[256,512]{1,0:T(8,128)(2,1)S(1)} collective-permute-done((bf16[256,512]{1,0:T(8,128)(2,1)}, bf16[256,512]{1,0:T(8,128)(2,1)S(1)}, u32[]{:S(2)}, u32[]{:S(2)}) %collective-permute-start.33) | collective-permute-done | bytes 262176 | tf_op jit(solution)/shard_map/ppermute | solution.py:517
  398.4 4.7 %collective-permute-done.34 = bf16[256,512]{1,0:T(8,128)(2,1)S(1)} collective-permute-done((bf16[256,512]{1,0:T(8,128)(2,1)}, bf16[256,512]{1,0:T(8,128)(2,1)S(1)}, u32[]{:S(2)}, u32[]{:S(2)}) %collective-permute-start.34) | collective-permute-done | bytes 262176 | tf_op jit(solution)/shard_map/ppermute | solution.py:517
  (329 shorter events, 144.1 us)
Async XLA Ops:
  3.4 26.3 %collective-permute-start = (bf16[1024,512]{1,0:T(8,128)(2,1)}, bf16[1024,512]{1,0:T(8,128)(2,1)S(1)}, u32[]{:S(2)}, u32[]{:S(2)}) collective-permute-start(bf16[1024,512]{1,0:T(8,128)(2,1)} %bitcast.129), channel_id=1, source_target_pairs={{0,2},{1,3},{2,0},{3,1},{4,6},{5,7},{6,4},{7,5},{8,10},{9,11},{10,... | collective-permute-start | bytes 3145736 | tf_op jit(solution)/shard_map/ppermute | solution.py:517
  6.4 23.5 %collective-permute-start.2 = (bf16[1024,512]{1,0:T(8,128)(2,1)}, bf16[1024,512]{1,0:T(8,128)(2,1)S(1)}, u32[]{:S(2)}, u32[]{:S(2)}) collective-permute-start(bf16[1024,512]{1,0:T(8,128)(2,1)} %bitcast.129), channel_id=1, source_target_pairs={{0,1},{1,0},{2,3},{3,2},{4,5},{5,4},{6,7},{7,6},{8,9},{9,8},{10,11... | collective-permute-start | bytes 3145736 | tf_op jit(solution)/shard_map/ppermute | solution.py:517
  37.6 8.6 %collective-permute-start.3 = (bf16[32,2048]{1,0:T(8,128)(2,1)S(1)}, bf16[32,2048]{1,0:T(8,128)(2,1)S(1)}, u32[]{:S(2)}, u32[]{:S(2)}) collective-permute-start(bf16[32,2048]{1,0:T(8,128)(2,1)S(1)} %slice.272), channel_id=1, source_target_pairs={{0,4},{4,8},{8,12},{12,16},{16,20},{20,24},{24,28},{1,5},{5,9},{9,... | collective-permute-start | bytes 393224 | tf_op jit(solution)/shard_map/ppermute | solution.py:522
  55.3 9.8 %collective-permute-start.5 = (bf16[160,1024]{1,0:T(8,128)(2,1)S(1)}, bf16[160,1024]{1,0:T(8,128)(2,1)S(1)}, u32[]{:S(2)}, u32[]{:S(2)}) collective-permute-start(bf16[160,1024]{1,0:T(8,128)(2,1)S(1)} %get-tuple-element.370), channel_id=1, source_target_pairs={{0,2},{1,3},{2,0},{3,1},{4,6},{5,7},{6,4},{7,5},{8,10},{9,11},{10,... | collective-permute-start | bytes 983048 | tf_op jit(solution)/shard_map/ppermute | solution.py:517
  65.1 27.6 %collective-permute-start.7 = (bf16[1024,512]{1,0:T(8,128)(2,1)S(1)}, bf16[1024,512]{1,0:T(8,128)(2,1)S(1)}, u32[]{:S(2)}, u32[]{:S(2)}) collective-permute-start(bf16[1024,512]{1,0:T(8,128)(2,1)S(1)} %bitcast.137), channel_id=1, source_target_pairs={{0,2},{1,3},{2,0},{3,1},{4,6},{5,7},{6,4},{7,5},{8,10},{9,11},{10,... | collective-permute-start | bytes 3145736 | tf_op jit(solution)/shard_map/ppermute | solution.py:517
  66.7 31.2 %collective-permute-start.9 = (bf16[1024,512]{1,0:T(8,128)(2,1)S(1)}, bf16[1024,512]{1,0:T(8,128)(2,1)}, u32[]{:S(2)}, u32[]{:S(2)}) collective-permute-start(bf16[1024,512]{1,0:T(8,128)(2,1)S(1)} %bitcast.138), channel_id=1, source_target_pairs={{0,1},{1,0},{2,3},{3,2},{4,5},{5,4},{6,7},{7,6},{8,9},{9,8},{10,11... | collective-permute-start | bytes 3145736 | tf_op jit(solution)/shard_map/ppermute | solution.py:517
  94.4 14.7 %collective-permute-start.6 = (bf16[18,8,1024]{2,1,0:T(8,128)(2,1)S(1)}, bf16[18,8,1024]{2,1,0:T(8,128)(2,1)S(1)}, u32[]{:S(2)}, u32[]{:S(2)}) collective-permute-start(bf16[18,8,1024]{2,1,0:T(8,128)(2,1)S(1)} %pad_maximum_fusion.10), channel_id=1, source_target_pairs={{0,4},{4,8},{8,12},{12,16},{16,20},{20,24},{24,28},{1,5},{5,9},{9,... | collective-permute-start | bytes 884744 | tf_op jit(solution)/shard_map/ppermute | solution.py:522
  109.4 18.1 %collective-permute-start.10 = (bf16[18,8,1024]{2,1,0:T(8,128)(2,1)S(1)}, bf16[18,8,1024]{2,1,0:T(8,128)(2,1)S(1)}, u32[]{:S(2)}, u32[]{:S(2)}) collective-permute-start(bf16[18,8,1024]{2,1,0:T(8,128)(2,1)S(1)} %pad_maximum_fusion.13), channel_id=1, source_target_pairs={{0,8},{4,12},{8,16},{12,20},{16,24},{20,28},{1,9},{5,13},{9,17},{1... | collective-permute-start | bytes 884744 | tf_op jit(solution)/shard_map/ppermute | solution.py:522
  127.9 14.0 %collective-permute-start.11 = (bf16[18,8,1024]{2,1,0:T(8,128)(2,1)S(1)}, bf16[18,8,1024]{2,1,0:T(8,128)(2,1)S(1)}, u32[]{:S(2)}, u32[]{:S(2)}) collective-permute-start(bf16[18,8,1024]{2,1,0:T(8,128)(2,1)S(1)} %pad_maximum_fusion.14), channel_id=1, source_target_pairs={{0,16},{4,20},{8,24},{12,28},{1,17},{5,21},{9,25},{13,29},{2,18},{... | collective-permute-start | bytes 884744 | tf_op jit(solution)/shard_map/ppermute | solution.py:522
  132.8 10.5 %collective-permute-start.12 = (bf16[18,8,1024]{2,1,0:T(8,128)(2,1)S(1)}, bf16[18,8,1024]{2,1,0:T(8,128)(2,1)S(1)}, u32[]{:S(2)}, u32[]{:S(2)}) collective-permute-start(bf16[18,8,1024]{2,1,0:T(8,128)(2,1)S(1)} %pad_maximum_fusion.9), channel_id=1, source_target_pairs={{4,0},{8,4},{12,8},{16,12},{20,16},{24,20},{28,24},{5,1},{9,5},{13... | collective-permute-start | bytes 884744 | tf_op jit(solution)/shard_map/ppermute | solution.py:522
  143.6 18.1 %collective-permute-start.13 = (bf16[18,8,1024]{2,1,0:T(8,128)(2,1)S(1)}, bf16[18,8,1024]{2,1,0:T(8,128)(2,1)S(1)}, u32[]{:S(2)}, u32[]{:S(2)}) collective-permute-start(bf16[18,8,1024]{2,1,0:T(8,128)(2,1)S(1)} %pad_maximum_fusion.15), channel_id=1, source_target_pairs={{8,0},{12,4},{16,8},{20,12},{24,16},{28,20},{9,1},{13,5},{17,9},{2... | collective-permute-start | bytes 884744 | tf_op jit(solution)/shard_map/ppermute | solution.py:522
  162.1 18.5 %collective-permute-start.14 = (bf16[18,8,1024]{2,1,0:T(8,128)(2,1)S(1)}, bf16[18,8,1024]{2,1,0:T(8,128)(2,1)S(1)}, u32[]{:S(2)}, u32[]{:S(2)}) collective-permute-start(bf16[18,8,1024]{2,1,0:T(8,128)(2,1)S(1)} %pad_maximum_fusion.16), channel_id=1, source_target_pairs={{16,0},{20,4},{24,8},{28,12},{17,1},{21,5},{25,9},{29,13},{18,2},{... | collective-permute-start | bytes 884744 | tf_op jit(solution)/shard_map/ppermute | solution.py:522
  190.8 50.6 %collective-permute-start.15 = (bf16[1024,1024]{1,0:T(8,128)(2,1)}, bf16[1024,1024]{1,0:T(8,128)(2,1)}, u32[]{:S(2)}, u32[]{:S(2)}) collective-permute-start(bf16[1024,1024]{1,0:T(8,128)(2,1)} %fusion.57), channel_id=1, source_target_pairs={{0,4},{4,0},{8,12},{12,8},{16,20},{20,16},{24,28},{28,24},{1,5},{5... | collective-permute-start | bytes 6291464 | tf_op jit(solution)/shard_map/ppermute | solution.py:517
  192.3 49.2 %collective-permute-start.16 = (bf16[1024,1024]{1,0:T(8,128)(2,1)}, bf16[1024,1024]{1,0:T(8,128)(2,1)}, u32[]{:S(2)}, u32[]{:S(2)}) collective-permute-start(bf16[1024,1024]{1,0:T(8,128)(2,1)} %fusion.58), channel_id=1, source_target_pairs={{0,8},{4,12},{8,0},{12,4},{16,24},{20,28},{24,16},{28,20},{1,9},{5... | collective-permute-start | bytes 6291464 | tf_op jit(solution)/shard_map/ppermute | solution.py:517
  248.7 25.9 %collective-permute-start.19 = (bf16[512,1024]{1,0:T(8,128)(2,1)}, bf16[512,1024]{1,0:T(8,128)(2,1)}, u32[]{:S(2)}, u32[]{:S(2)}) collective-permute-start(bf16[512,1024]{1,0:T(8,128)(2,1)} %get-tuple-element.246), channel_id=1, source_target_pairs={{0,8},{4,12},{8,0},{12,4},{16,24},{20,28},{24,16},{28,20},{1,9},{5... | collective-permute-start | bytes 3145736 | tf_op jit(solution)/shard_map/ppermute | solution.py:517
  248.7 25.9 %collective-permute-start.20 = (bf16[512,1024]{1,0:T(8,128)(2,1)}, bf16[512,1024]{1,0:T(8,128)(2,1)}, u32[]{:S(2)}, u32[]{:S(2)}) collective-permute-start(bf16[512,1024]{1,0:T(8,128)(2,1)} %get-tuple-element.247), channel_id=1, source_target_pairs={{0,4},{4,0},{8,12},{12,8},{16,20},{20,16},{24,28},{28,24},{1,5},{5... | collective-permute-start | bytes 3145736 | tf_op jit(solution)/shard_map/ppermute | solution.py:517
  250.2 10.7 %collective-permute-start.18 = (bf16[160,1024]{1,0:T(8,128)(2,1)}, bf16[160,1024]{1,0:T(8,128)(2,1)S(1)}, u32[]{:S(2)}, u32[]{:S(2)}) collective-permute-start(bf16[160,1024]{1,0:T(8,128)(2,1)} %get-tuple-element.360), channel_id=1, source_target_pairs={{0,2},{1,3},{2,0},{3,1},{4,6},{5,7},{6,4},{7,5},{8,10},{9,11},{10,... | collective-permute-start | bytes 983048 | tf_op jit(solution)/shard_map/ppermute | solution.py:517
  271.4 16.5 %collective-permute-start.22 = (f32[24,1024]{1,0:T(8,128)}, f32[24,1024]{1,0:T(8,128)S(1)}, u32[]{:S(2)}, u32[]{:S(2)}) collective-permute-start(f32[24,1024]{1,0:T(8,128)} %get-tuple-element.262), channel_id=1, source_target_pairs={{4,0},{8,4},{12,8},{16,12},{20,16},{24,20},{28,24},{5,1},{9,5},{13... | collective-permute-start | bytes 294920 | tf_op jit(solution)/shard_map/ppermute | solution.py:522
  292.1 41.7 %collective-permute-start.21 = (bf16[2,1024,512]{2,1,0:T(8,128)(2,1)}, bf16[2,1024,512]{2,1,0:T(8,128)(2,1)}, u32[]{:S(2)}, u32[]{:S(2)}) collective-permute-start(bf16[2,1024,512]{2,1,0:T(8,128)(2,1)} %get-tuple-element.252), channel_id=1, source_target_pairs={{0,1},{1,0},{2,3},{3,2},{4,5},{5,4},{6,7},{7,6},{8,9},{9,8},{10,11... | collective-permute-start | bytes 6291464 | tf_op jit(solution)/shard_map/ppermute | solution.py:517
  294.2 32.6 %collective-permute-start.25 = (bf16[256,1024]{1,0:T(8,128)(2,1)}, bf16[256,1024]{1,0:T(8,128)(2,1)}, u32[]{:S(2)}, u32[]{:S(2)}) collective-permute-start(bf16[256,1024]{1,0:T(8,128)(2,1)} %get-tuple-element.268), channel_id=1, source_target_pairs={{0,16},{4,20},{8,24},{12,28},{16,0},{20,4},{24,8},{28,12},{1,17},{... | collective-permute-start | bytes 1572872 | tf_op jit(solution)/shard_map/ppermute | solution.py:517
  297.8 29.0 %collective-permute-start.23 = (bf16[1024,512]{1,0:T(8,128)(2,1)}, bf16[1024,512]{1,0:T(8,128)(2,1)}, u32[]{:S(2)}, u32[]{:S(2)}) collective-permute-start(bf16[1024,512]{1,0:T(8,128)(2,1)} %bitcast.148), channel_id=1, source_target_pairs={{0,4},{4,0},{8,12},{12,8},{16,20},{20,16},{24,28},{28,24},{1,5},{5... | collective-permute-start | bytes 3145736 | tf_op jit(solution)/shard_map/ppermute | solution.py:517
  298.3 35.4 %collective-permute-start.24 = (bf16[1024,512]{1,0:T(8,128)(2,1)}, bf16[1024,512]{1,0:T(8,128)(2,1)}, u32[]{:S(2)}, u32[]{:S(2)}) collective-permute-start(bf16[1024,512]{1,0:T(8,128)(2,1)} %bitcast.147), channel_id=1, source_target_pairs={{0,8},{4,12},{8,0},{12,4},{16,24},{20,28},{24,16},{28,20},{1,9},{5... | collective-permute-start | bytes 3145736 | tf_op jit(solution)/shard_map/ppermute | solution.py:517
  337.0 26.3 %collective-permute-start.26 = (bf16[1024,512]{1,0:T(8,128)(2,1)}, bf16[1024,512]{1,0:T(8,128)(2,1)}, u32[]{:S(2)}, u32[]{:S(2)}) collective-permute-start(bf16[1024,512]{1,0:T(8,128)(2,1)} %dynamic-slice_bitcast_fusion.1), channel_id=1, source_target_pairs={{0,2},{1,3},{2,0},{3,1},{4,6},{5,7},{6,4},{7,5},{8,10},{9,11},{10,... | collective-permute-start | bytes 3145736 | tf_op jit(solution)/shard_map/ppermute | solution.py:517
  346.1 39.3 %collective-permute-start.36 = (bf16[1024,512]{1,0:T(8,128)(2,1)}, bf16[1024,512]{1,0:T(8,128)(2,1)}, u32[]{:S(2)}, u32[]{:S(2)}) collective-permute-start(bf16[1024,512]{1,0:T(8,128)(2,1)} %dynamic-slice_bitcast_fusion), channel_id=1, source_target_pairs={{0,2},{1,3},{2,0},{3,1},{4,6},{5,7},{6,4},{7,5},{8,10},{9,11},{10,... | collective-permute-start | bytes 3145736 | tf_op jit(solution)/shard_map/ppermute | solution.py:517
  347.1 27.6 %collective-permute-start.29 = (bf16[512,512]{1,0:T(8,128)(2,1)}, bf16[512,512]{1,0:T(8,128)(2,1)}, u32[]{:S(2)}, u32[]{:S(2)}) collective-permute-start(bf16[512,512]{1,0:T(8,128)(2,1)} %get-tuple-element.298), channel_id=1, source_target_pairs={{0,8},{4,12},{8,0},{12,4},{16,24},{20,28},{24,16},{28,20},{1,9},{5... | collective-permute-start | bytes 1572872 | tf_op jit(solution)/shard_map/ppermute | solution.py:517
  348.3 26.4 %collective-permute-start.30 = (bf16[512,512]{1,0:T(8,128)(2,1)}, bf16[512,512]{1,0:T(8,128)(2,1)}, u32[]{:S(2)}, u32[]{:S(2)}) collective-permute-start(bf16[512,512]{1,0:T(8,128)(2,1)} %get-tuple-element.299), channel_id=1, source_target_pairs={{0,4},{4,0},{8,12},{12,8},{16,20},{20,16},{24,28},{28,24},{1,5},{5... | collective-permute-start | bytes 1572872 | tf_op jit(solution)/shard_map/ppermute | solution.py:517
  348.8 26.0 %collective-permute-start.32 = (bf16[256,1024]{1,0:T(8,128)(2,1)}, bf16[256,1024]{1,0:T(8,128)(2,1)}, u32[]{:S(2)}, u32[]{:S(2)}) collective-permute-start(bf16[256,1024]{1,0:T(8,128)(2,1)} %get-tuple-element.301), channel_id=1, source_target_pairs={{0,16},{4,20},{8,24},{12,28},{16,0},{20,4},{24,8},{28,12},{1,17},{... | collective-permute-start | bytes 1572872 | tf_op jit(solution)/shard_map/ppermute | solution.py:517
  363.3 11.4 %collective-permute-start.31 = (bf16[416,512]{1,0:T(8,128)(2,1)}, bf16[416,512]{1,0:T(8,128)(2,1)}, u32[]{:S(2)}, u32[]{:S(2)}) collective-permute-start(bf16[416,512]{1,0:T(8,128)(2,1)} %pad_maximum_fusion.8), channel_id=1, source_target_pairs={{0,4},{4,0},{8,12},{12,8},{16,20},{20,16},{24,28},{28,24},{1,5},{5... | collective-permute-start | bytes 1277960 | tf_op jit(solution)/shard_map/ppermute | solution.py:517
  379.4 19.0 %collective-permute-start.33 = (bf16[256,512]{1,0:T(8,128)(2,1)}, bf16[256,512]{1,0:T(8,128)(2,1)S(1)}, u32[]{:S(2)}, u32[]{:S(2)}) collective-permute-start(bf16[256,512]{1,0:T(8,128)(2,1)} %get-tuple-element.311), channel_id=1, source_target_pairs={{0,16},{4,20},{8,24},{12,28},{16,0},{20,4},{24,8},{28,12},{1,17},{... | collective-permute-start | bytes 786440 | tf_op jit(solution)/shard_map/ppermute | solution.py:517
  380.4 22.7 %collective-permute-start.34 = (bf16[256,512]{1,0:T(8,128)(2,1)}, bf16[256,512]{1,0:T(8,128)(2,1)S(1)}, u32[]{:S(2)}, u32[]{:S(2)}) collective-permute-start(bf16[256,512]{1,0:T(8,128)(2,1)} %get-tuple-element.312), channel_id=1, source_target_pairs={{0,16},{4,20},{8,24},{12,28},{16,0},{20,4},{24,8},{28,12},{1,17},{... | collective-permute-start | bytes 786440 | tf_op jit(solution)/shard_map/ppermute | solution.py:517
  382.4 20.8 %collective-permute-start.35 = (bf16[256,512]{1,0:T(8,128)(2,1)}, bf16[256,512]{1,0:T(8,128)(2,1)S(1)}, u32[]{:S(2)}, u32[]{:S(2)}) collective-permute-start(bf16[256,512]{1,0:T(8,128)(2,1)} %get-tuple-element.313), channel_id=1, source_target_pairs={{0,8},{4,12},{8,0},{12,4},{16,24},{20,28},{24,16},{28,20},{1,9},{5... | collective-permute-start | bytes 786440 | tf_op jit(solution)/shard_map/ppermute | solution.py:517
  409.2 10.8 %collective-permute-start.42 = (bf16[176,512]{1,0:T(8,128)(2,1)}, bf16[176,512]{1,0:T(8,128)(2,1)S(1)}, u32[]{:S(2)}, u32[]{:S(2)}) collective-permute-start(bf16[176,512]{1,0:T(8,128)(2,1)} %get-tuple-element.332), channel_id=1, source_target_pairs={{0,16},{4,20},{8,24},{12,28},{16,0},{20,4},{24,8},{28,12},{1,17},{... | collective-permute-start | bytes 540680 | tf_op jit(solution)/shard_map/ppermute | solution.py:517
  (82 other events, 832.7 us)

commit v7 on v6

--- a/solution.py
+++ b/solution.py
@@ -54,7 +54,7 @@
             h_ref[n, :, lanes] = h[n]
         return 0
 
-    lax.fori_loop(0, width // LANES, tile_step, 0, unroll=4)
+    lax.fori_loop(0, width // LANES, tile_step, 0, unroll=width // LANES)
 
 
 def starts_kernel(chunk, step_ref, yg_ref, spread_ref, rate_ref, q_ref):
@@ -76,7 +76,7 @@
             q_ref[n, :, lanes] = q[n]
         return 0
 
-    lax.fori_loop(0, width // LANES, tile_step, 0, unroll=4)
+    lax.fori_loop(0, width // LANES, tile_step, 0, unroll=width // LANES)
 
 
 def spread_spec(chunk, count, seqs, part, at):
@@ -178,7 +178,7 @@
             state_ref[n, :, lanes] = h[n]
         return 0
 
-    lax.fori_loop(0, width // LANES, tile_step, 0, unroll=4)
+    lax.fori_loop(0, width // LANES, tile_step, 0, unroll=width // LANES)
 
 
 def forward(arrays, skip, carried, filled, shapes, chunk, first, last):
@@ -284,7 +284,7 @@
         skipg_ref[:, lanes] = skipg
         return 0
 
-    lax.fori_loop(0, width // LANES, tile_step, 0, unroll=4)
+    lax.fori_loop(0, width // LANES, tile_step, 0, unroll=width // LANES)
     wide = 2 * span
     row = lax.broadcasted_iota(jnp.int32, (2 * seqs, wide), 0)
     col = lax.broadcasted_iota(jnp.int32, (2 * seqs, wide), 1)
@@ -384,7 +384,7 @@
             sums_ref[k, :, lanes] = sums[k]
         return 0
 
-    lax.fori_loop(0, width // LANES, tile_step, 0, unroll=4)
+    lax.fori_loop(0, width // LANES, tile_step, 0, unroll=width // LANES)
 
     @pl.when(block == 0)
     def _():

time: 430 us -> 427 us (level)
  Pallas kernels: 159 us -> 152 us
  waiting for transfers between devices: 49.7 us -> 55.2 us
    ppermute x32, waiting for transfers between devices: 48.6 us -> 53.2 us  [swapped(): return lax.ppermute(value, axis, [(i, i ^ 1 << bit) for i in range(count)])]
  transfers between devices with their start and end apart: 43 -> 43, of which waited for: 17 -> 18; matrix products, arithmetic and copies ran while one was open for 28% -> 28% of each run, Pallas kernels for 36% -> 35%
where the time goes in v7:
time: 427 us; the launch traced here: 421 us
  Pallas kernels  152 us (36%)
  starting transfers between devices  56.4 us (13%)
  other arithmetic  55.3 us (13%)
  waiting for transfers between devices  55.2 us (13%)
  matrix products  52.1 us (12%)
  local copies, waits for them, and re-layouts  47.3 us (11%)
    ppermute x32, waiting for transfers between devices, swapped(): return lax.ppermute(value, axis, [(i, i ^ 1 << bit) for i in range(count)])  53.2 us
    dot_general x14, matrix products, dot(): return lax.dot_general(a, b, dims, preferred_element_type=out)  52.1 us
    pallas_call x1, Pallas kernels, backward(): pl.pallas_call(functools.partial(bwd_kernel, chunk), grid=(grid,), in_spe...  35.9 us
    ppermute x32, starting transfers between devices, swapped(): return lax.ppermute(value, axis, [(i, i ^ 1 << bit) for i in range(count)])  32.6 us
    pallas_call x2, Pallas kernels, forward(): pl.pallas_call(functools.partial(fwd_kernel, chunk), grid=(last - first,)...  31.1 us
    pallas_call x2, Pallas kernels, product_sides(): pl.pallas_call(functools.partial(product_kernel, len(pairs)), grid_spec=p...  24.1 us
    ppermute x8, starting transfers between devices, moved(): lax.ppermute(value, axis, [(i, i + distance) for i in range(count) if 0 <...  20.3 us
    pallas_call x5, Pallas kernels, merge(): pl.pallas_call(functools.partial(merge_kernel, plan, len(messages)), in_s...  19.4 us
  transfers between devices with their start and end apart: 43, of which 18 were waited for; matrix products, arithmetic and copies ran while one was open for 28% of the time, Pallas kernels for 35%

profile of v7, /device:TPU:0, one launch (start us, length us, event | category | flops | bytes accessed | tf_op | source)
XLA Modules:
  0.0 420.6 jit_solution(10648005756306892377)
XLA Ops:
  6.4 16.3 %fusion.49 = (bf16[2048,1,1024]{2,1,0:T(2,128)(2,1)S(1)}, bf16[2048,1,1024]{2,1,0:T(2,128)(2,1)S(1)}) fusion(bf16[2048,2,1024]{2,1,0:T(2,128)(2,1)} %param.14), kind=kLoop, calls=%fused_computation.190 | loop fusion | bytes 16777216 | tf_op jit(solution)/shard_map/slice | solution.py:794
  22.7 5.9 %copy_bitcast_fusion = (bf16[2048,1024]{1,0:T(8,128)(2,1)}, bf16[2048,1024]{1,0:T(8,128)(2,1)}) fusion(bf16[2048,1,1024]{2,1,0:T(2,128)(2,1)S(1)} %get-tuple-element.374, bf16[2048,1,1024]{2,1,0:T(2,128)(2,1)S(1)} %get-tuple-element.375), kind=kLoop, calls=%fused_computation.16 | loop fusion | bytes 16777216 | tf_op jit(solution)/shard_map/squeeze | solution.py:794
  37.6 4.2 collective-permute-start.3
  41.8 4.7 %fusion.55.in_ref = bf16[1024,1024]{1,0:T(8,128)(2,1)S(1)} fusion(bf16[1024,2048]{1,0:T(8,128)(2,1)S(1)} %fusion.2, bf16[2048,1024]{1,0:T(8,128)(2,1)S(1)} %copy-done.6), kind=kOutput, calls=%fused_computation.196 | convolution fusion | flops 4294967296 | bytes 10485760 | tf_op jit(solution)/shard_map/dot_general | solution.py:508
  48.0 3.8 multiply_convert_fusion
  58.7 4.5 %fusion.56.gate_ref = f32[1024,1024]{1,0:T(8,128)S(1)} fusion(bf16[1024,2048]{1,0:T(8,128)(2,1)S(1)} %fusion.2, bf16[2048,1024]{1,0:T(8,128)(2,1)S(1)} %copy-done.13), kind=kOutput, calls=%fused_computation.197 | convolution fusion | flops 4294967296 | bytes 12582912 | tf_op jit(solution)/shard_map/dot_general | solution.py:508
  67.9 4.7 %bitcast_reduce_fusion = (f32[8,1024]{1,0:T(8,128)S(1)}, f32[1024,1024]{1,0:T(8,128)}) fusion(f32[1024]{0:T(1024)S(1)} %convert_element_type.288, bf16[128,1024]{1,0:T(8,128)(2,1)S(1)} %copy-done.41, f32[160,1024]{1,0:T(8,128)S(1)} %convert_add_fusion.4), kind=kOutput, calls=%fused_computation.18 | convolution fusion | flops 276815872 | bytes 4755456 | tf_op jit(solution)/shard_map/dot_general | solution.py:508
  73.4 18.3 %local_ends.1 = (f32[16,8,1024]{2,1,0:T(8,128)}, f32[128,32,8,128]{3,2,1,0:T(8,128)}, bf16[128,256,128]{2,1,0:T(8,128)(2,1)}) custom-call(f32[1024,1024]{1,0:T(8,128)} %get-tuple-element.437.step_ref, bf16[1024,1024]{1,0:T(8,128)(2,1)} %copy-done, f32[32,1024]{1,0:T(8,128)} %slice.282.rows_ref, f32[16,8,1024]{2,1,0:T(8,128)} %broadcast_in_dim.8.rate_ref), custom_call_target="tpu_custom_call" | custom-call | flops 16777216 | bytes 16777216 | tf_op jit(solution)/shard_map/local_ends/pallas_call | solution.py:105
  100.9 7.1 %multiply_multiply_fusion = (f32[1024,1024]{1,0:T(8,128)}, f32[1024,1024]{1,0:T(8,128)}) fusion(f32[1024,1024]{1,0:T(8,128)S(1)} %fusion.56.gate_ref, bf16[1024,2048]{1,0:T(8,128)(2,1)S(1)} %pad_maximum_fusion.1, bf16[2048,1024]{1,0:T(8,128)(2,1)S(1)} %copy-done.23), kind=kOutput, calls=%fused_computation.22 | convolution fusion | flops 4300210176 | bytes 20971520 | tf_op jit(solution)/shard_map/dot_general | solution.py:508
  108.3 3.5 collective-permute-start.10
  111.8 14.2 %local_starts.1 = f32[16,8,1024]{2,1,0:T(8,128)} custom-call(f32[1024,1024]{1,0:T(8,128)} %get-tuple-element.437.step_ref, f32[1024,1024]{1,0:T(8,128)} %get-tuple-element.187.yg_ref, f32[128,32,8,128]{3,2,1,0:T(8,128)} %get-tuple-element.188.spread_ref, f32[16,8,1024]{2,1,0:T(8,128)} %broadcast_in_dim.8.rate_ref), custom_call_target="tpu_custom_call" | custom-call | flops 16777216 | bytes 16777216 | tf_op jit(solution)/shard_map/local_starts/pallas_call | solution.py:127
  143.8 15.5 %scan_forward.2 = (f32[16,8,1024]{2,1,0:T(8,128)}, bf16[128,8,128,128]{3,2,1,0:T(8,128)(2,1)}, bf16[8,16,8,1024]{3,2,1,0:T(8,128)(2,1)}, bf16[1024,1024]{1,0:T(8,128)(2,1)}, bf16[1024,1024]{1,0:T(8,128)(2,1)}) custom-call(f32[1024,1024]{1,0:T(8,128)} %get-tuple-element.437.step_ref, bf16[1024,1024]{1,0:T(8,128)(2,1)} %copy-done, ...), custom_call_target="tpu_custom_call", output_to_operand_aliasing={{0}: (8, {})} | custom-call | flops 8388608 | bytes 8388608 | tf_op jit(solution)/shard_map/scan_forward/pallas_call | solution.py:193
  161.3 15.6 %scan_forward.3 = (f32[16,8,1024]{2,1,0:T(8,128)}, bf16[128,8,128,128]{3,2,1,0:T(8,128)(2,1)}, bf16[8,16,8,1024]{3,2,1,0:T(8,128)(2,1)}, bf16[1024,1024]{1,0:T(8,128)(2,1)}, bf16[1024,1024]{1,0:T(8,128)(2,1)}) custom-call(f32[1024,1024]{1,0:T(8,128)} %get-tuple-element.437.step_ref, ...), custom_call_target="tpu_custom_call", output_to_operand_aliasing={{0}: (8, {}), {1}: (9, {}), {2}: (10, {}), {3}: (11, {}), {... | custom-call | flops 8388608 | bytes 8388608 | tf_op jit(solution)/shard_map/scan_forward/pallas_call | solution.py:193
  178.4 5.4 %fusion.58 = bf16[1024,1024]{1,0:T(8,128)(2,1)} fusion(bf16[1024,1024]{1,0:T(8,128)(2,1)S(1)} %copy-done.33, bf16[1024,1024]{1,0:T(8,128)(2,1)} %get-tuple-element.231.refs_1_), kind=kOutput, calls=%fused_computation.199 | convolution fusion | flops 2147483648 | bytes 6291456 | tf_op jit(solution)/shard_map/dot_general | solution.py:508
  183.8 3.8 fusion.57
  192.2 3.7 fusion.60.refs_2_
  195.9 3.8 fusion.59.refs_0_
  199.8 35.9 %scan_backward.1 = (f32[18,1024]{1,0:T(8,128)}, bf16[1024,1024]{1,0:T(8,128)(2,1)}, f32[1024,1024]{1,0:T(8,128)}, f32[160,1024]{1,0:T(8,128)}) custom-call(f32[1024,1024]{1,0:T(8,128)} %get-tuple-element.437.step_ref, bf16[1024,1024]{1,0:T(8,128)(2,1)} %copy-done, f32[1024,1024]{1,0:T(8,128)} %get-tuple-element.187.yg_ref, ...), custom_call_target="tpu_custom_call" | custom-call | flops 16777216 | bytes 16777216 | tf_op jit(solution)/shard_map/scan_backward/pallas_call | solution.py:321
  237.3 6.5 %merge_messages.5 = (bf16[512,1024]{1,0:T(8,128)(2,1)}, bf16[512,1024]{1,0:T(8,128)(2,1)}, bf16[512,1024]{1,0:T(8,128)(2,1)}, bf16[512,1024]{1,0:T(8,128)(2,1)}) custom-call(s32[2]{0:T(128)} %get-tuple-element.440.bits_ref, bf16[1024,1024]{1,0:T(8,128)(2,1)} %fusion.59.refs_0_, bf16[1024,1024]{1,0:T(8,128)(2,1)} %collective-permute-done.15.refs_1_, ...), custom_call_target="tpu_custom_call" | custom-call | flops 1024 | bytes 1024 | tf_op jit(solution)/shard_map/merge_messages/pallas_call | solution.py:701
  248.6 9.6 %product_sides.2 = (bf16[2,1024,512]{2,1,0:T(8,128)(2,1)}, bf16[2,1024,512]{2,1,0:T(8,128)(2,1)}) custom-call(s32[1]{0:T(128)} %bitcast.21.core_ref, bf16[1024,1024]{1,0:T(8,128)(2,1)} %get-tuple-element.241.refs_0_, bf16[2048,1024]{1,0:T(8,128)(2,1)} %refs_1_.1), custom_call_target="tpu_custom_call" | custom-call | flops 1024 | bytes 1024 | tf_op jit(solution)/shard_map/product_sides/pallas_call | solution.py:486
  259.0 9.3 %conv_backward.1 = (bf16[1056,1024]{1,0:T(8,128)(2,1)}, f32[24,1024]{1,0:T(8,128)}, f32[5,8,1024]{2,1,0:T(8,128)}) custom-call(bf16[160,1024]{1,0:T(8,128)(2,1)} %add_convert_fusion.2.proj_ref, bf16[160,1024]{1,0:T(8,128)(2,1)} %weight_ref.1, f32[1024,1024]{1,0:T(8,128)} %get-tuple-element.249.part_ref, f32[1024,1024]{1,0:T(8,128)} %get-tuple-element.373.conv_ref, ...), custom_call_target="tpu_custom_call" | custom-call | flops 1048576 | bytes 1048576 | tf_op jit(solution)/shard_map/conv_backward/pallas_call | solution.py:415
  271.1 4.7 %fusion.16 = bf16[2048,512]{1,0:T(8,128)(2,1)S(1)} fusion(bf16[1056,2048]{1,0:T(8,128)(2,1)S(1)} %bitcast.165, bf16[1056,1024]{1,0:T(8,128)(2,1)} %get-tuple-element.264), kind=kOutput, calls=%fused_computation.47 | convolution fusion | flops 2214592512 | bytes 7503872 | tf_op jit(solution)/shard_map/dot_general | solution.py:508
  275.8 5.5 %fusion.18 = bf16[2048,512]{1,0:T(8,128)(2,1)S(1)} fusion(bf16[1056,2048]{1,0:T(8,128)(2,1)} %copy-done.66, bf16[1056,1024]{1,0:T(8,128)(2,1)S(1)} %copy-done.34), kind=kOutput, calls=%fused_computation.49 | convolution fusion | flops 2214592512 | bytes 7503872 | tf_op jit(solution)/shard_map/dot_general | solution.py:508
  284.4 4.1 merge_messages.6
  307.4 14.5 %product_sides.3 = (bf16[2,1024,512]{2,1,0:T(8,128)(2,1)}, bf16[2,1024,512]{2,1,0:T(8,128)(2,1)}) custom-call(s32[1]{0:T(128)} %bitcast.21.core_ref, bf16[1024,1024]{1,0:T(8,128)(2,1)} %pad_maximum_fusion.6.refs_0_, bf16[1024,1024]{1,0:T(8,128)(2,1)} %get-tuple-element.231.refs_1_, bf16[2048,1024]{1,0:T(8,128)(2,1)} %get-tuple-element.175.refs_2_, ...), custom_call_target="tpu_custom_call" | custom-call | flops 1024 | bytes 1024 | tf_op jit(solution)/shard_map/product_sides/pallas_call | solution.py:486
  322.0 8.6 %collective-permute-done.24.refs_3_ = bf16[1024,512]{1,0:T(8,128)(2,1)} collective-permute-done((bf16[1024,512]{1,0:T(8,128)(2,1)}, bf16[1024,512]{1,0:T(8,128)(2,1)}, u32[]{:S(2)}, u32[]{:S(2)}) %collective-permute-start.24) | collective-permute-done | bytes 1048608 | tf_op jit(solution)/shard_map/ppermute | solution.py:517
  334.5 3.9 merge_messages.7
  346.7 13.4 %collective-permute-done.26 = bf16[1024,512]{1,0:T(8,128)(2,1)} collective-permute-done((bf16[1024,512]{1,0:T(8,128)(2,1)}, bf16[1024,512]{1,0:T(8,128)(2,1)}, u32[]{:S(2)}, u32[]{:S(2)}) %collective-permute-start.26) | collective-permute-done | bytes 1048608 | tf_op jit(solution)/shard_map/ppermute | solution.py:517
  365.2 6.3 %collective-permute-done.31.refs_5_ = bf16[416,512]{1,0:T(8,128)(2,1)} collective-permute-done((bf16[416,512]{1,0:T(8,128)(2,1)}, bf16[416,512]{1,0:T(8,128)(2,1)}, u32[]{:S(2)}, u32[]{:S(2)}) %collective-permute-start.31) | collective-permute-done | bytes 426016 | tf_op jit(solution)/shard_map/ppermute | solution.py:517
  382.3 4.5 %fusion.12 = (f32[512]{0:T(512)S(1)}, bf16[128,8,512]{2,1,0:T(8,128)(2,1)S(1)}, bf16[128,8,512]{2,1,0:T(8,128)(2,1)S(1)}) fusion(bf16[1024,512]{1,0:T(8,128)(2,1)} %collective-permute-done.36, f32[1024]{0:T(1024)S(1)} %copy-done.55, bf16[2,1024,512]{2,1,0:T(8,128)(2,1)S(1)} %copy-done.17, s32[]{:T(128)S(6)} %select_n.192, ...), kind=kLoop, calls=%fused_computation.33 | loop fusion | flops 10485248 | bytes 8404996 | tf_op jit(solution)/shard_map/reduce_sum | solution.py:965
  388.1 6.4 %collective-permute-done.33 = bf16[256,512]{1,0:T(8,128)(2,1)S(1)} collective-permute-done((bf16[256,512]{1,0:T(8,128)(2,1)}, bf16[256,512]{1,0:T(8,128)(2,1)S(1)}, u32[]{:S(2)}, u32[]{:S(2)}) %collective-permute-start.33) | collective-permute-done | bytes 262176 | tf_op jit(solution)/shard_map/ppermute | solution.py:517
  394.5 5.5 %collective-permute-done.34 = bf16[256,512]{1,0:T(8,128)(2,1)S(1)} collective-permute-done((bf16[256,512]{1,0:T(8,128)(2,1)}, bf16[256,512]{1,0:T(8,128)(2,1)S(1)}, u32[]{:S(2)}, u32[]{:S(2)}) %collective-permute-start.34) | collective-permute-done | bytes 262176 | tf_op jit(solution)/shard_map/ppermute | solution.py:517
  (329 shorter events, 144.9 us)
Async XLA Ops:
  3.4 26.3 %collective-permute-start = (bf16[1024,512]{1,0:T(8,128)(2,1)}, bf16[1024,512]{1,0:T(8,128)(2,1)S(1)}, u32[]{:S(2)}, u32[]{:S(2)}) collective-permute-start(bf16[1024,512]{1,0:T(8,128)(2,1)} %bitcast.129), channel_id=1, source_target_pairs={{0,2},{1,3},{2,0},{3,1},{4,6},{5,7},{6,4},{7,5},{8,10},{9,11},{10,... | collective-permute-start | bytes 3145736 | tf_op jit(solution)/shard_map/ppermute | solution.py:517
  6.4 23.5 %collective-permute-start.2 = (bf16[1024,512]{1,0:T(8,128)(2,1)}, bf16[1024,512]{1,0:T(8,128)(2,1)S(1)}, u32[]{:S(2)}, u32[]{:S(2)}) collective-permute-start(bf16[1024,512]{1,0:T(8,128)(2,1)} %bitcast.129), channel_id=1, source_target_pairs={{0,1},{1,0},{2,3},{3,2},{4,5},{5,4},{6,7},{7,6},{8,9},{9,8},{10,11... | collective-permute-start | bytes 3145736 | tf_op jit(solution)/shard_map/ppermute | solution.py:517
  37.6 8.9 %collective-permute-start.3 = (bf16[32,2048]{1,0:T(8,128)(2,1)S(1)}, bf16[32,2048]{1,0:T(8,128)(2,1)S(1)}, u32[]{:S(2)}, u32[]{:S(2)}) collective-permute-start(bf16[32,2048]{1,0:T(8,128)(2,1)S(1)} %slice.272), channel_id=1, source_target_pairs={{0,4},{4,8},{8,12},{12,16},{16,20},{20,24},{24,28},{1,5},{5,9},{9,... | collective-permute-start | bytes 393224 | tf_op jit(solution)/shard_map/ppermute | solution.py:522
  55.6 9.8 %collective-permute-start.5 = (bf16[160,1024]{1,0:T(8,128)(2,1)S(1)}, bf16[160,1024]{1,0:T(8,128)(2,1)S(1)}, u32[]{:S(2)}, u32[]{:S(2)}) collective-permute-start(bf16[160,1024]{1,0:T(8,128)(2,1)S(1)} %get-tuple-element.370), channel_id=1, source_target_pairs={{0,2},{1,3},{2,0},{3,1},{4,6},{5,7},{6,4},{7,5},{8,10},{9,11},{10,... | collective-permute-start | bytes 983048 | tf_op jit(solution)/shard_map/ppermute | solution.py:517
  65.4 26.2 %collective-permute-start.7 = (bf16[1024,512]{1,0:T(8,128)(2,1)S(1)}, bf16[1024,512]{1,0:T(8,128)(2,1)S(1)}, u32[]{:S(2)}, u32[]{:S(2)}) collective-permute-start(bf16[1024,512]{1,0:T(8,128)(2,1)S(1)} %bitcast.137), channel_id=1, source_target_pairs={{0,2},{1,3},{2,0},{3,1},{4,6},{5,7},{6,4},{7,5},{8,10},{9,11},{10,... | collective-permute-start | bytes 3145736 | tf_op jit(solution)/shard_map/ppermute | solution.py:517
  67.0 29.8 %collective-permute-start.9 = (bf16[1024,512]{1,0:T(8,128)(2,1)S(1)}, bf16[1024,512]{1,0:T(8,128)(2,1)}, u32[]{:S(2)}, u32[]{:S(2)}) collective-permute-start(bf16[1024,512]{1,0:T(8,128)(2,1)S(1)} %bitcast.138), channel_id=1, source_target_pairs={{0,1},{1,0},{2,3},{3,2},{4,5},{5,4},{6,7},{7,6},{8,9},{9,8},{10,11... | collective-permute-start | bytes 3145736 | tf_op jit(solution)/shard_map/ppermute | solution.py:517
  93.3 14.7 %collective-permute-start.6 = (bf16[18,8,1024]{2,1,0:T(8,128)(2,1)S(1)}, bf16[18,8,1024]{2,1,0:T(8,128)(2,1)S(1)}, u32[]{:S(2)}, u32[]{:S(2)}) collective-permute-start(bf16[18,8,1024]{2,1,0:T(8,128)(2,1)S(1)} %pad_maximum_fusion.10), channel_id=1, source_target_pairs={{0,4},{4,8},{8,12},{12,16},{16,20},{20,24},{24,28},{1,5},{5,9},{9,... | collective-permute-start | bytes 884744 | tf_op jit(solution)/shard_map/ppermute | solution.py:522
  108.3 17.7 %collective-permute-start.10 = (bf16[18,8,1024]{2,1,0:T(8,128)(2,1)S(1)}, bf16[18,8,1024]{2,1,0:T(8,128)(2,1)S(1)}, u32[]{:S(2)}, u32[]{:S(2)}) collective-permute-start(bf16[18,8,1024]{2,1,0:T(8,128)(2,1)S(1)} %pad_maximum_fusion.13), channel_id=1, source_target_pairs={{0,8},{4,12},{8,16},{12,20},{16,24},{20,28},{1,9},{5,13},{9,17},{1... | collective-permute-start | bytes 884744 | tf_op jit(solution)/shard_map/ppermute | solution.py:522
  126.4 13.7 %collective-permute-start.11 = (bf16[18,8,1024]{2,1,0:T(8,128)(2,1)S(1)}, bf16[18,8,1024]{2,1,0:T(8,128)(2,1)S(1)}, u32[]{:S(2)}, u32[]{:S(2)}) collective-permute-start(bf16[18,8,1024]{2,1,0:T(8,128)(2,1)S(1)} %pad_maximum_fusion.14), channel_id=1, source_target_pairs={{0,16},{4,20},{8,24},{12,28},{1,17},{5,21},{9,25},{13,29},{2,18},{... | collective-permute-start | bytes 884744 | tf_op jit(solution)/shard_map/ppermute | solution.py:522
  131.0 10.6 %collective-permute-start.12 = (bf16[18,8,1024]{2,1,0:T(8,128)(2,1)S(1)}, bf16[18,8,1024]{2,1,0:T(8,128)(2,1)S(1)}, u32[]{:S(2)}, u32[]{:S(2)}) collective-permute-start(bf16[18,8,1024]{2,1,0:T(8,128)(2,1)S(1)} %pad_maximum_fusion.9), channel_id=1, source_target_pairs={{4,0},{8,4},{12,8},{16,12},{20,16},{24,20},{28,24},{5,1},{9,5},{13... | collective-permute-start | bytes 884744 | tf_op jit(solution)/shard_map/ppermute | solution.py:522
  141.8 17.4 %collective-permute-start.13 = (bf16[18,8,1024]{2,1,0:T(8,128)(2,1)S(1)}, bf16[18,8,1024]{2,1,0:T(8,128)(2,1)S(1)}, u32[]{:S(2)}, u32[]{:S(2)}) collective-permute-start(bf16[18,8,1024]{2,1,0:T(8,128)(2,1)S(1)} %pad_maximum_fusion.15), channel_id=1, source_target_pairs={{8,0},{12,4},{16,8},{20,12},{24,16},{28,20},{9,1},{13,5},{17,9},{2... | collective-permute-start | bytes 884744 | tf_op jit(solution)/shard_map/ppermute | solution.py:522
  159.7 18.7 %collective-permute-start.14 = (bf16[18,8,1024]{2,1,0:T(8,128)(2,1)S(1)}, bf16[18,8,1024]{2,1,0:T(8,128)(2,1)S(1)}, u32[]{:S(2)}, u32[]{:S(2)}) collective-permute-start(bf16[18,8,1024]{2,1,0:T(8,128)(2,1)S(1)} %pad_maximum_fusion.16), channel_id=1, source_target_pairs={{16,0},{20,4},{24,8},{28,12},{17,1},{21,5},{25,9},{29,13},{18,2},{... | collective-permute-start | bytes 884744 | tf_op jit(solution)/shard_map/ppermute | solution.py:522
  188.6 47.0 %collective-permute-start.15 = (bf16[1024,1024]{1,0:T(8,128)(2,1)}, bf16[1024,1024]{1,0:T(8,128)(2,1)}, u32[]{:S(2)}, u32[]{:S(2)}) collective-permute-start(bf16[1024,1024]{1,0:T(8,128)(2,1)} %fusion.57), channel_id=1, source_target_pairs={{0,4},{4,0},{8,12},{12,8},{16,20},{20,16},{24,28},{28,24},{1,5},{5... | collective-permute-start | bytes 6291464 | tf_op jit(solution)/shard_map/ppermute | solution.py:517
  189.6 47.1 %collective-permute-start.16 = (bf16[1024,1024]{1,0:T(8,128)(2,1)}, bf16[1024,1024]{1,0:T(8,128)(2,1)}, u32[]{:S(2)}, u32[]{:S(2)}) collective-permute-start(bf16[1024,1024]{1,0:T(8,128)(2,1)} %fusion.58), channel_id=1, source_target_pairs={{0,8},{4,12},{8,0},{12,4},{16,24},{20,28},{24,16},{28,20},{1,9},{5... | collective-permute-start | bytes 6291464 | tf_op jit(solution)/shard_map/ppermute | solution.py:517
  243.8 25.9 %collective-permute-start.19 = (bf16[512,1024]{1,0:T(8,128)(2,1)}, bf16[512,1024]{1,0:T(8,128)(2,1)}, u32[]{:S(2)}, u32[]{:S(2)}) collective-permute-start(bf16[512,1024]{1,0:T(8,128)(2,1)} %get-tuple-element.246), channel_id=1, source_target_pairs={{0,8},{4,12},{8,0},{12,4},{16,24},{20,28},{24,16},{28,20},{1,9},{5... | collective-permute-start | bytes 3145736 | tf_op jit(solution)/shard_map/ppermute | solution.py:517
  245.5 25.6 %collective-permute-start.20 = (bf16[512,1024]{1,0:T(8,128)(2,1)}, bf16[512,1024]{1,0:T(8,128)(2,1)}, u32[]{:S(2)}, u32[]{:S(2)}) collective-permute-start(bf16[512,1024]{1,0:T(8,128)(2,1)} %get-tuple-element.247), channel_id=1, source_target_pairs={{0,4},{4,0},{8,12},{12,8},{16,20},{20,16},{24,28},{28,24},{1,5},{5... | collective-permute-start | bytes 3145736 | tf_op jit(solution)/shard_map/ppermute | solution.py:517
  247.4 10.7 %collective-permute-start.18 = (bf16[160,1024]{1,0:T(8,128)(2,1)}, bf16[160,1024]{1,0:T(8,128)(2,1)S(1)}, u32[]{:S(2)}, u32[]{:S(2)}) collective-permute-start(bf16[160,1024]{1,0:T(8,128)(2,1)} %get-tuple-element.360), channel_id=1, source_target_pairs={{0,2},{1,3},{2,0},{3,1},{4,6},{5,7},{6,4},{7,5},{8,10},{9,11},{10,... | collective-permute-start | bytes 983048 | tf_op jit(solution)/shard_map/ppermute | solution.py:517
  268.3 16.1 %collective-permute-start.22 = (f32[24,1024]{1,0:T(8,128)}, f32[24,1024]{1,0:T(8,128)S(1)}, u32[]{:S(2)}, u32[]{:S(2)}) collective-permute-start(f32[24,1024]{1,0:T(8,128)} %get-tuple-element.262), channel_id=1, source_target_pairs={{4,0},{8,4},{12,8},{16,12},{20,16},{24,20},{28,24},{5,1},{9,5},{13... | collective-permute-start | bytes 294920 | tf_op jit(solution)/shard_map/ppermute | solution.py:522
  288.5 42.1 %collective-permute-start.21 = (bf16[2,1024,512]{2,1,0:T(8,128)(2,1)}, bf16[2,1024,512]{2,1,0:T(8,128)(2,1)}, u32[]{:S(2)}, u32[]{:S(2)}) collective-permute-start(bf16[2,1024,512]{2,1,0:T(8,128)(2,1)} %get-tuple-element.252), channel_id=1, source_target_pairs={{0,1},{1,0},{2,3},{3,2},{4,5},{5,4},{6,7},{7,6},{8,9},{9,8},{10,11... | collective-permute-start | bytes 6291464 | tf_op jit(solution)/shard_map/ppermute | solution.py:517
  290.6 31.4 %collective-permute-start.25 = (bf16[256,1024]{1,0:T(8,128)(2,1)}, bf16[256,1024]{1,0:T(8,128)(2,1)}, u32[]{:S(2)}, u32[]{:S(2)}) collective-permute-start(bf16[256,1024]{1,0:T(8,128)(2,1)} %get-tuple-element.268), channel_id=1, source_target_pairs={{0,16},{4,20},{8,24},{12,28},{16,0},{20,4},{24,8},{28,12},{1,17},{... | collective-permute-start | bytes 1572872 | tf_op jit(solution)/shard_map/ppermute | solution.py:517
  293.9 28.1 %collective-permute-start.23 = (bf16[1024,512]{1,0:T(8,128)(2,1)}, bf16[1024,512]{1,0:T(8,128)(2,1)}, u32[]{:S(2)}, u32[]{:S(2)}) collective-permute-start(bf16[1024,512]{1,0:T(8,128)(2,1)} %bitcast.148), channel_id=1, source_target_pairs={{0,4},{4,0},{8,12},{12,8},{16,20},{20,16},{24,28},{28,24},{1,5},{5... | collective-permute-start | bytes 3145736 | tf_op jit(solution)/shard_map/ppermute | solution.py:517
  295.1 35.5 %collective-permute-start.24 = (bf16[1024,512]{1,0:T(8,128)(2,1)}, bf16[1024,512]{1,0:T(8,128)(2,1)}, u32[]{:S(2)}, u32[]{:S(2)}) collective-permute-start(bf16[1024,512]{1,0:T(8,128)(2,1)} %bitcast.147), channel_id=1, source_target_pairs={{0,8},{4,12},{8,0},{12,4},{16,24},{20,28},{24,16},{28,20},{1,9},{5... | collective-permute-start | bytes 3145736 | tf_op jit(solution)/shard_map/ppermute | solution.py:517
  333.8 26.3 %collective-permute-start.26 = (bf16[1024,512]{1,0:T(8,128)(2,1)}, bf16[1024,512]{1,0:T(8,128)(2,1)}, u32[]{:S(2)}, u32[]{:S(2)}) collective-permute-start(bf16[1024,512]{1,0:T(8,128)(2,1)} %dynamic-slice_bitcast_fusion.1), channel_id=1, source_target_pairs={{0,2},{1,3},{2,0},{3,1},{4,6},{5,7},{6,4},{7,5},{8,10},{9,11},{10,... | collective-permute-start | bytes 3145736 | tf_op jit(solution)/shard_map/ppermute | solution.py:517
  342.5 39.7 %collective-permute-start.36 = (bf16[1024,512]{1,0:T(8,128)(2,1)}, bf16[1024,512]{1,0:T(8,128)(2,1)}, u32[]{:S(2)}, u32[]{:S(2)}) collective-permute-start(bf16[1024,512]{1,0:T(8,128)(2,1)} %dynamic-slice_bitcast_fusion), channel_id=1, source_target_pairs={{0,2},{1,3},{2,0},{3,1},{4,6},{5,7},{6,4},{7,5},{8,10},{9,11},{10,... | collective-permute-start | bytes 3145736 | tf_op jit(solution)/shard_map/ppermute | solution.py:517
  343.9 27.6 %collective-permute-start.29 = (bf16[512,512]{1,0:T(8,128)(2,1)}, bf16[512,512]{1,0:T(8,128)(2,1)}, u32[]{:S(2)}, u32[]{:S(2)}) collective-permute-start(bf16[512,512]{1,0:T(8,128)(2,1)} %get-tuple-element.298), channel_id=1, source_target_pairs={{0,8},{4,12},{8,0},{12,4},{16,24},{20,28},{24,16},{28,20},{1,9},{5... | collective-permute-start | bytes 1572872 | tf_op jit(solution)/shard_map/ppermute | solution.py:517
  344.4 27.1 %collective-permute-start.30 = (bf16[512,512]{1,0:T(8,128)(2,1)}, bf16[512,512]{1,0:T(8,128)(2,1)}, u32[]{:S(2)}, u32[]{:S(2)}) collective-permute-start(bf16[512,512]{1,0:T(8,128)(2,1)} %get-tuple-element.299), channel_id=1, source_target_pairs={{0,4},{4,0},{8,12},{12,8},{16,20},{20,16},{24,28},{28,24},{1,5},{5... | collective-permute-start | bytes 1572872 | tf_op jit(solution)/shard_map/ppermute | solution.py:517
  345.8 26.0 %collective-permute-start.32 = (bf16[256,1024]{1,0:T(8,128)(2,1)}, bf16[256,1024]{1,0:T(8,128)(2,1)}, u32[]{:S(2)}, u32[]{:S(2)}) collective-permute-start(bf16[256,1024]{1,0:T(8,128)(2,1)} %get-tuple-element.301), channel_id=1, source_target_pairs={{0,16},{4,20},{8,24},{12,28},{16,0},{20,4},{24,8},{28,12},{1,17},{... | collective-permute-start | bytes 1572872 | tf_op jit(solution)/shard_map/ppermute | solution.py:517
  360.1 11.5 %collective-permute-start.31 = (bf16[416,512]{1,0:T(8,128)(2,1)}, bf16[416,512]{1,0:T(8,128)(2,1)}, u32[]{:S(2)}, u32[]{:S(2)}) collective-permute-start(bf16[416,512]{1,0:T(8,128)(2,1)} %pad_maximum_fusion.8), channel_id=1, source_target_pairs={{0,4},{4,0},{8,12},{12,8},{16,20},{20,16},{24,28},{28,24},{1,5},{5... | collective-permute-start | bytes 1277960 | tf_op jit(solution)/shard_map/ppermute | solution.py:517
  376.1 18.4 %collective-permute-start.33 = (bf16[256,512]{1,0:T(8,128)(2,1)}, bf16[256,512]{1,0:T(8,128)(2,1)S(1)}, u32[]{:S(2)}, u32[]{:S(2)}) collective-permute-start(bf16[256,512]{1,0:T(8,128)(2,1)} %get-tuple-element.311), channel_id=1, source_target_pairs={{0,16},{4,20},{8,24},{12,28},{16,0},{20,4},{24,8},{28,12},{1,17},{... | collective-permute-start | bytes 786440 | tf_op jit(solution)/shard_map/ppermute | solution.py:517
  376.4 23.7 %collective-permute-start.34 = (bf16[256,512]{1,0:T(8,128)(2,1)}, bf16[256,512]{1,0:T(8,128)(2,1)S(1)}, u32[]{:S(2)}, u32[]{:S(2)}) collective-permute-start(bf16[256,512]{1,0:T(8,128)(2,1)} %get-tuple-element.312), channel_id=1, source_target_pairs={{0,16},{4,20},{8,24},{12,28},{16,0},{20,4},{24,8},{28,12},{1,17},{... | collective-permute-start | bytes 786440 | tf_op jit(solution)/shard_map/ppermute | solution.py:517
  379.0 21.0 %collective-permute-start.35 = (bf16[256,512]{1,0:T(8,128)(2,1)}, bf16[256,512]{1,0:T(8,128)(2,1)S(1)}, u32[]{:S(2)}, u32[]{:S(2)}) collective-permute-start(bf16[256,512]{1,0:T(8,128)(2,1)} %get-tuple-element.313), channel_id=1, source_target_pairs={{0,8},{4,12},{8,0},{12,4},{16,24},{20,28},{24,16},{28,20},{1,9},{5... | collective-permute-start | bytes 786440 | tf_op jit(solution)/shard_map/ppermute | solution.py:517
  406.2 11.0 %collective-permute-start.42 = (bf16[176,512]{1,0:T(8,128)(2,1)}, bf16[176,512]{1,0:T(8,128)(2,1)S(1)}, u32[]{:S(2)}, u32[]{:S(2)}) collective-permute-start(bf16[176,512]{1,0:T(8,128)(2,1)} %get-tuple-element.332), channel_id=1, source_target_pairs={{0,16},{4,20},{8,24},{12,28},{16,0},{20,4},{24,8},{28,12},{1,17},{... | collective-permute-start | bytes 540680 | tf_op jit(solution)/shard_map/ppermute | solution.py:517
  (82 other events, 832.7 us)
